TPU v7x, 32 devices: a whole 2x2x4 slice. The times are simulated.
32 devices in a mesh: seq: 8 (over z, y), ch: 4 (over x, core).
Axes of the slice: x: 2, y: 2, z: 4, core: 2. Of those that a mesh axis runs over, the one named last changes fastest.
Arguments:
- queries: bfloat16 [8192, 8192], P('seq', 'ch'), may hold values from -6 to 6
- keys: bfloat16 [8192, 8192], P('seq', 'ch'), may hold values from -6 to 6
- values: bfloat16 [8192, 8192], P('seq', 'ch'), may hold values from -6 to 6
- filters: bfloat16 [512, 128], P('ch'), may hold values from -0.5 to 0.5
- grad_out: bfloat16 [8192, 4096], P('seq', 'ch'), may hold values from -6 to 6
- out_weight: bfloat16 [4096, 8192], P('seq', 'ch'), may hold values from -0.09375 to 0.09375
Outputs:
- grad_queries: bfloat16 [8192, 8192], P('seq', 'ch')
- grad_keys: bfloat16 [8192, 8192], P('seq', 'ch')
- grad_values: bfloat16 [8192, 8192], P('seq', 'ch')
- grad_filters: float32 [512, 128], P('ch', 'seq')
- grad_weight: bfloat16 [4096, 8192], P('seq', 'ch')
All inputs are finite; a program needn't handle non-finite values.
Results may differ from a plain program's by a relative error of at most 0.022.
Values may be sent and summed in bfloat16 or wider, within the bound.
No kernel may reach another device: no remote copies, remote signals or barrier semaphores. Data moves between devices by JAX's collectives and lax.ppermute only.
A program may use at most 192 MiB of HBM per device.

v0:
```python
import jax
import jax.numpy as jnp
from jax import lax
from jax.sharding import PartitionSpec as P

GROUP = 16
FILT = 128


def from_behind(x, axis, by):
    size = lax.axis_size(axis)
    pairs = [(i, i + by) for i in range(size) if 0 <= i + by < size]
    return lax.ppermute(x, axis, pairs)


def lag_tables(filter_taps):
    taps = jnp.arange(FILT, dtype=jnp.int32)[:, None, None]
    inner = jnp.arange(FILT, dtype=jnp.int32)[None, :, None]
    outer = jnp.arange(2 * FILT, dtype=jnp.int32)[None, None, :]
    back_pick = (inner + FILT - outer == taps).astype(filter_taps.dtype)
    ahead_pick = (outer - inner == taps).astype(filter_taps.dtype)
    back = jnp.einsum(
        "gj,jim->gim", filter_taps, back_pick, preferred_element_type=jnp.float32
    ).astype(filter_taps.dtype)
    ahead = jnp.einsum(
        "gj,jim->gim", filter_taps, ahead_pick, preferred_element_type=jnp.float32
    ).astype(filter_taps.dtype)
    return (back, ahead)


def paired(extended, groups):
    blocks = extended.reshape(-1, FILT, groups, GROUP)
    return jnp.concatenate([blocks[:-1], blocks[1:]], axis=1)


def lag_sums(lag_matrix):
    groups, inner, outer = lag_matrix.shape
    flat = lag_matrix.reshape(groups, inner * outer)
    flat = jnp.pad(flat, ((0, 0), (0, inner)))
    skewed = flat.reshape(groups, inner, outer + 1)
    return jnp.sum(skewed[:, :, 1 : inner + 1], axis=1)[:, ::-1]


def shards(queries, keys, values, filters, grad_out, out_weight):
    single = jnp.float32
    local_rows, width = queries.shape
    groups = width // GROUP
    nblocks = local_rows // FILT
    product = (keys.astype(single) * values.astype(single)).astype(jnp.bfloat16)
    prior = from_behind(product[local_rows - FILT + 1 :], "seq", 1)
    extended = jnp.concatenate([jnp.zeros((1, width), jnp.bfloat16), prior, product], axis=0)
    pairs = paired(extended, groups)
    back, ahead = lag_tables(filters)
    mixed = jnp.einsum("gim,bmgs->bigs", back, pairs, preferred_element_type=single).reshape(
        local_rows, width
    )
    gated = (queries.astype(single) * mixed).astype(jnp.bfloat16)
    full_cot = lax.all_gather(grad_out, "ch", axis=1, tiled=True)
    columns = full_cot
    grad_gated = jnp.dot(
        columns,
        lax.all_gather(out_weight, "seq", axis=0, tiled=True),
        preferred_element_type=single,
    )
    grad_gated = grad_gated.astype(jnp.bfloat16)
    grad_queries = (grad_gated.astype(single) * mixed).astype(jnp.bfloat16)
    grad_mixed = (grad_gated.astype(single) * queries.astype(single)).astype(jnp.bfloat16)
    later = from_behind(grad_mixed[: FILT - 1], "seq", -1)
    grad_ext = jnp.concatenate([grad_mixed, later, jnp.zeros((1, width), jnp.bfloat16)], axis=0)
    grad_pairs = paired(grad_ext, groups)
    grad_product = jnp.einsum(
        "gim,bmgs->bigs", ahead, grad_pairs, preferred_element_type=single
    ).reshape(local_rows, width)
    grad_keys = (grad_product * values.astype(single)).astype(jnp.bfloat16)
    grad_values = (grad_product * keys.astype(single)).astype(jnp.bfloat16)
    own_blocks = grad_mixed.reshape(nblocks, FILT, groups, GROUP)
    lag_matrix = jnp.einsum("bigs,bmgs->gim", own_blocks, pairs, preferred_element_type=single)
    filter_part = lag_sums(lag_matrix)
    grad_filters = lax.psum_scatter(
        filter_part.astype(jnp.bfloat16), "seq", scatter_dimension=1, tiled=True
    ).astype(jnp.float32)
    columns = full_cot
    grad_weight = lax.psum_scatter(
        jnp.dot(columns.T, gated, preferred_element_type=single).astype(jnp.bfloat16),
        "seq",
        scatter_dimension=0,
        tiled=True,
    )
    return (grad_queries, grad_keys, grad_values, grad_filters, grad_weight)


def solution(mesh):
    return jax.shard_map(
        shards,
        mesh=mesh,
        in_specs=(
            P("seq", "ch"),
            P("seq", "ch"),
            P("seq", "ch"),
            P("ch", None),
            P("seq", "ch"),
            P("seq", "ch"),
        ),
        out_specs=(P("seq", "ch"), P("seq", "ch"), P("seq", "ch"), P("ch", "seq"), P("seq", "ch")),
        check_vma=False,
    )
```

profile of v0, /device:TPU:10, one launch (start us, length us, event | category | flops | bytes accessed | tf_op | source)
XLA Modules:
  0.0 955.7 jit_solution(4183750484766296470)
XLA Ops:
  7.2 0.0 copy-start
  7.2 0.0 all-gather.3.cloned.1.call-start
  7.2 0.7 all-gather.3.cloned.1.call-update
  7.9 0.0 all-gather.5.cloned.1.call-start
  8.0 0.7 all-gather.5.cloned.1.call-update
  8.7 0.0 reduce-scatter.3.cloned.1.call-start
  8.7 0.1 iota_subtract_fusion.1
  8.8 4.5 iota_compare_fusion
  13.3 4.5 iota_compare_fusion.1
  17.8 50.3 %all-gather.3.cloned.1.call-done = bf16[1024,4096]{1,0:T(8,128)(2,1)} async-done(((bf16[1024,1024]{1,0:T(8,128)(2,1)}), bf16[1024,4096]{1,0:T(8,128)(2,1)}) %all-gather.3.cloned.1.call-update) | async-done | bytes 8388624 | tf_op jit(solution)/shard_map/all_gather | solution.py:58
  68.1 228.8 %all-gather.5.cloned.1.call-done = bf16[4096,2048]{1,0:T(8,128)(2,1)} async-done(((bf16[512,2048]{1,0:T(8,128)(2,1)}), bf16[4096,2048]{1,0:T(8,128)(2,1)}) %all-gather.5.cloned.1.call-update) | async-done | bytes 16777232 | tf_op jit(solution)/shard_map/all_gather | solution.py:62
  297.0 24.1 %fusion.8 = (bf16[1024,2048]{1,0:T(8,128)(2,1)S(1)}, bf16[1024,2048]{1,0:T(8,128)(2,1)}) fusion(bf16[1024,2048]{1,0:T(8,128)(2,1)} %param.6, bf16[1024,4096]{1,0:T(8,128)(2,1)} %all-gather.3.cloned.1.call-done, bf16[4096,2048]{1,0:T(8,128)(2,1)} %all-gather.5.cloned.1.call-done), kind=kOutput, calls=%fused_computation.18 | convolution fusion | flops 17190354944 | bytes 37748736 | tf_op jit(solution)/shard_map/dot_general | solution.py:60
  321.1 2.0 copy-done.4
  323.1 4.5 collective-permute-start.1
  327.6 14.3 %fusion = bf16[128,256,128]{2,1,0:T(8,128)(2,1)} fusion(pred[128,128,256]{2,1,0:T(32,128)(4,1)S(1)} %copy-done.8, bf16[128,128]{1,0:T(8,128)(2,1)S(1)} %copy-done), kind=kOutput, calls=%fused_computation.3 | convolution fusion | flops 1073741824 | bytes 12615680 | tf_op jit(solution)/shard_map/gj,jim->gim/dot_general | solution.py:25
  342.0 12.7 %copy.38 = bf16[128,256,128]{1,0,2:T(8,128)(2,1)} copy(bf16[128,256,128]{2,1,0:T(8,128)(2,1)} %fusion) | data formatting | bytes 16777216 | tf_op jit(solution)/shard_map/gj,jim->gim/dot_general | solution.py:25
  354.7 6.4 copy.16
  361.1 6.3 copy.17
  367.5 6.4 copy.23
  373.8 3.3 copy.47
  377.1 1.9 copy-done.3
  379.0 3.3 copy.25
  382.4 0.0 collective-permute-done.1
  382.4 20.6 %concatenate.14 = bf16[1152,2048]{1,0:T(8,128)(2,1)} concatenate(bf16[1024,2048]{1,0:T(8,128)(2,1)} %copy-done.4, bf16[127,2048]{1,0:T(8,128)(2,1)S(1)} %collective-permute-done.1, bf16[1,2048]{1,0:T(2,128)(2,1)S(1)} %broadcast.32), dimensions={0} | concatenate | bytes 9437184 | tf_op jit(solution)/shard_map/concatenate | solution.py:69
  403.0 4.8 slice.41
  407.8 6.8 copy.24
  414.6 3.3 copy.48
  417.9 3.4 copy.26
  421.3 11.4 %fusion.24 = f32[8,128,128,16]{1,3,0,2:T(8,128)} fusion(bf16[128,256,128]{1,0,2:T(8,128)(2,1)} %copy.38, bf16[8,128,128,16]{1,3,0,2:T(8,128)(2,1)} %copy.26, bf16[8,128,128,16]{1,3,0,2:T(8,128)(2,1)} %copy.25), kind=kOutput, calls=%fused_computation.37 | convolution fusion | flops 1090519040 | bytes 25165824 | tf_op jit(solution)/shard_map/gim,bmgs->bigs/dot_general | solution.py:71
  432.7 7.7 copy.27
  440.5 6.8 fusion.5
  447.2 2.0 copy-done.2
  449.2 0.2 slice.38
  449.5 2.1 collective-permute-start
  451.6 16.6 %fusion.2 = bf16[128,256,128]{2,1,0:T(8,128)(2,1)} fusion(pred[128,128,256]{2,1,0:T(32,128)(4,1)} %iota_compare_fusion.1, bf16[128,128]{1,0:T(8,128)(2,1)S(1)} %copy-done), kind=kOutput, calls=%fused_computation.5 | convolution fusion | flops 1073741824 | bytes 12615680 | tf_op jit(solution)/shard_map/gj,jim->gim/dot_general | solution.py:22
  468.2 12.4 %copy.35 = bf16[128,256,128]{1,0,2:T(8,128)(2,1)} copy(bf16[128,256,128]{2,1,0:T(8,128)(2,1)} %fusion.2) | data formatting | bytes 16777216 | tf_op jit(solution)/shard_map/gj,jim->gim/dot_general | solution.py:22
  480.5 5.3 copy.45
  485.8 0.1 broadcast.32.clone
  485.9 8.5 concatenate.12
  494.4 3.1 slice_bitcast_fusion
  497.6 1.1 copy.44
  498.7 3.4 copy_dynamic-update-slice_fusion.1
  502.1 3.4 copy_dynamic-update-slice_fusion
  505.6 14.0 %convolution_bitcast_fusion = f32[128,128,256]{2,1,0:T(8,128)} fusion(bf16[8,128,128,16]{1,0,3,2:T(8,128)(2,1)} %bitcast.78, bf16[8,256,128,16]{1,3,0,2:T(8,128)(2,1)} %copy_dynamic-update-slice_fusion), kind=kOutput, calls=%fused_computation.13 | convolution fusion | flops 1073741824 | bytes 29360128 | tf_op jit(solution)/shard_map/bigs,bmgs->gim/dot_general | solution.py:77
  519.5 11.3 %fusion.21 = f32[8,128,128,16]{1,3,0,2:T(8,128)} fusion(bf16[8,256,128,16]{1,3,0,2:T(8,128)(2,1)} %copy_dynamic-update-slice_fusion, bf16[128,256,128]{1,0,2:T(8,128)(2,1)} %copy.35), kind=kOutput, calls=%fused_computation.36 | convolution fusion | flops 1073741824 | bytes 25165824 | tf_op jit(solution)/shard_map/gim,bmgs->bigs/dot_general | solution.py:54
  530.9 7.7 copy.21
  538.6 5.3 copy.61
  543.8 9.2 copy.22
  553.1 17.9 %copy.43 = f32[128,128,256]{0,2,1:T(8,128)} copy(f32[128,128,256]{2,1,0:T(8,128)} %convolution_bitcast_fusion) | data formatting | bytes 33554432 | tf_op jit(solution)/shard_map/reshape | solution.py:38
  570.9 13.4 %pad.4 = f32[128,32896]{0,1:T(8,128)} pad(f32[128,32768]{0,1:T(8,128)} %bitcast.75, f32[]{:T(128)} %constant.2.clone.1), padding=0_0x0_128 | pad | bytes 33619972 | tf_op jit(solution)/shard_map/jit(_pad)/pad | solution.py:39
  584.3 17.5 %reshape.75 = f32[128,128,257]{0,2,1:T(8,128)} reshape(f32[128,32896]{0,1:T(8,128)} %pad.4) | data formatting | bytes 33685504 | tf_op jit(solution)/shard_map/reshape | solution.py:40
  601.9 4.4 slice_reduce_fusion
  606.3 0.6 rev.3
  606.9 0.0 reduce-scatter.3.cloned.1.call-update
  607.0 0.0 reduce-scatter.5.cloned.1.call-start
  607.0 26.6 %convert_bitcast_fusion = bf16[4096,2048]{0,1:T(8,128)(2,1)} fusion(bf16[1024,4096]{1,0:T(8,128)(2,1)} %all-gather.3.cloned.1.call-done, f32[1024,2048]{1,0:T(8,128)} %copy.22, bf16[1024,2048]{1,0:T(8,128)(2,1)} %param.6), kind=kOutput, calls=%fused_computation | convolution fusion | flops 17194549248 | bytes 37748736 | tf_op jit(solution)/shard_map/dot_general | solution.py:84
  633.6 0.0 reduce-scatter.5.cloned.1.call-update
  633.7 6.4 copy.32
  640.1 6.4 copy.31
  646.5 8.3 fusion.4
  654.8 6.3 reduce-scatter.3.cloned.1.call-done
  661.2 1.3 convert_element_type.80
  662.4 282.7 %reduce-scatter.5.cloned.1.call-done = bf16[512,2048]{0,1:T(8,128)(2,1)} async-done(((bf16[4096,2048]{0,1:T(8,128)(2,1)}), bf16[512,2048]{0,1:T(8,128)(2,1)}) %reduce-scatter.5.cloned.1.call-update) | async-done | bytes 2097168 | tf_op jit(solution)/shard_map/reduce_scatter | solution.py:83
  945.1 3.9 copy.33
  (19 shorter events, 0.1 us)
Async XLA Ops:
  7.2 320.5 %copy-start = (bf16[128,128]{1,0:T(8,128)(2,1)S(1)}, bf16[128,128]{1,0:T(8,128)(2,1)}, u32[]{:S(2)}) copy-start(bf16[128,128]{1,0:T(8,128)(2,1)} %param.9) | copy-start | bytes 98308
  7.2 60.9 %all-gather.3.cloned.1.call-start = ((), (), s32[]{:S(2)}) async-start(), calls=%async_computation.2 | async-start | bytes 10485760 | tf_op jit(solution)/shard_map/all_gather | solution.py:58
  7.9 289.0 %all-gather.5.cloned.1.call-start = ((), (), s32[]{:S(2)}) async-start(), calls=%async_computation.3 | async-start | bytes 18874368 | tf_op jit(solution)/shard_map/all_gather | solution.py:62
  8.7 652.5 %reduce-scatter.3.cloned.1.call-start = ((), (), s32[]{:S(2)}) async-start(), calls=%async_computation.4 | async-start | bytes 36864 | tf_op jit(solution)/shard_map/reduce_scatter | solution.py:79
  297.0 30.7 %copy-start.8 = (pred[128,128,256]{2,1,0:T(32,128)(4,1)S(1)}, pred[128,128,256]{2,1,0:T(32,128)(4,1)}, u32[]{:S(2)}) copy-start(pred[128,128,256]{2,1,0:T(32,128)(4,1)} %iota_compare_fusion) | copy-start | bytes 12582916
  321.1 2.0 copy-start.4
  323.1 59.3 %collective-permute-start.1 = (bf16[127,2048]{1,0:T(8,128)(2,1)S(1)}, bf16[127,2048]{1,0:T(8,128)(2,1)S(1)}, u32[]{:S(2)}, u32[]{:S(2)}) collective-permute-start(bf16[127,2048]{1,0:T(8,128)(2,1)S(1)} %slice.40), channel_id=1, source_target_pairs={{4,0},{8,4},{12,8},{16,12},{20,16},{24,20},{28,24},{5,1},{9,5},{13... | collective-permute-start | bytes 1560584 | tf_op jit(solution)/shard_map/ppermute | solution.py:13
  377.1 1.9 copy-start.3
  432.7 7.7 copy-start.5
  432.7 7.8 copy-start.6
  447.2 2.0 copy-start.2
  449.5 36.3 %collective-permute-start = (bf16[127,2048]{0,1:T(8,128)(2,1)S(1)}, bf16[127,2048]{0,1:T(8,128)(2,1)S(1)}, u32[]{:S(2)}, u32[]{:S(2)}) collective-permute-start(bf16[127,2048]{0,1:T(8,128)(2,1)S(1)} %slice.38), channel_id=1, source_target_pairs={{0,4},{4,8},{8,12},{12,16},{16,20},{20,24},{24,28},{1,5},{5,9},{9,... | collective-permute-start | bytes 1560584 | tf_op jit(solution)/shard_map/ppermute | solution.py:13
  497.6 4.6 copy-start.7
  607.0 338.1 %reduce-scatter.5.cloned.1.call-start = ((), (), s32[]{:S(2)}) async-start(), calls=%async_computation.5 | async-start | bytes 18874368 | tf_op jit(solution)/shard_map/reduce_scatter | solution.py:83
  646.5 302.5 %copy-start.1 = (bf16[128,128]{1,0:T(8,128)(2,1)S(1)}, bf16[128,128]{1,0:T(8,128)(2,1)}, u32[]{:S(2)}) copy-start(bf16[128,128]{1,0:T(8,128)(2,1)} %param.9) | copy-start | bytes 98308
Sparse Core Ops, SparseCore 0:
  9.6 58.5 all-gather.2
  70.2 226.6 all-gather.4
  607.1 54.0 reduce-scatter.2
  664.8 280.2 reduce-scatter.4
where the time goes:
time: 968 us; the launch traced here: 956 us
  waiting for transfers between devices  570 us (59%)
  local copies, waits for them, and re-layouts  217 us (22%)
  matrix products  118 us (12%)
  other arithmetic  29.8 us (3%)
  between operations  14.1 us (1%)
    reduce_scatter x1, waiting for transfers between devices, shards(): lax.psum_scatter(jnp.dot(columns.T, gated, preferred_element_type=single)...  283 us
    all_gather x1, waiting for transfers between devices, shards(): lax.all_gather(out_weight, 'seq', axis=0, tiled=True)  229 us
    unnamed x30, local copies, waits for them, and re-layouts  60.3 us
    all_gather x1, waiting for transfers between devices, shards(): full_cot = lax.all_gather(grad_out, 'ch', axis=1, tiled=True)  50.3 us
    dot_general x1, matrix products, shards(): jnp.dot(columns.T, gated, preferred_element_type=single)  26.6 us
    dot_general x1, matrix products, shards(): jnp.dot(columns, lax.all_gather(out_weight, 'seq', axis=0, tiled=True), p...  24.1 us
    concatenate x1, local copies, waits for them, and re-layouts, shards(): jnp.concatenate([grad_mixed, later, jnp.zeros((1, width), jnp.bfloat16)],...  20.6 us
  transfers between devices with their start and end apart: 6, of which 4 were waited for; matrix products, arithmetic and copies ran while one was open for 15% of the time, Pallas kernels for 0%

commit v1 on v0

v1 whole, which is shorter than its diff:
```python
import functools

import jax
import jax.numpy as jnp
from jax import lax
from jax.experimental import pallas as pl
from jax.experimental.pallas import tpu as pltpu
from jax.sharding import PartitionSpec as P

GROUP = 16
FILT = 128
LANES = 128
GPT = LANES // GROUP
LINE = 4
F32 = jnp.float32
BF16 = jnp.bfloat16
VMEM_LIMIT = 48 * 1024 * 1024


def params():
    return pltpu.CompilerParams(vmem_limit_bytes=VMEM_LIMIT)


def cost(flops, nbytes):
    return pl.CostEstimate(flops=int(flops), bytes_accessed=int(nbytes), transcendentals=0)


def table_kernel(back_ref, ahead_ref, back_out, ahead_out):
    for seed, out in ((back_ref, back_out), (ahead_ref, ahead_out)):
        for g in range(GPT):
            rows = jnp.broadcast_to(seed[g : g + 1, :], (FILT, 2 * FILT))
            turned = pltpu.roll(rows, 0, 1, stride=1, stride_axis=0)
            out[g * FILT : (g + 1) * FILT, :] = turned.astype(BF16)


def tables(filters):
    groups = filters.shape[0]
    taps = filters.astype(F32)
    back = jnp.concatenate(
        [jnp.zeros((groups, 1), F32), taps[:, ::-1], jnp.zeros((groups, FILT - 1), F32)], axis=1
    )
    ahead = jnp.concatenate([taps, jnp.zeros((groups, FILT), F32)], axis=1)
    seed = pl.BlockSpec((GPT, 2 * FILT), lambda i: (i, 0))
    full = pl.BlockSpec((GPT * FILT, 2 * FILT), lambda i: (i, 0))
    shape = jax.ShapeDtypeStruct((groups * FILT, 2 * FILT), BF16)
    return pl.pallas_call(
        table_kernel,
        grid=(groups // GPT,),
        in_specs=[seed, seed],
        out_specs=[full, full],
        out_shape=[shape, shape],
        compiler_params=params(),
        cost_estimate=cost(groups * 2**18, groups * 2**17),
    )(back, ahead)


def group_of_lane(rows, cols):
    return (lax.broadcasted_iota(jnp.int32, (rows, cols), 1) % LANES) // GROUP


def windows(ext, b):
    lo = b * FILT
    return jnp.concatenate([ext[lo : lo + 2 * FILT], ext[lo + FILT : lo + 3 * FILT]], axis=1)


def toeplitz(table, ext, blocks):
    group = group_of_lane(FILT, 2 * LANES)
    rows = []
    for b in range(0, blocks, 2):
        out = jnp.dot(table, windows(ext, b), preferred_element_type=F32)
        picked = out[:FILT]
        for g in range(1, GPT):
            picked = jnp.where(group == g, out[g * FILT : (g + 1) * FILT], picked)
        rows += [picked[:, :LANES], picked[:, LANES:]]
    return jnp.concatenate(rows, axis=0)


def product_of(k, v):
    return (k.astype(F32) * v.astype(F32)).astype(BF16)


def forward_kernel(q, k, v, prior, table, gated, mixed_out):
    blocks = q.shape[0] // FILT
    ext = jnp.concatenate([prior[...], product_of(k[...], v[...])], axis=0)
    mixed = toeplitz(table[...], ext, blocks)
    mixed_out[...] = mixed.astype(BF16)
    gated[...] = (q[...].astype(F32) * mixed).astype(BF16)


def forward(q, k, v, prior, table, chunk, chunks):
    rows, width = q.shape
    tiles = width // LANES // chunks
    here = pl.BlockSpec((rows, LANES), lambda i: (0, chunk * tiles + i))
    out = pl.BlockSpec((rows, LANES), lambda i: (0, i))
    shape = jax.ShapeDtypeStruct((rows, width // chunks), BF16)
    return pl.pallas_call(
        forward_kernel,
        grid=(tiles,),
        in_specs=[
            here,
            here,
            here,
            pl.BlockSpec((FILT, LANES), lambda i: (0, chunk * tiles + i)),
            pl.BlockSpec((GPT * FILT, 2 * FILT), lambda i: (chunk * tiles + i, 0)),
        ],
        out_specs=[out, out],
        out_shape=[shape, shape],
        compiler_params=params(),
        cost_estimate=cost(tiles * rows * 2 * 2**18, tiles * rows * 5 * 256 + tiles * 2**19),
    )(q, k, v, prior, table)


def middle_kernel(own, others, q, k, v, mixed, prior, *rest):
    gq_out, gm_out, taps_out = rest[-3:]
    blocks = q.shape[0] // FILT
    total = own[...].astype(F32)
    for other in others:
        total = total + other[...].astype(F32)
    gg = total.astype(BF16).astype(F32)
    gq_out[...] = (gg * mixed[...].astype(F32)).astype(BF16)
    gm = (gg * q[...].astype(F32)).astype(BF16)
    gm_out[...] = gm
    ext = jnp.concatenate([prior[...], product_of(k[...], v[...])], axis=0)
    group = group_of_lane(FILT, 2 * LANES)
    lag = jnp.zeros((GPT * FILT, 2 * FILT), F32)
    for b in range(0, blocks, 2):
        lo = b * FILT
        pair = jnp.concatenate([gm[lo : lo + FILT], gm[lo + FILT : lo + 2 * FILT]], axis=1)
        stack = jnp.concatenate(
            [jnp.where(group == g, pair, jnp.zeros_like(pair)) for g in range(GPT)], axis=0
        )
        lag = lag + lax.dot_general(
            stack, windows(ext, b), (((1,), (1,)), ((), ())), preferred_element_type=F32
        )
    lag = lag.reshape(GPT, FILT, 2 * FILT)
    half = FILT // 2
    while half >= 8:
        lag = lag[:, :half] + pltpu.roll(lag[:, half:], 2 * FILT - half, 2)
        half //= 2
    while half >= 1:
        lag = lag + pltpu.roll(pltpu.roll(lag, 2 * FILT - half, 2), 8 - half, 1)
        half //= 2
    taps_out[...] = lag[:, 0, :]


def middle(own, others, q, k, v, mixed, prior, filled, chunk, chunks):
    rows, width = q.shape
    tiles = width // LANES // chunks
    groups = width // GROUP // chunks
    here = pl.BlockSpec((rows, LANES), lambda i: (0, chunk * tiles + i))
    part = pl.BlockSpec((rows, LANES), lambda i: (0, i))
    n_other = len(others)

    def kernel(own_ref, *refs):
        middle_kernel(own_ref, refs[:n_other], *refs[n_other:])

    args = [own, *others, q, k, v, mixed, prior]
    in_specs = [part] * (1 + n_other) + [here] * 3 + [part]
    in_specs.append(pl.BlockSpec((FILT, LANES), lambda i: (0, chunk * tiles + i)))
    aliases = {}
    if filled is not None:
        aliases = {len(args): 0}
        args.append(filled)
        in_specs.append(pl.BlockSpec(memory_space=pl.ANY))
    return pl.pallas_call(
        kernel,
        grid=(tiles,),
        in_specs=in_specs,
        out_specs=[here, part, pl.BlockSpec((GPT, 2 * FILT), lambda i: (i, 0))],
        out_shape=[
            jax.ShapeDtypeStruct((rows, width), BF16),
            jax.ShapeDtypeStruct((rows, width // chunks), BF16),
            jax.ShapeDtypeStruct((groups, 2 * FILT), F32),
        ],
        input_output_aliases=aliases,
        compiler_params=params(),
        cost_estimate=cost(tiles * rows * 2 * 2**18, tiles * rows * 9 * 256),
    )(*args)


def backward_kernel(gm, later, k, v, table, *rest):
    gk_out, gv_out = rest[-2:]
    blocks = gm.shape[0] // FILT
    ext = jnp.concatenate([gm[...], later[...]], axis=0)
    gp = toeplitz(table[...], ext, blocks)
    gk_out[...] = (gp * v[...].astype(F32)).astype(BF16)
    gv_out[...] = (gp * k[...].astype(F32)).astype(BF16)


def backward(gm, later, k, v, table, filled, chunk, chunks):
    rows, width = k.shape
    tiles = width // LANES // chunks
    here = pl.BlockSpec((rows, LANES), lambda i: (0, chunk * tiles + i))
    part = pl.BlockSpec((rows, LANES), lambda i: (0, i))
    args = [gm, later, k, v, table]
    in_specs = [
        part,
        pl.BlockSpec((FILT, LANES), lambda i: (0, i)),
        here,
        here,
        pl.BlockSpec((GPT * FILT, 2 * FILT), lambda i: (chunk * tiles + i, 0)),
    ]
    aliases = {}
    if filled is not None:
        aliases = {len(args): 0, len(args) + 1: 1}
        args += filled
        in_specs += [pl.BlockSpec(memory_space=pl.ANY)] * 2
    shape = jax.ShapeDtypeStruct((rows, width), BF16)
    return pl.pallas_call(
        backward_kernel,
        grid=(tiles,),
        in_specs=in_specs,
        out_specs=[here, here],
        out_shape=[shape, shape],
        input_output_aliases=aliases,
        compiler_params=params(),
        cost_estimate=cost(tiles * rows * 2 * 2**18, tiles * rows * 5 * 256 + tiles * 2**19),
    )(*args)


def gate_kernel(order, *refs):
    out = refs[-1]
    total = jnp.dot(refs[0][0], refs[LINE][...], preferred_element_type=F32)
    for j in range(1, LINE):
        total = total + jnp.dot(refs[j][0], refs[LINE + j][...], preferred_element_type=F32)
    out[...] = total.astype(out.dtype)


def gate_grad(order, cot, weights, chunk, chunks, dtype):
    _, rows, depth = cot.shape
    width = weights[0].shape[1] // chunks
    tile = min(256, rows)

    def cot_spec(j):
        return pl.BlockSpec((1, tile, depth), lambda i, order: (order[j], i, 0))

    weight_spec = pl.BlockSpec((depth, width), lambda i, order: (0, chunk))
    return pl.pallas_call(
        gate_kernel,
        grid_spec=pltpu.PrefetchScalarGridSpec(
            num_scalar_prefetch=1,
            grid=(rows // tile,),
            in_specs=[cot_spec(j) for j in range(LINE)] + [weight_spec] * LINE,
            out_specs=pl.BlockSpec((tile, width), lambda i, order: (i, 0)),
        ),
        out_shape=jax.ShapeDtypeStruct((rows, width), dtype),
        compiler_params=params(),
        cost_estimate=cost(
            2 * rows * LINE * depth * width, 2 * LINE * depth * (rows + width) + 4 * rows * width
        ),
    )(order, *([cot] * LINE), *weights)


def shards(seq, ch, queries, keys, values, filters, grad_out, out_weight):
    inner = seq // LINE
    rows, width = queries.shape
    depth = out_weight.shape[0]
    chunks = 2 if width % (2 * LANES) == 0 else 1
    cols = width // chunks
    place = lax.axis_index("seq")
    z, y = place // inner, place % inner

    def send(x, pairs):
        return lax.ppermute(x, "seq", pairs)

    def along_line(x, pairs):
        return send(x, [(a * inner + i, b * inner + i) for a, b in pairs for i in range(inner)])

    def around_inner(x, shift):
        return send(
            x, [(a * inner + i, a * inner + (i + shift) % inner) for a in range(LINE) for i in range(inner)]
        )

    prior = send(
        product_of(keys[rows - FILT :], values[rows - FILT :]), [(i, i + 1) for i in range(seq - 1)]
    )

    up1 = along_line(out_weight, [(0, 1), (1, 2), (2, 3)])
    down1 = along_line(out_weight, [(1, 0), (2, 1), (3, 2)])

    cots = []
    if inner == 2 and ch == LINE:
        kept = lax.dynamic_slice(grad_out, (0, y * depth), (rows, depth))
        other = lax.dynamic_slice(grad_out, (0, (1 - y) * depth), (rows, depth))
        cots.append(lax.all_gather(kept, "ch", axis=0, tiled=False))
        cots.append(lax.all_gather(around_inner(other, 1), "ch", axis=0, tiled=False))
    else:
        full = lax.all_gather(grad_out, "ch", axis=1, tiled=True)
        full = full.reshape(rows, LINE, inner, depth).transpose(2, 1, 0, 3)
        for shift in range(inner):
            part = lax.dynamic_index_in_dim(full, (y + shift) % inner, 0, keepdims=False)
            cots.append(part if shift == 0 else around_inner(part, shift))

    back, ahead = tables(filters)

    gateds, mixeds = [], []
    for h in range(chunks):
        gated, mixed = forward(queries, keys, values, prior, back, h, chunks)
        gateds.append([gated] + [around_inner(gated, r) for r in range(1, inner)])
        mixeds.append(mixed)

    up2 = along_line(up1, [(1, 2), (2, 3)])
    down2 = along_line(down1, [(2, 1), (1, 0)])
    second = jnp.where(z >= 2, up2, down2)
    third = along_line(second, [(2, 3), (1, 0)])
    slot_a = jnp.where(z == 0, down1, up1)
    slot_c = jnp.where((z == 0) | (z == 3), third, down1)
    weights = [out_weight, slot_a, second, slot_c]
    order = jnp.stack(
        [
            z,
            jnp.where(z == 0, 1, z - 1),
            jnp.where(z >= 2, z - 2, z + 2),
            jnp.where(z == 3, 0, jnp.where(z == 1, 2, 3)),
        ]
    ).astype(jnp.int32)

    def partial(block, h):
        total = None
        for cot, gated in zip(cots, gateds[h]):
            lhs = lax.dynamic_index_in_dim(cot, block, 0, keepdims=False)
            term = lax.dot_general(lhs, gated, (((0,), (0,)), ((), ())), preferred_element_type=F32)
            total = term if total is None else total + term
        return total

    grad_weights = []
    for h in range(chunks):
        first = partial(jnp.where(z == 0, 3, 0), h).astype(BF16)
        got = along_line(first, [(0, 1), (3, 2)])
        block = jnp.where(z == 0, 2, jnp.where(z == 1, 3, jnp.where(z == 2, 0, 1)))
        mid = (partial(block, h) + got.astype(F32)).astype(BF16)
        outer_in = along_line(mid, [(0, 1), (3, 2)])
        inner_in = along_line(mid, [(1, 2), (2, 1)])
        add_up = jnp.where(z == 1, outer_in, inner_in).astype(F32)
        add_down = jnp.where(z == 1, inner_in, outer_in).astype(F32)
        last_up = (partial(jnp.minimum(z + 1, 3), h) + add_up).astype(BF16)
        last_down = (partial(jnp.maximum(z - 1, 0), h) + add_down).astype(BF16)
        from_below = along_line(last_up, [(0, 1), (1, 2), (2, 3)])
        from_above = along_line(last_down, [(1, 0), (2, 1), (3, 2)])
        total = partial(z, h) + from_below.astype(F32) + from_above.astype(F32)
        grad_weights.append(total.astype(BF16))
    grad_weight = jnp.concatenate(grad_weights, axis=1)

    owns, others = [], []
    for h in range(chunks):
        others.append(
            [
                around_inner(gate_grad(order, cots[r], weights, h, chunks, BF16), inner - r)
                for r in range(1, inner)
            ]
        )
    for h in range(chunks):
        owns.append(gate_grad(order, cots[0], weights, h, chunks, F32))

    grad_queries = None
    grad_kv = None
    taps = []
    for h in range(chunks):
        here = slice(h * cols, (h + 1) * cols)
        grad_queries, gm, lag = middle(
            owns[h], others[h], queries, keys, values, mixeds[h], prior, grad_queries, h, chunks
        )
        later = send(gm[:FILT], [(i + 1, i) for i in range(seq - 1)])
        grad_kv = backward(gm, later, keys, values, ahead, grad_kv, h, chunks)
        taps.append(lag)
    taps = jnp.concatenate(taps, axis=0)[:, 1 : FILT + 1][:, ::-1]
    taps = taps.T.reshape(seq, FILT // seq, -1)
    taps = jnp.sum(lax.all_to_all(taps, "seq", 0, 0), axis=0)
    return grad_queries, *grad_kv, taps.T, grad_weight


def solution(mesh):
    sizes = dict(mesh.shape)
    return jax.shard_map(
        functools.partial(shards, sizes["seq"], sizes["ch"]),
        mesh=mesh,
        in_specs=(
            P("seq", "ch"),
            P("seq", "ch"),
            P("seq", "ch"),
            P("ch", None),
            P("seq", "ch"),
            P("seq", "ch"),
        ),
        out_specs=(P("seq", "ch"), P("seq", "ch"), P("seq", "ch"), P("ch", "seq"), P("seq", "ch")),
        check_vma=False,
    )
```

time: 968 us -> 454 us (0.47)
  waiting for transfers between devices: 570 us -> 110 us
  local copies, waits for them, and re-layouts: 217 us -> 10.2 us
  Pallas kernels: 0 us -> 111 us
  starting transfers between devices: 6.75 us -> 113 us
  matrix products: 118 us -> 75.1 us
  other arithmetic: 29.8 us -> 15.3 us
    reduce_scatter x2 -> x0, waiting for transfers between devices: 289 us -> none  [the longest x1 283 us: shards(): lax.psum_scatter(jnp.dot(columns.T, gated, preferred_element_type=single)...]
    all_gather x2, waiting for transfers between devices: 279 us -> 0.02 us  [the longest x1 0.02 us: shards(): lax.all_gather(around_inner(other, 1), 'ch', axis=0, tiled=False)]
    pallas_call x0 -> x11, Pallas kernels: none -> 111 us  [the longest x4 34.2 us: gate_grad(): pl.pallas_call(gate_kernel, grid_spec=pltpu.PrefetchScalarGridSpec(num_sc...]
    ppermute x2 -> x23, waiting for transfers between devices: 0.01 us -> 110 us  [send(): return lax.ppermute(x, 'seq', pairs)]
    ppermute x2 -> x23, starting transfers between devices: 6.59 us -> 109 us  [send(): return lax.ppermute(x, 'seq', pairs)]
    unnamed x30 -> x44, local copies, waits for them, and re-layouts: 60.3 us -> 5.47 us
    reshape x3 -> x0, local copies, waits for them, and re-layouts: 44.6 us -> none  [the longest x1 17.9 us: lag_sums(): flat = lag_matrix.reshape(groups, inner * outer)]
    dot_general x7 -> x20, matrix products: 118 us -> 75.1 us  [partial(): lax.dot_general(lhs, gated, (((0,), (0,)), ((), ())), preferred_element_t...]
  transfers between devices with their start and end apart: 6 -> 26, of which waited for: 4 -> 9; matrix products, arithmetic and copies ran while one was open for 15% -> 20% of each run, Pallas kernels for 0% -> 25%
where the time goes in v1:
time: 454 us; the launch traced here: 449 us
  starting transfers between devices  113 us (25%)
  Pallas kernels  111 us (24%)
  waiting for transfers between devices  110 us (24%)
  matrix products  75.1 us (17%)
  other arithmetic  15.3 us (3%)
  between operations  14.6 us (3%)
  local copies, waits for them, and re-layouts  10.2 us (2%)
    ppermute x23, waiting for transfers between devices, send(): return lax.ppermute(x, 'seq', pairs)  110 us
    ppermute x23, starting transfers between devices, send(): return lax.ppermute(x, 'seq', pairs)  109 us
    dot_general x20, matrix products, partial(): lax.dot_general(lhs, gated, (((0,), (0,)), ((), ())), preferred_element_t...  75.1 us
    pallas_call x4, Pallas kernels, gate_grad(): pl.pallas_call(gate_kernel, grid_spec=pltpu.PrefetchScalarGridSpec(num_sc...  34.2 us
    pallas_call x2, Pallas kernels, middle(): pl.pallas_call(kernel, grid=(tiles,), in_specs=in_specs, out_specs=[here,...  24.9 us
    pallas_call x2, Pallas kernels, backward(): pl.pallas_call(backward_kernel, grid=(tiles,), in_specs=in_specs, out_spe...  21.2 us
    pallas_call x2, Pallas kernels, forward(): pl.pallas_call(forward_kernel, grid=(tiles,), in_specs=[here, here, here,...  20.6 us
    pallas_call x1, Pallas kernels, tables(): pl.pallas_call(table_kernel, grid=(groups // GPT,), in_specs=[seed, seed]...  10.4 us
  transfers between devices with their start and end apart: 26, of which 9 were waited for; matrix products, arithmetic and copies ran while one was open for 20% of the time, Pallas kernels for 25%

profile of v1, /device:TPU:10, one launch (start us, length us, event | category | flops | bytes accessed | tf_op | source)
XLA Modules:
  0.0 449.4 jit_solution(11603957569648598786)
XLA Ops:
  7.2 2.8 constant_dynamic-slice_fusion
  10.1 3.5 collective-permute-start.1
  13.6 3.6 collective-permute-start
  17.3 42.2 %collective-permute-done.1 = bf16[512,2048]{1,0:T(8,128)(2,1)} collective-permute-done((bf16[512,2048]{1,0:T(8,128)(2,1)S(1)}, bf16[512,2048]{1,0:T(8,128)(2,1)}, u32[]{:S(2)}, u32[]{:S(2)}) %collective-permute-start.1) | collective-permute-done | bytes 2097184 | tf_op jit(solution)/shard_map/ppermute | solution.py:264
  59.5 4.8 %collective-permute-start.2 = (bf16[512,2048]{1,0:T(8,128)(2,1)}, bf16[512,2048]{1,0:T(8,128)(2,1)}, u32[]{:S(2)}, u32[]{:S(2)}) collective-permute-start(bf16[512,2048]{1,0:T(8,128)(2,1)} %collective-permute-done.1), channel_id=1, source_target_pairs={{8,16},{12,20},{16,24},{20,28},{9,17},{13,21},{17,25},{21,29},{10,... | collective-permute-start | bytes 6291464 | tf_op jit(solution)/shard_map/ppermute | solution.py:264
  64.3 2.0 collective-permute-start.3
  66.4 1.6 collective-permute-start.5
  67.9 22.1 %collective-permute-done.5 = bf16[1024,512]{1,0:T(8,128)(2,1)S(1)} collective-permute-done((bf16[1024,512]{1,0:T(8,128)(2,1)S(1)}, bf16[1024,512]{1,0:T(8,128)(2,1)S(1)}, u32[]{:S(2)}, u32[]{:S(2)}) %collective-permute-start.5) | collective-permute-done | bytes 1048608 | tf_op jit(solution)/shard_map/ppermute | solution.py:264
  91.1 16.2 %collective-permute-done.2 = bf16[512,2048]{1,0:T(8,128)(2,1)} collective-permute-done((bf16[512,2048]{1,0:T(8,128)(2,1)}, bf16[512,2048]{1,0:T(8,128)(2,1)}, u32[]{:S(2)}, u32[]{:S(2)}) %collective-permute-start.2) | collective-permute-done | bytes 2097184 | tf_op jit(solution)/shard_map/ppermute | solution.py:264
  107.3 5.4 %collective-permute-done.3 = bf16[512,2048]{1,0:T(8,128)(2,1)} collective-permute-done((bf16[512,2048]{1,0:T(8,128)(2,1)}, bf16[512,2048]{1,0:T(8,128)(2,1)}, u32[]{:S(2)}, u32[]{:S(2)}) %collective-permute-start.3) | collective-permute-done | bytes 2097184 | tf_op jit(solution)/shard_map/ppermute | solution.py:264
  112.7 1.8 broadcast_select_fusion.1.refs_6_
  114.5 3.6 collective-permute-start.4
  119.4 3.4 collective-permute-start.7
  123.2 10.4 %shard_map.103 = (bf16[16384,256]{1,0:T(8,128)(2,1)}, bf16[16384,256]{1,0:T(8,128)(2,1)}) custom-call(f32[128,256]{1,0:T(8,128)S(1)} %maximum_maximum_fusion.back_ref, f32[128,256]{1,0:T(8,128)S(1)} %concatenate.13.ahead_ref), custom_call_target="tpu_custom_call" | custom-call | flops 33554432 | bytes 16777216 | tf_op jit(solution)/shard_map/pallas_call | solution.py:46
  133.7 10.3 %shard_map.107 = (bf16[1024,1024]{1,0:T(8,128)(2,1)}, bf16[1024,1024]{1,0:T(8,128)(2,1)S(1)}) custom-call(bf16[1024,2048]{1,0:T(8,128)(2,1)} %refs_1_.3, bf16[1024,2048]{1,0:T(8,128)(2,1)} %k.7, bf16[1024,2048]{1,0:T(8,128)(2,1)} %v.7, bf16[128,2048]{1,0:T(8,128)(2,1)S(1)} %collective-permute-done.7.prior.refs_5_, bf16[16384,256]{1,0:T(8,128)(2,1)} %get-tuple-element.21.table), custom_call_target="tpu_custom_call" | custom-call | flops 4294967296 | bytes 14680064 | tf_op jit(solution)/shard_map/pallas_call | solution.py:96
  146.1 10.3 %shard_map.104 = (bf16[1024,1024]{1,0:T(8,128)(2,1)}, bf16[1024,1024]{1,0:T(8,128)(2,1)S(1)}) custom-call(bf16[1024,2048]{1,0:T(8,128)(2,1)} %refs_1_.3, bf16[1024,2048]{1,0:T(8,128)(2,1)} %k.7, bf16[1024,2048]{1,0:T(8,128)(2,1)} %v.7, bf16[128,2048]{1,0:T(8,128)(2,1)S(1)} %collective-permute-done.7.prior.refs_5_, bf16[16384,256]{1,0:T(8,128)(2,1)} %get-tuple-element.21.table), custom_call_target="tpu_custom_call" | custom-call | flops 4294967296 | bytes 14680064 | tf_op jit(solution)/shard_map/pallas_call | solution.py:96
  157.6 1.4 collective-permute-start.17
  159.7 3.9 broadcast_select_fusion
  163.6 5.3 %fusion.20 = f32[512,1024]{1,0:T(8,128)} fusion(bf16[1024,1024]{1,0:T(8,128)(2,1)} %get-tuple-element.35, bf16[4,1024,512]{2,1,0:T(8,128)(2,1)} %bitcast.106, s32[]{:T(128)S(6)} %select_n.133), kind=kOutput, calls=%fused_computation.34 | convolution fusion | flops 1073741824 | bytes 5242884 | tf_op jit(solution)/shard_map/dot_general | solution.py:322
  168.9 4.2 fusion.18
  173.1 4.4 fusion.36
  177.5 8.9 %shard_map.105.own_ref = f32[1024,1024]{1,0:T(8,128)} custom-call(s32[4]{0:T(128)S(1)} %pad_add_fusion.order, bf16[4,1024,512]{2,1,0:T(8,128)(2,1)} %bitcast.107, bf16[4,1024,512]{2,1,0:T(8,128)(2,1)} %bitcast.108, bf16[4,1024,512]{2,1,0:T(8,128)(2,1)} %bitcast.109, bf16[4,1024,512]{2,1,0:T(8,128)(2,1)} %bitcast.110, bf16[512,2048]{1,0:T(8,128)(2,1)S(1)} %copy-done.2, ...), custom_call_target="tpu_custom_call" | custom-call | flops 4294967296 | bytes 12582912 | tf_op jit(solution)/shard_map/pallas_call | solution.py:238
  186.4 4.5 %fusion.34 = f32[512,1024]{1,0:T(8,128)} fusion(bf16[1024,1024]{1,0:T(8,128)(2,1)} %get-tuple-element.36, bf16[4,1024,512]{2,1,0:T(8,128)(2,1)} %bitcast.111, s32[]{:T(128)S(6)} %select_n.128), kind=kOutput, calls=%fused_computation.48 | convolution fusion | flops 1073741824 | bytes 5242884 | tf_op jit(solution)/shard_map/dot_general | solution.py:322
  190.9 8.9 %shard_map.101.own_ref = f32[1024,1024]{1,0:T(8,128)} custom-call(s32[4]{0:T(128)S(1)} %pad_add_fusion.order, bf16[4,1024,512]{2,1,0:T(8,128)(2,1)} %bitcast.112, bf16[4,1024,512]{2,1,0:T(8,128)(2,1)} %bitcast.113, bf16[4,1024,512]{2,1,0:T(8,128)(2,1)} %bitcast.114, bf16[4,1024,512]{2,1,0:T(8,128)(2,1)} %bitcast.115, bf16[512,2048]{1,0:T(8,128)(2,1)S(1)} %copy-done.2, ...), custom_call_target="tpu_custom_call" | custom-call | flops 4294967296 | bytes 12582912 | tf_op jit(solution)/shard_map/pallas_call | solution.py:238
  199.9 3.2 fusion.10
  203.1 3.3 add_convert_fusion.9
  206.4 1.5 collective-permute-start.12
  207.9 8.1 %shard_map.106 = bf16[1024,1024]{1,0:T(8,128)(2,1)S(1)} custom-call(s32[4]{0:T(128)S(1)} %pad_add_fusion.order, bf16[4,1024,512]{2,1,0:T(8,128)(2,1)} %bitcast.89, bf16[4,1024,512]{2,1,0:T(8,128)(2,1)} %bitcast.90, bf16[4,1024,512]{2,1,0:T(8,128)(2,1)} %bitcast.91, bf16[4,1024,512]{2,1,0:T(8,128)(2,1)} %bitcast.92, bf16[512,2048]{1,0:T(8,128)(2,1)S(1)} %copy-done.3, ...), custom_call_target="tpu_custom_call" | custom-call | flops 4294967296 | bytes 12582912 | tf_op jit(solution)/shard_map/pallas_call | solution.py:238
  216.0 8.3 %shard_map.102 = bf16[1024,1024]{1,0:T(8,128)(2,1)S(1)} custom-call(s32[4]{0:T(128)S(1)} %pad_add_fusion.order, bf16[4,1024,512]{2,1,0:T(8,128)(2,1)} %bitcast.93, bf16[4,1024,512]{2,1,0:T(8,128)(2,1)} %bitcast.94, bf16[4,1024,512]{2,1,0:T(8,128)(2,1)} %bitcast.95, bf16[4,1024,512]{2,1,0:T(8,128)(2,1)} %bitcast.96, bf16[512,2048]{1,0:T(8,128)(2,1)S(1)} %copy-done.3, ...), custom_call_target="tpu_custom_call" | custom-call | flops 4294967296 | bytes 12582912 | tf_op jit(solution)/shard_map/pallas_call | solution.py:238
  224.3 11.3 %collective-permute-done.17 = bf16[1024,1024]{1,0:T(8,128)(2,1)} collective-permute-done((bf16[1024,1024]{1,0:T(8,128)(2,1)}, bf16[1024,1024]{1,0:T(8,128)(2,1)}, u32[]{:S(2)}, u32[]{:S(2)}) %collective-permute-start.17) | collective-permute-done | bytes 2097184 | tf_op jit(solution)/shard_map/ppermute | solution.py:264
  235.6 2.9 fusion.8
  238.4 2.9 add_convert_fusion.4
  243.0 1.7 collective-permute-start.6
  244.7 2.9 fusion.16
  247.6 4.2 fusion.32
  251.8 2.9 fusion.14
  254.7 2.9 fusion.24
  257.5 3.0 fusion.22
  262.5 2.9 fusion.2
  265.4 37.6 %collective-permute-start.14 = (bf16[512,1024]{1,0:T(8,128)(2,1)S(1)}, bf16[512,1024]{1,0:T(8,128)(2,1)S(1)}, u32[]{:S(2)}, u32[]{:S(2)}) collective-permute-start(bf16[512,1024]{1,0:T(8,128)(2,1)S(1)} %add_convert_fusion.8), channel_id=1, source_target_pairs={{8,16},{12,20},{16,8},{20,12},{9,17},{13,21},{17,9},{21,13},{10,18... | collective-permute-start | bytes 3145736 | tf_op jit(solution)/shard_map/ppermute | solution.py:264
  303.0 4.2 fusion
  307.8 1.5 collective-permute-start.19
  309.4 19.3 %collective-permute-start.20 = (bf16[512,1024]{1,0:T(8,128)(2,1)S(1)}, bf16[512,1024]{1,0:T(8,128)(2,1)S(1)}, u32[]{:S(2)}, u32[]{:S(2)}) collective-permute-start(bf16[512,1024]{1,0:T(8,128)(2,1)S(1)} %add_convert_fusion.3), channel_id=1, source_target_pairs={{8,16},{12,20},{16,8},{20,12},{9,17},{13,21},{17,9},{21,13},{10,18... | collective-permute-start | bytes 3145736 | tf_op jit(solution)/shard_map/ppermute | solution.py:264
  328.7 4.2 fusion.30
  332.8 4.0 add_convert_fusion.7
  336.8 1.9 collective-permute-start.15
  338.7 4.0 add_convert_fusion.6
  342.7 4.9 %collective-permute-start.16 = (bf16[512,1024]{1,0:T(8,128)(2,1)}, bf16[512,1024]{1,0:T(8,128)(2,1)}, u32[]{:S(2)}, u32[]{:S(2)}) collective-permute-start(bf16[512,1024]{1,0:T(8,128)(2,1)} %add_convert_fusion.6), channel_id=1, source_target_pairs={{8,0},{12,4},{16,8},{20,12},{24,16},{28,20},{9,1},{13,5},{17,9},{2... | collective-permute-start | bytes 3145736 | tf_op jit(solution)/shard_map/ppermute | solution.py:264
  347.6 4.7 %collective-permute-done.20 = bf16[512,1024]{1,0:T(8,128)(2,1)S(1)} collective-permute-done((bf16[512,1024]{1,0:T(8,128)(2,1)S(1)}, bf16[512,1024]{1,0:T(8,128)(2,1)S(1)}, u32[]{:S(2)}, u32[]{:S(2)}) %collective-permute-start.20) | collective-permute-done | bytes 1048608 | tf_op jit(solution)/shard_map/ppermute | solution.py:264
  352.3 4.4 add_convert_fusion.2
  356.7 4.4 collective-permute-start.21
  361.1 12.4 %shard_map.108 = (bf16[1024,2048]{1,0:T(8,128)(2,1)}, bf16[1024,1024]{1,0:T(8,128)(2,1)S(1)}, f32[64,256]{1,0:T(8,128)S(1)}) custom-call(f32[1024,1024]{1,0:T(8,128)} %shard_map.105.own_ref, bf16[1024,1024]{1,0:T(8,128)(2,1)S(1)} %collective-permute-done.8.refs_0_, bf16[1024,2048]{1,0:T(8,128)(2,1)} %refs_1_.3, bf16[1024,2048]{1,0:T(8,128)(2,1)} %k.7, ...), custom_call_target="tpu_custom_call" | custom-call | flops 4294967296 | bytes 18874368 | tf_op jit(solution)/shard_map/pallas_call | solution.py:165
  373.5 12.5 %shard_map.109 = (bf16[1024,2048]{1,0:T(8,128)(2,1)}, bf16[1024,1024]{1,0:T(8,128)(2,1)S(1)}, f32[64,256]{1,0:T(8,128)S(1)}) custom-call(f32[1024,1024]{1,0:T(8,128)} %shard_map.101.own_ref, bf16[1024,1024]{1,0:T(8,128)(2,1)S(1)} %collective-permute-done.6.refs_0_, bf16[1024,2048]{1,0:T(8,128)(2,1)} %refs_1_.3, ...), custom_call_target="tpu_custom_call", output_to_operand_aliasing={{0}: (7, {})} | custom-call | flops 4294967296 | bytes 18874368 | tf_op jit(solution)/shard_map/pallas_call | solution.py:165
  388.3 3.8 all-to-all-start
  392.1 3.4 collective-permute-start.10
  395.4 5.1 %add_convert_fusion.1 = bf16[512,1024]{1,0:T(8,128)(2,1)} fusion(f32[512,1024]{1,0:T(8,128)} %fusion, bf16[512,1024]{1,0:T(8,128)(2,1)} %copy-done.21, bf16[512,1024]{1,0:T(8,128)(2,1)} %copy-done.20, pred[]{:T(512)S(6)} %eq.12, bf16[1024,1024]{1,0:T(8,128)(2,1)} %get-tuple-element.36, bf16[4,1024,512]{2,1,0:T(8,128)(2,1)} %bitcast.117, s32[]{:T(128)S(6)} %max.4), kind=kOutput, calls=%fused_computation.2 | convolution fusion | flops 1076363264 | bytes 8388613 | tf_op jit(solution)/shard_map/dot_general | solution.py:322
  400.5 1.9 collective-permute-start.22
  404.1 3.4 collective-permute-start.9
  407.5 10.6 %shard_map.110 = (bf16[1024,2048]{1,0:T(8,128)(2,1)}, bf16[1024,2048]{1,0:T(8,128)(2,1)}) custom-call(bf16[1024,1024]{1,0:T(8,128)(2,1)S(1)} %get-tuple-element.28.gm, bf16[128,1024]{1,0:T(8,128)(2,1)S(1)} %collective-permute-done.10.later, bf16[1024,2048]{1,0:T(8,128)(2,1)} %k.7, bf16[1024,2048]{1,0:T(8,128)(2,1)} %v.7, ...), custom_call_target="tpu_custom_call" | custom-call | flops 4294967296 | bytes 14680064 | tf_op jit(solution)/shard_map/pallas_call | solution.py:209
  418.1 7.3 %collective-permute-done.9.later = bf16[128,1024]{1,0:T(8,128)(2,1)S(1)} collective-permute-done((bf16[128,1024]{1,0:T(8,128)(2,1)S(1)}, bf16[128,1024]{1,0:T(8,128)(2,1)S(1)}, u32[]{:S(2)}, u32[]{:S(2)}) %collective-permute-start.9) | collective-permute-done | bytes 262176 | tf_op jit(solution)/shard_map/ppermute | solution.py:264
  425.3 10.6 %shard_map.111 = (bf16[1024,2048]{1,0:T(8,128)(2,1)}, bf16[1024,2048]{1,0:T(8,128)(2,1)}) custom-call(bf16[1024,1024]{1,0:T(8,128)(2,1)S(1)} %copy-done.5, bf16[128,1024]{1,0:T(8,128)(2,1)S(1)} %collective-permute-done.9.later, bf16[1024,2048]{1,0:T(8,128)(2,1)} %k.7, bf16[1024,2048]{1,0:T(8,128)(2,1)} %v.7, ...), custom_call_target="tpu_custom_call", output_to_operand_aliasing={{0}: (5, {}), {1}: (6, {})} | custom-call | flops 4294967296 | bytes 14680064 | tf_op jit(solution)/shard_map/pallas_call | solution.py:209
  436.0 2.4 add_convert_fusion.5
  438.8 2.2 add_convert_fusion
  441.0 1.5 pad_maximum_fusion
  (87 shorter events, 15.4 us)
Async XLA Ops:
  7.2 156.4 %all-gather.5.cloned.1.call-start = ((), (), s32[]{:S(2)}) async-start(), calls=%async_computation.1 | async-start | bytes 5242880 | tf_op jit(solution)/shard_map/all_gather | solution.py:285
  7.2 2.9 copy-start.1
  10.1 189.8 %all-gather.7.cloned.1.call-start = ((), (), s32[]{:S(2)}) async-start(), calls=%async_computation.2 | async-start | bytes 5242880 | tf_op jit(solution)/shard_map/all_gather | solution.py:286
  10.1 49.4 %collective-permute-start.1 = (bf16[512,2048]{1,0:T(8,128)(2,1)S(1)}, bf16[512,2048]{1,0:T(8,128)(2,1)}, u32[]{:S(2)}, u32[]{:S(2)}) collective-permute-start(bf16[512,2048]{1,0:T(8,128)(2,1)S(1)} %copy-done.1), channel_id=1, source_target_pairs={{0,8},{4,12},{8,16},{12,20},{16,24},{20,28},{1,9},{5,13},{9,17},{1... | collective-permute-start | bytes 6291464 | tf_op jit(solution)/shard_map/ppermute | solution.py:264
  13.6 50.7 %collective-permute-start = (bf16[512,2048]{1,0:T(8,128)(2,1)S(1)}, bf16[512,2048]{1,0:T(8,128)(2,1)}, u32[]{:S(2)}, u32[]{:S(2)}) collective-permute-start(bf16[512,2048]{1,0:T(8,128)(2,1)S(1)} %copy-done.1), channel_id=1, source_target_pairs={{8,0},{12,4},{16,8},{20,12},{24,16},{28,20},{9,1},{13,5},{17,9},{2... | collective-permute-start | bytes 6291464 | tf_op jit(solution)/shard_map/ppermute | solution.py:264
  59.5 47.8 %collective-permute-start.2 = (bf16[512,2048]{1,0:T(8,128)(2,1)}, bf16[512,2048]{1,0:T(8,128)(2,1)}, u32[]{:S(2)}, u32[]{:S(2)}) collective-permute-start(bf16[512,2048]{1,0:T(8,128)(2,1)} %collective-permute-done.1), channel_id=1, source_target_pairs={{8,16},{12,20},{16,24},{20,28},{9,17},{13,21},{17,25},{21,29},{10,... | collective-permute-start | bytes 6291464 | tf_op jit(solution)/shard_map/ppermute | solution.py:264
  64.3 48.4 %collective-permute-start.3 = (bf16[512,2048]{1,0:T(8,128)(2,1)}, bf16[512,2048]{1,0:T(8,128)(2,1)}, u32[]{:S(2)}, u32[]{:S(2)}) collective-permute-start(bf16[512,2048]{1,0:T(8,128)(2,1)} %collective-permute-done), channel_id=1, source_target_pairs={{16,8},{20,12},{8,0},{12,4},{17,9},{21,13},{9,1},{13,5},{18,10},{2... | collective-permute-start | bytes 6291464 | tf_op jit(solution)/shard_map/ppermute | solution.py:264
  66.4 23.7 %collective-permute-start.5 = (bf16[1024,512]{1,0:T(8,128)(2,1)S(1)}, bf16[1024,512]{1,0:T(8,128)(2,1)S(1)}, u32[]{:S(2)}, u32[]{:S(2)}) collective-permute-start(bf16[1024,512]{1,0:T(8,128)(2,1)S(1)} %get-tuple-element.37), channel_id=1, source_target_pairs={{0,4},{4,0},{8,12},{12,8},{16,20},{20,16},{24,28},{28,24},{1,5},{5... | collective-permute-start | bytes 3145736 | tf_op jit(solution)/shard_map/ppermute | solution.py:264
  90.0 1.0 copy-start.18
  91.1 31.8 %copy-start.19 = (bf16[128,128]{1,0:T(8,128)(2,1)S(1)}, bf16[128,128]{1,0:T(8,128)(2,1)}, u32[]{:S(2)}) copy-start(bf16[128,128]{1,0:T(8,128)(2,1)} %param.9) | copy-start | bytes 98308
  114.5 29.5 %copy-start.11 = (bf16[512,2048]{1,0:T(8,128)(2,1)}, bf16[512,2048]{1,0:T(8,128)(2,1)S(1)}, u32[]{:S(2)}) copy-start(bf16[512,2048]{1,0:T(8,128)(2,1)S(1)} %broadcast_select_fusion.1.refs_6_) | copy-start | bytes 6291460
  114.5 45.2 %collective-permute-start.4 = (bf16[512,2048]{1,0:T(8,128)(2,1)S(1)}, bf16[512,2048]{1,0:T(8,128)(2,1)}, u32[]{:S(2)}, u32[]{:S(2)}) collective-permute-start(bf16[512,2048]{1,0:T(8,128)(2,1)S(1)} %broadcast_select_fusion.1.refs_6_), channel_id=1, source_target_pairs={{16,24},{20,28},{8,0},{12,4},{17,25},{21,29},{9,1},{13,5},{18,26},... | collective-permute-start | bytes 6291464 | tf_op jit(solution)/shard_map/ppermute | solution.py:264
  119.4 14.3 %collective-permute-start.7 = (bf16[128,2048]{1,0:T(8,128)(2,1)S(1)}, bf16[128,2048]{1,0:T(8,128)(2,1)S(1)}, u32[]{:S(2)}, u32[]{:S(2)}) collective-permute-start(bf16[128,2048]{1,0:T(8,128)(2,1)S(1)} %multiply_convert_fusion), channel_id=1, source_target_pairs={{0,4},{4,8},{8,12},{12,16},{16,20},{20,24},{24,28},{1,5},{5,9},{9,... | collective-permute-start | bytes 1572872 | tf_op jit(solution)/shard_map/ppermute | solution.py:264
  144.1 1.4 copy-start.7
  145.5 54.4 %collective-permute-start.11 = (bf16[1024,1024]{1,0:T(8,128)(2,1)}, bf16[1024,1024]{1,0:T(8,128)(2,1)}, u32[]{:S(2)}, u32[]{:S(2)}) collective-permute-start(bf16[1024,1024]{1,0:T(8,128)(2,1)} %get-tuple-element.35), channel_id=1, source_target_pairs={{0,4},{4,0},{8,12},{12,8},{16,20},{20,16},{24,28},{28,24},{1,5},{5... | collective-permute-start | bytes 6291464 | tf_op jit(solution)/shard_map/ppermute | solution.py:264
  156.3 1.3 copy-start.6
  157.6 77.9 %collective-permute-start.17 = (bf16[1024,1024]{1,0:T(8,128)(2,1)}, bf16[1024,1024]{1,0:T(8,128)(2,1)}, u32[]{:S(2)}, u32[]{:S(2)}) collective-permute-start(bf16[1024,1024]{1,0:T(8,128)(2,1)} %get-tuple-element.36), channel_id=1, source_target_pairs={{0,4},{4,0},{8,12},{12,8},{16,20},{20,16},{24,28},{28,24},{1,5},{5... | collective-permute-start | bytes 6291464 | tf_op jit(solution)/shard_map/ppermute | solution.py:264
  163.6 27.3 %copy-start = (bf16[512,2048]{1,0:T(8,128)(2,1)}, bf16[512,2048]{1,0:T(8,128)(2,1)S(1)}, u32[]{:S(2)}) copy-start(bf16[512,2048]{1,0:T(8,128)(2,1)S(1)} %get-tuple-element.40.refs_5_) | copy-start | bytes 6291460
  163.6 5.3 %copy-start.9 = (bf16[4096,512]{1,0:T(8,128)(2,1)S(1)}, bf16[4096,512]{1,0:T(8,128)(2,1)}, u32[]{:S(2)}) copy-start(bf16[4096,512]{1,0:T(8,128)(2,1)} %all-gather.5.cloned.1.call-done) | copy-start | bytes 12582916
  173.1 4.4 copy-start.2
  203.1 4.8 %copy-start.3 = (bf16[512,2048]{1,0:T(8,128)(2,1)S(1)}, bf16[512,2048]{1,0:T(8,128)(2,1)}, u32[]{:S(2)}) copy-start(bf16[512,2048]{1,0:T(8,128)(2,1)} %refs_4_.7) | copy-start | bytes 6291460
  206.4 54.2 %collective-permute-start.12 = (bf16[512,1024]{1,0:T(8,128)(2,1)S(1)}, bf16[512,1024]{1,0:T(8,128)(2,1)S(1)}, u32[]{:S(2)}, u32[]{:S(2)}) collective-permute-start(bf16[512,1024]{1,0:T(8,128)(2,1)S(1)} %add_convert_fusion.9), channel_id=1, source_target_pairs={{0,8},{4,12},{24,16},{28,20},{1,9},{5,13},{25,17},{29,21},{2,10},{... | collective-permute-start | bytes 3145736 | tf_op jit(solution)/shard_map/ppermute | solution.py:264
  216.0 19.6 %copy-start.8 = (bf16[4096,512]{1,0:T(8,128)(2,1)S(1)}, bf16[4096,512]{1,0:T(8,128)(2,1)}, u32[]{:S(2)}) copy-start(bf16[4096,512]{1,0:T(8,128)(2,1)} %all-gather.7.cloned.1.call-done) | copy-start | bytes 12582916
  224.2 14.2 %copy-start.10 = (bf16[4096,512]{1,0:T(8,128)(2,1)S(1)}, bf16[4096,512]{1,0:T(8,128)(2,1)}, u32[]{:S(2)}) copy-start(bf16[4096,512]{1,0:T(8,128)(2,1)} %all-gather.5.cloned.1.call-done) | copy-start | bytes 12582916
  241.3 65.9 %collective-permute-start.18 = (bf16[512,1024]{1,0:T(8,128)(2,1)S(1)}, bf16[512,1024]{1,0:T(8,128)(2,1)S(1)}, u32[]{:S(2)}, u32[]{:S(2)}) collective-permute-start(bf16[512,1024]{1,0:T(8,128)(2,1)S(1)} %add_convert_fusion.4), channel_id=1, source_target_pairs={{0,8},{4,12},{24,16},{28,20},{1,9},{5,13},{25,17},{29,21},{2,10},{... | collective-permute-start | bytes 3145736 | tf_op jit(solution)/shard_map/ppermute | solution.py:264
  242.6 118.5 %collective-permute-start.8 = (bf16[1024,1024]{1,0:T(8,128)(2,1)S(1)}, bf16[1024,1024]{1,0:T(8,128)(2,1)S(1)}, u32[]{:S(2)}, u32[]{:S(2)}) collective-permute-start(bf16[1024,1024]{1,0:T(8,128)(2,1)S(1)} %shard_map.106), channel_id=1, source_target_pairs={{0,4},{4,0},{8,12},{12,8},{16,20},{20,16},{24,28},{28,24},{1,5},{5... | collective-permute-start | bytes 6291464 | tf_op jit(solution)/shard_map/ppermute | solution.py:264
  243.0 130.5 %collective-permute-start.6 = (bf16[1024,1024]{1,0:T(8,128)(2,1)S(1)}, bf16[1024,1024]{1,0:T(8,128)(2,1)S(1)}, u32[]{:S(2)}, u32[]{:S(2)}) collective-permute-start(bf16[1024,1024]{1,0:T(8,128)(2,1)S(1)} %shard_map.102), channel_id=1, source_target_pairs={{0,4},{4,0},{8,12},{12,8},{16,20},{20,16},{24,28},{28,24},{1,5},{5... | collective-permute-start | bytes 6291464 | tf_op jit(solution)/shard_map/ppermute | solution.py:264
  257.5 3.0 copy-start.17
  261.2 48.2 %collective-permute-start.13 = (bf16[512,1024]{1,0:T(8,128)(2,1)S(1)}, bf16[512,1024]{1,0:T(8,128)(2,1)S(1)}, u32[]{:S(2)}, u32[]{:S(2)}) collective-permute-start(bf16[512,1024]{1,0:T(8,128)(2,1)S(1)} %add_convert_fusion.8), channel_id=1, source_target_pairs={{0,8},{4,12},{24,16},{28,20},{1,9},{5,13},{25,17},{29,21},{2,10},{... | collective-permute-start | bytes 3145736 | tf_op jit(solution)/shard_map/ppermute | solution.py:264
  265.4 41.8 %copy-start.16 = (f32[512,1024]{1,0:T(8,128)S(1)}, f32[512,1024]{1,0:T(8,128)}, u32[]{:S(2)}) copy-start(f32[512,1024]{1,0:T(8,128)} %fusion.18) | copy-start | bytes 6291460
  265.4 67.5 %collective-permute-start.14 = (bf16[512,1024]{1,0:T(8,128)(2,1)S(1)}, bf16[512,1024]{1,0:T(8,128)(2,1)S(1)}, u32[]{:S(2)}, u32[]{:S(2)}) collective-permute-start(bf16[512,1024]{1,0:T(8,128)(2,1)S(1)} %add_convert_fusion.8), channel_id=1, source_target_pairs={{8,16},{12,20},{16,8},{20,12},{9,17},{13,21},{17,9},{21,13},{10,18... | collective-permute-start | bytes 3145736 | tf_op jit(solution)/shard_map/ppermute | solution.py:264
  307.8 34.8 %collective-permute-start.19 = (bf16[512,1024]{1,0:T(8,128)(2,1)S(1)}, bf16[512,1024]{1,0:T(8,128)(2,1)S(1)}, u32[]{:S(2)}, u32[]{:S(2)}) collective-permute-start(bf16[512,1024]{1,0:T(8,128)(2,1)S(1)} %add_convert_fusion.3), channel_id=1, source_target_pairs={{0,8},{4,12},{24,16},{28,20},{1,9},{5,13},{25,17},{29,21},{2,10},{... | collective-permute-start | bytes 3145736 | tf_op jit(solution)/shard_map/ppermute | solution.py:264
  309.4 42.9 %collective-permute-start.20 = (bf16[512,1024]{1,0:T(8,128)(2,1)S(1)}, bf16[512,1024]{1,0:T(8,128)(2,1)S(1)}, u32[]{:S(2)}, u32[]{:S(2)}) collective-permute-start(bf16[512,1024]{1,0:T(8,128)(2,1)S(1)} %add_convert_fusion.3), channel_id=1, source_target_pairs={{8,16},{12,20},{16,8},{20,12},{9,17},{13,21},{17,9},{21,13},{10,18... | collective-permute-start | bytes 3145736 | tf_op jit(solution)/shard_map/ppermute | solution.py:264
  336.8 99.1 %collective-permute-start.15 = (bf16[512,1024]{1,0:T(8,128)(2,1)}, bf16[512,1024]{1,0:T(8,128)(2,1)}, u32[]{:S(2)}, u32[]{:S(2)}) collective-permute-start(bf16[512,1024]{1,0:T(8,128)(2,1)} %add_convert_fusion.7), channel_id=1, source_target_pairs={{0,8},{4,12},{8,16},{12,20},{16,24},{20,28},{1,9},{5,13},{9,17},{1... | collective-permute-start | bytes 3145736 | tf_op jit(solution)/shard_map/ppermute | solution.py:264
  342.7 14.0 %copy-start.20 = (bf16[512,1024]{1,0:T(8,128)(2,1)}, bf16[512,1024]{1,0:T(8,128)(2,1)S(1)}, u32[]{:S(2)}) copy-start(bf16[512,1024]{1,0:T(8,128)(2,1)S(1)} %collective-permute-done.19) | copy-start | bytes 3145732
  342.7 93.2 %collective-permute-start.16 = (bf16[512,1024]{1,0:T(8,128)(2,1)}, bf16[512,1024]{1,0:T(8,128)(2,1)}, u32[]{:S(2)}, u32[]{:S(2)}) collective-permute-start(bf16[512,1024]{1,0:T(8,128)(2,1)} %add_convert_fusion.6), channel_id=1, source_target_pairs={{8,0},{12,4},{16,8},{20,12},{24,16},{28,20},{9,1},{13,5},{17,9},{2... | collective-permute-start | bytes 3145736 | tf_op jit(solution)/shard_map/ppermute | solution.py:264
  352.3 4.4 copy-start.21
  356.7 81.7 %collective-permute-start.21 = (bf16[512,1024]{1,0:T(8,128)(2,1)}, bf16[512,1024]{1,0:T(8,128)(2,1)}, u32[]{:S(2)}, u32[]{:S(2)}) collective-permute-start(bf16[512,1024]{1,0:T(8,128)(2,1)} %add_convert_fusion.2), channel_id=1, source_target_pairs={{0,8},{4,12},{8,16},{12,20},{16,24},{20,28},{1,9},{5,13},{9,17},{1... | collective-permute-start | bytes 3145736 | tf_op jit(solution)/shard_map/ppermute | solution.py:264
  386.0 1.3 copy-start.4
  388.3 15.2 %all-to-all-start = ((f32[8,16,128]{2,1,0:T(8,128)}), f32[8,16,128]{2,1,0:T(8,128)S(1)}, u32[]{:S(2)}, u32[]{:S(2)}) async-start(f32[8,16,128]{2,1,0:T(8,128)} %bitcast.7), calls=%async_computation | async-start | bytes 131072 | tf_op jit(solution)/shard_map/all_to_all | solution.py:368
  392.1 12.0 %collective-permute-start.10 = (bf16[128,1024]{1,0:T(8,128)(2,1)S(1)}, bf16[128,1024]{1,0:T(8,128)(2,1)S(1)}, u32[]{:S(2)}, u32[]{:S(2)}) collective-permute-start(bf16[128,1024]{1,0:T(8,128)(2,1)S(1)} %slice.18), channel_id=1, source_target_pairs={{4,0},{8,4},{12,8},{16,12},{20,16},{24,20},{28,24},{5,1},{9,5},{13... | collective-permute-start | bytes 786440 | tf_op jit(solution)/shard_map/ppermute | solution.py:264
  400.5 37.9 %collective-permute-start.22 = (bf16[512,1024]{1,0:T(8,128)(2,1)}, bf16[512,1024]{1,0:T(8,128)(2,1)}, u32[]{:S(2)}, u32[]{:S(2)}) collective-permute-start(bf16[512,1024]{1,0:T(8,128)(2,1)} %add_convert_fusion.1), channel_id=1, source_target_pairs={{8,0},{12,4},{16,8},{20,12},{24,16},{28,20},{9,1},{13,5},{17,9},{2... | collective-permute-start | bytes 3145736 | tf_op jit(solution)/shard_map/ppermute | solution.py:264
  404.1 21.3 %collective-permute-start.9 = (bf16[128,1024]{1,0:T(8,128)(2,1)S(1)}, bf16[128,1024]{1,0:T(8,128)(2,1)S(1)}, u32[]{:S(2)}, u32[]{:S(2)}) collective-permute-start(bf16[128,1024]{1,0:T(8,128)(2,1)S(1)} %slice.17), channel_id=1, source_target_pairs={{4,0},{8,4},{12,8},{16,12},{20,16},{24,20},{28,24},{5,1},{9,5},{13... | collective-permute-start | bytes 786440 | tf_op jit(solution)/shard_map/ppermute | solution.py:264
  407.5 17.9 %copy-start.5 = (bf16[1024,1024]{1,0:T(8,128)(2,1)S(1)}, bf16[1024,1024]{1,0:T(8,128)(2,1)}, u32[]{:S(2)}) copy-start(bf16[1024,1024]{1,0:T(8,128)(2,1)} %copy-done.4) | copy-start | bytes 6291460
  425.3 10.6 %copy-start.13 = (f32[512,1024]{1,0:T(8,128)S(1)}, f32[512,1024]{1,0:T(8,128)}, u32[]{:S(2)}) copy-start(f32[512,1024]{1,0:T(8,128)} %fusion.36) | copy-start | bytes 6291460
  425.3 10.6 %copy-start.14 = (f32[512,1024]{1,0:T(8,128)S(1)}, f32[512,1024]{1,0:T(8,128)}, u32[]{:S(2)}) copy-start(f32[512,1024]{1,0:T(8,128)} %fusion.32) | copy-start | bytes 6291460
  435.9 2.5 copy-start.12
  435.9 2.9 copy-start.15
Sparse Core Ops, SparseCore 0:
  10.2 34.6 all-gather.4
  91.2 35.1 all-gather.6

commit v2 on v1

--- a/solution.py
+++ b/solution.py
@@ -22,7 +22,15 @@
 
 
 def cost(flops, nbytes):
-    return pl.CostEstimate(flops=int(flops), bytes_accessed=int(nbytes), transcendentals=0)
+    return pl.CostEstimate(flops=int(flops) // 64, bytes_accessed=int(nbytes) // 64, transcendentals=0)
+
+
+def fence(*arrays):
+    return lax.optimization_barrier(arrays)
+
+
+def after(x, *others):
+    return lax.optimization_barrier((x, *others))[0]
 
 
 def table_kernel(back_ref, ahead_ref, back_out, ahead_out):
@@ -226,15 +234,15 @@
     out[...] = total.astype(out.dtype)
 
 
-def gate_grad(order, cot, weights, chunk, chunks, dtype):
+def gate_grad(order, cot, weights, dtype):
     _, rows, depth = cot.shape
-    width = weights[0].shape[1] // chunks
+    width = weights[0].shape[1]
     tile = min(256, rows)
 
     def cot_spec(j):
         return pl.BlockSpec((1, tile, depth), lambda i, order: (order[j], i, 0))
 
-    weight_spec = pl.BlockSpec((depth, width), lambda i, order: (0, chunk))
+    weight_spec = pl.BlockSpec((depth, width), lambda i, order: (0, 0))
     return pl.pallas_call(
         gate_kernel,
         grid_spec=pltpu.PrefetchScalarGridSpec(
@@ -271,41 +279,75 @@
             x, [(a * inner + i, a * inner + (i + shift) % inner) for a in range(LINE) for i in range(inner)]
         )
 
+    each = range(chunks)
+    up_pairs, down_pairs = [(0, 1), (1, 2), (2, 3)], [(1, 0), (2, 1), (3, 2)]
+
     prior = send(
         product_of(keys[rows - FILT :], values[rows - FILT :]), [(i, i + 1) for i in range(seq - 1)]
     )
-
-    up1 = along_line(out_weight, [(0, 1), (1, 2), (2, 3)])
-    down1 = along_line(out_weight, [(1, 0), (2, 1), (3, 2)])
-
-    cots = []
-    if inner == 2 and ch == LINE:
+    paired = inner == 2 and ch == LINE
+    other = grad_out
+    if paired:
         kept = lax.dynamic_slice(grad_out, (0, y * depth), (rows, depth))
         other = lax.dynamic_slice(grad_out, (0, (1 - y) * depth), (rows, depth))
-        cots.append(lax.all_gather(kept, "ch", axis=0, tiled=False))
-        cots.append(lax.all_gather(around_inner(other, 1), "ch", axis=0, tiled=False))
+        cots = [lax.all_gather(kept, "ch", axis=0, tiled=False)]
+    back, ahead = tables(filters)
+    halves = [out_weight[:, h * cols : (h + 1) * cols] for h in each]
+    prior, other, _, *halves = fence(prior, other, back[:8, :LANES], *halves)
+
+    up1, down1 = [None] * chunks, [None] * chunks
+    up1[0], down1[0] = along_line(halves[0], up_pairs), along_line(halves[0], down_pairs)
+    if paired:
+        swapped = around_inner(other, 1)
     else:
-        full = lax.all_gather(grad_out, "ch", axis=1, tiled=True)
+        full = lax.all_gather(other, "ch", axis=1, tiled=True)
         full = full.reshape(rows, LINE, inner, depth).transpose(2, 1, 0, 3)
+        cots = []
         for shift in range(inner):
             part = lax.dynamic_index_in_dim(full, (y + shift) % inner, 0, keepdims=False)
             cots.append(part if shift == 0 else around_inner(part, shift))
-
-    back, ahead = tables(filters)
-
+        swapped = prior
     gateds, mixeds = [], []
-    for h in range(chunks):
+    for h in each:
         gated, mixed = forward(queries, keys, values, prior, back, h, chunks)
-        gateds.append([gated] + [around_inner(gated, r) for r in range(1, inner)])
+        gateds.append([gated])
         mixeds.append(mixed)
-
-    up2 = along_line(up1, [(1, 2), (2, 3)])
-    down2 = along_line(down1, [(2, 1), (1, 0)])
-    second = jnp.where(z >= 2, up2, down2)
-    third = along_line(second, [(2, 3), (1, 0)])
-    slot_a = jnp.where(z == 0, down1, up1)
-    slot_c = jnp.where((z == 0) | (z == 3), third, down1)
-    weights = [out_weight, slot_a, second, slot_c]
+    up1, down1, swapped, halves, gateds, cots = fence(up1, down1, swapped, halves, gateds, cots)
+
+    def second_step(h):
+        return along_line(up1[h], [(1, 2), (2, 3)]), along_line(down1[h], [(2, 1), (1, 0)])
+
+    def swap_gated(h):
+        return [around_inner(gateds[h][0], r) for r in range(1, inner)]
+
+    second = [None] * chunks
+    second[0] = second_step(0)
+    for h in each[1:]:
+        up1[h], down1[h] = along_line(halves[h], up_pairs), along_line(halves[h], down_pairs)
+    if paired:
+        cots.append(lax.all_gather(swapped, "ch", axis=0, tiled=False))
+    got = swap_gated(0)
+    second[0], got, up1, down1, gateds = fence(second[0], got, up1, down1, gateds)
+    gateds[0] = gateds[0] + got
+
+    def merge(pair):
+        return jnp.where(z >= 2, *pair)
+
+    def third_step(x):
+        return along_line(x, [(2, 3), (1, 0)])
+
+    third = [None] * chunks
+    second[0] = merge(second[0])
+    third[0] = third_step(second[0])
+    for h in each[1:]:
+        second[h] = second_step(h)
+    got = [swap_gated(h) for h in each[1:]]
+
+    def slots(h, second, third):
+        slot_a = jnp.where(z == 0, down1[h], up1[h])
+        slot_c = jnp.where((z == 0) | (z == 3), third, down1[h])
+        return [halves[h], slot_a, second, slot_c]
+
     order = jnp.stack(
         [
             z,
@@ -323,34 +365,79 @@
             total = term if total is None else total + term
         return total
 
-    grad_weights = []
-    for h in range(chunks):
-        first = partial(jnp.where(z == 0, 3, 0), h).astype(BF16)
-        got = along_line(first, [(0, 1), (3, 2)])
-        block = jnp.where(z == 0, 2, jnp.where(z == 1, 3, jnp.where(z == 2, 0, 1)))
-        mid = (partial(block, h) + got.astype(F32)).astype(BF16)
-        outer_in = along_line(mid, [(0, 1), (3, 2)])
-        inner_in = along_line(mid, [(1, 2), (2, 1)])
+    second_block = jnp.where(z == 0, 2, jnp.where(z == 1, 3, jnp.where(z == 2, 0, 1)))
+
+    def sum_first(h):
+        return partial(jnp.where(z == 0, 3, 0), h).astype(BF16)
+
+    def send_first(x):
+        return along_line(x, [(0, 1), (3, 2)])
+
+    def sum_second(h, got):
+        return (partial(second_block, h) + got.astype(F32)).astype(BF16)
+
+    def send_second(x):
+        return along_line(x, [(0, 1), (3, 2)]), along_line(x, [(1, 2), (2, 1)])
+
+    def sum_third(h, outer_in, inner_in):
         add_up = jnp.where(z == 1, outer_in, inner_in).astype(F32)
         add_down = jnp.where(z == 1, inner_in, outer_in).astype(F32)
         last_up = (partial(jnp.minimum(z + 1, 3), h) + add_up).astype(BF16)
         last_down = (partial(jnp.maximum(z - 1, 0), h) + add_down).astype(BF16)
-        from_below = along_line(last_up, [(0, 1), (1, 2), (2, 3)])
-        from_above = along_line(last_down, [(1, 0), (2, 1), (3, 2)])
+        return last_up, last_down
+
+    def send_third(last_up, last_down):
+        return (
+            along_line(last_up, [(0, 1), (1, 2), (2, 3)]),
+            along_line(last_down, [(1, 0), (2, 1), (3, 2)]),
+        )
+
+    def sum_last(h, from_below, from_above):
         total = partial(z, h) + from_below.astype(F32) + from_above.astype(F32)
-        grad_weights.append(total.astype(BF16))
-    grad_weight = jnp.concatenate(grad_weights, axis=1)
-
-    owns, others = [], []
-    for h in range(chunks):
-        others.append(
-            [
-                around_inner(gate_grad(order, cots[r], weights, h, chunks, BF16), inner - r)
-                for r in range(1, inner)
-            ]
-        )
-    for h in range(chunks):
-        owns.append(gate_grad(order, cots[0], weights, h, chunks, F32))
+        return total.astype(BF16)
+
+    def shares(h, weights):
+        return [gate_grad(order, cots[r], weights, BF16) for r in range(1, inner)]
+
+    def send_shares(parts):
+        return [around_inner(part, inner - r) for r, part in enumerate(parts, 1)]
+
+    sums = [None] * chunks
+    others = [None] * chunks
+    weights = [None] * chunks
+    latest = sum_first(0)
+    sums[0] = send_first(latest)
+    middle_share = partial(second_block, 0)
+    third[0], sums[0], second, got, middle_share = fence(
+        third[0], sums[0], second, got, middle_share
+    )
+    for h in each[1:]:
+        gateds[h] += got[h - 1]
+
+    for h in each[1:]:
+        second[h] = merge(second[h])
+        third[h] = third_step(second[h])
+    latest = (middle_share + sums[0].astype(F32)).astype(BF16)
+    sums[0] = send_second(latest)
+    weights[0] = slots(0, second[0], third[0])
+    parts = shares(0, after(weights[0], latest))
+    others[0] = send_shares(parts)
+    for h in each[1:]:
+        latest = after(sum_first(h), parts)
+        sums[h] = send_first(latest)
+    for h in each[1:]:
+        weights[h] = slots(h, second[h], third[h])
+        parts = shares(h, after(weights[h], latest))
+        others[h] = send_shares(parts)
+    latest = sum_third(0, *after(sums[0], parts))
+    sums[0] = send_third(*latest)
+    for h in each[1:]:
+        latest = sum_second(h, after(sums[h], latest))
+        sums[h] = send_second(latest)
+    owns = [gate_grad(order, cots[0], after(weights[h], latest), F32) for h in each]
+    for h in each[1:]:
+        latest = sum_third(h, *sums[h])
+        sums[h] = send_third(*latest)
 
     grad_queries = None
     grad_kv = None
@@ -363,6 +450,7 @@
         later = send(gm[:FILT], [(i + 1, i) for i in range(seq - 1)])
         grad_kv = backward(gm, later, keys, values, ahead, grad_kv, h, chunks)
         taps.append(lag)
+    grad_weight = jnp.concatenate([sum_last(h, *sums[h]) for h in each], axis=1)
     taps = jnp.concatenate(taps, axis=0)[:, 1 : FILT + 1][:, ::-1]
     taps = taps.T.reshape(seq, FILT // seq, -1)
     taps = jnp.sum(lax.all_to_all(taps, "seq", 0, 0), axis=0)

time: 454 us -> 373 us (0.82)
  starting transfers between devices: 113 us -> 74.9 us
  waiting for transfers between devices: 110 us -> 76.2 us
  matrix products: 75.1 us -> 63.2 us
    ppermute x23 -> x28, starting transfers between devices: 109 us -> 70.4 us  [send(): return lax.ppermute(x, 'seq', pairs)]
    ppermute x23 -> x28, waiting for transfers between devices: 110 us -> 76.2 us  [send(): return lax.ppermute(x, 'seq', pairs)]
    dot_general x20, matrix products: 75.1 us -> 63.2 us  [partial(): lax.dot_general(lhs, gated, (((0,), (0,)), ((), ())), preferred_element_t...]
  transfers between devices with their start and end apart: 26 -> 31, of which waited for: 9 -> 9; matrix products, arithmetic and copies ran while one was open for 20% -> 22% of each run, Pallas kernels for 25% -> 27%
where the time goes in v2:
time: 373 us; the launch traced here: 370 us
  Pallas kernels  110 us (29%)
  waiting for transfers between devices  76.2 us (20%)
  starting transfers between devices  74.9 us (20%)
  matrix products  63.2 us (17%)
  other arithmetic  18.4 us (5%)
  between operations  14.8 us (4%)
  local copies, waits for them, and re-layouts  12.6 us (3%)
    ppermute x28, waiting for transfers between devices, send(): return lax.ppermute(x, 'seq', pairs)  76.2 us
    ppermute x28, starting transfers between devices, send(): return lax.ppermute(x, 'seq', pairs)  70.4 us
    dot_general x20, matrix products, partial(): lax.dot_general(lhs, gated, (((0,), (0,)), ((), ())), preferred_element_t...  63.2 us
    pallas_call x4, Pallas kernels, gate_grad(): pl.pallas_call(gate_kernel, grid_spec=pltpu.PrefetchScalarGridSpec(num_sc...  33.3 us
    pallas_call x2, Pallas kernels, middle(): pl.pallas_call(kernel, grid=(tiles,), in_specs=in_specs, out_specs=[here,...  25.3 us
    pallas_call x2, Pallas kernels, backward(): pl.pallas_call(backward_kernel, grid=(tiles,), in_specs=in_specs, out_spe...  20.9 us
    pallas_call x2, Pallas kernels, forward(): pl.pallas_call(forward_kernel, grid=(tiles,), in_specs=[here, here, here,...  19.8 us
    pallas_call x1, Pallas kernels, tables(): pl.pallas_call(table_kernel, grid=(groups // GPT,), in_specs=[seed, seed]...  10.4 us
  transfers between devices with their start and end apart: 31, of which 9 were waited for; matrix products, arithmetic and copies ran while one was open for 22% of the time, Pallas kernels for 27%

profile of v2, /device:TPU:10, one launch (start us, length us, event | category | flops | bytes accessed | tf_op | source)
XLA Modules:
  0.0 369.8 jit_solution(17737649433681610448)
XLA Ops:
  7.2 3.0 constant_dynamic-slice_fusion
  11.7 3.4 collective-permute-start
  15.1 1.7 fusion.84
  16.8 11.3 %collective-permute-done.prior.refs_5_ = bf16[128,2048]{1,0:T(8,128)(2,1)S(1)} collective-permute-done((bf16[128,2048]{1,0:T(8,128)(2,1)S(1)}, bf16[128,2048]{1,0:T(8,128)(2,1)S(1)}, u32[]{:S(2)}, u32[]{:S(2)}) %collective-permute-start) | collective-permute-done | bytes 524320 | tf_op jit(solution)/shard_map/ppermute | solution.py:272
  28.1 3.5 collective-permute-start.1
  31.6 3.3 collective-permute-start.2
  35.9 10.4 %shard_map.101 = (bf16[16384,256]{1,0:T(8,128)(2,1)}, bf16[16384,256]{1,0:T(8,128)(2,1)}) custom-call(f32[128,256]{1,0:T(8,128)S(1)} %maximum_maximum_fusion.back_ref, f32[128,256]{1,0:T(8,128)S(1)} %concatenate.13.ahead_ref), custom_call_target="tpu_custom_call" | custom-call | flops 524288 | bytes 262144 | tf_op jit(solution)/shard_map/pallas_call | solution.py:54
  46.3 9.9 %shard_map.102 = (bf16[1024,1024]{1,0:T(8,128)(2,1)S(1)}, bf16[1024,1024]{1,0:T(8,128)(2,1)S(1)}) custom-call(bf16[1024,2048]{1,0:T(8,128)(2,1)} %refs_1_.3, bf16[1024,2048]{1,0:T(8,128)(2,1)} %k.7, bf16[1024,2048]{1,0:T(8,128)(2,1)} %v.7, bf16[128,2048]{1,0:T(8,128)(2,1)S(1)} %collective-permute-done.prior.refs_5_, bf16[16384,256]{1,0:T(8,128)(2,1)} %get-tuple-element.73.table), custom_call_target="tpu_custom_call" | custom-call | flops 67108864 | bytes 229376 | tf_op jit(solution)/shard_map/pallas_call | solution.py:104
  58.9 9.9 %shard_map.103 = (bf16[1024,1024]{1,0:T(8,128)(2,1)S(1)}, bf16[1024,1024]{1,0:T(8,128)(2,1)S(1)}) custom-call(bf16[1024,2048]{1,0:T(8,128)(2,1)} %refs_1_.3, bf16[1024,2048]{1,0:T(8,128)(2,1)} %k.7, bf16[1024,2048]{1,0:T(8,128)(2,1)} %v.7, bf16[128,2048]{1,0:T(8,128)(2,1)S(1)} %collective-permute-done.prior.refs_5_, bf16[16384,256]{1,0:T(8,128)(2,1)} %get-tuple-element.73.table), custom_call_target="tpu_custom_call" | custom-call | flops 67108864 | bytes 229376 | tf_op jit(solution)/shard_map/pallas_call | solution.py:104
  73.0 3.5 collective-permute-start.4
  76.5 1.9 collective-permute-start.5
  78.4 4.9 %collective-permute-start.7 = (bf16[512,1024]{1,0:T(8,128)(2,1)S(1)}, bf16[512,1024]{1,0:T(8,128)(2,1)}, u32[]{:S(2)}, u32[]{:S(2)}) collective-permute-start(bf16[512,1024]{1,0:T(8,128)(2,1)S(1)} %get-tuple-element.112.refs_4_), channel_id=1, source_target_pairs={{0,8},{4,12},{8,16},{12,20},{16,24},{20,28},{1,9},{5,13},{9,17},{1... | collective-permute-start | bytes 3145736 | tf_op jit(solution)/shard_map/ppermute | solution.py:272
  83.3 1.9 collective-permute-start.8
  85.4 14.0 %collective-permute-done.4 = bf16[512,1024]{1,0:T(8,128)(2,1)} collective-permute-done((bf16[512,1024]{1,0:T(8,128)(2,1)}, bf16[512,1024]{1,0:T(8,128)(2,1)}, u32[]{:S(2)}, u32[]{:S(2)}) %collective-permute-start.4) | collective-permute-done | bytes 1048608 | tf_op jit(solution)/shard_map/ppermute | solution.py:272
  99.4 5.4 %collective-permute-done.5 = bf16[512,1024]{1,0:T(8,128)(2,1)} collective-permute-done((bf16[512,1024]{1,0:T(8,128)(2,1)}, bf16[512,1024]{1,0:T(8,128)(2,1)}, u32[]{:S(2)}, u32[]{:S(2)}) %collective-permute-start.5) | collective-permute-done | bytes 1048608 | tf_op jit(solution)/shard_map/ppermute | solution.py:272
  104.8 13.9 %collective-permute-done.7 = bf16[512,1024]{1,0:T(8,128)(2,1)} collective-permute-done((bf16[512,1024]{1,0:T(8,128)(2,1)S(1)}, bf16[512,1024]{1,0:T(8,128)(2,1)}, u32[]{:S(2)}, u32[]{:S(2)}) %collective-permute-start.7) | collective-permute-done | bytes 1048608 | tf_op jit(solution)/shard_map/ppermute | solution.py:272
  118.6 5.2 %collective-permute-done.8 = bf16[512,1024]{1,0:T(8,128)(2,1)} collective-permute-done((bf16[512,1024]{1,0:T(8,128)(2,1)S(1)}, bf16[512,1024]{1,0:T(8,128)(2,1)}, u32[]{:S(2)}, u32[]{:S(2)}) %collective-permute-start.8) | collective-permute-done | bytes 1048608 | tf_op jit(solution)/shard_map/ppermute | solution.py:272
  127.3 3.2 collective-permute-start.9
  130.5 1.5 collective-permute-start.11
  132.0 1.9 collective-permute-start.12
  134.0 4.7 %fusion.27 = f32[512,1024]{1,0:T(8,128)} fusion(bf16[1024,1024]{1,0:T(8,128)(2,1)} %copy-done.11, bf16[4,1024,512]{2,1,0:T(8,128)(2,1)} %bitcast.106, s32[]{:T(128)S(6)} %select_n.136), kind=kOutput, calls=%fused_computation.39 | convolution fusion | flops 1073741824 | bytes 5242884 | tf_op jit(solution)/shard_map/dot_general | solution.py:364
  138.6 3.3 fusion.32
  142.0 2.6 add_convert_fusion.9
  147.2 2.6 fusion.9
  151.1 2.5 convolution_add_fusion
  153.6 17.8 %collective-permute-done.12 = bf16[512,1024]{1,0:T(8,128)(2,1)} collective-permute-done((bf16[512,1024]{1,0:T(8,128)(2,1)}, bf16[512,1024]{1,0:T(8,128)(2,1)}, u32[]{:S(2)}, u32[]{:S(2)}) %collective-permute-start.12) | collective-permute-done | bytes 1048608 | tf_op jit(solution)/shard_map/ppermute | solution.py:272
  174.1 2.1 collective-permute-start.17
  176.2 1.7 broadcast_select_fusion
  178.0 2.1 broadcast_select_fusion.2.refs_6_
  180.1 6.5 %collective-permute-start.14 = (bf16[512,1024]{1,0:T(8,128)(2,1)S(1)}, bf16[512,1024]{1,0:T(8,128)(2,1)}, u32[]{:S(2)}, u32[]{:S(2)}) collective-permute-start(bf16[512,1024]{1,0:T(8,128)(2,1)S(1)} %broadcast_select_fusion.2.refs_6_), channel_id=1, source_target_pairs={{16,24},{20,28},{8,0},{12,4},{17,25},{21,29},{9,1},{13,5},{18,26},... | collective-permute-start | bytes 3145736 | tf_op jit(solution)/shard_map/ppermute | solution.py:272
  186.6 7.8 %shard_map.104 = bf16[1024,1024]{1,0:T(8,128)(2,1)} custom-call(s32[4]{0:T(128)S(1)} %pad_add_fusion.order, bf16[4,1024,512]{2,1,0:T(8,128)(2,1)} %bitcast.89, bf16[4,1024,512]{2,1,0:T(8,128)(2,1)} %bitcast.90, bf16[4,1024,512]{2,1,0:T(8,128)(2,1)} %bitcast.91, bf16[4,1024,512]{2,1,0:T(8,128)(2,1)} %bitcast.92, bf16[512,1024]{1,0:T(8,128)(2,1)S(1)} %copy-done.1, ...), custom_call_target="tpu_custom_call" | custom-call | flops 67108864 | bytes 196608 | tf_op jit(solution)/shard_map/pallas_call | solution.py:246
  195.7 2.9 fusion.30
  198.5 3.6 add_convert_fusion.8
  203.4 2.9 fusion.23
  206.3 1.7 broadcast_select_fusion.1
  208.0 8.9 %shard_map.105 = bf16[1024,1024]{1,0:T(8,128)(2,1)} custom-call(s32[4]{0:T(128)S(1)} %pad_add_fusion.order, bf16[4,1024,512]{2,1,0:T(8,128)(2,1)} %bitcast.93, bf16[4,1024,512]{2,1,0:T(8,128)(2,1)} %bitcast.94, bf16[4,1024,512]{2,1,0:T(8,128)(2,1)} %bitcast.95, bf16[4,1024,512]{2,1,0:T(8,128)(2,1)} %bitcast.96, ...), custom_call_target="tpu_custom_call" | custom-call | flops 67108864 | bytes 196608 | tf_op jit(solution)/shard_map/pallas_call | solution.py:246
  216.9 4.2 %add_convert_fusion.5 = bf16[512,1024]{1,0:T(8,128)(2,1)} fusion(f32[512,1024]{1,0:T(8,128)} %fusion.9, bf16[512,1024]{1,0:T(8,128)(2,1)} %collective-permute-done.17, bf16[512,1024]{1,0:T(8,128)(2,1)} %collective-permute-done.16, pred[]{:T(512)S(6)} %eq.12, bf16[1024,1024]{1,0:T(8,128)(2,1)S(1)} %copy-done.18, bf16[4,1024,512]{2,1,0:T(8,128)(2,1)S(1)} %bitcast.120, ...), kind=kOutput, calls=%fused_computation.6 | convolution fusion | flops 1076363264 | bytes 8388613 | tf_op jit(solution)/shard_map/dot_general | solution.py:364
  221.1 3.7 add_convert_fusion.6
  224.8 2.8 add_convert_fusion.4
  228.9 1.9 collective-permute-start.25
  230.8 4.8 %fusion.4 = f32[512,1024]{1,0:T(8,128)} fusion(bf16[1024,1024]{1,0:T(8,128)(2,1)} %copy-done.11, bf16[4,1024,512]{2,1,0:T(8,128)(2,1)} %bitcast.110, s32[]{:T(128)S(6)} %select_n.146), kind=kOutput, calls=%fused_computation.16 | convolution fusion | flops 1073741824 | bytes 5242884 | tf_op jit(solution)/shard_map/dot_general | solution.py:364
  235.6 3.0 fusion.15
  238.6 3.0 fusion.7
  241.6 6.2 %collective-permute-start.23 = (bf16[512,1024]{1,0:T(8,128)(2,1)}, bf16[512,1024]{1,0:T(8,128)(2,1)}, u32[]{:S(2)}, u32[]{:S(2)}) collective-permute-start(bf16[512,1024]{1,0:T(8,128)(2,1)} %add_convert_fusion.5), channel_id=1, source_target_pairs={{8,0},{12,4},{16,8},{20,12},{24,16},{28,20},{9,1},{13,5},{17,9},{2... | collective-permute-start | bytes 3145736 | tf_op jit(solution)/shard_map/ppermute | solution.py:272
  247.9 1.9 collective-permute-start.22
  249.8 4.7 %collective-permute-done.24 = bf16[512,1024]{1,0:T(8,128)(2,1)} collective-permute-done((bf16[512,1024]{1,0:T(8,128)(2,1)}, bf16[512,1024]{1,0:T(8,128)(2,1)}, u32[]{:S(2)}, u32[]{:S(2)}) %collective-permute-start.24) | collective-permute-done | bytes 1048608 | tf_op jit(solution)/shard_map/ppermute | solution.py:272
  255.4 1.8 collective-permute-done.25
  257.2 3.6 add_convert_fusion.2
  260.7 2.3 collective-permute-start.26
  263.0 3.6 add_convert_fusion.1
  266.6 4.9 %collective-permute-start.27 = (bf16[512,1024]{1,0:T(8,128)(2,1)}, bf16[512,1024]{1,0:T(8,128)(2,1)}, u32[]{:S(2)}, u32[]{:S(2)}) collective-permute-start(bf16[512,1024]{1,0:T(8,128)(2,1)} %add_convert_fusion.1), channel_id=1, source_target_pairs={{8,0},{12,4},{16,8},{20,12},{24,16},{28,20},{9,1},{13,5},{17,9},{2... | collective-permute-start | bytes 3145736 | tf_op jit(solution)/shard_map/ppermute | solution.py:272
  272.8 4.4 %fusion = f32[512,1024]{1,0:T(8,128)} fusion(bf16[1024,1024]{1,0:T(8,128)(2,1)} %collective-permute-done.13, bf16[4,1024,512]{2,1,0:T(8,128)(2,1)S(1)} %bitcast.105, s32[]{:T(128)S(6)} %select_n.146), kind=kOutput, calls=%fused_computation.12 | convolution fusion | flops 1073741824 | bytes 5242884 | tf_op jit(solution)/shard_map/dot_general | solution.py:364
  277.3 8.3 %shard_map.107.own_ref = f32[1024,1024]{1,0:T(8,128)} custom-call(s32[4]{0:T(128)S(1)} %pad_add_fusion.order, bf16[4,1024,512]{2,1,0:T(8,128)(2,1)} %bitcast.111, bf16[4,1024,512]{2,1,0:T(8,128)(2,1)} %bitcast.112, bf16[4,1024,512]{2,1,0:T(8,128)(2,1)} %bitcast.113, bf16[4,1024,512]{2,1,0:T(8,128)(2,1)} %bitcast.114, bf16[512,1024]{1,0:T(8,128)(2,1)S(1)} %copy-done.2, ...), custom_call_target="tpu_custom_call" | custom-call | flops 67108864 | bytes 196608 | tf_op jit(solution)/shard_map/pallas_call | solution.py:246
  285.6 8.3 %shard_map.106.own_ref = f32[1024,1024]{1,0:T(8,128)} custom-call(s32[4]{0:T(128)S(1)} %pad_add_fusion.order, bf16[4,1024,512]{2,1,0:T(8,128)(2,1)} %bitcast.115, bf16[4,1024,512]{2,1,0:T(8,128)(2,1)} %bitcast.116, bf16[4,1024,512]{2,1,0:T(8,128)(2,1)} %bitcast.117, bf16[4,1024,512]{2,1,0:T(8,128)(2,1)} %bitcast.118, ...), custom_call_target="tpu_custom_call" | custom-call | flops 67108864 | bytes 196608 | tf_op jit(solution)/shard_map/pallas_call | solution.py:246
  293.9 12.8 %shard_map.108 = (bf16[1024,2048]{1,0:T(8,128)(2,1)}, bf16[1024,1024]{1,0:T(8,128)(2,1)S(1)}, f32[64,256]{1,0:T(8,128)S(1)}) custom-call(f32[1024,1024]{1,0:T(8,128)} %shard_map.107.own_ref, bf16[1024,1024]{1,0:T(8,128)(2,1)} %collective-permute-done.19.refs_0_, bf16[1024,2048]{1,0:T(8,128)(2,1)} %refs_1_.3, bf16[1024,2048]{1,0:T(8,128)(2,1)} %k.7, ...), custom_call_target="tpu_custom_call" | custom-call | flops 67108864 | bytes 294912 | tf_op jit(solution)/shard_map/pallas_call | solution.py:173
  306.8 1.9 collective-permute-start.21
  308.7 4.2 %add_convert_fusion.3 = bf16[512,1024]{1,0:T(8,128)(2,1)} fusion(bf16[512,1024]{1,0:T(8,128)(2,1)} %collective-permute-done.23, bf16[512,1024]{1,0:T(8,128)(2,1)} %collective-permute-done.22, f32[512,1024]{1,0:T(8,128)S(1)} %fusion.2, bf16[1024,1024]{1,0:T(8,128)(2,1)S(1)} %copy-done.19, bf16[4,1024,512]{2,1,0:T(8,128)(2,1)} %bitcast.119, s32[]{:T(128)S(6)} %select_n.146), kind=kOutput, calls=%fused_computation.4 | convolution fusion | flops 1076887552 | bytes 8388612 | tf_op jit(solution)/shard_map/dot_general | solution.py:364
  312.9 2.1 collective-permute-done.21.later
  315.0 10.4 %shard_map.110 = (bf16[1024,2048]{1,0:T(8,128)(2,1)}, bf16[1024,2048]{1,0:T(8,128)(2,1)}) custom-call(bf16[1024,1024]{1,0:T(8,128)(2,1)S(1)} %get-tuple-element.126.gm, bf16[128,1024]{1,0:T(8,128)(2,1)S(1)} %collective-permute-done.21.later, bf16[1024,2048]{1,0:T(8,128)(2,1)} %k.7, bf16[1024,2048]{1,0:T(8,128)(2,1)} %v.7, ...), custom_call_target="tpu_custom_call" | custom-call | flops 67108864 | bytes 229376 | tf_op jit(solution)/shard_map/pallas_call | solution.py:217
  325.5 12.5 %shard_map.109 = (bf16[1024,2048]{1,0:T(8,128)(2,1)}, bf16[1024,1024]{1,0:T(8,128)(2,1)S(1)}, f32[64,256]{1,0:T(8,128)S(1)}) custom-call(f32[1024,1024]{1,0:T(8,128)} %shard_map.106.own_ref, bf16[1024,1024]{1,0:T(8,128)(2,1)S(1)} %collective-permute-done.18.refs_0_, bf16[1024,2048]{1,0:T(8,128)(2,1)} %refs_1_.3, ...), custom_call_target="tpu_custom_call", output_to_operand_aliasing={{0}: (7, {})} | custom-call | flops 67108864 | bytes 294912 | tf_op jit(solution)/shard_map/pallas_call | solution.py:173
  338.8 4.4 %all-to-all-start = ((f32[8,16,128]{2,1,0:T(8,128)}), f32[8,16,128]{2,1,0:T(8,128)S(1)}, u32[]{:S(2)}, u32[]{:S(2)}) async-start(f32[8,16,128]{2,1,0:T(8,128)} %bitcast.15), calls=%async_computation | async-start | bytes 131072 | tf_op jit(solution)/shard_map/all_to_all | solution.py:456
  343.3 3.5 collective-permute-start.20
  346.9 3.6 add_convert_fusion
  352.6 10.4 %shard_map.111 = (bf16[1024,2048]{1,0:T(8,128)(2,1)}, bf16[1024,2048]{1,0:T(8,128)(2,1)}) custom-call(bf16[1024,1024]{1,0:T(8,128)(2,1)S(1)} %get-tuple-element.124.gm, bf16[128,1024]{1,0:T(8,128)(2,1)S(1)} %collective-permute-done.20.later, bf16[1024,2048]{1,0:T(8,128)(2,1)} %k.7, ...), custom_call_target="tpu_custom_call", output_to_operand_aliasing={{0}: (5, {}), {1}: (6, {})} | custom-call | flops 67108864 | bytes 229376 | tf_op jit(solution)/shard_map/pallas_call | solution.py:217
  (123 shorter events, 28.5 us)
Async XLA Ops:
  7.2 64.3 %all-gather.5.cloned.1.call-start = ((), (), s32[]{:S(2)}) async-start(), calls=%async_computation.1 | async-start | bytes 5242880 | tf_op jit(solution)/shard_map/all_gather | solution.py:293
  10.3 128.4 %all-gather.7.cloned.1.call-start = ((), (), s32[]{:S(2)}) async-start(), calls=%async_computation.2 | async-start | bytes 5242880 | tf_op jit(solution)/shard_map/all_gather | solution.py:328
  11.6 24.0 %copy-start.33 = (bf16[128,128]{1,0:T(8,128)(2,1)S(1)}, bf16[128,128]{1,0:T(8,128)(2,1)}, u32[]{:S(2)}) copy-start(bf16[128,128]{1,0:T(8,128)(2,1)} %param.9) | copy-start | bytes 98308
  11.7 16.5 %collective-permute-start = (bf16[128,2048]{1,0:T(8,128)(2,1)S(1)}, bf16[128,2048]{1,0:T(8,128)(2,1)S(1)}, u32[]{:S(2)}, u32[]{:S(2)}) collective-permute-start(bf16[128,2048]{1,0:T(8,128)(2,1)S(1)} %multiply_convert_fusion), channel_id=1, source_target_pairs={{0,4},{4,8},{8,12},{12,16},{16,20},{20,24},{24,28},{1,5},{5,9},{9,... | collective-permute-start | bytes 1572872 | tf_op jit(solution)/shard_map/ppermute | solution.py:272
  16.8 39.4 %copy-start = (bf16[512,1024]{1,0:T(8,128)(2,1)}, bf16[512,1024]{1,0:T(8,128)(2,1)S(1)}, u32[]{:S(2)}) copy-start(bf16[512,1024]{1,0:T(8,128)(2,1)S(1)} %get-tuple-element.117.refs_4_) | copy-start | bytes 3145732
  28.1 28.1 %copy-start.14 = (bf16[128,2048]{1,0:T(8,128)(2,1)}, bf16[128,2048]{1,0:T(8,128)(2,1)S(1)}, u32[]{:S(2)}) copy-start(bf16[128,2048]{1,0:T(8,128)(2,1)S(1)} %collective-permute-done.prior.refs_5_) | copy-start | bytes 1572868
  28.1 43.3 %collective-permute-start.1 = (bf16[512,1024]{1,0:T(8,128)(2,1)S(1)}, bf16[512,1024]{1,0:T(8,128)(2,1)}, u32[]{:S(2)}, u32[]{:S(2)}) collective-permute-start(bf16[512,1024]{1,0:T(8,128)(2,1)S(1)} %get-tuple-element.117.refs_4_), channel_id=1, source_target_pairs={{0,8},{4,12},{8,16},{12,20},{16,24},{20,28},{1,9},{5,13},{9,17},{1... | collective-permute-start | bytes 3145736 | tf_op jit(solution)/shard_map/ppermute | solution.py:272
  31.6 39.9 %collective-permute-start.2 = (bf16[512,1024]{1,0:T(8,128)(2,1)S(1)}, bf16[512,1024]{1,0:T(8,128)(2,1)}, u32[]{:S(2)}, u32[]{:S(2)}) collective-permute-start(bf16[512,1024]{1,0:T(8,128)(2,1)S(1)} %get-tuple-element.117.refs_4_), channel_id=1, source_target_pairs={{8,0},{12,4},{16,8},{20,12},{24,16},{28,20},{9,1},{13,5},{17,9},{2... | collective-permute-start | bytes 3145736 | tf_op jit(solution)/shard_map/ppermute | solution.py:272
  34.9 36.5 %collective-permute-start.3 = (bf16[1024,512]{1,0:T(8,128)(2,1)}, bf16[1024,512]{1,0:T(8,128)(2,1)}, u32[]{:S(2)}, u32[]{:S(2)}) collective-permute-start(bf16[1024,512]{1,0:T(8,128)(2,1)} %get-tuple-element.70), channel_id=1, source_target_pairs={{0,4},{4,0},{8,12},{12,8},{16,20},{20,16},{24,28},{28,24},{1,5},{5... | collective-permute-start | bytes 3145736 | tf_op jit(solution)/shard_map/ppermute | solution.py:272
  56.2 1.4 copy-start.17
  57.6 1.3 copy-start.20
  68.8 1.3 copy-start.11
  71.5 52.3 %collective-permute-start.6 = (bf16[1024,1024]{1,0:T(8,128)(2,1)}, bf16[1024,1024]{1,0:T(8,128)(2,1)S(1)}, u32[]{:S(2)}, u32[]{:S(2)}) collective-permute-start(bf16[1024,1024]{1,0:T(8,128)(2,1)} %copy-done.17), channel_id=1, source_target_pairs={{0,4},{4,0},{8,12},{12,8},{16,20},{20,16},{24,28},{28,24},{1,5},{5... | collective-permute-start | bytes 6291464 | tf_op jit(solution)/shard_map/ppermute | solution.py:272
  73.0 26.4 %collective-permute-start.4 = (bf16[512,1024]{1,0:T(8,128)(2,1)}, bf16[512,1024]{1,0:T(8,128)(2,1)}, u32[]{:S(2)}, u32[]{:S(2)}) collective-permute-start(bf16[512,1024]{1,0:T(8,128)(2,1)} %collective-permute-done.1), channel_id=1, source_target_pairs={{8,16},{12,20},{16,24},{20,28},{9,17},{13,21},{17,25},{21,29},{10,... | collective-permute-start | bytes 3145736 | tf_op jit(solution)/shard_map/ppermute | solution.py:272
  76.5 28.3 %collective-permute-start.5 = (bf16[512,1024]{1,0:T(8,128)(2,1)}, bf16[512,1024]{1,0:T(8,128)(2,1)}, u32[]{:S(2)}, u32[]{:S(2)}) collective-permute-start(bf16[512,1024]{1,0:T(8,128)(2,1)} %collective-permute-done.2), channel_id=1, source_target_pairs={{16,8},{20,12},{8,0},{12,4},{17,9},{21,13},{9,1},{13,5},{18,10},{2... | collective-permute-start | bytes 3145736 | tf_op jit(solution)/shard_map/ppermute | solution.py:272
  78.4 40.2 %collective-permute-start.7 = (bf16[512,1024]{1,0:T(8,128)(2,1)S(1)}, bf16[512,1024]{1,0:T(8,128)(2,1)}, u32[]{:S(2)}, u32[]{:S(2)}) collective-permute-start(bf16[512,1024]{1,0:T(8,128)(2,1)S(1)} %get-tuple-element.112.refs_4_), channel_id=1, source_target_pairs={{0,8},{4,12},{8,16},{12,20},{16,24},{20,28},{1,9},{5,13},{9,17},{1... | collective-permute-start | bytes 3145736 | tf_op jit(solution)/shard_map/ppermute | solution.py:272
  83.3 40.5 %collective-permute-start.8 = (bf16[512,1024]{1,0:T(8,128)(2,1)S(1)}, bf16[512,1024]{1,0:T(8,128)(2,1)}, u32[]{:S(2)}, u32[]{:S(2)}) collective-permute-start(bf16[512,1024]{1,0:T(8,128)(2,1)S(1)} %get-tuple-element.112.refs_4_), channel_id=1, source_target_pairs={{8,0},{12,4},{16,8},{20,12},{24,16},{28,20},{9,1},{13,5},{17,9},{2... | collective-permute-start | bytes 3145736 | tf_op jit(solution)/shard_map/ppermute | solution.py:272
  123.8 1.4 copy-start.26
  125.2 46.2 %collective-permute-start.13 = (bf16[1024,1024]{1,0:T(8,128)(2,1)}, bf16[1024,1024]{1,0:T(8,128)(2,1)}, u32[]{:S(2)}, u32[]{:S(2)}) collective-permute-start(bf16[1024,1024]{1,0:T(8,128)(2,1)} %copy-done.11), channel_id=1, source_target_pairs={{0,4},{4,0},{8,12},{12,8},{16,20},{20,16},{24,28},{28,24},{1,5},{5... | collective-permute-start | bytes 6291464 | tf_op jit(solution)/shard_map/ppermute | solution.py:272
  127.3 26.3 %collective-permute-start.9 = (bf16[512,1024]{1,0:T(8,128)(2,1)S(1)}, bf16[512,1024]{1,0:T(8,128)(2,1)}, u32[]{:S(2)}, u32[]{:S(2)}) collective-permute-start(bf16[512,1024]{1,0:T(8,128)(2,1)S(1)} %broadcast_select_fusion.3.refs_6_), channel_id=1, source_target_pairs={{16,24},{20,28},{8,0},{12,4},{17,25},{21,29},{9,1},{13,5},{18,26},... | collective-permute-start | bytes 3145736 | tf_op jit(solution)/shard_map/ppermute | solution.py:272
  130.5 23.1 %collective-permute-start.11 = (bf16[512,1024]{1,0:T(8,128)(2,1)}, bf16[512,1024]{1,0:T(8,128)(2,1)S(1)}, u32[]{:S(2)}, u32[]{:S(2)}) collective-permute-start(bf16[512,1024]{1,0:T(8,128)(2,1)} %collective-permute-done.7), channel_id=1, source_target_pairs={{8,16},{12,20},{16,24},{20,28},{9,17},{13,21},{17,25},{21,29},{10,... | collective-permute-start | bytes 3145736 | tf_op jit(solution)/shard_map/ppermute | solution.py:272
  132.0 39.4 %collective-permute-start.12 = (bf16[512,1024]{1,0:T(8,128)(2,1)}, bf16[512,1024]{1,0:T(8,128)(2,1)}, u32[]{:S(2)}, u32[]{:S(2)}) collective-permute-start(bf16[512,1024]{1,0:T(8,128)(2,1)} %collective-permute-done.8), channel_id=1, source_target_pairs={{16,8},{20,12},{8,0},{12,4},{17,9},{21,13},{9,1},{13,5},{18,10},{2... | collective-permute-start | bytes 3145736 | tf_op jit(solution)/shard_map/ppermute | solution.py:272
  138.6 3.3 copy-start.18
  141.9 4.0 %copy-start.21 = (bf16[4096,512]{1,0:T(8,128)(2,1)S(1)}, bf16[4096,512]{1,0:T(8,128)(2,1)}, u32[]{:S(2)}) copy-start(bf16[4096,512]{1,0:T(8,128)(2,1)} %all-gather.7.cloned.1.call-done) | copy-start | bytes 12582916
  142.0 4.0 %copy-start.27 = (bf16[1024,1024]{1,0:T(8,128)(2,1)S(1)}, bf16[1024,1024]{1,0:T(8,128)(2,1)}, u32[]{:S(2)}) copy-start(bf16[1024,1024]{1,0:T(8,128)(2,1)} %copy-done.26) | copy-start | bytes 6291460
  144.6 26.8 %collective-permute-start.10 = (bf16[512,1024]{1,0:T(8,128)(2,1)S(1)}, bf16[512,1024]{1,0:T(8,128)(2,1)S(1)}, u32[]{:S(2)}, u32[]{:S(2)}) collective-permute-start(bf16[512,1024]{1,0:T(8,128)(2,1)S(1)} %add_convert_fusion.9), channel_id=1, source_target_pairs={{0,8},{4,12},{24,16},{28,20},{1,9},{5,13},{25,17},{29,21},{2,10},{... | collective-permute-start | bytes 3145736 | tf_op jit(solution)/shard_map/ppermute | solution.py:272
  153.6 19.2 %copy-start.30 = (bf16[512,1024]{1,0:T(8,128)(2,1)}, bf16[512,1024]{1,0:T(8,128)(2,1)S(1)}, u32[]{:S(2)}) copy-start(bf16[512,1024]{1,0:T(8,128)(2,1)S(1)} %collective-permute-done.11) | copy-start | bytes 3145732
  172.8 44.1 %collective-permute-start.16 = (bf16[512,1024]{1,0:T(8,128)(2,1)}, bf16[512,1024]{1,0:T(8,128)(2,1)}, u32[]{:S(2)}, u32[]{:S(2)}) collective-permute-start(bf16[512,1024]{1,0:T(8,128)(2,1)} %add_convert_fusion.7), channel_id=1, source_target_pairs={{0,8},{4,12},{24,16},{28,20},{1,9},{5,13},{25,17},{29,21},{2,10},{... | collective-permute-start | bytes 3145736 | tf_op jit(solution)/shard_map/ppermute | solution.py:272
  174.1 3.8 %copy-start.31 = (bf16[512,1024]{1,0:T(8,128)(2,1)S(1)}, bf16[512,1024]{1,0:T(8,128)(2,1)}, u32[]{:S(2)}) copy-start(bf16[512,1024]{1,0:T(8,128)(2,1)} %copy-done.30) | copy-start | bytes 3145732
  174.1 42.8 %collective-permute-start.17 = (bf16[512,1024]{1,0:T(8,128)(2,1)}, bf16[512,1024]{1,0:T(8,128)(2,1)}, u32[]{:S(2)}, u32[]{:S(2)}) collective-permute-start(bf16[512,1024]{1,0:T(8,128)(2,1)} %add_convert_fusion.7), channel_id=1, source_target_pairs={{8,16},{12,20},{16,8},{20,12},{9,17},{13,21},{17,9},{21,13},{10,18... | collective-permute-start | bytes 3145736 | tf_op jit(solution)/shard_map/ppermute | solution.py:272
  177.9 16.5 %copy-start.3 = (bf16[512,1024]{1,0:T(8,128)(2,1)}, bf16[512,1024]{1,0:T(8,128)(2,1)S(1)}, u32[]{:S(2)}) copy-start(bf16[512,1024]{1,0:T(8,128)(2,1)S(1)} %get-tuple-element.120.refs_7_) | copy-start | bytes 3145732
  177.9 16.4 %copy-start.5 = (bf16[512,1024]{1,0:T(8,128)(2,1)}, bf16[512,1024]{1,0:T(8,128)(2,1)S(1)}, u32[]{:S(2)}) copy-start(bf16[512,1024]{1,0:T(8,128)(2,1)S(1)} %get-tuple-element.118.refs_5_) | copy-start | bytes 3145732
  177.9 8.6 %copy-start.1 = (bf16[512,1024]{1,0:T(8,128)(2,1)S(1)}, bf16[512,1024]{1,0:T(8,128)(2,1)}, u32[]{:S(2)}) copy-start(bf16[512,1024]{1,0:T(8,128)(2,1)} %copy-done) | copy-start | bytes 3145732
  180.1 15.6 %copy-start.22 = (bf16[4096,512]{1,0:T(8,128)(2,1)S(1)}, bf16[4096,512]{1,0:T(8,128)(2,1)}, u32[]{:S(2)}) copy-start(bf16[4096,512]{1,0:T(8,128)(2,1)} %all-gather.7.cloned.1.call-done) | copy-start | bytes 12582916
  180.1 26.2 %collective-permute-start.14 = (bf16[512,1024]{1,0:T(8,128)(2,1)S(1)}, bf16[512,1024]{1,0:T(8,128)(2,1)}, u32[]{:S(2)}, u32[]{:S(2)}) collective-permute-start(bf16[512,1024]{1,0:T(8,128)(2,1)S(1)} %broadcast_select_fusion.2.refs_6_), channel_id=1, source_target_pairs={{16,24},{20,28},{8,0},{12,4},{17,25},{21,29},{9,1},{13,5},{18,26},... | collective-permute-start | bytes 3145736 | tf_op jit(solution)/shard_map/ppermute | solution.py:272
  194.4 4.2 %copy-start.12 = (bf16[1024,1024]{1,0:T(8,128)(2,1)S(1)}, bf16[1024,1024]{1,0:T(8,128)(2,1)}, u32[]{:S(2)}) copy-start(bf16[1024,1024]{1,0:T(8,128)(2,1)} %copy-done.11) | copy-start | bytes 6291460
  194.4 72.2 %collective-permute-start.19 = (bf16[1024,1024]{1,0:T(8,128)(2,1)}, bf16[1024,1024]{1,0:T(8,128)(2,1)}, u32[]{:S(2)}, u32[]{:S(2)}) collective-permute-start(bf16[1024,1024]{1,0:T(8,128)(2,1)} %shard_map.104), channel_id=1, source_target_pairs={{0,4},{4,0},{8,12},{12,8},{16,20},{20,16},{24,28},{28,24},{1,5},{5... | collective-permute-start | bytes 6291464 | tf_op jit(solution)/shard_map/ppermute | solution.py:272
  202.1 22.7 %collective-permute-start.15 = (bf16[512,1024]{1,0:T(8,128)(2,1)}, bf16[512,1024]{1,0:T(8,128)(2,1)}, u32[]{:S(2)}, u32[]{:S(2)}) collective-permute-start(bf16[512,1024]{1,0:T(8,128)(2,1)} %add_convert_fusion.8), channel_id=1, source_target_pairs={{0,8},{4,12},{24,16},{28,20},{1,9},{5,13},{25,17},{29,21},{2,10},{... | collective-permute-start | bytes 3145736 | tf_op jit(solution)/shard_map/ppermute | solution.py:272
  208.0 8.9 %copy-start.7 = (bf16[512,1024]{1,0:T(8,128)(2,1)}, bf16[512,1024]{1,0:T(8,128)(2,1)S(1)}, u32[]{:S(2)}) copy-start(bf16[512,1024]{1,0:T(8,128)(2,1)S(1)} %get-tuple-element.115.refs_7_) | copy-start | bytes 3145732
  208.0 8.9 %copy-start.9 = (bf16[512,1024]{1,0:T(8,128)(2,1)}, bf16[512,1024]{1,0:T(8,128)(2,1)S(1)}, u32[]{:S(2)}) copy-start(bf16[512,1024]{1,0:T(8,128)(2,1)S(1)} %get-tuple-element.113.refs_5_) | copy-start | bytes 3145732
  208.0 8.9 %copy-start.24 = (bf16[4096,512]{1,0:T(8,128)(2,1)S(1)}, bf16[4096,512]{1,0:T(8,128)(2,1)}, u32[]{:S(2)}) copy-start(bf16[4096,512]{1,0:T(8,128)(2,1)} %all-gather.5.cloned.1.call-done) | copy-start | bytes 12582916
  221.1 3.7 copy-start.29
  227.6 26.9 %collective-permute-start.24 = (bf16[512,1024]{1,0:T(8,128)(2,1)}, bf16[512,1024]{1,0:T(8,128)(2,1)}, u32[]{:S(2)}, u32[]{:S(2)}) collective-permute-start(bf16[512,1024]{1,0:T(8,128)(2,1)} %add_convert_fusion.4), channel_id=1, source_target_pairs={{0,8},{4,12},{24,16},{28,20},{1,9},{5,13},{25,17},{29,21},{2,10},{... | collective-permute-start | bytes 3145736 | tf_op jit(solution)/shard_map/ppermute | solution.py:272
  228.9 28.3 %collective-permute-start.25 = (bf16[512,1024]{1,0:T(8,128)(2,1)}, bf16[512,1024]{1,0:T(8,128)(2,1)}, u32[]{:S(2)}, u32[]{:S(2)}) collective-permute-start(bf16[512,1024]{1,0:T(8,128)(2,1)} %add_convert_fusion.4), channel_id=1, source_target_pairs={{8,16},{12,20},{16,8},{20,12},{9,17},{13,21},{17,9},{21,13},{10,18... | collective-permute-start | bytes 3145736 | tf_op jit(solution)/shard_map/ppermute | solution.py:272
  230.8 4.8 %copy-start.23 = (bf16[4096,512]{1,0:T(8,128)(2,1)S(1)}, bf16[4096,512]{1,0:T(8,128)(2,1)}, u32[]{:S(2)}) copy-start(bf16[4096,512]{1,0:T(8,128)(2,1)} %all-gather.7.cloned.1.call-done) | copy-start | bytes 12582916
  235.6 21.6 %copy-start.25 = (bf16[4096,512]{1,0:T(8,128)(2,1)S(1)}, bf16[4096,512]{1,0:T(8,128)(2,1)}, u32[]{:S(2)}) copy-start(bf16[4096,512]{1,0:T(8,128)(2,1)} %all-gather.5.cloned.1.call-done) | copy-start | bytes 12582916
  238.6 18.6 %copy-start.13 = (bf16[1024,1024]{1,0:T(8,128)(2,1)S(1)}, bf16[1024,1024]{1,0:T(8,128)(2,1)}, u32[]{:S(2)}) copy-start(bf16[1024,1024]{1,0:T(8,128)(2,1)} %copy-done.11) | copy-start | bytes 6291460
  241.6 65.1 %collective-permute-start.23 = (bf16[512,1024]{1,0:T(8,128)(2,1)}, bf16[512,1024]{1,0:T(8,128)(2,1)}, u32[]{:S(2)}, u32[]{:S(2)}) collective-permute-start(bf16[512,1024]{1,0:T(8,128)(2,1)} %add_convert_fusion.5), channel_id=1, source_target_pairs={{8,0},{12,4},{16,8},{20,12},{24,16},{28,20},{9,1},{13,5},{17,9},{2... | collective-permute-start | bytes 3145736 | tf_op jit(solution)/shard_map/ppermute | solution.py:272
  247.9 60.8 %collective-permute-start.22 = (bf16[512,1024]{1,0:T(8,128)(2,1)}, bf16[512,1024]{1,0:T(8,128)(2,1)}, u32[]{:S(2)}, u32[]{:S(2)}) collective-permute-start(bf16[512,1024]{1,0:T(8,128)(2,1)} %add_convert_fusion.6), channel_id=1, source_target_pairs={{0,8},{4,12},{8,16},{12,20},{16,24},{20,28},{1,9},{5,13},{9,17},{1... | collective-permute-start | bytes 3145736 | tf_op jit(solution)/shard_map/ppermute | solution.py:272
  254.5 71.0 %collective-permute-start.18 = (bf16[1024,1024]{1,0:T(8,128)(2,1)}, bf16[1024,1024]{1,0:T(8,128)(2,1)S(1)}, u32[]{:S(2)}, u32[]{:S(2)}) collective-permute-start(bf16[1024,1024]{1,0:T(8,128)(2,1)} %shard_map.105), channel_id=1, source_target_pairs={{0,4},{4,0},{8,12},{12,8},{16,20},{20,16},{24,28},{28,24},{1,5},{5... | collective-permute-start | bytes 6291464 | tf_op jit(solution)/shard_map/ppermute | solution.py:272
  260.7 10.8 %copy-start.28 = (bf16[1024,1024]{1,0:T(8,128)(2,1)S(1)}, bf16[1024,1024]{1,0:T(8,128)(2,1)}, u32[]{:S(2)}) copy-start(bf16[1024,1024]{1,0:T(8,128)(2,1)} %copy-done.26) | copy-start | bytes 6291460
  260.7 86.1 %collective-permute-start.26 = (bf16[512,1024]{1,0:T(8,128)(2,1)}, bf16[512,1024]{1,0:T(8,128)(2,1)}, u32[]{:S(2)}, u32[]{:S(2)}) collective-permute-start(bf16[512,1024]{1,0:T(8,128)(2,1)} %add_convert_fusion.2), channel_id=1, source_target_pairs={{0,8},{4,12},{8,16},{12,20},{16,24},{20,28},{1,9},{5,13},{9,17},{1... | collective-permute-start | bytes 3145736 | tf_op jit(solution)/shard_map/ppermute | solution.py:272
  266.6 80.2 %collective-permute-start.27 = (bf16[512,1024]{1,0:T(8,128)(2,1)}, bf16[512,1024]{1,0:T(8,128)(2,1)}, u32[]{:S(2)}, u32[]{:S(2)}) collective-permute-start(bf16[512,1024]{1,0:T(8,128)(2,1)} %add_convert_fusion.1), channel_id=1, source_target_pairs={{8,0},{12,4},{16,8},{20,12},{24,16},{28,20},{9,1},{13,5},{17,9},{2... | collective-permute-start | bytes 3145736 | tf_op jit(solution)/shard_map/ppermute | solution.py:272
  272.8 4.5 %copy-start.2 = (bf16[512,1024]{1,0:T(8,128)(2,1)S(1)}, bf16[512,1024]{1,0:T(8,128)(2,1)}, u32[]{:S(2)}) copy-start(bf16[512,1024]{1,0:T(8,128)(2,1)} %copy-done) | copy-start | bytes 3145732
  272.8 4.4 %copy-start.4 = (bf16[512,1024]{1,0:T(8,128)(2,1)S(1)}, bf16[512,1024]{1,0:T(8,128)(2,1)}, u32[]{:S(2)}) copy-start(bf16[512,1024]{1,0:T(8,128)(2,1)} %copy-done.3) | copy-start | bytes 3145732
  272.8 4.4 %copy-start.6 = (bf16[512,1024]{1,0:T(8,128)(2,1)S(1)}, bf16[512,1024]{1,0:T(8,128)(2,1)}, u32[]{:S(2)}) copy-start(bf16[512,1024]{1,0:T(8,128)(2,1)} %copy-done.5) | copy-start | bytes 3145732
  277.3 8.3 %copy-start.8 = (bf16[512,1024]{1,0:T(8,128)(2,1)S(1)}, bf16[512,1024]{1,0:T(8,128)(2,1)}, u32[]{:S(2)}) copy-start(bf16[512,1024]{1,0:T(8,128)(2,1)} %copy-done.7) | copy-start | bytes 3145732
  277.3 8.3 %copy-start.10 = (bf16[512,1024]{1,0:T(8,128)(2,1)S(1)}, bf16[512,1024]{1,0:T(8,128)(2,1)}, u32[]{:S(2)}) copy-start(bf16[512,1024]{1,0:T(8,128)(2,1)} %copy-done.9) | copy-start | bytes 3145732
  285.6 8.3 %copy-start.15 = (bf16[128,2048]{1,0:T(8,128)(2,1)S(1)}, bf16[128,2048]{1,0:T(8,128)(2,1)}, u32[]{:S(2)}) copy-start(bf16[128,2048]{1,0:T(8,128)(2,1)} %copy-done.14) | copy-start | bytes 1572868
  293.9 14.8 %copy-start.19 = (bf16[1024,1024]{1,0:T(8,128)(2,1)S(1)}, bf16[1024,1024]{1,0:T(8,128)(2,1)}, u32[]{:S(2)}) copy-start(bf16[1024,1024]{1,0:T(8,128)(2,1)} %copy-done.17) | copy-start | bytes 6291460
  306.8 8.3 %collective-permute-start.21 = (bf16[128,1024]{1,0:T(8,128)(2,1)S(1)}, bf16[128,1024]{1,0:T(8,128)(2,1)S(1)}, u32[]{:S(2)}, u32[]{:S(2)}) collective-permute-start(bf16[128,1024]{1,0:T(8,128)(2,1)S(1)} %slice.27), channel_id=1, source_target_pairs={{4,0},{8,4},{12,8},{16,12},{20,16},{24,20},{28,24},{5,1},{9,5},{13... | collective-permute-start | bytes 786440 | tf_op jit(solution)/shard_map/ppermute | solution.py:272
  338.8 13.1 %all-to-all-start = ((f32[8,16,128]{2,1,0:T(8,128)}), f32[8,16,128]{2,1,0:T(8,128)S(1)}, u32[]{:S(2)}, u32[]{:S(2)}) async-start(f32[8,16,128]{2,1,0:T(8,128)} %bitcast.15), calls=%async_computation | async-start | bytes 131072 | tf_op jit(solution)/shard_map/all_to_all | solution.py:456
  343.3 7.1 %copy-start.32 = (bf16[512,1024]{1,0:T(8,128)(2,1)S(1)}, bf16[512,1024]{1,0:T(8,128)(2,1)}, u32[]{:S(2)}) copy-start(bf16[512,1024]{1,0:T(8,128)(2,1)} %add_convert_fusion.3) | copy-start | bytes 3145732
  343.3 9.3 %collective-permute-start.20 = (bf16[128,1024]{1,0:T(8,128)(2,1)S(1)}, bf16[128,1024]{1,0:T(8,128)(2,1)S(1)}, u32[]{:S(2)}, u32[]{:S(2)}) collective-permute-start(bf16[128,1024]{1,0:T(8,128)(2,1)S(1)} %slice.26), channel_id=1, source_target_pairs={{4,0},{8,4},{12,8},{16,12},{20,16},{24,20},{28,24},{5,1},{9,5},{13... | collective-permute-start | bytes 786440 | tf_op jit(solution)/shard_map/ppermute | solution.py:272
  (1 other events, 1.3 us)
Sparse Core Ops, SparseCore 0:
  10.4 34.6 all-gather.4
  71.6 34.5 all-gather.6

commit v3 on v2

--- a/solution.py
+++ b/solution.py
@@ -108,7 +108,7 @@
             here,
             here,
             here,
-            pl.BlockSpec((FILT, LANES), lambda i: (0, chunk * tiles + i)),
+            pl.BlockSpec((FILT, LANES), lambda i: (0, i)),
             pl.BlockSpec((GPT * FILT, 2 * FILT), lambda i: (chunk * tiles + i, 0)),
         ],
         out_specs=[out, out],
@@ -164,7 +164,7 @@
 
     args = [own, *others, q, k, v, mixed, prior]
     in_specs = [part] * (1 + n_other) + [here] * 3 + [part]
-    in_specs.append(pl.BlockSpec((FILT, LANES), lambda i: (0, chunk * tiles + i)))
+    in_specs.append(pl.BlockSpec((FILT, LANES), lambda i: (0, i)))
     aliases = {}
     if filled is not None:
         aliases = {len(args): 0}
@@ -259,6 +259,41 @@
     )(order, *([cot] * LINE), *weights)
 
 
+def rows_kernel(n, pick, *refs):
+    out = refs[-1]
+    total = None
+    for cot, gated in zip(refs[:n], refs[n : 2 * n]):
+        term = lax.dot_general(
+            cot[0], gated[...], (((0,), (0,)), ((), ())), preferred_element_type=F32
+        )
+        total = term if total is None else total + term
+    for j, came in enumerate(refs[2 * n : -1], 1):
+        total = total + came[...].astype(F32) * pick[j].astype(F32)
+    out[...] = total.astype(out.dtype)
+
+
+def weight_rows(pick, cots, gateds, came, dtype):
+    _, rows, depth = cots[0].shape
+    width = gateds[0].shape[1]
+    tile = min(512, width)
+    n = len(cots)
+    cot_spec = pl.BlockSpec((1, rows, depth), lambda i, pick: (pick[0], 0, 0))
+    gated_spec = pl.BlockSpec((rows, tile), lambda i, pick: (0, i))
+    out_spec = pl.BlockSpec((depth, tile), lambda i, pick: (0, i))
+    return pl.pallas_call(
+        functools.partial(rows_kernel, n),
+        grid_spec=pltpu.PrefetchScalarGridSpec(
+            num_scalar_prefetch=1,
+            grid=(width // tile,),
+            in_specs=[cot_spec] * n + [gated_spec] * n + [out_spec] * len(came),
+            out_specs=out_spec,
+        ),
+        out_shape=jax.ShapeDtypeStruct((depth, width), dtype),
+        compiler_params=params(),
+        cost_estimate=cost(2 * n * rows * depth * width, 2 * n * rows * (depth + width)),
+    )(pick, *cots, *gateds, *came)
+
+
 def shards(seq, ch, queries, keys, values, filters, grad_out, out_weight):
     inner = seq // LINE
     rows, width = queries.shape
@@ -282,53 +317,55 @@
     each = range(chunks)
     up_pairs, down_pairs = [(0, 1), (1, 2), (2, 3)], [(1, 0), (2, 1), (3, 2)]
 
-    prior = send(
-        product_of(keys[rows - FILT :], values[rows - FILT :]), [(i, i + 1) for i in range(seq - 1)]
-    )
+    priors = []
+    for h in each:
+        tail = (slice(rows - FILT, rows), slice(h * cols, (h + 1) * cols))
+        priors.append(
+            send(product_of(keys[tail], values[tail]), [(i, i + 1) for i in range(seq - 1)])
+        )
     paired = inner == 2 and ch == LINE
     other = grad_out
+    cots = []
     if paired:
         kept = lax.dynamic_slice(grad_out, (0, y * depth), (rows, depth))
         other = lax.dynamic_slice(grad_out, (0, (1 - y) * depth), (rows, depth))
         cots = [lax.all_gather(kept, "ch", axis=0, tiled=False)]
     back, ahead = tables(filters)
     halves = [out_weight[:, h * cols : (h + 1) * cols] for h in each]
-    prior, other, _, *halves = fence(prior, other, back[:8, :LANES], *halves)
+    priors[0], other, halves = fence(priors[0], other, halves)
 
     up1, down1 = [None] * chunks, [None] * chunks
     up1[0], down1[0] = along_line(halves[0], up_pairs), along_line(halves[0], down_pairs)
+    swapped = around_inner(other, 1) if paired else other
+    gateds, mixeds = [None] * chunks, [None] * chunks
+    gateds[0], mixeds[0] = forward(queries, keys, values, priors[0], back, 0, chunks)
+    up1, down1, swapped, halves, gateds, cots, priors = fence(
+        up1, down1, swapped, halves, gateds, cots, priors
+    )
+
+    def second_step(h):
+        return along_line(up1[h], [(1, 2), (2, 3)]), along_line(down1[h], [(2, 1), (1, 0)])
+
+    def swap_gated(h):
+        return [around_inner(gateds[h], r) for r in range(1, inner)]
+
+    second = [None] * chunks
+    second[0] = second_step(0)
+    for h in each[1:]:
+        up1[h], down1[h] = along_line(halves[h], up_pairs), along_line(halves[h], down_pairs)
     if paired:
-        swapped = around_inner(other, 1)
+        cots.append(lax.all_gather(swapped, "ch", axis=0, tiled=False))
     else:
-        full = lax.all_gather(other, "ch", axis=1, tiled=True)
+        full = lax.all_gather(swapped, "ch", axis=1, tiled=True)
         full = full.reshape(rows, LINE, inner, depth).transpose(2, 1, 0, 3)
-        cots = []
         for shift in range(inner):
             part = lax.dynamic_index_in_dim(full, (y + shift) % inner, 0, keepdims=False)
             cots.append(part if shift == 0 else around_inner(part, shift))
-        swapped = prior
-    gateds, mixeds = [], []
-    for h in each:
-        gated, mixed = forward(queries, keys, values, prior, back, h, chunks)
-        gateds.append([gated])
-        mixeds.append(mixed)
-    up1, down1, swapped, halves, gateds, cots = fence(up1, down1, swapped, halves, gateds, cots)
-
-    def second_step(h):
-        return along_line(up1[h], [(1, 2), (2, 3)]), along_line(down1[h], [(2, 1), (1, 0)])
-
-    def swap_gated(h):
-        return [around_inner(gateds[h][0], r) for r in range(1, inner)]
-
-    second = [None] * chunks
-    second[0] = second_step(0)
-    for h in each[1:]:
-        up1[h], down1[h] = along_line(halves[h], up_pairs), along_line(halves[h], down_pairs)
-    if paired:
-        cots.append(lax.all_gather(swapped, "ch", axis=0, tiled=False))
-    got = swap_gated(0)
+    got = [None] * chunks
+    got[0] = swap_gated(0)
+    for h in each[1:]:
+        gateds[h], mixeds[h] = forward(queries, keys, values, priors[h], back, h, chunks)
     second[0], got, up1, down1, gateds = fence(second[0], got, up1, down1, gateds)
-    gateds[0] = gateds[0] + got
 
     def merge(pair):
         return jnp.where(z >= 2, *pair)
@@ -336,17 +373,10 @@
     def third_step(x):
         return along_line(x, [(2, 3), (1, 0)])
 
-    third = [None] * chunks
-    second[0] = merge(second[0])
-    third[0] = third_step(second[0])
-    for h in each[1:]:
-        second[h] = second_step(h)
-    got = [swap_gated(h) for h in each[1:]]
-
-    def slots(h, second, third):
+    def slots(h):
         slot_a = jnp.where(z == 0, down1[h], up1[h])
-        slot_c = jnp.where((z == 0) | (z == 3), third, down1[h])
-        return [halves[h], slot_a, second, slot_c]
+        slot_c = jnp.where((z == 0) | (z == 3), third[h], down1[h])
+        return [halves[h], slot_a, second[h], slot_c]
 
     order = jnp.stack(
         [
@@ -357,44 +387,29 @@
         ]
     ).astype(jnp.int32)
 
-    def partial(block, h):
-        total = None
-        for cot, gated in zip(cots, gateds[h]):
-            lhs = lax.dynamic_index_in_dim(cot, block, 0, keepdims=False)
-            term = lax.dot_general(lhs, gated, (((0,), (0,)), ((), ())), preferred_element_type=F32)
-            total = term if total is None else total + term
-        return total
-
+    first_block = jnp.where(z == 0, 3, 0)
     second_block = jnp.where(z == 0, 2, jnp.where(z == 1, 3, jnp.where(z == 2, 0, 1)))
-
-    def sum_first(h):
-        return partial(jnp.where(z == 0, 3, 0), h).astype(BF16)
+    at_one, at_two = z == 1, z == 2
+
+    def block_rows(block, h, *came):
+        pick = [block] + [flag for _, flag in came]
+        pick = jnp.stack([jnp.asarray(p, jnp.int32) for p in pick])
+        return weight_rows(pick, cots, [gateds[h]] + got[h], [x for x, _ in came], BF16)
 
     def send_first(x):
         return along_line(x, [(0, 1), (3, 2)])
 
-    def sum_second(h, got):
-        return (partial(second_block, h) + got.astype(F32)).astype(BF16)
-
     def send_second(x):
         return along_line(x, [(0, 1), (3, 2)]), along_line(x, [(1, 2), (2, 1)])
 
     def sum_third(h, outer_in, inner_in):
-        add_up = jnp.where(z == 1, outer_in, inner_in).astype(F32)
-        add_down = jnp.where(z == 1, inner_in, outer_in).astype(F32)
-        last_up = (partial(jnp.minimum(z + 1, 3), h) + add_up).astype(BF16)
-        last_down = (partial(jnp.maximum(z - 1, 0), h) + add_down).astype(BF16)
-        return last_up, last_down
+        return (
+            block_rows(jnp.minimum(z + 1, 3), h, (outer_in, at_one), (inner_in, at_two)),
+            block_rows(jnp.maximum(z - 1, 0), h, (inner_in, at_one), (outer_in, at_two)),
+        )
 
     def send_third(last_up, last_down):
-        return (
-            along_line(last_up, [(0, 1), (1, 2), (2, 3)]),
-            along_line(last_down, [(1, 0), (2, 1), (3, 2)]),
-        )
-
-    def sum_last(h, from_below, from_above):
-        total = partial(z, h) + from_below.astype(F32) + from_above.astype(F32)
-        return total.astype(BF16)
+        return along_line(last_up, up_pairs), along_line(last_down, down_pairs)
 
     def shares(h, weights):
         return [gate_grad(order, cots[r], weights, BF16) for r in range(1, inner)]
@@ -402,55 +417,55 @@
     def send_shares(parts):
         return [around_inner(part, inner - r) for r, part in enumerate(parts, 1)]
 
-    sums = [None] * chunks
-    others = [None] * chunks
-    weights = [None] * chunks
-    latest = sum_first(0)
-    sums[0] = send_first(latest)
-    middle_share = partial(second_block, 0)
-    third[0], sums[0], second, got, middle_share = fence(
-        third[0], sums[0], second, got, middle_share
-    )
-    for h in each[1:]:
-        gateds[h] += got[h - 1]
+    third, sums, parts, others, owns = ([None] * chunks for _ in range(5))
+    second[0] = merge(second[0])
+    third[0] = third_step(second[0])
+    for h in each[1:]:
+        second[h] = second_step(h)
+        got[h] = swap_gated(h)
+    sums[0] = send_first(block_rows(first_block, 0))
+    weights = slots(0)
+    parts[0] = shares(0, weights)
+    owns[0] = gate_grad(order, cots[0], weights, F32)
+    others[0] = send_shares(parts[0])
+    sums, second, got, parts, owns = fence(sums, second, got, parts, owns)
 
     for h in each[1:]:
         second[h] = merge(second[h])
         third[h] = third_step(second[h])
-    latest = (middle_share + sums[0].astype(F32)).astype(BF16)
-    sums[0] = send_second(latest)
-    weights[0] = slots(0, second[0], third[0])
-    parts = shares(0, after(weights[0], latest))
-    others[0] = send_shares(parts)
-    for h in each[1:]:
-        latest = after(sum_first(h), parts)
-        sums[h] = send_first(latest)
-    for h in each[1:]:
-        weights[h] = slots(h, second[h], third[h])
-        parts = shares(h, after(weights[h], latest))
-        others[h] = send_shares(parts)
-    latest = sum_third(0, *after(sums[0], parts))
-    sums[0] = send_third(*latest)
-    for h in each[1:]:
-        latest = sum_second(h, after(sums[h], latest))
-        sums[h] = send_second(latest)
-    owns = [gate_grad(order, cots[0], after(weights[h], latest), F32) for h in each]
-    for h in each[1:]:
-        latest = sum_third(h, *sums[h])
-        sums[h] = send_third(*latest)
+    sums[0] = send_second(block_rows(second_block, 0, (sums[0], 1)))
+    for h in each[1:]:
+        sums[h] = send_first(block_rows(first_block, h))
+    for h in each[1:]:
+        weights = slots(h)
+        parts[h] = shares(h, weights)
+        owns[h] = gate_grad(order, cots[0], weights, F32)
+        others[h] = send_shares(parts[h])
+    sums, parts, owns = fence(sums, parts, owns)
+
+    ready = [block_rows(second_block, h, (sums[h], 1)) for h in each[1:]]
+    last = sum_third(0, *sums[0])
+    ready, last, others[0] = fence(ready, last, others[0])
+    sums[0] = send_third(*last)
+    for h in each[1:]:
+        sums[h] = send_second(ready[h - 1])
 
     grad_queries = None
     grad_kv = None
-    taps = []
-    for h in range(chunks):
-        here = slice(h * cols, (h + 1) * cols)
-        grad_queries, gm, lag = middle(
-            owns[h], others[h], queries, keys, values, mixeds[h], prior, grad_queries, h, chunks
+    taps = [None] * chunks
+    for h in each:
+        grad_queries, gm, taps[h] = middle(
+            owns[h], others[h], queries, keys, values, mixeds[h], priors[h], grad_queries, h, chunks
         )
         later = send(gm[:FILT], [(i + 1, i) for i in range(seq - 1)])
         grad_kv = backward(gm, later, keys, values, ahead, grad_kv, h, chunks)
-        taps.append(lag)
-    grad_weight = jnp.concatenate([sum_last(h, *sums[h]) for h in each], axis=1)
+        if h == 0:
+            sums, grad_kv, others = fence(sums, grad_kv, others)
+            for g in each[1:]:
+                sums[g] = send_third(*sum_third(g, *sums[g]))
+    sums[-1], grad_kv = fence(sums[-1], grad_kv)
+    done = [block_rows(z, h, *((x, 1) for x in sums[h])) for h in each]
+    grad_weight = jnp.concatenate(done, axis=1)
     taps = jnp.concatenate(taps, axis=0)[:, 1 : FILT + 1][:, ::-1]
     taps = taps.T.reshape(seq, FILT // seq, -1)
     taps = jnp.sum(lax.all_to_all(taps, "seq", 0, 0), axis=0)

time: 373 us -> 376 us (level)
  matrix products: 63.2 us -> 0 us
  Pallas kernels: 110 us -> 168 us
  local copies, waits for them, and re-layouts: 12.6 us -> 24.7 us
  other arithmetic: 18.4 us -> 9.28 us
    dot_general x20 -> x0, matrix products: 63.2 us -> none  [partial(): lax.dot_general(lhs, gated, (((0,), (0,)), ((), ())), preferred_element_t...]
    pallas_call x0 -> x10, Pallas kernels: none -> 57.6 us  [weight_rows(): pl.pallas_call(functools.partial(rows_kernel, n), grid_spec=pltpu.Prefetc...]
    unnamed x68 -> x56, local copies, waits for them, and re-layouts: 6.82 us -> 18.7 us
    convert_element_type x3 -> x0, other arithmetic: 7.8 us -> none  [the longest x1 3.58 us: sum_last(): return total.astype(BF16)]
    ppermute x28 -> x29, waiting for transfers between devices: 76.2 us -> 79.5 us  [send(): return lax.ppermute(x, 'seq', pairs)]
    ppermute x28 -> x29, starting transfers between devices: 70.4 us -> 71 us  [send(): return lax.ppermute(x, 'seq', pairs)]
  transfers between devices with their start and end apart: 31 -> 32, of which waited for: 9 -> 14; matrix products, arithmetic and copies ran while one was open for 22% -> 3% of each run, Pallas kernels for 27% -> 40%
where the time goes in v3:
time: 376 us; the launch traced here: 373 us
  Pallas kernels  168 us (45%)
  waiting for transfers between devices  79.6 us (21%)
  starting transfers between devices  76.9 us (20%)
  local copies, waits for them, and re-layouts  24.7 us (7%)
  between operations  14.6 us (4%)
  other arithmetic  9.28 us (2%)
    ppermute x29, waiting for transfers between devices, send(): return lax.ppermute(x, 'seq', pairs)  79.5 us
    ppermute x29, starting transfers between devices, send(): return lax.ppermute(x, 'seq', pairs)  71 us
    pallas_call x10, Pallas kernels, weight_rows(): pl.pallas_call(functools.partial(rows_kernel, n), grid_spec=pltpu.Prefetc...  57.6 us
    pallas_call x4, Pallas kernels, gate_grad(): pl.pallas_call(gate_kernel, grid_spec=pltpu.PrefetchScalarGridSpec(num_sc...  33.2 us
    pallas_call x2, Pallas kernels, middle(): pl.pallas_call(kernel, grid=(tiles,), in_specs=in_specs, out_specs=[here,...  25.4 us
    pallas_call x2, Pallas kernels, backward(): pl.pallas_call(backward_kernel, grid=(tiles,), in_specs=in_specs, out_spe...  20.9 us
    pallas_call x2, Pallas kernels, forward(): pl.pallas_call(forward_kernel, grid=(tiles,), in_specs=[here, here, here,...  20.2 us
    unnamed x56, local copies, waits for them, and re-layouts  18.7 us
  transfers between devices with their start and end apart: 32, of which 14 were waited for; matrix products, arithmetic and copies ran while one was open for 3% of the time, Pallas kernels for 40%

profile of v3, /device:TPU:10, one launch (start us, length us, event | category | flops | bytes accessed | tf_op | source)
XLA Modules:
  0.0 372.7 jit_solution(12117239008716709503)
XLA Ops:
  7.2 3.1 constant_dynamic-slice_fusion
  10.4 2.1 multiply_convert_fusion
  12.5 3.4 collective-permute-start
  17.1 6.2 %collective-permute-done.prior.refs_5_ = bf16[128,1024]{1,0:T(8,128)(2,1)S(1)} collective-permute-done((bf16[128,1024]{1,0:T(8,128)(2,1)S(1)}, bf16[128,1024]{1,0:T(8,128)(2,1)S(1)}, u32[]{:S(2)}, u32[]{:S(2)}) %collective-permute-start) | collective-permute-done | bytes 262176 | tf_op jit(solution)/shard_map/ppermute | solution.py:307
  24.1 3.5 collective-permute-start.1
  27.5 3.3 collective-permute-start.2
  31.6 3.3 collective-permute-start.4
  35.2 10.5 %shard_map.101 = (bf16[16384,256]{1,0:T(8,128)(2,1)}, bf16[16384,256]{1,0:T(8,128)(2,1)}) custom-call(f32[128,256]{1,0:T(8,128)S(1)} %maximum_maximum_fusion.back_ref, f32[128,256]{1,0:T(8,128)S(1)} %concatenate.13.ahead_ref), custom_call_target="tpu_custom_call" | custom-call | flops 524288 | bytes 262144 | tf_op jit(solution)/shard_map/pallas_call | solution.py:54
  46.6 9.9 %shard_map.102 = (bf16[1024,1024]{1,0:T(8,128)(2,1)S(1)}, bf16[1024,1024]{1,0:T(8,128)(2,1)S(1)}) custom-call(bf16[1024,2048]{1,0:T(8,128)(2,1)} %refs_1_.3, bf16[1024,2048]{1,0:T(8,128)(2,1)} %k.7, bf16[1024,2048]{1,0:T(8,128)(2,1)} %v.7, bf16[128,1024]{1,0:T(8,128)(2,1)S(1)} %copy-done.18, bf16[16384,256]{1,0:T(8,128)(2,1)} %get-tuple-element.73.table), custom_call_target="tpu_custom_call" | custom-call | flops 67108864 | bytes 229376 | tf_op jit(solution)/shard_map/pallas_call | solution.py:104
  58.5 1.9 collective-permute-done.3
  61.0 2.6 collective-permute-start.5
  63.6 1.9 collective-permute-start.6
  65.5 4.0 %collective-permute-start.8 = (bf16[512,1024]{1,0:T(8,128)(2,1)S(1)}, bf16[512,1024]{1,0:T(8,128)(2,1)S(1)}, u32[]{:S(2)}, u32[]{:S(2)}) collective-permute-start(bf16[512,1024]{1,0:T(8,128)(2,1)S(1)} %get-tuple-element.80.refs_4_), channel_id=1, source_target_pairs={{0,8},{4,12},{8,16},{12,20},{16,24},{20,28},{1,9},{5,13},{9,17},{1... | collective-permute-start | bytes 3145736 | tf_op jit(solution)/shard_map/ppermute | solution.py:307
  69.5 1.9 collective-permute-start.9
  71.4 10.3 %shard_map.103 = (bf16[1024,1024]{1,0:T(8,128)(2,1)}, bf16[1024,1024]{1,0:T(8,128)(2,1)S(1)}) custom-call(bf16[1024,2048]{1,0:T(8,128)(2,1)} %refs_1_.3, bf16[1024,2048]{1,0:T(8,128)(2,1)} %k.7, bf16[1024,2048]{1,0:T(8,128)(2,1)} %v.7, bf16[128,1024]{1,0:T(8,128)(2,1)S(1)} %collective-permute-done.4.prior.refs_5_, bf16[16384,256]{1,0:T(8,128)(2,1)} %get-tuple-element.73.table), custom_call_target="tpu_custom_call" | custom-call | flops 67108864 | bytes 229376 | tf_op jit(solution)/shard_map/pallas_call | solution.py:104
  83.2 4.2 %collective-permute-done.5 = bf16[512,1024]{1,0:T(8,128)(2,1)S(1)} collective-permute-done((bf16[512,1024]{1,0:T(8,128)(2,1)}, bf16[512,1024]{1,0:T(8,128)(2,1)S(1)}, u32[]{:S(2)}, u32[]{:S(2)}) %collective-permute-start.5) | collective-permute-done | bytes 1048608 | tf_op jit(solution)/shard_map/ppermute | solution.py:307
  87.4 4.4 %collective-permute-done.6 = bf16[512,1024]{1,0:T(8,128)(2,1)S(1)} collective-permute-done((bf16[512,1024]{1,0:T(8,128)(2,1)}, bf16[512,1024]{1,0:T(8,128)(2,1)S(1)}, u32[]{:S(2)}, u32[]{:S(2)}) %collective-permute-start.6) | collective-permute-done | bytes 1048608 | tf_op jit(solution)/shard_map/ppermute | solution.py:307
  91.8 14.2 %collective-permute-done.8 = bf16[512,1024]{1,0:T(8,128)(2,1)S(1)} collective-permute-done((bf16[512,1024]{1,0:T(8,128)(2,1)S(1)}, bf16[512,1024]{1,0:T(8,128)(2,1)S(1)}, u32[]{:S(2)}, u32[]{:S(2)}) %collective-permute-start.8) | collective-permute-done | bytes 1048608 | tf_op jit(solution)/shard_map/ppermute | solution.py:307
  105.9 4.2 %collective-permute-done.9 = bf16[512,1024]{1,0:T(8,128)(2,1)S(1)} collective-permute-done((bf16[512,1024]{1,0:T(8,128)(2,1)S(1)}, bf16[512,1024]{1,0:T(8,128)(2,1)S(1)}, u32[]{:S(2)}, u32[]{:S(2)}) %collective-permute-start.9) | collective-permute-done | bytes 1048608 | tf_op jit(solution)/shard_map/ppermute | solution.py:307
  111.8 1.5 collective-permute-start.13
  114.7 3.2 collective-permute-start.14
  117.8 3.8 %collective-permute-start.11 = (bf16[512,1024]{1,0:T(8,128)(2,1)}, bf16[512,1024]{1,0:T(8,128)(2,1)}, u32[]{:S(2)}, u32[]{:S(2)}) collective-permute-start(bf16[512,1024]{1,0:T(8,128)(2,1)} %copy-done.23), channel_id=1, source_target_pairs={{8,16},{12,20},{16,24},{20,28},{9,17},{13,21},{17,25},{21,29},{10,... | collective-permute-start | bytes 3145736 | tf_op jit(solution)/shard_map/ppermute | solution.py:307
  121.6 1.9 collective-permute-start.12
  123.6 1.6 copy-done.1
  125.2 5.1 %shard_map.104 = bf16[512,1024]{1,0:T(8,128)(2,1)} custom-call(s32[1]{0:T(128)} %bitcast.3.pick, bf16[4,1024,512]{2,1,0:T(8,128)(2,1)} %bitcast.34, bf16[4,1024,512]{2,1,0:T(8,128)(2,1)} %bitcast.16, bf16[1024,1024]{1,0:T(8,128)(2,1)S(1)} %get-tuple-element.83.refs_2_, bf16[1024,1024]{1,0:T(8,128)(2,1)S(1)} %copy-done.1), custom_call_target="tpu_custom_call" | custom-call | flops 33554432 | bytes 98304 | tf_op jit(solution)/shard_map/pallas_call | solution.py:283
  131.7 8.7 %collective-permute-done.14 = bf16[512,1024]{1,0:T(8,128)(2,1)} collective-permute-done((bf16[512,1024]{1,0:T(8,128)(2,1)S(1)}, bf16[512,1024]{1,0:T(8,128)(2,1)}, u32[]{:S(2)}, u32[]{:S(2)}) %collective-permute-start.14) | collective-permute-done | bytes 1048608 | tf_op jit(solution)/shard_map/ppermute | solution.py:307
  140.4 1.7 broadcast_select_fusion.1
  142.1 8.7 %shard_map.106.own_ref = f32[1024,1024]{1,0:T(8,128)} custom-call(s32[4]{0:T(128)S(1)} %pad_add_fusion.1.order, bf16[4,1024,512]{2,1,0:T(8,128)(2,1)} %bitcast.35, bf16[4,1024,512]{2,1,0:T(8,128)(2,1)} %bitcast.36, bf16[4,1024,512]{2,1,0:T(8,128)(2,1)} %bitcast.37, bf16[4,1024,512]{2,1,0:T(8,128)(2,1)} %bitcast.38, ...), custom_call_target="tpu_custom_call" | custom-call | flops 67108864 | bytes 196608 | tf_op jit(solution)/shard_map/pallas_call | solution.py:246
  150.8 8.2 %shard_map.105 = bf16[1024,1024]{1,0:T(8,128)(2,1)} custom-call(s32[4]{0:T(128)S(1)} %pad_add_fusion.1.order, bf16[4,1024,512]{2,1,0:T(8,128)(2,1)} %bitcast.17, bf16[4,1024,512]{2,1,0:T(8,128)(2,1)} %bitcast.18, bf16[4,1024,512]{2,1,0:T(8,128)(2,1)} %bitcast.19, bf16[4,1024,512]{2,1,0:T(8,128)(2,1)} %bitcast.20, ...), custom_call_target="tpu_custom_call" | custom-call | flops 67108864 | bytes 196608 | tf_op jit(solution)/shard_map/pallas_call | solution.py:246
  160.4 5.5 %collective-permute-start.18 = (bf16[512,1024]{1,0:T(8,128)(2,1)S(1)}, bf16[512,1024]{1,0:T(8,128)(2,1)}, u32[]{:S(2)}, u32[]{:S(2)}) collective-permute-start(bf16[512,1024]{1,0:T(8,128)(2,1)S(1)} %broadcast_select_fusion.4.refs_6_), channel_id=1, source_target_pairs={{16,24},{20,28},{8,0},{12,4},{17,25},{21,29},{9,1},{13,5},{18,26},... | collective-permute-start | bytes 3145736 | tf_op jit(solution)/shard_map/ppermute | solution.py:307
  166.5 6.1 %shard_map.107 = bf16[512,1024]{1,0:T(8,128)(2,1)} custom-call(s32[2]{0:T(128)S(1)} %pad_add_fusion.pick, bf16[4,1024,512]{2,1,0:T(8,128)(2,1)} %bitcast.39, bf16[4,1024,512]{2,1,0:T(8,128)(2,1)} %bitcast.21, bf16[1024,1024]{1,0:T(8,128)(2,1)S(1)} %get-tuple-element.83.refs_2_, bf16[1024,1024]{1,0:T(8,128)(2,1)} %copy-done, ...), custom_call_target="tpu_custom_call" | custom-call | flops 33554432 | bytes 98304 | tf_op jit(solution)/shard_map/pallas_call | solution.py:283
  174.0 3.1 collective-permute-start.16
  177.2 5.7 %shard_map.108 = bf16[512,1024]{1,0:T(8,128)(2,1)} custom-call(s32[1]{0:T(128)} %bitcast.3.pick, bf16[4,1024,512]{2,1,0:T(8,128)(2,1)} %bitcast.40, bf16[4,1024,512]{2,1,0:T(8,128)(2,1)} %bitcast.22, bf16[1024,1024]{1,0:T(8,128)(2,1)} %get-tuple-element.89.refs_2_, bf16[1024,1024]{1,0:T(8,128)(2,1)} %collective-permute-done.13.refs_3_), custom_call_target="tpu_custom_call" | custom-call | flops 33554432 | bytes 98304 | tf_op jit(solution)/shard_map/pallas_call | solution.py:283
  182.8 1.6 collective-permute-start.17
  184.8 7.9 %shard_map.109 = bf16[1024,1024]{1,0:T(8,128)(2,1)} custom-call(s32[4]{0:T(128)S(1)} %pad_add_fusion.1.order, bf16[4,1024,512]{2,1,0:T(8,128)(2,1)} %bitcast.23, bf16[4,1024,512]{2,1,0:T(8,128)(2,1)} %bitcast.24, bf16[4,1024,512]{2,1,0:T(8,128)(2,1)} %bitcast.25, bf16[4,1024,512]{2,1,0:T(8,128)(2,1)} %bitcast.26, bf16[512,1024]{1,0:T(8,128)(2,1)S(1)} %copy-done.3, ...), custom_call_target="tpu_custom_call" | custom-call | flops 67108864 | bytes 196608 | tf_op jit(solution)/shard_map/pallas_call | solution.py:246
  192.7 1.5 collective-permute-start.25
  198.0 8.3 %shard_map.110.own_ref = f32[1024,1024]{1,0:T(8,128)} custom-call(s32[4]{0:T(128)S(1)} %pad_add_fusion.1.order, bf16[4,1024,512]{2,1,0:T(8,128)(2,1)} %bitcast.41, bf16[4,1024,512]{2,1,0:T(8,128)(2,1)} %bitcast.42, bf16[4,1024,512]{2,1,0:T(8,128)(2,1)} %bitcast.43, bf16[4,1024,512]{2,1,0:T(8,128)(2,1)} %bitcast.44, bf16[512,1024]{1,0:T(8,128)(2,1)S(1)} %copy-done.4, ...), custom_call_target="tpu_custom_call" | custom-call | flops 67108864 | bytes 196608 | tf_op jit(solution)/shard_map/pallas_call | solution.py:246
  206.3 9.5 %collective-permute-done.17.refs_4_ = bf16[512,1024]{1,0:T(8,128)(2,1)} collective-permute-done((bf16[512,1024]{1,0:T(8,128)(2,1)}, bf16[512,1024]{1,0:T(8,128)(2,1)}, u32[]{:S(2)}, u32[]{:S(2)}) %collective-permute-start.17) | collective-permute-done | bytes 1048608 | tf_op jit(solution)/shard_map/ppermute | solution.py:307
  215.8 5.5 %shard_map.113 = bf16[512,1024]{1,0:T(8,128)(2,1)S(1)} custom-call(s32[3]{0:T(128)S(1)} %get-tuple-element.144.pick, bf16[4,1024,512]{2,1,0:T(8,128)(2,1)} %bitcast.45, bf16[4,1024,512]{2,1,0:T(8,128)(2,1)} %bitcast.27, bf16[1024,1024]{1,0:T(8,128)(2,1)S(1)} %get-tuple-element.83.refs_2_, bf16[1024,1024]{1,0:T(8,128)(2,1)} %copy-done, ...), custom_call_target="tpu_custom_call" | custom-call | flops 33554432 | bytes 98304 | tf_op jit(solution)/shard_map/pallas_call | solution.py:283
  221.3 5.5 %shard_map.112 = bf16[512,1024]{1,0:T(8,128)(2,1)S(1)} custom-call(s32[3]{0:T(128)S(1)} %get-tuple-element.143.pick, bf16[4,1024,512]{2,1,0:T(8,128)(2,1)} %bitcast.46, bf16[4,1024,512]{2,1,0:T(8,128)(2,1)} %bitcast.28, bf16[1024,1024]{1,0:T(8,128)(2,1)S(1)} %get-tuple-element.83.refs_2_, bf16[1024,1024]{1,0:T(8,128)(2,1)} %copy-done, ...), custom_call_target="tpu_custom_call" | custom-call | flops 33554432 | bytes 98304 | tf_op jit(solution)/shard_map/pallas_call | solution.py:283
  226.9 5.9 %shard_map.111 = bf16[512,1024]{1,0:T(8,128)(2,1)S(1)} custom-call(s32[2]{0:T(128)S(1)} %pad_add_fusion.pick, bf16[4,1024,512]{2,1,0:T(8,128)(2,1)} %bitcast.47, bf16[4,1024,512]{2,1,0:T(8,128)(2,1)} %bitcast.29, bf16[1024,1024]{1,0:T(8,128)(2,1)} %get-tuple-element.89.refs_2_, bf16[1024,1024]{1,0:T(8,128)(2,1)} %collective-permute-done.13.refs_3_, ...), custom_call_target="tpu_custom_call" | custom-call | flops 33554432 | bytes 98304 | tf_op jit(solution)/shard_map/pallas_call | solution.py:283
  232.8 12.7 %shard_map.114 = (bf16[1024,2048]{1,0:T(8,128)(2,1)}, bf16[1024,1024]{1,0:T(8,128)(2,1)S(1)}, f32[64,256]{1,0:T(8,128)S(1)}) custom-call(f32[1024,1024]{1,0:T(8,128)} %shard_map.106.own_ref, bf16[1024,1024]{1,0:T(8,128)(2,1)} %collective-permute-done.19.refs_0_, bf16[1024,2048]{1,0:T(8,128)(2,1)} %refs_1_.3, bf16[1024,2048]{1,0:T(8,128)(2,1)} %k.7, ...), custom_call_target="tpu_custom_call" | custom-call | flops 67108864 | bytes 294912 | tf_op jit(solution)/shard_map/pallas_call | solution.py:173
  245.5 2.4 collective-permute-start.24
  247.9 4.4 %collective-permute-start.20 = (bf16[512,1024]{1,0:T(8,128)(2,1)S(1)}, bf16[512,1024]{1,0:T(8,128)(2,1)S(1)}, u32[]{:S(2)}, u32[]{:S(2)}) collective-permute-start(bf16[512,1024]{1,0:T(8,128)(2,1)S(1)} %shard_map.112), channel_id=1, source_target_pairs={{0,8},{4,12},{8,16},{12,20},{16,24},{20,28},{1,9},{5,13},{9,17},{1... | collective-permute-start | bytes 3145736 | tf_op jit(solution)/shard_map/ppermute | solution.py:307
  252.3 1.9 collective-permute-start.21
  255.5 2.3 collective-permute-done.24.later
  257.8 2.8 collective-permute-start.23
  260.6 10.5 %shard_map.115 = (bf16[1024,2048]{1,0:T(8,128)(2,1)}, bf16[1024,2048]{1,0:T(8,128)(2,1)}) custom-call(bf16[1024,1024]{1,0:T(8,128)(2,1)S(1)} %get-tuple-element.110.gm, bf16[128,1024]{1,0:T(8,128)(2,1)S(1)} %collective-permute-done.24.later, bf16[1024,2048]{1,0:T(8,128)(2,1)} %k.7, bf16[1024,2048]{1,0:T(8,128)(2,1)} %v.7, ...), custom_call_target="tpu_custom_call" | custom-call | flops 67108864 | bytes 229376 | tf_op jit(solution)/shard_map/pallas_call | solution.py:217
  271.0 4.8 %collective-permute-done.20.refs_4_ = bf16[512,1024]{1,0:T(8,128)(2,1)S(1)} collective-permute-done((bf16[512,1024]{1,0:T(8,128)(2,1)S(1)}, bf16[512,1024]{1,0:T(8,128)(2,1)S(1)}, u32[]{:S(2)}, u32[]{:S(2)}) %collective-permute-start.20) | collective-permute-done | bytes 1048608 | tf_op jit(solution)/shard_map/ppermute | solution.py:307
  276.9 3.4 collective-permute-done.21.refs_5_
  281.2 8.2 %collective-permute-done.22.refs_4_.refs_5_ = bf16[512,1024]{1,0:T(8,128)(2,1)S(1)} collective-permute-done((bf16[512,1024]{1,0:T(8,128)(2,1)S(1)}, bf16[512,1024]{1,0:T(8,128)(2,1)S(1)}, u32[]{:S(2)}, u32[]{:S(2)}) %collective-permute-start.22) | collective-permute-done | bytes 1048608 | tf_op jit(solution)/shard_map/ppermute | solution.py:307
  289.4 6.9 %collective-permute-done.23.refs_5_.refs_4_ = bf16[512,1024]{1,0:T(8,128)(2,1)S(1)} collective-permute-done((bf16[512,1024]{1,0:T(8,128)(2,1)S(1)}, bf16[512,1024]{1,0:T(8,128)(2,1)S(1)}, u32[]{:S(2)}, u32[]{:S(2)}) %collective-permute-start.23) | collective-permute-done | bytes 1048608 | tf_op jit(solution)/shard_map/ppermute | solution.py:307
  296.3 6.2 %shard_map.118 = bf16[512,1024]{1,0:T(8,128)(2,1)} custom-call(s32[3]{0:T(128)S(1)} %get-tuple-element.144.pick, bf16[4,1024,512]{2,1,0:T(8,128)(2,1)} %bitcast.48, bf16[4,1024,512]{2,1,0:T(8,128)(2,1)} %bitcast.30, bf16[1024,1024]{1,0:T(8,128)(2,1)} %get-tuple-element.89.refs_2_, bf16[1024,1024]{1,0:T(8,128)(2,1)} %collective-permute-done.13.refs_3_, ...), custom_call_target="tpu_custom_call" | custom-call | flops 33554432 | bytes 98304 | tf_op jit(solution)/shard_map/pallas_call | solution.py:283
  302.6 6.2 %shard_map.117 = bf16[512,1024]{1,0:T(8,128)(2,1)} custom-call(s32[3]{0:T(128)S(1)} %get-tuple-element.143.pick, bf16[4,1024,512]{2,1,0:T(8,128)(2,1)} %bitcast.49, bf16[4,1024,512]{2,1,0:T(8,128)(2,1)} %bitcast.31, bf16[1024,1024]{1,0:T(8,128)(2,1)} %get-tuple-element.89.refs_2_, bf16[1024,1024]{1,0:T(8,128)(2,1)} %collective-permute-done.13.refs_3_, ...), custom_call_target="tpu_custom_call" | custom-call | flops 33554432 | bytes 98304 | tf_op jit(solution)/shard_map/pallas_call | solution.py:283
  308.8 1.9 collective-permute-start.27
  310.7 3.9 %collective-permute-start.26 = (bf16[512,1024]{1,0:T(8,128)(2,1)}, bf16[512,1024]{1,0:T(8,128)(2,1)}, u32[]{:S(2)}, u32[]{:S(2)}) collective-permute-start(bf16[512,1024]{1,0:T(8,128)(2,1)} %shard_map.117), channel_id=1, source_target_pairs={{0,8},{4,12},{8,16},{12,20},{16,24},{20,28},{1,9},{5,13},{9,17},{1... | collective-permute-start | bytes 3145736 | tf_op jit(solution)/shard_map/ppermute | solution.py:307
  314.6 12.7 %shard_map.116 = (bf16[1024,2048]{1,0:T(8,128)(2,1)}, bf16[1024,1024]{1,0:T(8,128)(2,1)S(1)}, f32[64,256]{1,0:T(8,128)S(1)}) custom-call(f32[1024,1024]{1,0:T(8,128)} %shard_map.110.own_ref, bf16[1024,1024]{1,0:T(8,128)(2,1)} %collective-permute-done.25.refs_0_, bf16[1024,2048]{1,0:T(8,128)(2,1)} %refs_1_.3, ...), custom_call_target="tpu_custom_call", output_to_operand_aliasing={{0}: (7, {})} | custom-call | flops 67108864 | bytes 294912 | tf_op jit(solution)/shard_map/pallas_call | solution.py:173
  329.4 1.9 collective-permute-start.28
  332.2 5.8 %all-to-all-start = ((f32[8,16,128]{2,1,0:T(8,128)}), f32[8,16,128]{2,1,0:T(8,128)S(1)}, u32[]{:S(2)}, u32[]{:S(2)}) async-start(f32[8,16,128]{2,1,0:T(8,128)} %bitcast.13), calls=%async_computation | async-start | bytes 131072 | tf_op jit(solution)/shard_map/all_to_all | solution.py:471
  340.4 5.2 %shard_map.120 = bf16[512,1024]{1,0:T(8,128)(2,1)S(1)} custom-call(s32[3]{0:T(128)S(1)} %stack.83.pick, bf16[4,1024,512]{2,1,0:T(8,128)(2,1)} %bitcast.50, bf16[4,1024,512]{2,1,0:T(8,128)(2,1)} %bitcast.32, bf16[1024,1024]{1,0:T(8,128)(2,1)S(1)} %get-tuple-element.83.refs_2_, bf16[1024,1024]{1,0:T(8,128)(2,1)} %copy-done, bf16[512,1024]{1,0:T(8,128)(2,1)S(1)} %copy-done.14, ...), custom_call_target="tpu_custom_call" | custom-call | flops 33554432 | bytes 98304 | tf_op jit(solution)/shard_map/pallas_call | solution.py:283
  346.2 1.6 copy-done.10
  347.8 10.4 %shard_map.119 = (bf16[1024,2048]{1,0:T(8,128)(2,1)}, bf16[1024,2048]{1,0:T(8,128)(2,1)}) custom-call(bf16[1024,1024]{1,0:T(8,128)(2,1)S(1)} %copy-done.10, bf16[128,1024]{1,0:T(8,128)(2,1)S(1)} %collective-permute-done.28.later, bf16[1024,2048]{1,0:T(8,128)(2,1)} %k.7, bf16[1024,2048]{1,0:T(8,128)(2,1)} %v.7, ...), custom_call_target="tpu_custom_call", output_to_operand_aliasing={{0}: (5, {}), {1}: (6, {})} | custom-call | flops 67108864 | bytes 229376 | tf_op jit(solution)/shard_map/pallas_call | solution.py:217
  358.3 6.1 %shard_map.121 = bf16[512,1024]{1,0:T(8,128)(2,1)S(1)} custom-call(s32[3]{0:T(128)S(1)} %stack.83.pick, bf16[4,1024,512]{2,1,0:T(8,128)(2,1)} %bitcast.51, bf16[4,1024,512]{2,1,0:T(8,128)(2,1)} %bitcast.33, bf16[1024,1024]{1,0:T(8,128)(2,1)} %get-tuple-element.89.refs_2_, bf16[1024,1024]{1,0:T(8,128)(2,1)} %collective-permute-done.13.refs_3_, ...), custom_call_target="tpu_custom_call" | custom-call | flops 33554432 | bytes 98304 | tf_op jit(solution)/shard_map/pallas_call | solution.py:283
  364.4 1.5 pad_maximum_fusion
  (103 shorter events, 29.1 us)
Async XLA Ops:
  7.2 8.8 %copy-start.20 = (bf16[512,2048]{1,0:T(8,128)(2,1)S(1)}, bf16[512,2048]{1,0:T(8,128)(2,1)}, u32[]{:S(2)}) copy-start(bf16[512,2048]{1,0:T(8,128)(2,1)} %param.11) | copy-start | bytes 6291460
  7.2 53.2 %all-gather.5.cloned.1.call-start = ((), (), s32[]{:S(2)}) async-start(), calls=%async_computation.1 | async-start | bytes 5242880 | tf_op jit(solution)/shard_map/all_gather | solution.py:332
  10.4 24.5 %copy-start.27 = (bf16[128,128]{1,0:T(8,128)(2,1)S(1)}, bf16[128,128]{1,0:T(8,128)(2,1)}, u32[]{:S(2)}) copy-start(bf16[128,128]{1,0:T(8,128)(2,1)} %param.9) | copy-start | bytes 98308
  10.4 113.2 %all-gather.7.cloned.1.call-start = ((), (), s32[]{:S(2)}) async-start(), calls=%async_computation.2 | async-start | bytes 5242880 | tf_op jit(solution)/shard_map/all_gather | solution.py:357
  12.5 10.8 %collective-permute-start = (bf16[128,1024]{1,0:T(8,128)(2,1)S(1)}, bf16[128,1024]{1,0:T(8,128)(2,1)S(1)}, u32[]{:S(2)}, u32[]{:S(2)}) collective-permute-start(bf16[128,1024]{1,0:T(8,128)(2,1)S(1)} %get-tuple-element.134), channel_id=1, source_target_pairs={{0,4},{4,8},{8,12},{12,16},{16,20},{20,24},{24,28},{1,5},{5,9},{9,... | collective-permute-start | bytes 786440 | tf_op jit(solution)/shard_map/ppermute | solution.py:307
  17.1 52.4 %copy-start.2 = (bf16[512,1024]{1,0:T(8,128)(2,1)}, bf16[512,1024]{1,0:T(8,128)(2,1)S(1)}, u32[]{:S(2)}) copy-start(bf16[512,1024]{1,0:T(8,128)(2,1)S(1)} %get-tuple-element.80.refs_4_) | copy-start | bytes 3145732
  23.3 0.7 copy-start.17
  24.1 34.4 %collective-permute-start.1 = (bf16[512,1024]{1,0:T(8,128)(2,1)}, bf16[512,1024]{1,0:T(8,128)(2,1)}, u32[]{:S(2)}, u32[]{:S(2)}) collective-permute-start(bf16[512,1024]{1,0:T(8,128)(2,1)} %get-tuple-element.90.refs_4_), channel_id=1, source_target_pairs={{0,8},{4,12},{8,16},{12,20},{16,24},{20,28},{1,9},{5,13},{9,17},{1... | collective-permute-start | bytes 3145736 | tf_op jit(solution)/shard_map/ppermute | solution.py:307
  27.5 30.9 %collective-permute-start.2 = (bf16[512,1024]{1,0:T(8,128)(2,1)}, bf16[512,1024]{1,0:T(8,128)(2,1)}, u32[]{:S(2)}, u32[]{:S(2)}) collective-permute-start(bf16[512,1024]{1,0:T(8,128)(2,1)} %get-tuple-element.90.refs_4_), channel_id=1, source_target_pairs={{8,0},{12,4},{16,8},{20,12},{24,16},{28,20},{9,1},{13,5},{17,9},{2... | collective-permute-start | bytes 3145736 | tf_op jit(solution)/shard_map/ppermute | solution.py:307
  30.9 29.5 %collective-permute-start.3 = (bf16[1024,512]{1,0:T(8,128)(2,1)}, bf16[1024,512]{1,0:T(8,128)(2,1)}, u32[]{:S(2)}, u32[]{:S(2)}) collective-permute-start(bf16[1024,512]{1,0:T(8,128)(2,1)} %get-tuple-element.70), channel_id=1, source_target_pairs={{0,4},{4,0},{8,12},{12,8},{16,20},{20,16},{24,28},{28,24},{1,5},{5... | collective-permute-start | bytes 3145736 | tf_op jit(solution)/shard_map/ppermute | solution.py:307
  31.6 26.9 %collective-permute-start.4 = (bf16[128,1024]{1,0:T(8,128)(2,1)}, bf16[128,1024]{1,0:T(8,128)(2,1)S(1)}, u32[]{:S(2)}, u32[]{:S(2)}) collective-permute-start(bf16[128,1024]{1,0:T(8,128)(2,1)} %get-tuple-element.133), channel_id=1, source_target_pairs={{0,4},{4,8},{8,12},{12,16},{16,20},{20,24},{24,28},{1,5},{5,9},{9,... | collective-permute-start | bytes 786440 | tf_op jit(solution)/shard_map/ppermute | solution.py:307
  45.7 0.9 copy-start.18
  56.5 1.3 copy-start.12
  60.4 49.8 %collective-permute-start.7 = (bf16[1024,1024]{1,0:T(8,128)(2,1)S(1)}, bf16[1024,1024]{1,0:T(8,128)(2,1)S(1)}, u32[]{:S(2)}, u32[]{:S(2)}) collective-permute-start(bf16[1024,1024]{1,0:T(8,128)(2,1)S(1)} %get-tuple-element.83.refs_2_), channel_id=1, source_target_pairs={{0,4},{4,0},{8,12},{12,8},{16,20},{20,16},{24,28},{28,24},{1,5},{5... | collective-permute-start | bytes 6291464 | tf_op jit(solution)/shard_map/ppermute | solution.py:307
  61.0 26.4 %collective-permute-start.5 = (bf16[512,1024]{1,0:T(8,128)(2,1)}, bf16[512,1024]{1,0:T(8,128)(2,1)S(1)}, u32[]{:S(2)}, u32[]{:S(2)}) collective-permute-start(bf16[512,1024]{1,0:T(8,128)(2,1)} %collective-permute-done.1), channel_id=1, source_target_pairs={{8,16},{12,20},{16,24},{20,28},{9,17},{13,21},{17,25},{21,29},{10,... | collective-permute-start | bytes 3145736 | tf_op jit(solution)/shard_map/ppermute | solution.py:307
  63.6 28.2 %collective-permute-start.6 = (bf16[512,1024]{1,0:T(8,128)(2,1)}, bf16[512,1024]{1,0:T(8,128)(2,1)S(1)}, u32[]{:S(2)}, u32[]{:S(2)}) collective-permute-start(bf16[512,1024]{1,0:T(8,128)(2,1)} %collective-permute-done.2), channel_id=1, source_target_pairs={{16,8},{20,12},{8,0},{12,4},{17,9},{21,13},{9,1},{13,5},{18,10},{2... | collective-permute-start | bytes 3145736 | tf_op jit(solution)/shard_map/ppermute | solution.py:307
  65.5 40.5 %collective-permute-start.8 = (bf16[512,1024]{1,0:T(8,128)(2,1)S(1)}, bf16[512,1024]{1,0:T(8,128)(2,1)S(1)}, u32[]{:S(2)}, u32[]{:S(2)}) collective-permute-start(bf16[512,1024]{1,0:T(8,128)(2,1)S(1)} %get-tuple-element.80.refs_4_), channel_id=1, source_target_pairs={{0,8},{4,12},{8,16},{12,20},{16,24},{20,28},{1,9},{5,13},{9,17},{1... | collective-permute-start | bytes 3145736 | tf_op jit(solution)/shard_map/ppermute | solution.py:307
  69.5 40.7 %collective-permute-start.9 = (bf16[512,1024]{1,0:T(8,128)(2,1)S(1)}, bf16[512,1024]{1,0:T(8,128)(2,1)S(1)}, u32[]{:S(2)}, u32[]{:S(2)}) collective-permute-start(bf16[512,1024]{1,0:T(8,128)(2,1)S(1)} %get-tuple-element.80.refs_4_), channel_id=1, source_target_pairs={{8,0},{12,4},{16,8},{20,12},{24,16},{28,20},{9,1},{13,5},{17,9},{2... | collective-permute-start | bytes 3145736 | tf_op jit(solution)/shard_map/ppermute | solution.py:307
  81.8 1.4 copy-start.11
  87.4 22.8 %copy-start.21 = (bf16[512,1024]{1,0:T(8,128)(2,1)}, bf16[512,1024]{1,0:T(8,128)(2,1)S(1)}, u32[]{:S(2)}) copy-start(bf16[512,1024]{1,0:T(8,128)(2,1)S(1)} %collective-permute-done.5) | copy-start | bytes 3145732
  91.8 19.8 %copy-start.22 = (bf16[512,1024]{1,0:T(8,128)(2,1)}, bf16[512,1024]{1,0:T(8,128)(2,1)S(1)}, u32[]{:S(2)}) copy-start(bf16[512,1024]{1,0:T(8,128)(2,1)S(1)} %collective-permute-done.6) | copy-start | bytes 3145732
  105.9 5.6 %copy-start.23 = (bf16[512,1024]{1,0:T(8,128)(2,1)}, bf16[512,1024]{1,0:T(8,128)(2,1)S(1)}, u32[]{:S(2)}) copy-start(bf16[512,1024]{1,0:T(8,128)(2,1)S(1)} %collective-permute-done.8) | copy-start | bytes 3145732
  110.2 1.6 copy-start.25
  110.2 1.3 copy-start
  111.8 47.2 %collective-permute-start.13 = (bf16[1024,1024]{1,0:T(8,128)(2,1)}, bf16[1024,1024]{1,0:T(8,128)(2,1)}, u32[]{:S(2)}, u32[]{:S(2)}) collective-permute-start(bf16[1024,1024]{1,0:T(8,128)(2,1)} %get-tuple-element.89.refs_2_), channel_id=1, source_target_pairs={{0,4},{4,0},{8,12},{12,8},{16,20},{20,16},{24,28},{28,24},{1,5},{5... | collective-permute-start | bytes 6291464 | tf_op jit(solution)/shard_map/ppermute | solution.py:307
  114.7 25.7 %collective-permute-start.14 = (bf16[512,1024]{1,0:T(8,128)(2,1)S(1)}, bf16[512,1024]{1,0:T(8,128)(2,1)}, u32[]{:S(2)}, u32[]{:S(2)}) collective-permute-start(bf16[512,1024]{1,0:T(8,128)(2,1)S(1)} %broadcast_select_fusion.5.refs_6_), channel_id=1, source_target_pairs={{16,24},{20,28},{8,0},{12,4},{17,25},{21,29},{9,1},{13,5},{18,26},... | collective-permute-start | bytes 3145736 | tf_op jit(solution)/shard_map/ppermute | solution.py:307
  117.8 41.2 %collective-permute-start.11 = (bf16[512,1024]{1,0:T(8,128)(2,1)}, bf16[512,1024]{1,0:T(8,128)(2,1)}, u32[]{:S(2)}, u32[]{:S(2)}) collective-permute-start(bf16[512,1024]{1,0:T(8,128)(2,1)} %copy-done.23), channel_id=1, source_target_pairs={{8,16},{12,20},{16,24},{20,28},{9,17},{13,21},{17,25},{21,29},{10,... | collective-permute-start | bytes 3145736 | tf_op jit(solution)/shard_map/ppermute | solution.py:307
  121.6 37.4 %collective-permute-start.12 = (bf16[512,1024]{1,0:T(8,128)(2,1)}, bf16[512,1024]{1,0:T(8,128)(2,1)}, u32[]{:S(2)}, u32[]{:S(2)}) collective-permute-start(bf16[512,1024]{1,0:T(8,128)(2,1)} %copy-done.25), channel_id=1, source_target_pairs={{16,8},{20,12},{8,0},{12,4},{17,9},{21,13},{9,1},{13,5},{18,10},{2... | collective-permute-start | bytes 3145736 | tf_op jit(solution)/shard_map/ppermute | solution.py:307
  123.6 1.6 copy-start.1
  130.3 28.8 %collective-permute-start.10 = (bf16[512,1024]{1,0:T(8,128)(2,1)}, bf16[512,1024]{1,0:T(8,128)(2,1)}, u32[]{:S(2)}, u32[]{:S(2)}) collective-permute-start(bf16[512,1024]{1,0:T(8,128)(2,1)} %shard_map.104), channel_id=1, source_target_pairs={{0,8},{4,12},{24,16},{28,20},{1,9},{5,13},{25,17},{29,21},{2,10},{... | collective-permute-start | bytes 3145736 | tf_op jit(solution)/shard_map/ppermute | solution.py:307
  160.4 24.0 %collective-permute-start.18 = (bf16[512,1024]{1,0:T(8,128)(2,1)S(1)}, bf16[512,1024]{1,0:T(8,128)(2,1)}, u32[]{:S(2)}, u32[]{:S(2)}) collective-permute-start(bf16[512,1024]{1,0:T(8,128)(2,1)S(1)} %broadcast_select_fusion.4.refs_6_), channel_id=1, source_target_pairs={{16,24},{20,28},{8,0},{12,4},{17,25},{21,29},{9,1},{13,5},{18,26},... | collective-permute-start | bytes 3145736 | tf_op jit(solution)/shard_map/ppermute | solution.py:307
  165.9 66.9 %collective-permute-start.19 = (bf16[1024,1024]{1,0:T(8,128)(2,1)}, bf16[1024,1024]{1,0:T(8,128)(2,1)}, u32[]{:S(2)}, u32[]{:S(2)}) collective-permute-start(bf16[1024,1024]{1,0:T(8,128)(2,1)} %shard_map.105), channel_id=1, source_target_pairs={{0,4},{4,0},{8,12},{12,8},{16,20},{20,16},{24,28},{28,24},{1,5},{5... | collective-permute-start | bytes 6291464 | tf_op jit(solution)/shard_map/ppermute | solution.py:307
  172.6 11.8 %copy-start.24 = (bf16[512,1024]{1,0:T(8,128)(2,1)S(1)}, bf16[512,1024]{1,0:T(8,128)(2,1)}, u32[]{:S(2)}) copy-start(bf16[512,1024]{1,0:T(8,128)(2,1)} %copy-done.23) | copy-start | bytes 3145732
  172.6 11.8 %copy-start.26 = (bf16[512,1024]{1,0:T(8,128)(2,1)S(1)}, bf16[512,1024]{1,0:T(8,128)(2,1)}, u32[]{:S(2)}) copy-start(bf16[512,1024]{1,0:T(8,128)(2,1)} %copy-done.25) | copy-start | bytes 3145732
  172.6 43.2 %collective-permute-start.15 = (bf16[512,1024]{1,0:T(8,128)(2,1)}, bf16[512,1024]{1,0:T(8,128)(2,1)}, u32[]{:S(2)}, u32[]{:S(2)}) collective-permute-start(bf16[512,1024]{1,0:T(8,128)(2,1)} %shard_map.107), channel_id=1, source_target_pairs={{0,8},{4,12},{24,16},{28,20},{1,9},{5,13},{25,17},{29,21},{2,10},{... | collective-permute-start | bytes 3145736 | tf_op jit(solution)/shard_map/ppermute | solution.py:307
  174.0 41.8 %collective-permute-start.16 = (bf16[512,1024]{1,0:T(8,128)(2,1)}, bf16[512,1024]{1,0:T(8,128)(2,1)}, u32[]{:S(2)}, u32[]{:S(2)}) collective-permute-start(bf16[512,1024]{1,0:T(8,128)(2,1)} %shard_map.107), channel_id=1, source_target_pairs={{8,16},{12,20},{16,8},{20,12},{9,17},{13,21},{17,9},{21,13},{10,18... | collective-permute-start | bytes 3145736 | tf_op jit(solution)/shard_map/ppermute | solution.py:307
  182.8 1.9 copy-start.3
  182.8 33.0 %collective-permute-start.17 = (bf16[512,1024]{1,0:T(8,128)(2,1)}, bf16[512,1024]{1,0:T(8,128)(2,1)}, u32[]{:S(2)}, u32[]{:S(2)}) collective-permute-start(bf16[512,1024]{1,0:T(8,128)(2,1)} %shard_map.108), channel_id=1, source_target_pairs={{0,8},{4,12},{24,16},{28,20},{1,9},{5,13},{25,17},{29,21},{2,10},{... | collective-permute-start | bytes 3145736 | tf_op jit(solution)/shard_map/ppermute | solution.py:307
  184.7 8.0 %copy-start.5 = (bf16[512,1024]{1,0:T(8,128)(2,1)}, bf16[512,1024]{1,0:T(8,128)(2,1)S(1)}, u32[]{:S(2)}) copy-start(bf16[512,1024]{1,0:T(8,128)(2,1)S(1)} %get-tuple-element.139.refs_7_) | copy-start | bytes 3145732
  184.8 8.0 %copy-start.7 = (bf16[512,1024]{1,0:T(8,128)(2,1)}, bf16[512,1024]{1,0:T(8,128)(2,1)S(1)}, u32[]{:S(2)}) copy-start(bf16[512,1024]{1,0:T(8,128)(2,1)S(1)} %get-tuple-element.140.refs_5_) | copy-start | bytes 3145732
  192.7 103.6 %collective-permute-start.25 = (bf16[1024,1024]{1,0:T(8,128)(2,1)}, bf16[1024,1024]{1,0:T(8,128)(2,1)}, u32[]{:S(2)}, u32[]{:S(2)}) collective-permute-start(bf16[1024,1024]{1,0:T(8,128)(2,1)} %shard_map.109), channel_id=1, source_target_pairs={{0,4},{4,0},{8,12},{12,8},{16,20},{20,16},{24,28},{28,24},{1,5},{5... | collective-permute-start | bytes 6291464 | tf_op jit(solution)/shard_map/ppermute | solution.py:307
  194.3 1.2 copy-start.4
  195.6 1.2 copy-start.6
  196.8 1.2 copy-start.8
  226.9 5.9 %copy-start.19 = (bf16[128,1024]{1,0:T(8,128)(2,1)S(1)}, bf16[128,1024]{1,0:T(8,128)(2,1)}, u32[]{:S(2)}) copy-start(bf16[128,1024]{1,0:T(8,128)(2,1)} %copy-done.17) | copy-start | bytes 786436
  245.5 12.3 %collective-permute-start.24 = (bf16[128,1024]{1,0:T(8,128)(2,1)S(1)}, bf16[128,1024]{1,0:T(8,128)(2,1)S(1)}, u32[]{:S(2)}, u32[]{:S(2)}) collective-permute-start(bf16[128,1024]{1,0:T(8,128)(2,1)S(1)} %slice.33), channel_id=1, source_target_pairs={{4,0},{8,4},{12,8},{16,12},{20,16},{24,20},{28,24},{5,1},{9,5},{13... | collective-permute-start | bytes 786440 | tf_op jit(solution)/shard_map/ppermute | solution.py:307
  247.9 28.0 %collective-permute-start.20 = (bf16[512,1024]{1,0:T(8,128)(2,1)S(1)}, bf16[512,1024]{1,0:T(8,128)(2,1)S(1)}, u32[]{:S(2)}, u32[]{:S(2)}) collective-permute-start(bf16[512,1024]{1,0:T(8,128)(2,1)S(1)} %shard_map.112), channel_id=1, source_target_pairs={{0,8},{4,12},{8,16},{12,20},{16,24},{20,28},{1,9},{5,13},{9,17},{1... | collective-permute-start | bytes 3145736 | tf_op jit(solution)/shard_map/ppermute | solution.py:307
  252.3 28.0 %collective-permute-start.21 = (bf16[512,1024]{1,0:T(8,128)(2,1)S(1)}, bf16[512,1024]{1,0:T(8,128)(2,1)S(1)}, u32[]{:S(2)}, u32[]{:S(2)}) collective-permute-start(bf16[512,1024]{1,0:T(8,128)(2,1)S(1)} %shard_map.113), channel_id=1, source_target_pairs={{8,0},{12,4},{16,8},{20,12},{24,16},{28,20},{9,1},{13,5},{17,9},{2... | collective-permute-start | bytes 3145736 | tf_op jit(solution)/shard_map/ppermute | solution.py:307
  254.2 35.2 %collective-permute-start.22 = (bf16[512,1024]{1,0:T(8,128)(2,1)S(1)}, bf16[512,1024]{1,0:T(8,128)(2,1)S(1)}, u32[]{:S(2)}, u32[]{:S(2)}) collective-permute-start(bf16[512,1024]{1,0:T(8,128)(2,1)S(1)} %shard_map.111), channel_id=1, source_target_pairs={{0,8},{4,12},{24,16},{28,20},{1,9},{5,13},{25,17},{29,21},{2,10},{... | collective-permute-start | bytes 3145736 | tf_op jit(solution)/shard_map/ppermute | solution.py:307
  257.8 38.6 %collective-permute-start.23 = (bf16[512,1024]{1,0:T(8,128)(2,1)S(1)}, bf16[512,1024]{1,0:T(8,128)(2,1)S(1)}, u32[]{:S(2)}, u32[]{:S(2)}) collective-permute-start(bf16[512,1024]{1,0:T(8,128)(2,1)S(1)} %shard_map.111), channel_id=1, source_target_pairs={{8,16},{12,20},{16,8},{20,12},{9,17},{13,21},{17,9},{21,13},{10,18... | collective-permute-start | bytes 3145736 | tf_op jit(solution)/shard_map/ppermute | solution.py:307
  275.9 1.0 copy-start.13
  280.3 1.0 copy-start.15
  308.8 49.5 %collective-permute-start.27 = (bf16[512,1024]{1,0:T(8,128)(2,1)}, bf16[512,1024]{1,0:T(8,128)(2,1)}, u32[]{:S(2)}, u32[]{:S(2)}) collective-permute-start(bf16[512,1024]{1,0:T(8,128)(2,1)} %shard_map.118), channel_id=1, source_target_pairs={{8,0},{12,4},{16,8},{20,12},{24,16},{28,20},{9,1},{13,5},{17,9},{2... | collective-permute-start | bytes 3145736 | tf_op jit(solution)/shard_map/ppermute | solution.py:307
  310.7 47.6 %collective-permute-start.26 = (bf16[512,1024]{1,0:T(8,128)(2,1)}, bf16[512,1024]{1,0:T(8,128)(2,1)}, u32[]{:S(2)}, u32[]{:S(2)}) collective-permute-start(bf16[512,1024]{1,0:T(8,128)(2,1)} %shard_map.117), channel_id=1, source_target_pairs={{0,8},{4,12},{8,16},{12,20},{16,24},{20,28},{1,9},{5,13},{9,17},{1... | collective-permute-start | bytes 3145736 | tf_op jit(solution)/shard_map/ppermute | solution.py:307
  328.0 1.3 copy-start.9
  329.4 16.9 %collective-permute-start.28 = (bf16[128,1024]{1,0:T(8,128)(2,1)}, bf16[128,1024]{1,0:T(8,128)(2,1)S(1)}, u32[]{:S(2)}, u32[]{:S(2)}) collective-permute-start(bf16[128,1024]{1,0:T(8,128)(2,1)} %slice.34), channel_id=1, source_target_pairs={{4,0},{8,4},{12,8},{16,12},{20,16},{24,20},{28,24},{5,1},{9,5},{13... | collective-permute-start | bytes 786440 | tf_op jit(solution)/shard_map/ppermute | solution.py:307
  332.2 13.4 %all-to-all-start = ((f32[8,16,128]{2,1,0:T(8,128)}), f32[8,16,128]{2,1,0:T(8,128)S(1)}, u32[]{:S(2)}, u32[]{:S(2)}) async-start(f32[8,16,128]{2,1,0:T(8,128)} %bitcast.13), calls=%async_computation | async-start | bytes 131072 | tf_op jit(solution)/shard_map/all_to_all | solution.py:471
  337.9 1.2 copy-start.14
  339.2 1.2 copy-start.16
  346.2 1.6 copy-start.10
Sparse Core Ops, SparseCore 0:
  10.5 34.6 all-gather.4
  60.5 33.6 all-gather.6

commit v4 on v3

--- a/solution.py
+++ b/solution.py
@@ -108,7 +108,7 @@
             here,
             here,
             here,
-            pl.BlockSpec((FILT, LANES), lambda i: (0, i)),
+            pl.BlockSpec((FILT, LANES), lambda i: (0, chunk * tiles + i)),
             pl.BlockSpec((GPT * FILT, 2 * FILT), lambda i: (chunk * tiles + i, 0)),
         ],
         out_specs=[out, out],
@@ -164,7 +164,7 @@
 
     args = [own, *others, q, k, v, mixed, prior]
     in_specs = [part] * (1 + n_other) + [here] * 3 + [part]
-    in_specs.append(pl.BlockSpec((FILT, LANES), lambda i: (0, i)))
+    in_specs.append(pl.BlockSpec((FILT, LANES), lambda i: (0, chunk * tiles + i)))
     aliases = {}
     if filled is not None:
         aliases = {len(args): 0}
@@ -267,31 +267,28 @@
             cot[0], gated[...], (((0,), (0,)), ((), ())), preferred_element_type=F32
         )
         total = term if total is None else total + term
-    for j, came in enumerate(refs[2 * n : -1], 1):
-        total = total + came[...].astype(F32) * pick[j].astype(F32)
     out[...] = total.astype(out.dtype)
 
 
-def weight_rows(pick, cots, gateds, came, dtype):
+def weight_rows(pick, cots, gateds, dtype):
     _, rows, depth = cots[0].shape
     width = gateds[0].shape[1]
     tile = min(512, width)
     n = len(cots)
     cot_spec = pl.BlockSpec((1, rows, depth), lambda i, pick: (pick[0], 0, 0))
     gated_spec = pl.BlockSpec((rows, tile), lambda i, pick: (0, i))
-    out_spec = pl.BlockSpec((depth, tile), lambda i, pick: (0, i))
     return pl.pallas_call(
         functools.partial(rows_kernel, n),
         grid_spec=pltpu.PrefetchScalarGridSpec(
             num_scalar_prefetch=1,
             grid=(width // tile,),
-            in_specs=[cot_spec] * n + [gated_spec] * n + [out_spec] * len(came),
-            out_specs=out_spec,
+            in_specs=[cot_spec] * n + [gated_spec] * n,
+            out_specs=pl.BlockSpec((depth, tile), lambda i, pick: (0, i)),
         ),
         out_shape=jax.ShapeDtypeStruct((depth, width), dtype),
         compiler_params=params(),
         cost_estimate=cost(2 * n * rows * depth * width, 2 * n * rows * (depth + width)),
-    )(pick, *cots, *gateds, *came)
+    )(pick, *cots, *gateds)
 
 
 def shards(seq, ch, queries, keys, values, filters, grad_out, out_weight):
@@ -317,12 +314,73 @@
     each = range(chunks)
     up_pairs, down_pairs = [(0, 1), (1, 2), (2, 3)], [(1, 0), (2, 1), (3, 2)]
 
-    priors = []
-    for h in each:
-        tail = (slice(rows - FILT, rows), slice(h * cols, (h + 1) * cols))
-        priors.append(
-            send(product_of(keys[tail], values[tail]), [(i, i + 1) for i in range(seq - 1)])
-        )
+    def second_step(h):
+        return along_line(up1[h], [(1, 2), (2, 3)]), along_line(down1[h], [(2, 1), (1, 0)])
+
+    def third_step(x):
+        return along_line(x, [(2, 3), (1, 0)])
+
+    def merge(pair):
+        return jnp.where(z >= 2, *pair)
+
+    def slots(h):
+        slot_a = jnp.where(z == 0, down1[h], up1[h])
+        slot_c = jnp.where((z == 0) | (z == 3), third[h], down1[h])
+        return [halves[h], slot_a, second[h], slot_c]
+
+    order = jnp.stack(
+        [
+            z,
+            jnp.where(z == 0, 1, z - 1),
+            jnp.where(z >= 2, z - 2, z + 2),
+            jnp.where(z == 3, 0, jnp.where(z == 1, 2, 3)),
+        ]
+    ).astype(jnp.int32)
+
+    def swap_gated(h):
+        return [around_inner(gateds[h], r) for r in range(1, inner)]
+
+    first_block = jnp.where(z == 0, 3, 0)
+    second_block = jnp.where(z == 0, 2, jnp.where(z == 1, 3, jnp.where(z == 2, 0, 1)))
+
+    def block_rows(block, h, dtype=F32):
+        pick = jnp.asarray(block, jnp.int32).reshape(1)
+        return weight_rows(pick, cots, [gateds[h]] + got[h], dtype)
+
+    def last_rows(h):
+        return block_rows(jnp.minimum(z + 1, 3), h), block_rows(jnp.maximum(z - 1, 0), h)
+
+    def send_first(x):
+        return along_line(x, [(0, 1), (3, 2)])
+
+    def send_second(rows_here, came):
+        x = (rows_here + came.astype(F32)).astype(BF16)
+        return along_line(x, [(0, 1), (3, 2)]), along_line(x, [(1, 2), (2, 1)])
+
+    def send_third(rows_here, outer_in, inner_in):
+        up, down = rows_here
+        outer_in, inner_in = outer_in.astype(F32), inner_in.astype(F32)
+        up = (up + jnp.where(z == 1, outer_in, inner_in)).astype(BF16)
+        down = (down + jnp.where(z == 1, inner_in, outer_in)).astype(BF16)
+        return along_line(up, up_pairs), along_line(down, down_pairs)
+
+    def last_sum(h):
+        below, above = sums[h]
+        return (finals[h] + below.astype(F32) + above.astype(F32)).astype(BF16)
+
+    def shares(h, weights):
+        return [gate_grad(order, cots[r], weights, BF16) for r in range(1, inner)]
+
+    def send_shares(parts):
+        return [around_inner(part, inner - r) for r, part in enumerate(parts, 1)]
+
+    up1, down1, gateds, mixeds, got = ([None] * chunks for _ in range(5))
+    second, third, sums, parts, others, owns = ([None] * chunks for _ in range(6))
+    later_halves = list(each[1:])
+
+    prior = send(
+        product_of(keys[rows - FILT :], values[rows - FILT :]), [(i, i + 1) for i in range(seq - 1)]
+    )
     paired = inner == 2 and ch == LINE
     other = grad_out
     cots = []
@@ -332,27 +390,19 @@
         cots = [lax.all_gather(kept, "ch", axis=0, tiled=False)]
     back, ahead = tables(filters)
     halves = [out_weight[:, h * cols : (h + 1) * cols] for h in each]
-    priors[0], other, halves = fence(priors[0], other, halves)
-
-    up1, down1 = [None] * chunks, [None] * chunks
+    prior, other, halves = fence(prior, other, halves)
+
     up1[0], down1[0] = along_line(halves[0], up_pairs), along_line(halves[0], down_pairs)
     swapped = around_inner(other, 1) if paired else other
-    gateds, mixeds = [None] * chunks, [None] * chunks
-    gateds[0], mixeds[0] = forward(queries, keys, values, priors[0], back, 0, chunks)
-    up1, down1, swapped, halves, gateds, cots, priors = fence(
-        up1, down1, swapped, halves, gateds, cots, priors
+    for h in later_halves:
+        held = after(halves[h], back)
+        up1[h], down1[h] = along_line(held, up_pairs), along_line(held, down_pairs)
+    gateds[0], mixeds[0] = forward(queries, keys, values, prior, back, 0, chunks)
+    up1[0], down1[0], swapped, gateds, cots, prior = fence(
+        up1[0], down1[0], swapped, gateds, cots, prior
     )
 
-    def second_step(h):
-        return along_line(up1[h], [(1, 2), (2, 3)]), along_line(down1[h], [(2, 1), (1, 0)])
-
-    def swap_gated(h):
-        return [around_inner(gateds[h], r) for r in range(1, inner)]
-
-    second = [None] * chunks
     second[0] = second_step(0)
-    for h in each[1:]:
-        up1[h], down1[h] = along_line(halves[h], up_pairs), along_line(halves[h], down_pairs)
     if paired:
         cots.append(lax.all_gather(swapped, "ch", axis=0, tiled=False))
     else:
@@ -361,110 +411,74 @@
         for shift in range(inner):
             part = lax.dynamic_index_in_dim(full, (y + shift) % inner, 0, keepdims=False)
             cots.append(part if shift == 0 else around_inner(part, shift))
-    got = [None] * chunks
     got[0] = swap_gated(0)
-    for h in each[1:]:
-        gateds[h], mixeds[h] = forward(queries, keys, values, priors[h], back, h, chunks)
-    second[0], got, up1, down1, gateds = fence(second[0], got, up1, down1, gateds)
-
-    def merge(pair):
-        return jnp.where(z >= 2, *pair)
-
-    def third_step(x):
-        return along_line(x, [(2, 3), (1, 0)])
-
-    def slots(h):
-        slot_a = jnp.where(z == 0, down1[h], up1[h])
-        slot_c = jnp.where((z == 0) | (z == 3), third[h], down1[h])
-        return [halves[h], slot_a, second[h], slot_c]
-
-    order = jnp.stack(
-        [
-            z,
-            jnp.where(z == 0, 1, z - 1),
-            jnp.where(z >= 2, z - 2, z + 2),
-            jnp.where(z == 3, 0, jnp.where(z == 1, 2, 3)),
-        ]
-    ).astype(jnp.int32)
-
-    first_block = jnp.where(z == 0, 3, 0)
-    second_block = jnp.where(z == 0, 2, jnp.where(z == 1, 3, jnp.where(z == 2, 0, 1)))
-    at_one, at_two = z == 1, z == 2
-
-    def block_rows(block, h, *came):
-        pick = [block] + [flag for _, flag in came]
-        pick = jnp.stack([jnp.asarray(p, jnp.int32) for p in pick])
-        return weight_rows(pick, cots, [gateds[h]] + got[h], [x for x, _ in came], BF16)
-
-    def send_first(x):
-        return along_line(x, [(0, 1), (3, 2)])
-
-    def send_second(x):
-        return along_line(x, [(0, 1), (3, 2)]), along_line(x, [(1, 2), (2, 1)])
-
-    def sum_third(h, outer_in, inner_in):
-        return (
-            block_rows(jnp.minimum(z + 1, 3), h, (outer_in, at_one), (inner_in, at_two)),
-            block_rows(jnp.maximum(z - 1, 0), h, (inner_in, at_one), (outer_in, at_two)),
-        )
-
-    def send_third(last_up, last_down):
-        return along_line(last_up, up_pairs), along_line(last_down, down_pairs)
-
-    def shares(h, weights):
-        return [gate_grad(order, cots[r], weights, BF16) for r in range(1, inner)]
-
-    def send_shares(parts):
-        return [around_inner(part, inner - r) for r, part in enumerate(parts, 1)]
-
-    third, sums, parts, others, owns = ([None] * chunks for _ in range(5))
+    for h in later_halves:
+        gateds[h], mixeds[h] = forward(queries, keys, values, prior, back, h, chunks)
+    up1, down1, gateds = fence(up1, down1, gateds)
+
+    for h in later_halves:
+        second[h] = second_step(h)
+    second[0], got[0], gateds, cots = fence(second[0], got[0], gateds, cots)
+
     second[0] = merge(second[0])
     third[0] = third_step(second[0])
-    for h in each[1:]:
-        second[h] = second_step(h)
+    for h in later_halves:
         got[h] = swap_gated(h)
-    sums[0] = send_first(block_rows(first_block, 0))
+    sums[0] = send_first(block_rows(first_block, 0, BF16))
+    mids, lasts, finals = ([None] * chunks for _ in range(3))
+    mids[0] = block_rows(second_block, 0)
+    second, mids[0] = fence(second, mids[0])
+
+    for h in later_halves:
+        second[h] = merge(second[h])
+        third[h] = third_step(second[h])
+    sums[0] = send_second(mids[0], sums[0])
+    lasts[0] = last_rows(0)
+    third[0], lasts[0] = fence(third[0], lasts[0])
+
     weights = slots(0)
     parts[0] = shares(0, weights)
+    parts[0], got[1:] = fence(parts[0], got[1:])
+    others[0] = send_shares(parts[0])
+
+    for h in later_halves:
+        sums[h] = send_first(block_rows(first_block, h, BF16))
+    sums[0] = send_third(lasts[0], *sums[0])
     owns[0] = gate_grad(order, cots[0], weights, F32)
-    others[0] = send_shares(parts[0])
-    sums, second, got, parts, owns = fence(sums, second, got, parts, owns)
-
-    for h in each[1:]:
-        second[h] = merge(second[h])
-        third[h] = third_step(second[h])
-    sums[0] = send_second(block_rows(second_block, 0, (sums[0], 1)))
-    for h in each[1:]:
-        sums[h] = send_first(block_rows(first_block, h))
-    for h in each[1:]:
+    for h in later_halves:
+        mids[h] = block_rows(second_block, h)
+    third, owns[0], mids = fence(third, owns[0], mids)
+
+    for h in later_halves:
         weights = slots(h)
         parts[h] = shares(h, weights)
         owns[h] = gate_grad(order, cots[0], weights, F32)
+    parts[1:], sums = fence(parts[1:], sums)
+    for h in later_halves:
         others[h] = send_shares(parts[h])
-    sums, parts, owns = fence(sums, parts, owns)
-
-    ready = [block_rows(second_block, h, (sums[h], 1)) for h in each[1:]]
-    last = sum_third(0, *sums[0])
-    ready, last, others[0] = fence(ready, last, others[0])
-    sums[0] = send_third(*last)
-    for h in each[1:]:
-        sums[h] = send_second(ready[h - 1])
+        sums[h] = send_second(mids[h], sums[h])
+        lasts[h] = last_rows(h)
+    finals = [block_rows(z, h) for h in each]
+    lasts, finals, others[0], owns = fence(lasts, finals, others[0], owns)
 
     grad_queries = None
     grad_kv = None
     taps = [None] * chunks
     for h in each:
         grad_queries, gm, taps[h] = middle(
-            owns[h], others[h], queries, keys, values, mixeds[h], priors[h], grad_queries, h, chunks
+            owns[h], others[h], queries, keys, values, mixeds[h], prior, grad_queries, h, chunks
         )
         later = send(gm[:FILT], [(i + 1, i) for i in range(seq - 1)])
+        if h == 0:
+            for g in later_halves:
+                sums[g] = send_third(lasts[g], *after(sums[g], gm))
         grad_kv = backward(gm, later, keys, values, ahead, grad_kv, h, chunks)
         if h == 0:
-            sums, grad_kv, others = fence(sums, grad_kv, others)
-            for g in each[1:]:
-                sums[g] = send_third(*sum_third(g, *sums[g]))
-    sums[-1], grad_kv = fence(sums[-1], grad_kv)
-    done = [block_rows(z, h, *((x, 1) for x in sums[h])) for h in each]
+            done = [last_sum(0)]
+            grad_kv, others, owns, done = fence(grad_kv, others, owns, done)
+    for h in later_halves:
+        sums[h], _ = fence(sums[h], gm)
+        done.append(last_sum(h))
     grad_weight = jnp.concatenate(done, axis=1)
     taps = jnp.concatenate(taps, axis=0)[:, 1 : FILT + 1][:, ::-1]
     taps = taps.T.reshape(seq, FILT // seq, -1)

time: 376 us -> 360 us (0.957)
  waiting for transfers between devices: 79.6 us -> 54.1 us
  other arithmetic: 9.28 us -> 25 us
  starting transfers between devices: 76.9 us -> 88.5 us
  Pallas kernels: 168 us -> 157 us
  local copies, waits for them, and re-layouts: 24.7 us -> 16.4 us
    ppermute x29 -> x28, waiting for transfers between devices: 79.5 us -> 54 us  [send(): return lax.ppermute(x, 'seq', pairs)]
    convert_element_type x0 -> x6, other arithmetic: none -> 15 us  [the longest x2 7.31 us: send_third(): down = (down + jnp.where(z == 1, inner_in, outer_in)).astype(BF16)]
    ppermute x29 -> x28, starting transfers between devices: 71 us -> 82.9 us  [send(): return lax.ppermute(x, 'seq', pairs)]
    pallas_call x10, Pallas kernels: 57.6 us -> 47 us  [weight_rows(): pl.pallas_call(functools.partial(rows_kernel, n), grid_spec=pltpu.Prefetc...]
    unnamed x56 -> x44, local copies, waits for them, and re-layouts: 18.7 us -> 9.57 us
  transfers between devices with their start and end apart: 32 -> 31, of which waited for: 14 -> 8; matrix products, arithmetic and copies ran while one was open for 3% -> 8% of each run, Pallas kernels for 40% -> 41%
where the time goes in v4:
time: 360 us; the launch traced here: 356 us
  Pallas kernels  157 us (44%)
  starting transfers between devices  88.5 us (25%)
  waiting for transfers between devices  54.1 us (15%)
  other arithmetic  25 us (7%)
  local copies, waits for them, and re-layouts  16.4 us (5%)
  between operations  14.8 us (4%)
    ppermute x28, starting transfers between devices, send(): return lax.ppermute(x, 'seq', pairs)  82.9 us
    ppermute x28, waiting for transfers between devices, send(): return lax.ppermute(x, 'seq', pairs)  54 us
    pallas_call x10, Pallas kernels, weight_rows(): pl.pallas_call(functools.partial(rows_kernel, n), grid_spec=pltpu.Prefetc...  47 us
    pallas_call x4, Pallas kernels, gate_grad(): pl.pallas_call(gate_kernel, grid_spec=pltpu.PrefetchScalarGridSpec(num_sc...  33.5 us
    pallas_call x2, Pallas kernels, middle(): pl.pallas_call(kernel, grid=(tiles,), in_specs=in_specs, out_specs=[here,...  25.5 us
    pallas_call x2, Pallas kernels, backward(): pl.pallas_call(backward_kernel, grid=(tiles,), in_specs=in_specs, out_spe...  20.9 us
    pallas_call x2, Pallas kernels, forward(): pl.pallas_call(forward_kernel, grid=(tiles,), in_specs=[here, here, here,...  19.8 us
    pallas_call x1, Pallas kernels, tables(): pl.pallas_call(table_kernel, grid=(groups // GPT,), in_specs=[seed, seed]...  10.4 us
  transfers between devices with their start and end apart: 31, of which 8 were waited for; matrix products, arithmetic and copies ran while one was open for 8% of the time, Pallas kernels for 41%

profile of v4, /device:TPU:10, one launch (start us, length us, event | category | flops | bytes accessed | tf_op | source)
XLA Modules:
  0.0 356.0 jit_solution(2922420681540468263)
XLA Ops:
  7.2 3.0 constant_dynamic-slice_fusion
  10.3 1.5 multiply_convert_fusion
  11.8 3.4 collective-permute-start
  16.4 11.8 %collective-permute-done.prior.refs_5_ = bf16[128,2048]{1,0:T(8,128)(2,1)S(1)} collective-permute-done((bf16[128,2048]{1,0:T(8,128)(2,1)S(1)}, bf16[128,2048]{1,0:T(8,128)(2,1)S(1)}, u32[]{:S(2)}, u32[]{:S(2)}) %collective-permute-start) | collective-permute-done | bytes 524320 | tf_op jit(solution)/shard_map/ppermute | solution.py:304
  29.7 2.3 collective-permute-start.2
  32.0 3.5 collective-permute-start.1
  35.8 10.4 %shard_map.101 = (bf16[16384,256]{1,0:T(8,128)(2,1)}, bf16[16384,256]{1,0:T(8,128)(2,1)}) custom-call(f32[128,256]{1,0:T(8,128)S(1)} %maximum_maximum_fusion.back_ref, f32[128,256]{1,0:T(8,128)S(1)} %concatenate.13.ahead_ref), custom_call_target="tpu_custom_call" | custom-call | flops 524288 | bytes 262144 | tf_op jit(solution)/shard_map/pallas_call | solution.py:54
  47.2 9.9 %shard_map.102 = (bf16[1024,1024]{1,0:T(8,128)(2,1)S(1)}, bf16[1024,1024]{1,0:T(8,128)(2,1)S(1)}) custom-call(bf16[1024,2048]{1,0:T(8,128)(2,1)} %refs_1_.3, bf16[1024,2048]{1,0:T(8,128)(2,1)} %k.7, bf16[1024,2048]{1,0:T(8,128)(2,1)} %v.7, bf16[128,2048]{1,0:T(8,128)(2,1)S(1)} %copy-done.9, bf16[16384,256]{1,0:T(8,128)(2,1)} %get-tuple-element.80.table), custom_call_target="tpu_custom_call" | custom-call | flops 67108864 | bytes 229376 | tf_op jit(solution)/shard_map/pallas_call | solution.py:104
  57.1 1.3 copy-done.15
  58.5 1.5 collective-permute-start.6
  60.0 2.9 collective-permute-start.8
  62.9 3.5 collective-permute-start.7
  66.4 6.0 %collective-permute-start.4 = (bf16[512,1024]{1,0:T(8,128)(2,1)}, bf16[512,1024]{1,0:T(8,128)(2,1)}, u32[]{:S(2)}, u32[]{:S(2)}) collective-permute-start(bf16[512,1024]{1,0:T(8,128)(2,1)} %collective-permute-done.1), channel_id=1, source_target_pairs={{8,16},{12,20},{16,24},{20,28},{9,17},{13,21},{17,25},{21,29},{10,... | collective-permute-start | bytes 3145736 | tf_op jit(solution)/shard_map/ppermute | solution.py:304
  72.3 1.9 collective-permute-start.5
  75.3 10.0 %shard_map.103 = (bf16[1024,1024]{1,0:T(8,128)(2,1)S(1)}, bf16[1024,1024]{1,0:T(8,128)(2,1)S(1)}) custom-call(bf16[1024,2048]{1,0:T(8,128)(2,1)} %refs_1_.3, bf16[1024,2048]{1,0:T(8,128)(2,1)} %k.7, bf16[1024,2048]{1,0:T(8,128)(2,1)} %v.7, bf16[128,2048]{1,0:T(8,128)(2,1)S(1)} %copy-done.10, bf16[16384,256]{1,0:T(8,128)(2,1)} %get-tuple-element.80.table), custom_call_target="tpu_custom_call" | custom-call | flops 67108864 | bytes 229376 | tf_op jit(solution)/shard_map/pallas_call | solution.py:104
  85.3 1.3 copy-done
  88.6 1.4 collective-permute-done.7
  90.0 5.9 %collective-permute-start.10 = (bf16[512,1024]{1,0:T(8,128)(2,1)}, bf16[512,1024]{1,0:T(8,128)(2,1)}, u32[]{:S(2)}, u32[]{:S(2)}) collective-permute-start(bf16[512,1024]{1,0:T(8,128)(2,1)} %collective-permute-done.7), channel_id=1, source_target_pairs={{8,16},{12,20},{16,24},{20,28},{9,17},{13,21},{17,25},{21,29},{10,... | collective-permute-start | bytes 3145736 | tf_op jit(solution)/shard_map/ppermute | solution.py:304
  95.8 1.9 collective-permute-start.11
  97.7 14.8 %collective-permute-done.4 = bf16[512,1024]{1,0:T(8,128)(2,1)} collective-permute-done((bf16[512,1024]{1,0:T(8,128)(2,1)}, bf16[512,1024]{1,0:T(8,128)(2,1)}, u32[]{:S(2)}, u32[]{:S(2)}) %collective-permute-start.4) | collective-permute-done | bytes 1048608 | tf_op jit(solution)/shard_map/ppermute | solution.py:304
  112.5 5.3 %shard_map.118 = bf16[512,1024]{1,0:T(8,128)(2,1)} custom-call(s32[1]{0:T(128)} %bitcast.9.pick, bf16[4,1024,512]{2,1,0:T(8,128)(2,1)} %bitcast.32, bf16[4,1024,512]{2,1,0:T(8,128)(2,1)} %bitcast.14, bf16[1024,1024]{1,0:T(8,128)(2,1)S(1)} %get-tuple-element.97.refs_2_, bf16[1024,1024]{1,0:T(8,128)(2,1)} %collective-permute-done.6.refs_3_), custom_call_target="tpu_custom_call" | custom-call | flops 33554432 | bytes 98304 | tf_op jit(solution)/shard_map/pallas_call | solution.py:280
  119.8 1.3 broadcast_select_fusion.5.refs_6_
  121.2 6.5 %collective-permute-start.9 = (bf16[512,1024]{1,0:T(8,128)(2,1)S(1)}, bf16[512,1024]{1,0:T(8,128)(2,1)}, u32[]{:S(2)}, u32[]{:S(2)}) collective-permute-start(bf16[512,1024]{1,0:T(8,128)(2,1)S(1)} %broadcast_select_fusion.5.refs_6_), channel_id=1, source_target_pairs={{16,24},{20,28},{8,0},{12,4},{17,25},{21,29},{9,1},{13,5},{18,26},... | collective-permute-start | bytes 3145736 | tf_op jit(solution)/shard_map/ppermute | solution.py:304
  127.7 4.6 %shard_map.106 = f32[512,1024]{1,0:T(8,128)S(1)} custom-call(s32[1]{0:T(128)} %bitcast.8.pick, bf16[4,1024,512]{2,1,0:T(8,128)(2,1)} %bitcast.33, bf16[4,1024,512]{2,1,0:T(8,128)(2,1)} %bitcast.15, bf16[1024,1024]{1,0:T(8,128)(2,1)S(1)} %get-tuple-element.97.refs_2_, bf16[1024,1024]{1,0:T(8,128)(2,1)} %collective-permute-done.6.refs_3_), custom_call_target="tpu_custom_call" | custom-call | flops 33554432 | bytes 98304 | tf_op jit(solution)/shard_map/pallas_call | solution.py:280
  132.3 6.5 %collective-permute-done.16 = bf16[512,1024]{1,0:T(8,128)(2,1)} collective-permute-done((bf16[512,1024]{1,0:T(8,128)(2,1)}, bf16[512,1024]{1,0:T(8,128)(2,1)}, u32[]{:S(2)}, u32[]{:S(2)}) %collective-permute-start.16) | collective-permute-done | bytes 1048608 | tf_op jit(solution)/shard_map/ppermute | solution.py:304
  138.9 2.5 add_convert_fusion.3
  141.4 4.5 %collective-permute-start.18 = (bf16[512,1024]{1,0:T(8,128)(2,1)}, bf16[512,1024]{1,0:T(8,128)(2,1)}, u32[]{:S(2)}, u32[]{:S(2)}) collective-permute-start(bf16[512,1024]{1,0:T(8,128)(2,1)} %add_convert_fusion.3), channel_id=1, source_target_pairs={{8,16},{12,20},{16,8},{20,12},{9,17},{13,21},{17,9},{21,13},{10,18... | collective-permute-start | bytes 3145736 | tf_op jit(solution)/shard_map/ppermute | solution.py:304
  147.3 1.3 broadcast_select_fusion.4.refs_6_
  148.7 6.5 %collective-permute-start.14 = (bf16[512,1024]{1,0:T(8,128)(2,1)S(1)}, bf16[512,1024]{1,0:T(8,128)(2,1)}, u32[]{:S(2)}, u32[]{:S(2)}) collective-permute-start(bf16[512,1024]{1,0:T(8,128)(2,1)S(1)} %broadcast_select_fusion.4.refs_6_), channel_id=1, source_target_pairs={{16,24},{20,28},{8,0},{12,4},{17,25},{21,29},{9,1},{13,5},{18,26},... | collective-permute-start | bytes 3145736 | tf_op jit(solution)/shard_map/ppermute | solution.py:304
  155.2 4.6 %shard_map.105 = f32[512,1024]{1,0:T(8,128)S(1)} custom-call(s32[1]{0:T(128)} %bitcast.3.pick, bf16[4,1024,512]{2,1,0:T(8,128)(2,1)} %bitcast.34, bf16[4,1024,512]{2,1,0:T(8,128)(2,1)} %bitcast.16, bf16[1024,1024]{1,0:T(8,128)(2,1)S(1)} %get-tuple-element.97.refs_2_, bf16[1024,1024]{1,0:T(8,128)(2,1)} %collective-permute-done.6.refs_3_), custom_call_target="tpu_custom_call" | custom-call | flops 33554432 | bytes 98304 | tf_op jit(solution)/shard_map/pallas_call | solution.py:280
  159.8 4.7 %shard_map.104 = f32[512,1024]{1,0:T(8,128)S(1)} custom-call(s32[1]{0:T(128)} %bitcast.2.pick, bf16[4,1024,512]{2,1,0:T(8,128)(2,1)} %bitcast.35, bf16[4,1024,512]{2,1,0:T(8,128)(2,1)} %bitcast.17, bf16[1024,1024]{1,0:T(8,128)(2,1)S(1)} %get-tuple-element.97.refs_2_, bf16[1024,1024]{1,0:T(8,128)(2,1)} %collective-permute-done.6.refs_3_), custom_call_target="tpu_custom_call" | custom-call | flops 33554432 | bytes 98304 | tf_op jit(solution)/shard_map/pallas_call | solution.py:280
  164.5 1.7 broadcast_select_fusion.1
  166.2 8.2 %shard_map.107 = bf16[1024,1024]{1,0:T(8,128)(2,1)} custom-call(s32[4]{0:T(128)S(1)} %pad_add_fusion.order, bf16[4,1024,512]{2,1,0:T(8,128)(2,1)} %bitcast.18, bf16[4,1024,512]{2,1,0:T(8,128)(2,1)} %bitcast.19, bf16[4,1024,512]{2,1,0:T(8,128)(2,1)} %bitcast.20, bf16[4,1024,512]{2,1,0:T(8,128)(2,1)} %bitcast.21, bf16[512,1024]{1,0:T(8,128)(2,1)} %get-tuple-element.77.refs_4_, ...), custom_call_target="tpu_custom_call" | custom-call | flops 67108864 | bytes 196608 | tf_op jit(solution)/shard_map/pallas_call | solution.py:246
  174.5 3.9 %fusion.3 = (bf16[512,1024]{1,0:T(8,128)(2,1)}, bf16[512,1024]{1,0:T(8,128)(2,1)}) fusion(f32[512,1024]{1,0:T(8,128)S(1)} %shard_map.105, bf16[512,1024]{1,0:T(8,128)(2,1)} %collective-permute-done.17, bf16[512,1024]{1,0:T(8,128)(2,1)} %collective-permute-done.18, pred[]{:T(512)S(6)} %eq.12, f32[512,1024]{1,0:T(8,128)S(1)} %shard_map.104), kind=kLoop, calls=%fused_computation.7 | loop fusion | flops 4194304 | bytes 8388609 | tf_op jit(solution)/shard_map/convert_element_type | solution.py:364
  178.3 1.9 collective-permute-start.20
  180.2 4.1 %collective-permute-start.19 = (bf16[512,1024]{1,0:T(8,128)(2,1)}, bf16[512,1024]{1,0:T(8,128)(2,1)S(1)}, u32[]{:S(2)}, u32[]{:S(2)}) collective-permute-start(bf16[512,1024]{1,0:T(8,128)(2,1)} %get-tuple-element.152), channel_id=1, source_target_pairs={{0,8},{4,12},{8,16},{12,20},{16,24},{20,28},{1,9},{5,13},{9,17},{1... | collective-permute-start | bytes 3145736 | tf_op jit(solution)/shard_map/ppermute | solution.py:304
  184.4 4.6 %shard_map.119 = bf16[512,1024]{1,0:T(8,128)(2,1)S(1)} custom-call(s32[1]{0:T(128)} %bitcast.9.pick, bf16[4,1024,512]{2,1,0:T(8,128)(2,1)} %bitcast.36, bf16[4,1024,512]{2,1,0:T(8,128)(2,1)} %bitcast.22, bf16[1024,1024]{1,0:T(8,128)(2,1)S(1)} %copy-done.1, bf16[1024,1024]{1,0:T(8,128)(2,1)} %collective-permute-done.12.refs_3_), custom_call_target="tpu_custom_call" | custom-call | flops 33554432 | bytes 98304 | tf_op jit(solution)/shard_map/pallas_call | solution.py:280
  191.2 8.6 %shard_map.112.own_ref = f32[1024,1024]{1,0:T(8,128)} custom-call(s32[4]{0:T(128)S(1)} %pad_add_fusion.order, bf16[4,1024,512]{2,1,0:T(8,128)(2,1)} %bitcast.37, bf16[4,1024,512]{2,1,0:T(8,128)(2,1)} %bitcast.38, bf16[4,1024,512]{2,1,0:T(8,128)(2,1)} %bitcast.39, bf16[4,1024,512]{2,1,0:T(8,128)(2,1)} %bitcast.40, ...), custom_call_target="tpu_custom_call" | custom-call | flops 67108864 | bytes 196608 | tf_op jit(solution)/shard_map/pallas_call | solution.py:246
  199.8 4.6 %shard_map.113 = f32[512,1024]{1,0:T(8,128)S(1)} custom-call(s32[1]{0:T(128)} %bitcast.8.pick, bf16[4,1024,512]{2,1,0:T(8,128)(2,1)} %bitcast.41, bf16[4,1024,512]{2,1,0:T(8,128)(2,1)} %bitcast.23, bf16[1024,1024]{1,0:T(8,128)(2,1)S(1)} %copy-done.1, bf16[1024,1024]{1,0:T(8,128)(2,1)} %collective-permute-done.12.refs_3_), custom_call_target="tpu_custom_call" | custom-call | flops 33554432 | bytes 98304 | tf_op jit(solution)/shard_map/pallas_call | solution.py:280
  204.4 1.8 broadcast_select_fusion
  206.3 8.0 %shard_map.117 = bf16[1024,1024]{1,0:T(8,128)(2,1)} custom-call(s32[4]{0:T(128)S(1)} %pad_add_fusion.order, bf16[4,1024,512]{2,1,0:T(8,128)(2,1)} %bitcast.24, bf16[4,1024,512]{2,1,0:T(8,128)(2,1)} %bitcast.25, bf16[4,1024,512]{2,1,0:T(8,128)(2,1)} %bitcast.26, bf16[4,1024,512]{2,1,0:T(8,128)(2,1)} %bitcast.27, bf16[512,1024]{1,0:T(8,128)(2,1)S(1)} %copy-done.3, ...), custom_call_target="tpu_custom_call" | custom-call | flops 67108864 | bytes 196608 | tf_op jit(solution)/shard_map/pallas_call | solution.py:246
  214.3 7.3 %collective-permute-done.21 = bf16[512,1024]{1,0:T(8,128)(2,1)} collective-permute-done((bf16[512,1024]{1,0:T(8,128)(2,1)S(1)}, bf16[512,1024]{1,0:T(8,128)(2,1)}, u32[]{:S(2)}, u32[]{:S(2)}) %collective-permute-start.21) | collective-permute-done | bytes 1048608 | tf_op jit(solution)/shard_map/ppermute | solution.py:304
  221.6 2.5 add_convert_fusion.1
  224.1 1.9 collective-permute-start.25
  228.4 4.6 %shard_map.110 = f32[512,1024]{1,0:T(8,128)S(1)} custom-call(s32[1]{0:T(128)} %bitcast.4.pick, bf16[4,1024,512]{2,1,0:T(8,128)(2,1)} %bitcast.42, bf16[4,1024,512]{2,1,0:T(8,128)(2,1)} %bitcast.28, bf16[1024,1024]{1,0:T(8,128)(2,1)S(1)} %get-tuple-element.97.refs_2_, bf16[1024,1024]{1,0:T(8,128)(2,1)} %collective-permute-done.6.refs_3_), custom_call_target="tpu_custom_call" | custom-call | flops 33554432 | bytes 98304 | tf_op jit(solution)/shard_map/pallas_call | solution.py:280
  233.0 4.7 %shard_map.111 = f32[512,1024]{1,0:T(8,128)S(1)} custom-call(s32[1]{0:T(128)} %bitcast.4.pick, bf16[4,1024,512]{2,1,0:T(8,128)(2,1)} %bitcast.43, bf16[4,1024,512]{2,1,0:T(8,128)(2,1)} %bitcast.29, bf16[1024,1024]{1,0:T(8,128)(2,1)S(1)} %copy-done.1, bf16[1024,1024]{1,0:T(8,128)(2,1)} %collective-permute-done.12.refs_3_), custom_call_target="tpu_custom_call" | custom-call | flops 33554432 | bytes 98304 | tf_op jit(solution)/shard_map/pallas_call | solution.py:280
  237.7 4.7 %shard_map.109 = f32[512,1024]{1,0:T(8,128)S(1)} custom-call(s32[1]{0:T(128)} %bitcast.3.pick, bf16[4,1024,512]{2,1,0:T(8,128)(2,1)} %bitcast.44, bf16[4,1024,512]{2,1,0:T(8,128)(2,1)} %bitcast.30, bf16[1024,1024]{1,0:T(8,128)(2,1)S(1)} %copy-done.1, bf16[1024,1024]{1,0:T(8,128)(2,1)} %collective-permute-done.12.refs_3_), custom_call_target="tpu_custom_call" | custom-call | flops 33554432 | bytes 98304 | tf_op jit(solution)/shard_map/pallas_call | solution.py:280
  242.4 1.4 copy-done.4
  243.8 4.6 %shard_map.108 = f32[512,1024]{1,0:T(8,128)S(1)} custom-call(s32[1]{0:T(128)} %bitcast.2.pick, bf16[4,1024,512]{2,1,0:T(8,128)(2,1)} %bitcast.45, bf16[4,1024,512]{2,1,0:T(8,128)(2,1)} %bitcast.31, bf16[1024,1024]{1,0:T(8,128)(2,1)S(1)} %copy-done.1, bf16[1024,1024]{1,0:T(8,128)(2,1)} %collective-permute-done.12.refs_3_), custom_call_target="tpu_custom_call" | custom-call | flops 33554432 | bytes 98304 | tf_op jit(solution)/shard_map/pallas_call | solution.py:280
  248.4 8.7 %shard_map.114.own_ref = f32[1024,1024]{1,0:T(8,128)} custom-call(s32[4]{0:T(128)S(1)} %pad_add_fusion.order, bf16[4,1024,512]{2,1,0:T(8,128)(2,1)} %bitcast.46, bf16[4,1024,512]{2,1,0:T(8,128)(2,1)} %bitcast.47, bf16[4,1024,512]{2,1,0:T(8,128)(2,1)} %bitcast.48, bf16[4,1024,512]{2,1,0:T(8,128)(2,1)} %bitcast.49, bf16[512,1024]{1,0:T(8,128)(2,1)S(1)} %copy-done.3, ...), custom_call_target="tpu_custom_call" | custom-call | flops 67108864 | bytes 196608 | tf_op jit(solution)/shard_map/pallas_call | solution.py:246
  257.2 12.8 %shard_map.115 = (bf16[1024,2048]{1,0:T(8,128)(2,1)}, bf16[1024,1024]{1,0:T(8,128)(2,1)S(1)}, f32[64,256]{1,0:T(8,128)S(1)}) custom-call(f32[1024,1024]{1,0:T(8,128)} %shard_map.112.own_ref, bf16[1024,1024]{1,0:T(8,128)(2,1)} %collective-permute-done.13.refs_0_, bf16[1024,2048]{1,0:T(8,128)(2,1)} %refs_1_.3, bf16[1024,2048]{1,0:T(8,128)(2,1)} %k.7, ...), custom_call_target="tpu_custom_call" | custom-call | flops 67108864 | bytes 294912 | tf_op jit(solution)/shard_map/pallas_call | solution.py:173
  270.1 3.4 fusion.7
  273.6 5.5 %collective-permute-start.27 = (bf16[512,1024]{1,0:T(8,128)(2,1)}, bf16[512,1024]{1,0:T(8,128)(2,1)}, u32[]{:S(2)}, u32[]{:S(2)}) collective-permute-start(bf16[512,1024]{1,0:T(8,128)(2,1)} %get-tuple-element.149), channel_id=1, source_target_pairs={{8,0},{12,4},{16,8},{20,12},{24,16},{28,20},{9,1},{13,5},{17,9},{2... | collective-permute-start | bytes 3145736 | tf_op jit(solution)/shard_map/ppermute | solution.py:304
  279.1 1.9 collective-permute-start.26
  281.0 5.6 %collective-permute-start.15 = (bf16[128,1024]{1,0:T(8,128)(2,1)S(1)}, bf16[128,1024]{1,0:T(8,128)(2,1)S(1)}, u32[]{:S(2)}, u32[]{:S(2)}) collective-permute-start(bf16[128,1024]{1,0:T(8,128)(2,1)S(1)} %slice.25), channel_id=1, source_target_pairs={{4,0},{8,4},{12,8},{16,12},{20,16},{24,20},{28,24},{5,1},{9,5},{13... | collective-permute-start | bytes 786440 | tf_op jit(solution)/shard_map/ppermute | solution.py:304
  287.2 10.5 %collective-permute-done.15.later = bf16[128,1024]{1,0:T(8,128)(2,1)S(1)} collective-permute-done((bf16[128,1024]{1,0:T(8,128)(2,1)S(1)}, bf16[128,1024]{1,0:T(8,128)(2,1)S(1)}, u32[]{:S(2)}, u32[]{:S(2)}) %collective-permute-start.15) | collective-permute-done | bytes 262176 | tf_op jit(solution)/shard_map/ppermute | solution.py:304
  297.7 10.4 %shard_map.116 = (bf16[1024,2048]{1,0:T(8,128)(2,1)}, bf16[1024,2048]{1,0:T(8,128)(2,1)}) custom-call(bf16[1024,1024]{1,0:T(8,128)(2,1)S(1)} %get-tuple-element.118.gm, bf16[128,1024]{1,0:T(8,128)(2,1)S(1)} %collective-permute-done.15.later, bf16[1024,2048]{1,0:T(8,128)(2,1)} %k.7, bf16[1024,2048]{1,0:T(8,128)(2,1)} %v.7, ...), custom_call_target="tpu_custom_call" | custom-call | flops 67108864 | bytes 229376 | tf_op jit(solution)/shard_map/pallas_call | solution.py:217
  308.2 12.7 %shard_map.120 = (bf16[1024,2048]{1,0:T(8,128)(2,1)}, bf16[1024,1024]{1,0:T(8,128)(2,1)S(1)}, f32[64,256]{1,0:T(8,128)S(1)}) custom-call(f32[1024,1024]{1,0:T(8,128)} %shard_map.114.own_ref, bf16[1024,1024]{1,0:T(8,128)(2,1)} %collective-permute-done.22.refs_0_, bf16[1024,2048]{1,0:T(8,128)(2,1)} %refs_1_.3, ...), custom_call_target="tpu_custom_call", output_to_operand_aliasing={{0}: (7, {})} | custom-call | flops 67108864 | bytes 294912 | tf_op jit(solution)/shard_map/pallas_call | solution.py:173
  323.1 5.5 %all-to-all-start = ((f32[8,16,128]{2,1,0:T(8,128)}), f32[8,16,128]{2,1,0:T(8,128)S(1)}, u32[]{:S(2)}, u32[]{:S(2)}) async-start(f32[8,16,128]{2,1,0:T(8,128)} %bitcast.11), calls=%async_computation | async-start | bytes 131072 | tf_op jit(solution)/shard_map/all_to_all | solution.py:485
  328.6 1.7 slice.26
  330.2 3.4 collective-permute-start.23
  333.6 2.0 add_convert_fusion
  335.7 1.5 pad_maximum_fusion
  338.7 10.4 %shard_map.121 = (bf16[1024,2048]{1,0:T(8,128)(2,1)}, bf16[1024,2048]{1,0:T(8,128)(2,1)}) custom-call(bf16[1024,1024]{1,0:T(8,128)(2,1)S(1)} %copy-done.13, bf16[128,1024]{1,0:T(8,128)(2,1)S(1)} %collective-permute-done.23.later, bf16[1024,2048]{1,0:T(8,128)(2,1)} %k.7, bf16[1024,2048]{1,0:T(8,128)(2,1)} %v.7, ...), custom_call_target="tpu_custom_call", output_to_operand_aliasing={{0}: (5, {}), {1}: (6, {})} | custom-call | flops 67108864 | bytes 229376 | tf_op jit(solution)/shard_map/pallas_call | solution.py:217
  (92 shorter events, 19.4 us)
Async XLA Ops:
  7.2 51.3 %all-gather.5.cloned.1.call-start = ((), (), s32[]{:S(2)}) async-start(), calls=%async_computation.1 | async-start | bytes 5242880 | tf_op jit(solution)/shard_map/all_gather | solution.py:390
  10.2 5.0 %copy-start.16 = (bf16[512,2048]{1,0:T(8,128)(2,1)S(1)}, bf16[512,2048]{1,0:T(8,128)(2,1)}, u32[]{:S(2)}) copy-start(bf16[512,2048]{1,0:T(8,128)(2,1)} %param.11) | copy-start | bytes 6291460
  10.3 102.3 %all-gather.7.cloned.1.call-start = ((), (), s32[]{:S(2)}) async-start(), calls=%async_computation.2 | async-start | bytes 5242880 | tf_op jit(solution)/shard_map/all_gather | solution.py:407
  11.8 23.7 %copy-start.21 = (bf16[128,128]{1,0:T(8,128)(2,1)S(1)}, bf16[128,128]{1,0:T(8,128)(2,1)}, u32[]{:S(2)}) copy-start(bf16[128,128]{1,0:T(8,128)(2,1)} %param.9) | copy-start | bytes 98308
  11.8 16.5 %collective-permute-start = (bf16[128,2048]{1,0:T(8,128)(2,1)S(1)}, bf16[128,2048]{1,0:T(8,128)(2,1)S(1)}, u32[]{:S(2)}, u32[]{:S(2)}) collective-permute-start(bf16[128,2048]{1,0:T(8,128)(2,1)S(1)} %multiply_convert_fusion), channel_id=1, source_target_pairs={{0,4},{4,8},{8,12},{12,16},{16,20},{20,24},{24,28},{1,5},{5,9},{9,... | collective-permute-start | bytes 1572872 | tf_op jit(solution)/shard_map/ppermute | solution.py:304
  16.4 46.5 %copy-start.2 = (bf16[512,1024]{1,0:T(8,128)(2,1)}, bf16[512,1024]{1,0:T(8,128)(2,1)S(1)}, u32[]{:S(2)}) copy-start(bf16[512,1024]{1,0:T(8,128)(2,1)S(1)} %get-tuple-element.86.refs_4_) | copy-start | bytes 3145732
  28.2 0.8 copy-start.8
  29.0 29.4 %collective-permute-start.3 = (bf16[1024,512]{1,0:T(8,128)(2,1)}, bf16[1024,512]{1,0:T(8,128)(2,1)}, u32[]{:S(2)}, u32[]{:S(2)}) collective-permute-start(bf16[1024,512]{1,0:T(8,128)(2,1)} %get-tuple-element.78), channel_id=1, source_target_pairs={{0,4},{4,0},{8,12},{12,8},{16,20},{20,16},{24,28},{28,24},{1,5},{5... | collective-permute-start | bytes 3145736 | tf_op jit(solution)/shard_map/ppermute | solution.py:304
  29.7 28.8 %collective-permute-start.2 = (bf16[512,1024]{1,0:T(8,128)(2,1)}, bf16[512,1024]{1,0:T(8,128)(2,1)}, u32[]{:S(2)}, u32[]{:S(2)}) collective-permute-start(bf16[512,1024]{1,0:T(8,128)(2,1)} %get-tuple-element.77.refs_4_), channel_id=1, source_target_pairs={{8,0},{12,4},{16,8},{20,12},{24,16},{28,20},{9,1},{13,5},{17,9},{2... | collective-permute-start | bytes 3145736 | tf_op jit(solution)/shard_map/ppermute | solution.py:304
  32.0 26.5 %collective-permute-start.1 = (bf16[512,1024]{1,0:T(8,128)(2,1)}, bf16[512,1024]{1,0:T(8,128)(2,1)}, u32[]{:S(2)}, u32[]{:S(2)}) collective-permute-start(bf16[512,1024]{1,0:T(8,128)(2,1)} %get-tuple-element.77.refs_4_), channel_id=1, source_target_pairs={{0,8},{4,12},{8,16},{12,20},{16,24},{20,28},{1,9},{5,13},{9,17},{1... | collective-permute-start | bytes 3145736 | tf_op jit(solution)/shard_map/ppermute | solution.py:304
  46.2 1.0 copy-start.9
  57.1 1.3 copy-start.15
  58.5 54.0 %collective-permute-start.6 = (bf16[1024,1024]{1,0:T(8,128)(2,1)S(1)}, bf16[1024,1024]{1,0:T(8,128)(2,1)}, u32[]{:S(2)}, u32[]{:S(2)}) collective-permute-start(bf16[1024,1024]{1,0:T(8,128)(2,1)S(1)} %get-tuple-element.97.refs_2_), channel_id=1, source_target_pairs={{0,4},{4,0},{8,12},{12,8},{16,20},{20,16},{24,28},{28,24},{1,5},{5... | collective-permute-start | bytes 6291464 | tf_op jit(solution)/shard_map/ppermute | solution.py:304
  60.0 28.6 %collective-permute-start.8 = (bf16[512,1024]{1,0:T(8,128)(2,1)S(1)}, bf16[512,1024]{1,0:T(8,128)(2,1)}, u32[]{:S(2)}, u32[]{:S(2)}) collective-permute-start(bf16[512,1024]{1,0:T(8,128)(2,1)S(1)} %get-tuple-element.86.refs_4_), channel_id=1, source_target_pairs={{8,0},{12,4},{16,8},{20,12},{24,16},{28,20},{9,1},{13,5},{17,9},{2... | collective-permute-start | bytes 3145736 | tf_op jit(solution)/shard_map/ppermute | solution.py:304
  62.9 27.1 %collective-permute-start.7 = (bf16[512,1024]{1,0:T(8,128)(2,1)S(1)}, bf16[512,1024]{1,0:T(8,128)(2,1)}, u32[]{:S(2)}, u32[]{:S(2)}) collective-permute-start(bf16[512,1024]{1,0:T(8,128)(2,1)S(1)} %get-tuple-element.86.refs_4_), channel_id=1, source_target_pairs={{0,8},{4,12},{8,16},{12,20},{16,24},{20,28},{1,9},{5,13},{9,17},{1... | collective-permute-start | bytes 3145736 | tf_op jit(solution)/shard_map/ppermute | solution.py:304
  66.4 46.2 %collective-permute-start.4 = (bf16[512,1024]{1,0:T(8,128)(2,1)}, bf16[512,1024]{1,0:T(8,128)(2,1)}, u32[]{:S(2)}, u32[]{:S(2)}) collective-permute-start(bf16[512,1024]{1,0:T(8,128)(2,1)} %collective-permute-done.1), channel_id=1, source_target_pairs={{8,16},{12,20},{16,24},{20,28},{9,17},{13,21},{17,25},{21,29},{10,... | collective-permute-start | bytes 3145736 | tf_op jit(solution)/shard_map/ppermute | solution.py:304
  72.3 40.2 %collective-permute-start.5 = (bf16[512,1024]{1,0:T(8,128)(2,1)}, bf16[512,1024]{1,0:T(8,128)(2,1)}, u32[]{:S(2)}, u32[]{:S(2)}) collective-permute-start(bf16[512,1024]{1,0:T(8,128)(2,1)} %collective-permute-done.2), channel_id=1, source_target_pairs={{16,8},{20,12},{8,0},{12,4},{17,9},{21,13},{9,1},{13,5},{18,10},{2... | collective-permute-start | bytes 3145736 | tf_op jit(solution)/shard_map/ppermute | solution.py:304
  74.3 1.0 copy-start.10
  85.3 1.3 copy-start
  86.6 1.3 copy-start.14
  90.0 42.4 %collective-permute-start.10 = (bf16[512,1024]{1,0:T(8,128)(2,1)}, bf16[512,1024]{1,0:T(8,128)(2,1)}, u32[]{:S(2)}, u32[]{:S(2)}) collective-permute-start(bf16[512,1024]{1,0:T(8,128)(2,1)} %collective-permute-done.7), channel_id=1, source_target_pairs={{8,16},{12,20},{16,24},{20,28},{9,17},{13,21},{17,25},{21,29},{10,... | collective-permute-start | bytes 3145736 | tf_op jit(solution)/shard_map/ppermute | solution.py:304
  95.8 36.5 %collective-permute-start.11 = (bf16[512,1024]{1,0:T(8,128)(2,1)}, bf16[512,1024]{1,0:T(8,128)(2,1)}, u32[]{:S(2)}, u32[]{:S(2)}) collective-permute-start(bf16[512,1024]{1,0:T(8,128)(2,1)} %collective-permute-done.8), channel_id=1, source_target_pairs={{16,8},{20,12},{8,0},{12,4},{17,9},{21,13},{9,1},{13,5},{18,10},{2... | collective-permute-start | bytes 3145736 | tf_op jit(solution)/shard_map/ppermute | solution.py:304
  117.9 21.0 %collective-permute-start.16 = (bf16[512,1024]{1,0:T(8,128)(2,1)}, bf16[512,1024]{1,0:T(8,128)(2,1)}, u32[]{:S(2)}, u32[]{:S(2)}) collective-permute-start(bf16[512,1024]{1,0:T(8,128)(2,1)} %shard_map.118), channel_id=1, source_target_pairs={{0,8},{4,12},{24,16},{28,20},{1,9},{5,13},{25,17},{29,21},{2,10},{... | collective-permute-start | bytes 3145736 | tf_op jit(solution)/shard_map/ppermute | solution.py:304
  119.2 65.2 %collective-permute-start.12 = (bf16[1024,1024]{1,0:T(8,128)(2,1)}, bf16[1024,1024]{1,0:T(8,128)(2,1)}, u32[]{:S(2)}, u32[]{:S(2)}) collective-permute-start(bf16[1024,1024]{1,0:T(8,128)(2,1)} %copy-done), channel_id=1, source_target_pairs={{0,4},{4,0},{8,12},{12,8},{16,20},{20,16},{24,28},{28,24},{1,5},{5... | collective-permute-start | bytes 6291464 | tf_op jit(solution)/shard_map/ppermute | solution.py:304
  121.2 43.3 %collective-permute-start.9 = (bf16[512,1024]{1,0:T(8,128)(2,1)S(1)}, bf16[512,1024]{1,0:T(8,128)(2,1)}, u32[]{:S(2)}, u32[]{:S(2)}) collective-permute-start(bf16[512,1024]{1,0:T(8,128)(2,1)S(1)} %broadcast_select_fusion.5.refs_6_), channel_id=1, source_target_pairs={{16,24},{20,28},{8,0},{12,4},{17,25},{21,29},{9,1},{13,5},{18,26},... | collective-permute-start | bytes 3145736 | tf_op jit(solution)/shard_map/ppermute | solution.py:304
  141.4 33.0 %collective-permute-start.18 = (bf16[512,1024]{1,0:T(8,128)(2,1)}, bf16[512,1024]{1,0:T(8,128)(2,1)}, u32[]{:S(2)}, u32[]{:S(2)}) collective-permute-start(bf16[512,1024]{1,0:T(8,128)(2,1)} %add_convert_fusion.3), channel_id=1, source_target_pairs={{8,16},{12,20},{16,8},{20,12},{9,17},{13,21},{17,9},{21,13},{10,18... | collective-permute-start | bytes 3145736 | tf_op jit(solution)/shard_map/ppermute | solution.py:304
  145.9 28.5 %collective-permute-start.17 = (bf16[512,1024]{1,0:T(8,128)(2,1)}, bf16[512,1024]{1,0:T(8,128)(2,1)}, u32[]{:S(2)}, u32[]{:S(2)}) collective-permute-start(bf16[512,1024]{1,0:T(8,128)(2,1)} %add_convert_fusion.3), channel_id=1, source_target_pairs={{0,8},{4,12},{24,16},{28,20},{1,9},{5,13},{25,17},{29,21},{2,10},{... | collective-permute-start | bytes 3145736 | tf_op jit(solution)/shard_map/ppermute | solution.py:304
  148.7 55.7 %collective-permute-start.14 = (bf16[512,1024]{1,0:T(8,128)(2,1)S(1)}, bf16[512,1024]{1,0:T(8,128)(2,1)}, u32[]{:S(2)}, u32[]{:S(2)}) collective-permute-start(bf16[512,1024]{1,0:T(8,128)(2,1)S(1)} %broadcast_select_fusion.4.refs_6_), channel_id=1, source_target_pairs={{16,24},{20,28},{8,0},{12,4},{17,25},{21,29},{9,1},{13,5},{18,26},... | collective-permute-start | bytes 3145736 | tf_op jit(solution)/shard_map/ppermute | solution.py:304
  174.4 9.9 %copy-start.1 = (bf16[1024,1024]{1,0:T(8,128)(2,1)S(1)}, bf16[1024,1024]{1,0:T(8,128)(2,1)}, u32[]{:S(2)}) copy-start(bf16[1024,1024]{1,0:T(8,128)(2,1)} %copy-done) | copy-start | bytes 6291460
  178.3 35.9 %collective-permute-start.20 = (bf16[512,1024]{1,0:T(8,128)(2,1)}, bf16[512,1024]{1,0:T(8,128)(2,1)S(1)}, u32[]{:S(2)}, u32[]{:S(2)}) collective-permute-start(bf16[512,1024]{1,0:T(8,128)(2,1)} %get-tuple-element.151), channel_id=1, source_target_pairs={{8,0},{12,4},{16,8},{20,12},{24,16},{28,20},{9,1},{13,5},{17,9},{2... | collective-permute-start | bytes 3145736 | tf_op jit(solution)/shard_map/ppermute | solution.py:304
  180.2 34.0 %collective-permute-start.19 = (bf16[512,1024]{1,0:T(8,128)(2,1)}, bf16[512,1024]{1,0:T(8,128)(2,1)S(1)}, u32[]{:S(2)}, u32[]{:S(2)}) collective-permute-start(bf16[512,1024]{1,0:T(8,128)(2,1)} %get-tuple-element.152), channel_id=1, source_target_pairs={{0,8},{4,12},{8,16},{12,20},{16,24},{20,28},{1,9},{5,13},{9,17},{1... | collective-permute-start | bytes 3145736 | tf_op jit(solution)/shard_map/ppermute | solution.py:304
  189.0 32.6 %collective-permute-start.21 = (bf16[512,1024]{1,0:T(8,128)(2,1)S(1)}, bf16[512,1024]{1,0:T(8,128)(2,1)}, u32[]{:S(2)}, u32[]{:S(2)}) collective-permute-start(bf16[512,1024]{1,0:T(8,128)(2,1)S(1)} %shard_map.119), channel_id=1, source_target_pairs={{0,8},{4,12},{24,16},{28,20},{1,9},{5,13},{25,17},{29,21},{2,10},{... | collective-permute-start | bytes 3145736 | tf_op jit(solution)/shard_map/ppermute | solution.py:304
  190.3 66.9 %collective-permute-start.13 = (bf16[1024,1024]{1,0:T(8,128)(2,1)}, bf16[1024,1024]{1,0:T(8,128)(2,1)}, u32[]{:S(2)}, u32[]{:S(2)}) collective-permute-start(bf16[1024,1024]{1,0:T(8,128)(2,1)} %shard_map.107), channel_id=1, source_target_pairs={{0,4},{4,0},{8,12},{12,8},{16,20},{20,16},{24,28},{28,24},{1,5},{5... | collective-permute-start | bytes 6291464 | tf_op jit(solution)/shard_map/ppermute | solution.py:304
  204.4 1.9 copy-start.3
  214.2 9.9 %copy-start.17 = (bf16[512,1024]{1,0:T(8,128)(2,1)}, bf16[512,1024]{1,0:T(8,128)(2,1)S(1)}, u32[]{:S(2)}) copy-start(bf16[512,1024]{1,0:T(8,128)(2,1)S(1)} %collective-permute-done.20) | copy-start | bytes 3145732
  214.3 9.9 %copy-start.19 = (bf16[512,1024]{1,0:T(8,128)(2,1)}, bf16[512,1024]{1,0:T(8,128)(2,1)S(1)}, u32[]{:S(2)}) copy-start(bf16[512,1024]{1,0:T(8,128)(2,1)S(1)} %collective-permute-done.19) | copy-start | bytes 3145732
  224.1 45.9 %collective-permute-start.25 = (bf16[512,1024]{1,0:T(8,128)(2,1)}, bf16[512,1024]{1,0:T(8,128)(2,1)S(1)}, u32[]{:S(2)}, u32[]{:S(2)}) collective-permute-start(bf16[512,1024]{1,0:T(8,128)(2,1)} %add_convert_fusion.1), channel_id=1, source_target_pairs={{8,16},{12,20},{16,8},{20,12},{9,17},{13,21},{17,9},{21,13},{10,18... | collective-permute-start | bytes 3145736 | tf_op jit(solution)/shard_map/ppermute | solution.py:304
  226.0 44.0 %collective-permute-start.24 = (bf16[512,1024]{1,0:T(8,128)(2,1)}, bf16[512,1024]{1,0:T(8,128)(2,1)}, u32[]{:S(2)}, u32[]{:S(2)}) collective-permute-start(bf16[512,1024]{1,0:T(8,128)(2,1)} %add_convert_fusion.1), channel_id=1, source_target_pairs={{0,8},{4,12},{24,16},{28,20},{1,9},{5,13},{25,17},{29,21},{2,10},{... | collective-permute-start | bytes 3145736 | tf_op jit(solution)/shard_map/ppermute | solution.py:304
  227.3 80.8 %collective-permute-start.22 = (bf16[1024,1024]{1,0:T(8,128)(2,1)}, bf16[1024,1024]{1,0:T(8,128)(2,1)}, u32[]{:S(2)}, u32[]{:S(2)}) collective-permute-start(bf16[1024,1024]{1,0:T(8,128)(2,1)} %shard_map.117), channel_id=1, source_target_pairs={{0,4},{4,0},{8,12},{12,8},{16,20},{20,16},{24,28},{28,24},{1,5},{5... | collective-permute-start | bytes 6291464 | tf_op jit(solution)/shard_map/ppermute | solution.py:304
  242.4 1.4 copy-start.4
  248.4 8.8 %copy-start.6 = (f32[512,1024]{1,0:T(8,128)}, f32[512,1024]{1,0:T(8,128)S(1)}, u32[]{:S(2)}) copy-start(f32[512,1024]{1,0:T(8,128)S(1)} %shard_map.108) | copy-start | bytes 6291460
  248.4 8.8 %copy-start.11 = (bf16[128,2048]{1,0:T(8,128)(2,1)S(1)}, bf16[128,2048]{1,0:T(8,128)(2,1)}, u32[]{:S(2)}) copy-start(bf16[128,2048]{1,0:T(8,128)(2,1)} %copy-done.8) | copy-start | bytes 1572868
  257.2 12.9 %copy-start.5 = (f32[512,1024]{1,0:T(8,128)S(1)}, f32[512,1024]{1,0:T(8,128)}, u32[]{:S(2)}) copy-start(f32[512,1024]{1,0:T(8,128)} %copy-done.4) | copy-start | bytes 6291460
  257.2 12.9 %copy-start.7 = (f32[512,1024]{1,0:T(8,128)S(1)}, f32[512,1024]{1,0:T(8,128)}, u32[]{:S(2)}) copy-start(f32[512,1024]{1,0:T(8,128)} %copy-done.6) | copy-start | bytes 6291460
  270.1 16.5 %copy-start.18 = (bf16[512,1024]{1,0:T(8,128)(2,1)S(1)}, bf16[512,1024]{1,0:T(8,128)(2,1)}, u32[]{:S(2)}) copy-start(bf16[512,1024]{1,0:T(8,128)(2,1)} %copy-done.17) | copy-start | bytes 3145732
  270.1 16.5 %copy-start.20 = (bf16[512,1024]{1,0:T(8,128)(2,1)S(1)}, bf16[512,1024]{1,0:T(8,128)(2,1)}, u32[]{:S(2)}) copy-start(bf16[512,1024]{1,0:T(8,128)(2,1)} %copy-done.19) | copy-start | bytes 3145732
  273.6 60.1 %collective-permute-start.27 = (bf16[512,1024]{1,0:T(8,128)(2,1)}, bf16[512,1024]{1,0:T(8,128)(2,1)}, u32[]{:S(2)}, u32[]{:S(2)}) collective-permute-start(bf16[512,1024]{1,0:T(8,128)(2,1)} %get-tuple-element.149), channel_id=1, source_target_pairs={{8,0},{12,4},{16,8},{20,12},{24,16},{28,20},{9,1},{13,5},{17,9},{2... | collective-permute-start | bytes 3145736 | tf_op jit(solution)/shard_map/ppermute | solution.py:304
  279.1 54.6 %collective-permute-start.26 = (bf16[512,1024]{1,0:T(8,128)(2,1)}, bf16[512,1024]{1,0:T(8,128)(2,1)}, u32[]{:S(2)}, u32[]{:S(2)}) collective-permute-start(bf16[512,1024]{1,0:T(8,128)(2,1)} %get-tuple-element.150), channel_id=1, source_target_pairs={{0,8},{4,12},{8,16},{12,20},{16,24},{20,28},{1,9},{5,13},{9,17},{1... | collective-permute-start | bytes 3145736 | tf_op jit(solution)/shard_map/ppermute | solution.py:304
  281.0 16.7 %collective-permute-start.15 = (bf16[128,1024]{1,0:T(8,128)(2,1)S(1)}, bf16[128,1024]{1,0:T(8,128)(2,1)S(1)}, u32[]{:S(2)}, u32[]{:S(2)}) collective-permute-start(bf16[128,1024]{1,0:T(8,128)(2,1)S(1)} %slice.25), channel_id=1, source_target_pairs={{4,0},{8,4},{12,8},{16,12},{20,16},{24,20},{28,24},{5,1},{9,5},{13... | collective-permute-start | bytes 786440 | tf_op jit(solution)/shard_map/ppermute | solution.py:304
  320.9 1.3 copy-start.12
  323.1 14.1 %all-to-all-start = ((f32[8,16,128]{2,1,0:T(8,128)}), f32[8,16,128]{2,1,0:T(8,128)S(1)}, u32[]{:S(2)}, u32[]{:S(2)}) async-start(f32[8,16,128]{2,1,0:T(8,128)} %bitcast.11), calls=%async_computation | async-start | bytes 131072 | tf_op jit(solution)/shard_map/all_to_all | solution.py:485
  330.2 8.5 %collective-permute-start.23 = (bf16[128,1024]{1,0:T(8,128)(2,1)}, bf16[128,1024]{1,0:T(8,128)(2,1)S(1)}, u32[]{:S(2)}, u32[]{:S(2)}) collective-permute-start(bf16[128,1024]{1,0:T(8,128)(2,1)} %slice.26), channel_id=1, source_target_pairs={{4,0},{8,4},{12,8},{16,12},{20,16},{24,20},{28,24},{5,1},{9,5},{13... | collective-permute-start | bytes 786440 | tf_op jit(solution)/shard_map/ppermute | solution.py:304
  335.7 3.0 copy-start.13
Sparse Core Ops, SparseCore 0:
  10.4 34.6 all-gather.4
  58.6 34.7 all-gather.6

commit v5 on v4

--- a/solution.py
+++ b/solution.py
@@ -108,7 +108,7 @@
             here,
             here,
             here,
-            pl.BlockSpec((FILT, LANES), lambda i: (0, chunk * tiles + i)),
+            pl.BlockSpec((FILT, LANES), lambda i: (0, i)),
             pl.BlockSpec((GPT * FILT, 2 * FILT), lambda i: (chunk * tiles + i, 0)),
         ],
         out_specs=[out, out],
@@ -119,7 +119,7 @@
 
 
 def middle_kernel(own, others, q, k, v, mixed, prior, *rest):
-    gq_out, gm_out, taps_out = rest[-3:]
+    gq_out, gm_out, edge_out, taps_out = rest[-4:]
     blocks = q.shape[0] // FILT
     total = own[...].astype(F32)
     for other in others:
@@ -128,18 +128,15 @@
     gq_out[...] = (gg * mixed[...].astype(F32)).astype(BF16)
     gm = (gg * q[...].astype(F32)).astype(BF16)
     gm_out[...] = gm
+    edge_out[...] = gm[:FILT]
     ext = jnp.concatenate([prior[...], product_of(k[...], v[...])], axis=0)
-    group = group_of_lane(FILT, 2 * LANES)
-    lag = jnp.zeros((GPT * FILT, 2 * FILT), F32)
-    for b in range(0, blocks, 2):
-        lo = b * FILT
-        pair = jnp.concatenate([gm[lo : lo + FILT], gm[lo + FILT : lo + 2 * FILT]], axis=1)
-        stack = jnp.concatenate(
-            [jnp.where(group == g, pair, jnp.zeros_like(pair)) for g in range(GPT)], axis=0
-        )
-        lag = lag + lax.dot_general(
-            stack, windows(ext, b), (((1,), (1,)), ((), ())), preferred_element_type=F32
-        )
+    wide = jnp.concatenate([gm[b * FILT : (b + 1) * FILT] for b in range(blocks)], axis=1)
+    group = group_of_lane(FILT, blocks * LANES)
+    stack = jnp.concatenate(
+        [jnp.where(group == g, wide, jnp.zeros_like(wide)) for g in range(GPT)], axis=0
+    )
+    near = jnp.concatenate([ext[b * FILT : (b + 2) * FILT] for b in range(blocks)], axis=1)
+    lag = lax.dot_general(stack, near, (((1,), (1,)), ((), ())), preferred_element_type=F32)
     lag = lag.reshape(GPT, FILT, 2 * FILT)
     half = FILT // 2
     while half >= 8:
@@ -157,14 +154,14 @@
     groups = width // GROUP // chunks
     here = pl.BlockSpec((rows, LANES), lambda i: (0, chunk * tiles + i))
     part = pl.BlockSpec((rows, LANES), lambda i: (0, i))
+    edge = pl.BlockSpec((FILT, LANES), lambda i: (0, i))
     n_other = len(others)
 
     def kernel(own_ref, *refs):
         middle_kernel(own_ref, refs[:n_other], *refs[n_other:])
 
     args = [own, *others, q, k, v, mixed, prior]
-    in_specs = [part] * (1 + n_other) + [here] * 3 + [part]
-    in_specs.append(pl.BlockSpec((FILT, LANES), lambda i: (0, chunk * tiles + i)))
+    in_specs = [part] * (1 + n_other) + [here] * 3 + [part, edge]
     aliases = {}
     if filled is not None:
         aliases = {len(args): 0}
@@ -174,10 +171,11 @@
         kernel,
         grid=(tiles,),
         in_specs=in_specs,
-        out_specs=[here, part, pl.BlockSpec((GPT, 2 * FILT), lambda i: (i, 0))],
+        out_specs=[here, part, edge, pl.BlockSpec((GPT, 2 * FILT), lambda i: (i, 0))],
         out_shape=[
             jax.ShapeDtypeStruct((rows, width), BF16),
             jax.ShapeDtypeStruct((rows, width // chunks), BF16),
+            jax.ShapeDtypeStruct((FILT, width // chunks), BF16),
             jax.ShapeDtypeStruct((groups, 2 * FILT), F32),
         ],
         input_output_aliases=aliases,
@@ -226,37 +224,43 @@
     )(*args)
 
 
-def gate_kernel(order, *refs):
-    out = refs[-1]
-    total = jnp.dot(refs[0][0], refs[LINE][...], preferred_element_type=F32)
+def gate_kernel(pick, *refs):
+    own, up, down, second, third, out = refs[LINE:]
+    slots = (
+        own[...],
+        jnp.where(pick[LINE] == 1, down[...], up[...]),
+        second[...],
+        jnp.where(pick[LINE + 1] == 1, third[...], down[...]),
+    )
+    total = jnp.dot(refs[0][0], slots[0], preferred_element_type=F32)
     for j in range(1, LINE):
-        total = total + jnp.dot(refs[j][0], refs[LINE + j][...], preferred_element_type=F32)
+        total = total + jnp.dot(refs[j][0], slots[j], preferred_element_type=F32)
     out[...] = total.astype(out.dtype)
 
 
-def gate_grad(order, cot, weights, dtype):
+def gate_grad(pick, cot, weights):
     _, rows, depth = cot.shape
     width = weights[0].shape[1]
-    tile = min(256, rows)
+    tile = min(256, width)
 
     def cot_spec(j):
-        return pl.BlockSpec((1, tile, depth), lambda i, order: (order[j], i, 0))
-
-    weight_spec = pl.BlockSpec((depth, width), lambda i, order: (0, 0))
+        return pl.BlockSpec((1, rows, depth), lambda i, pick: (pick[j], 0, 0))
+
     return pl.pallas_call(
         gate_kernel,
         grid_spec=pltpu.PrefetchScalarGridSpec(
             num_scalar_prefetch=1,
-            grid=(rows // tile,),
-            in_specs=[cot_spec(j) for j in range(LINE)] + [weight_spec] * LINE,
-            out_specs=pl.BlockSpec((tile, width), lambda i, order: (i, 0)),
+            grid=(width // tile,),
+            in_specs=[cot_spec(j) for j in range(LINE)]
+            + [pl.BlockSpec((depth, tile), lambda i, pick: (0, i))] * len(weights),
+            out_specs=pl.BlockSpec((rows, tile), lambda i, pick: (0, i)),
         ),
-        out_shape=jax.ShapeDtypeStruct((rows, width), dtype),
+        out_shape=jax.ShapeDtypeStruct((rows, width), BF16),
         compiler_params=params(),
         cost_estimate=cost(
-            2 * rows * LINE * depth * width, 2 * LINE * depth * (rows + width) + 4 * rows * width
+            2 * rows * LINE * depth * width, 2 * LINE * depth * (rows + width) + 2 * rows * width
         ),
-    )(order, *([cot] * LINE), *weights)
+    )(pick, *([cot] * LINE), *weights)
 
 
 def rows_kernel(n, pick, *refs):
@@ -267,25 +271,26 @@
             cot[0], gated[...], (((0,), (0,)), ((), ())), preferred_element_type=F32
         )
         total = term if total is None else total + term
-    out[...] = total.astype(out.dtype)
-
-
-def weight_rows(pick, cots, gateds, dtype):
+    out[0] = total.astype(out.dtype)
+
+
+def weight_rows(pick, cots, gateds):
     _, rows, depth = cots[0].shape
     width = gateds[0].shape[1]
-    tile = min(512, width)
+    blocks = pick.shape[0]
+    tile = width if blocks > 1 else min(512, width)
     n = len(cots)
-    cot_spec = pl.BlockSpec((1, rows, depth), lambda i, pick: (pick[0], 0, 0))
-    gated_spec = pl.BlockSpec((rows, tile), lambda i, pick: (0, i))
+    cot_spec = pl.BlockSpec((1, rows, depth), lambda j, i, pick: (pick[j], 0, 0))
+    gated_spec = pl.BlockSpec((rows, tile), lambda j, i, pick: (0, i))
     return pl.pallas_call(
         functools.partial(rows_kernel, n),
         grid_spec=pltpu.PrefetchScalarGridSpec(
             num_scalar_prefetch=1,
-            grid=(width // tile,),
+            grid=(blocks, width // tile),
             in_specs=[cot_spec] * n + [gated_spec] * n,
-            out_specs=pl.BlockSpec((depth, tile), lambda i, pick: (0, i)),
+            out_specs=pl.BlockSpec((1, depth, tile), lambda j, i, pick: (j, 0, i)),
         ),
-        out_shape=jax.ShapeDtypeStruct((depth, width), dtype),
+        out_shape=jax.ShapeDtypeStruct((blocks, depth, width), BF16),
         compiler_params=params(),
         cost_estimate=cost(2 * n * rows * depth * width, 2 * n * rows * (depth + width)),
     )(pick, *cots, *gateds)
@@ -323,85 +328,94 @@
     def merge(pair):
         return jnp.where(z >= 2, *pair)
 
-    def slots(h):
-        slot_a = jnp.where(z == 0, down1[h], up1[h])
-        slot_c = jnp.where((z == 0) | (z == 3), third[h], down1[h])
-        return [halves[h], slot_a, second[h], slot_c]
-
-    order = jnp.stack(
+    pick = jnp.stack(
         [
             z,
             jnp.where(z == 0, 1, z - 1),
             jnp.where(z >= 2, z - 2, z + 2),
             jnp.where(z == 3, 0, jnp.where(z == 1, 2, 3)),
+            jnp.where(z == 0, 1, 0),
+            jnp.where((z == 0) | (z == 3), 1, 0),
         ]
     ).astype(jnp.int32)
 
+    def weights(h):
+        return [halves[h], up1[h], down1[h], second[h], third[h]]
+
     def swap_gated(h):
         return [around_inner(gateds[h], r) for r in range(1, inner)]
 
-    first_block = jnp.where(z == 0, 3, 0)
-    second_block = jnp.where(z == 0, 2, jnp.where(z == 1, 3, jnp.where(z == 2, 0, 1)))
-
-    def block_rows(block, h, dtype=F32):
-        pick = jnp.asarray(block, jnp.int32).reshape(1)
-        return weight_rows(pick, cots, [gateds[h]] + got[h], dtype)
-
-    def last_rows(h):
-        return block_rows(jnp.minimum(z + 1, 3), h), block_rows(jnp.maximum(z - 1, 0), h)
+    even = z % 2 == 0
+    first_pick = jnp.where(even, 3, 0).astype(jnp.int32).reshape(1)
+    rest_pick = jnp.stack(
+        [
+            jnp.where(z == 0, 2, jnp.where(z == 1, 3, jnp.where(z == 2, 0, 1))),
+            jnp.where(even, 1, 2),
+            z,
+        ]
+    ).astype(jnp.int32)
+
+    def rows_of(order, h):
+        return weight_rows(order, cots, [gateds[h]] + got[h])
 
     def send_first(x):
         return along_line(x, [(0, 1), (3, 2)])
 
-    def send_second(rows_here, came):
-        x = (rows_here + came.astype(F32)).astype(BF16)
+    def send_second(h, came):
+        x = (rest[h][0].astype(F32) + came.astype(F32)).astype(BF16)
         return along_line(x, [(0, 1), (3, 2)]), along_line(x, [(1, 2), (2, 1)])
 
-    def send_third(rows_here, outer_in, inner_in):
-        up, down = rows_here
+    def send_third(h, outer_in, inner_in):
+        mine, other = rest[h][1].astype(F32), first[h].astype(F32)
         outer_in, inner_in = outer_in.astype(F32), inner_in.astype(F32)
-        up = (up + jnp.where(z == 1, outer_in, inner_in)).astype(BF16)
-        down = (down + jnp.where(z == 1, inner_in, outer_in)).astype(BF16)
-        return along_line(up, up_pairs), along_line(down, down_pairs)
+        up = jnp.where(z == 2, other, mine) + jnp.where(z == 1, outer_in, inner_in)
+        down = jnp.where(z == 1, other, mine) + jnp.where(z == 1, inner_in, outer_in)
+        return along_line(up.astype(BF16), up_pairs), along_line(down.astype(BF16), down_pairs)
 
     def last_sum(h):
         below, above = sums[h]
-        return (finals[h] + below.astype(F32) + above.astype(F32)).astype(BF16)
-
-    def shares(h, weights):
-        return [gate_grad(order, cots[r], weights, BF16) for r in range(1, inner)]
+        return (rest[h][2].astype(F32) + below.astype(F32) + above.astype(F32)).astype(BF16)
+
+    def shares(h):
+        return [gate_grad(pick, cots[r], weights(h)) for r in range(1, inner)]
 
     def send_shares(parts):
         return [around_inner(part, inner - r) for r, part in enumerate(parts, 1)]
 
     up1, down1, gateds, mixeds, got = ([None] * chunks for _ in range(5))
     second, third, sums, parts, others, owns = ([None] * chunks for _ in range(6))
+    first, rest = ([None] * chunks for _ in range(2))
     later_halves = list(each[1:])
 
-    prior = send(
-        product_of(keys[rows - FILT :], values[rows - FILT :]), [(i, i + 1) for i in range(seq - 1)]
-    )
+    priors = []
+    for h in each:
+        tail = (slice(rows - FILT, rows), slice(h * cols, (h + 1) * cols))
+        priors.append(product_of(keys[tail], values[tail]))
+    cot_here = after(grad_out, *priors)
+    next_pairs = [(i, i + 1) for i in range(seq - 1)]
+    priors[0] = send(priors[0], next_pairs)
     paired = inner == 2 and ch == LINE
-    other = grad_out
+    other = cot_here
     cots = []
     if paired:
-        kept = lax.dynamic_slice(grad_out, (0, y * depth), (rows, depth))
-        other = lax.dynamic_slice(grad_out, (0, (1 - y) * depth), (rows, depth))
+        kept = lax.dynamic_slice(cot_here, (0, y * depth), (rows, depth))
+        other = lax.dynamic_slice(cot_here, (0, (1 - y) * depth), (rows, depth))
         cots = [lax.all_gather(kept, "ch", axis=0, tiled=False)]
     back, ahead = tables(filters)
     halves = [out_weight[:, h * cols : (h + 1) * cols] for h in each]
-    prior, other, halves = fence(prior, other, halves)
+    priors, other, halves = fence(priors, other, halves)
+    for h in later_halves:
+        priors[h] = send(priors[h], next_pairs)
 
     up1[0], down1[0] = along_line(halves[0], up_pairs), along_line(halves[0], down_pairs)
     swapped = around_inner(other, 1) if paired else other
-    for h in later_halves:
-        held = after(halves[h], back)
-        up1[h], down1[h] = along_line(held, up_pairs), along_line(held, down_pairs)
-    gateds[0], mixeds[0] = forward(queries, keys, values, prior, back, 0, chunks)
-    up1[0], down1[0], swapped, gateds, cots, prior = fence(
-        up1[0], down1[0], swapped, gateds, cots, prior
+    gateds[0], mixeds[0] = forward(queries, keys, values, priors[0], back, 0, chunks)
+    up1[0], down1[0], swapped, gateds, cots, priors = fence(
+        up1[0], down1[0], swapped, gateds, cots, priors
     )
 
+    for h in later_halves:
+        up1[h], down1[h] = along_line(halves[h], up_pairs), along_line(halves[h], down_pairs)
     second[0] = second_step(0)
     if paired:
         cots.append(lax.all_gather(swapped, "ch", axis=0, tiled=False))
@@ -413,7 +427,7 @@
             cots.append(part if shift == 0 else around_inner(part, shift))
     got[0] = swap_gated(0)
     for h in later_halves:
-        gateds[h], mixeds[h] = forward(queries, keys, values, prior, back, h, chunks)
+        gateds[h], mixeds[h] = forward(queries, keys, values, priors[h], back, h, chunks)
     up1, down1, gateds = fence(up1, down1, gateds)
 
     for h in later_halves:
@@ -424,60 +438,55 @@
     third[0] = third_step(second[0])
     for h in later_halves:
         got[h] = swap_gated(h)
-    sums[0] = send_first(block_rows(first_block, 0, BF16))
-    mids, lasts, finals = ([None] * chunks for _ in range(3))
-    mids[0] = block_rows(second_block, 0)
-    second, mids[0] = fence(second, mids[0])
+    first[0] = rows_of(first_pick, 0)[0]
+    sums[0] = send_first(first[0])
+    rest[0] = rows_of(rest_pick, 0)
+    second, rest[0] = fence(second, rest[0])
 
     for h in later_halves:
         second[h] = merge(second[h])
         third[h] = third_step(second[h])
-    sums[0] = send_second(mids[0], sums[0])
-    lasts[0] = last_rows(0)
-    third[0], lasts[0] = fence(third[0], lasts[0])
-
-    weights = slots(0)
-    parts[0] = shares(0, weights)
+    sums[0] = send_second(0, sums[0])
+    third[0], second = fence(third[0], second)
+
+    parts[0] = shares(0)
     parts[0], got[1:] = fence(parts[0], got[1:])
     others[0] = send_shares(parts[0])
 
     for h in later_halves:
-        sums[h] = send_first(block_rows(first_block, h, BF16))
-    sums[0] = send_third(lasts[0], *sums[0])
-    owns[0] = gate_grad(order, cots[0], weights, F32)
-    for h in later_halves:
-        mids[h] = block_rows(second_block, h)
-    third, owns[0], mids = fence(third, owns[0], mids)
-
-    for h in later_halves:
-        weights = slots(h)
-        parts[h] = shares(h, weights)
-        owns[h] = gate_grad(order, cots[0], weights, F32)
+        first[h] = rows_of(first_pick, h)[0]
+        sums[h] = send_first(first[h])
+    sums[0] = send_third(0, *sums[0])
+    for h in later_halves:
+        rest[h] = rows_of(rest_pick, h)
+    third, rest[1:] = fence(third, rest[1:])
+
+    for h in later_halves:
+        parts[h] = shares(h)
     parts[1:], sums = fence(parts[1:], sums)
     for h in later_halves:
         others[h] = send_shares(parts[h])
-        sums[h] = send_second(mids[h], sums[h])
-        lasts[h] = last_rows(h)
-    finals = [block_rows(z, h) for h in each]
-    lasts, finals, others[0], owns = fence(lasts, finals, others[0], owns)
+        sums[h] = send_second(h, sums[h])
+    owns = [gate_grad(pick, cots[0], weights(h)) for h in each]
+    others[0], owns = fence(others[0], owns)
 
     grad_queries = None
     grad_kv = None
     taps = [None] * chunks
     for h in each:
-        grad_queries, gm, taps[h] = middle(
-            owns[h], others[h], queries, keys, values, mixeds[h], prior, grad_queries, h, chunks
+        grad_queries, gm, edge, taps[h] = middle(
+            owns[h], others[h], queries, keys, values, mixeds[h], priors[h], grad_queries, h, chunks
         )
-        later = send(gm[:FILT], [(i + 1, i) for i in range(seq - 1)])
+        later = send(edge, [(i + 1, i) for i in range(seq - 1)])
         if h == 0:
             for g in later_halves:
-                sums[g] = send_third(lasts[g], *after(sums[g], gm))
+                sums[g] = send_third(g, *after(sums[g], later))
         grad_kv = backward(gm, later, keys, values, ahead, grad_kv, h, chunks)
         if h == 0:
             done = [last_sum(0)]
             grad_kv, others, owns, done = fence(grad_kv, others, owns, done)
     for h in later_halves:
-        sums[h], _ = fence(sums[h], gm)
+        sums[h], _ = fence(sums[h], edge)
         done.append(last_sum(h))
     grad_weight = jnp.concatenate(done, axis=1)
     taps = jnp.concatenate(taps, axis=0)[:, 1 : FILT + 1][:, ::-1]

time: 360 us -> 348 us (0.967)
  Pallas kernels: 157 us -> 145 us
    pallas_call x10 -> x4, Pallas kernels: 47 us -> 31.7 us  [weight_rows(): pl.pallas_call(functools.partial(rows_kernel, n), grid_spec=pltpu.Prefetc...]
    ppermute x28 -> x29, waiting for transfers between devices: 54 us -> 50.1 us  [send(): return lax.ppermute(x, 'seq', pairs)]
    convert_element_type x6, other arithmetic: 15 us -> 18.8 us  [the longest x2 8.55 us: send_third(): down.astype(BF16)]
    ppermute x28 -> x29, starting transfers between devices: 82.9 us -> 84.3 us  [send(): return lax.ppermute(x, 'seq', pairs)]
    unnamed x44 -> x34, local copies, waits for them, and re-layouts: 9.57 us -> 10.2 us
  transfers between devices with their start and end apart: 31 -> 32, of which waited for: 8 -> 9; matrix products, arithmetic and copies ran while one was open for 8% -> 8% of each run, Pallas kernels for 41% -> 39%
where the time goes in v5:
time: 348 us; the launch traced here: 343 us
  Pallas kernels  145 us (42%)
  starting transfers between devices  90.1 us (26%)
  waiting for transfers between devices  51.9 us (15%)
  other arithmetic  26.2 us (8%)
  local copies, waits for them, and re-layouts  15.9 us (5%)
  between operations  14.6 us (4%)
    ppermute x29, starting transfers between devices, send(): return lax.ppermute(x, 'seq', pairs)  84.3 us
    ppermute x29, waiting for transfers between devices, send(): return lax.ppermute(x, 'seq', pairs)  50.1 us
    pallas_call x4, Pallas kernels, gate_grad(): pl.pallas_call(gate_kernel, grid_spec=pltpu.PrefetchScalarGridSpec(num_sc...  36.6 us
    pallas_call x4, Pallas kernels, weight_rows(): pl.pallas_call(functools.partial(rows_kernel, n), grid_spec=pltpu.Prefetc...  31.7 us
    pallas_call x2, Pallas kernels, middle(): pl.pallas_call(kernel, grid=(tiles,), in_specs=in_specs, out_specs=[here,...  25.2 us
    pallas_call x2, Pallas kernels, backward(): pl.pallas_call(backward_kernel, grid=(tiles,), in_specs=in_specs, out_spe...  21 us
    pallas_call x2, Pallas kernels, forward(): pl.pallas_call(forward_kernel, grid=(tiles,), in_specs=[here, here, here,...  19.9 us
    pallas_call x1, Pallas kernels, tables(): pl.pallas_call(table_kernel, grid=(groups // GPT,), in_specs=[seed, seed]...  10.4 us
  transfers between devices with their start and end apart: 32, of which 9 were waited for; matrix products, arithmetic and copies ran while one was open for 8% of the time, Pallas kernels for 39%

profile of v5, /device:TPU:10, one launch (start us, length us, event | category | flops | bytes accessed | tf_op | source)
XLA Modules:
  0.0 343.5 jit_solution(7550064147211756745)
XLA Ops:
  7.2 2.1 multiply_convert_fusion
  9.3 3.0 constant_dynamic-slice_fusion
  12.4 3.4 collective-permute-start
  15.8 1.7 fusion.14
  17.6 5.7 %collective-permute-done.prior.refs_5_ = bf16[128,1024]{1,0:T(8,128)(2,1)S(1)} collective-permute-done((bf16[128,1024]{1,0:T(8,128)(2,1)S(1)}, bf16[128,1024]{1,0:T(8,128)(2,1)S(1)}, u32[]{:S(2)}, u32[]{:S(2)}) %collective-permute-start) | collective-permute-done | bytes 262176 | tf_op jit(solution)/shard_map/ppermute | solution.py:309
  24.6 2.3 collective-permute-start.2
  26.9 3.5 %collective-permute-start.1 = (bf16[512,1024]{1,0:T(8,128)(2,1)S(1)}, bf16[512,1024]{1,0:T(8,128)(2,1)}, u32[]{:S(2)}, u32[]{:S(2)}) collective-permute-start(bf16[512,1024]{1,0:T(8,128)(2,1)S(1)} %get-tuple-element.78.refs_4_), channel_id=1, source_target_pairs={{0,8},{4,12},{8,16},{12,20},{16,24},{20,28},{1,9},{5,13},{9,17},{1... | collective-permute-start | bytes 3145736 | tf_op jit(solution)/shard_map/ppermute | solution.py:309
  30.4 3.3 collective-permute-start.4
  34.0 10.4 %shard_map.101 = (bf16[16384,256]{1,0:T(8,128)(2,1)}, bf16[16384,256]{1,0:T(8,128)(2,1)}) custom-call(f32[128,256]{1,0:T(8,128)S(1)} %maximum_maximum_fusion.back_ref, f32[128,256]{1,0:T(8,128)S(1)} %concatenate.13.ahead_ref), custom_call_target="tpu_custom_call" | custom-call | flops 524288 | bytes 262144 | tf_op jit(solution)/shard_map/pallas_call | solution.py:54
  45.4 9.9 %shard_map.102 = (bf16[1024,1024]{1,0:T(8,128)(2,1)S(1)}, bf16[1024,1024]{1,0:T(8,128)(2,1)S(1)}) custom-call(bf16[1024,2048]{1,0:T(8,128)(2,1)} %refs_1_.3, bf16[1024,2048]{1,0:T(8,128)(2,1)} %k.7, bf16[1024,2048]{1,0:T(8,128)(2,1)} %v.7, bf16[128,1024]{1,0:T(8,128)(2,1)S(1)} %copy-done.12, bf16[16384,256]{1,0:T(8,128)(2,1)} %get-tuple-element.81.table), custom_call_target="tpu_custom_call" | custom-call | flops 67108864 | bytes 229376 | tf_op jit(solution)/shard_map/pallas_call | solution.py:104
  55.3 1.3 copy-done.2
  56.6 1.3 copy-done.9
  59.8 2.3 collective-permute-start.9
  62.1 3.6 %collective-permute-start.8 = (bf16[512,1024]{1,0:T(8,128)(2,1)S(1)}, bf16[512,1024]{1,0:T(8,128)(2,1)}, u32[]{:S(2)}, u32[]{:S(2)}) collective-permute-start(bf16[512,1024]{1,0:T(8,128)(2,1)S(1)} %get-tuple-element.87.refs_4_), channel_id=1, source_target_pairs={{0,8},{4,12},{8,16},{12,20},{16,24},{20,28},{1,9},{5,13},{9,17},{1... | collective-permute-start | bytes 3145736 | tf_op jit(solution)/shard_map/ppermute | solution.py:309
  65.7 4.6 %collective-permute-start.5 = (bf16[512,1024]{1,0:T(8,128)(2,1)}, bf16[512,1024]{1,0:T(8,128)(2,1)}, u32[]{:S(2)}, u32[]{:S(2)}) collective-permute-start(bf16[512,1024]{1,0:T(8,128)(2,1)} %collective-permute-done.1.refs_5_), channel_id=1, source_target_pairs={{8,16},{12,20},{16,24},{20,28},{9,17},{13,21},{17,25},{21,29},{10,... | collective-permute-start | bytes 3145736 | tf_op jit(solution)/shard_map/ppermute | solution.py:309
  70.2 1.9 collective-permute-start.6
  72.2 10.0 %shard_map.103 = (bf16[1024,1024]{1,0:T(8,128)(2,1)S(1)}, bf16[1024,1024]{1,0:T(8,128)(2,1)S(1)}) custom-call(bf16[1024,2048]{1,0:T(8,128)(2,1)} %refs_1_.3, bf16[1024,2048]{1,0:T(8,128)(2,1)} %k.7, bf16[1024,2048]{1,0:T(8,128)(2,1)} %v.7, bf16[128,1024]{1,0:T(8,128)(2,1)S(1)} %collective-permute-done.4.prior.refs_5_, bf16[16384,256]{1,0:T(8,128)(2,1)} %get-tuple-element.81.table), custom_call_target="tpu_custom_call" | custom-call | flops 67108864 | bytes 229376 | tf_op jit(solution)/shard_map/pallas_call | solution.py:104
  82.2 1.3 copy-done
  83.5 1.4 copy-done.10
  84.8 3.1 collective-permute-done.9.refs_6_
  87.9 1.4 collective-permute-done.8.refs_5_
  89.3 5.5 %collective-permute-start.11 = (bf16[512,1024]{1,0:T(8,128)(2,1)}, bf16[512,1024]{1,0:T(8,128)(2,1)}, u32[]{:S(2)}, u32[]{:S(2)}) collective-permute-start(bf16[512,1024]{1,0:T(8,128)(2,1)} %collective-permute-done.8.refs_5_), channel_id=1, source_target_pairs={{8,16},{12,20},{16,24},{20,28},{9,17},{13,21},{17,25},{21,29},{10,... | collective-permute-start | bytes 3145736 | tf_op jit(solution)/shard_map/ppermute | solution.py:309
  94.7 1.9 collective-permute-start.12
  96.6 15.2 %collective-permute-done.5 = bf16[512,1024]{1,0:T(8,128)(2,1)} collective-permute-done((bf16[512,1024]{1,0:T(8,128)(2,1)}, bf16[512,1024]{1,0:T(8,128)(2,1)}, u32[]{:S(2)}, u32[]{:S(2)}) %collective-permute-start.5) | collective-permute-done | bytes 1048608 | tf_op jit(solution)/shard_map/ppermute | solution.py:309
  111.9 1.6 copy-done.3
  113.4 5.3 %shard_map.112 = bf16[1,512,1024]{2,1,0:T(8,128)(2,1)} custom-call(s32[1]{0:T(128)} %bitcast.10.pick, bf16[4,1024,512]{2,1,0:T(8,128)(2,1)} %bitcast.42, bf16[4,1024,512]{2,1,0:T(8,128)(2,1)} %bitcast.54, bf16[1024,1024]{1,0:T(8,128)(2,1)S(1)} %copy-done.3, bf16[1024,1024]{1,0:T(8,128)(2,1)} %collective-permute-done.7.refs_3_), custom_call_target="tpu_custom_call" | custom-call | flops 33554432 | bytes 98304 | tf_op jit(solution)/shard_map/pallas_call | solution.py:285
  121.1 1.5 broadcast_select_fusion.1.refs_7_
  122.6 6.4 %collective-permute-start.10 = (bf16[512,1024]{1,0:T(8,128)(2,1)S(1)}, bf16[512,1024]{1,0:T(8,128)(2,1)}, u32[]{:S(2)}, u32[]{:S(2)}) collective-permute-start(bf16[512,1024]{1,0:T(8,128)(2,1)S(1)} %broadcast_select_fusion.1.refs_7_), channel_id=1, source_target_pairs={{16,24},{20,28},{8,0},{12,4},{17,25},{21,29},{9,1},{13,5},{18,26},... | collective-permute-start | bytes 3145736 | tf_op jit(solution)/shard_map/ppermute | solution.py:309
  129.0 10.9 %shard_map.104 = bf16[3,512,1024]{2,1,0:T(8,128)(2,1)} custom-call(s32[3]{0:T(128)S(1)} %pad_add_fusion.pick, bf16[4,1024,512]{2,1,0:T(8,128)(2,1)} %bitcast.43, bf16[4,1024,512]{2,1,0:T(8,128)(2,1)} %bitcast.55, bf16[1024,1024]{1,0:T(8,128)(2,1)S(1)} %copy-done.4, bf16[1024,1024]{1,0:T(8,128)(2,1)} %collective-permute-done.7.refs_3_), custom_call_target="tpu_custom_call" | custom-call | flops 33554432 | bytes 98304 | tf_op jit(solution)/shard_map/pallas_call | solution.py:285
  140.0 2.9 fusion.13
  142.9 4.6 %collective-permute-start.19 = (bf16[512,1024]{1,0:T(8,128)(2,1)}, bf16[512,1024]{1,0:T(8,128)(2,1)}, u32[]{:S(2)}, u32[]{:S(2)}) collective-permute-start(bf16[512,1024]{1,0:T(8,128)(2,1)} %fusion.13), channel_id=1, source_target_pairs={{8,16},{12,20},{16,8},{20,12},{9,17},{13,21},{17,9},{21,13},{10,18... | collective-permute-start | bytes 3145736 | tf_op jit(solution)/shard_map/ppermute | solution.py:309
  148.9 1.4 broadcast_select_fusion.refs_7_
  150.4 5.8 %collective-permute-start.15 = (bf16[512,1024]{1,0:T(8,128)(2,1)S(1)}, bf16[512,1024]{1,0:T(8,128)(2,1)S(1)}, u32[]{:S(2)}, u32[]{:S(2)}) collective-permute-start(bf16[512,1024]{1,0:T(8,128)(2,1)S(1)} %broadcast_select_fusion.refs_7_), channel_id=1, source_target_pairs={{16,24},{20,28},{8,0},{12,4},{17,25},{21,29},{9,1},{13,5},{18,26},... | collective-permute-start | bytes 3145736 | tf_op jit(solution)/shard_map/ppermute | solution.py:309
  156.2 9.1 %shard_map.105 = bf16[1024,1024]{1,0:T(8,128)(2,1)} custom-call(s32[6]{0:T(128)S(1)} %stack.37.pick, bf16[4,1024,512]{2,1,0:T(8,128)(2,1)} %bitcast.56, bf16[4,1024,512]{2,1,0:T(8,128)(2,1)} %bitcast.57, bf16[4,1024,512]{2,1,0:T(8,128)(2,1)} %bitcast.58, bf16[4,1024,512]{2,1,0:T(8,128)(2,1)} %bitcast.59, bf16[512,1024]{1,0:T(8,128)(2,1)S(1)} %get-tuple-element.78.refs_4_, ...), custom_call_target="tpu_custom_call" | custom-call | flops 67108864 | bytes 163840 | tf_op jit(solution)/shard_map/pallas_call | solution.py:249
  165.9 4.3 %fusion.3 = (bf16[512,1024]{1,0:T(8,128)(2,1)}, bf16[512,1024]{1,0:T(8,128)(2,1)}) fusion(bf16[512,1024]{1,0:T(8,128)(2,1)} %collective-permute-done.18, bf16[512,1024]{1,0:T(8,128)(2,1)} %collective-permute-done.19, pred[]{:T(512)S(6)} %eq.15, bf16[3,512,1024]{2,1,0:T(8,128)(2,1)S(1)} %copy-done.14, bf16[1,512,1024]{2,1,0:T(8,128)(2,1)} %shard_map.112, ...), kind=kLoop, calls=%fused_computation.11 | loop fusion | flops 6291456 | bytes 6291458 | tf_op jit(solution)/shard_map/convert_element_type | solution.py:373
  170.2 1.9 collective-permute-start.21
  172.1 3.9 %collective-permute-start.20 = (bf16[512,1024]{1,0:T(8,128)(2,1)}, bf16[512,1024]{1,0:T(8,128)(2,1)}, u32[]{:S(2)}, u32[]{:S(2)}) collective-permute-start(bf16[512,1024]{1,0:T(8,128)(2,1)} %get-tuple-element.154), channel_id=1, source_target_pairs={{0,8},{4,12},{8,16},{12,20},{16,24},{20,28},{1,9},{5,13},{9,17},{1... | collective-permute-start | bytes 3145736 | tf_op jit(solution)/shard_map/ppermute | solution.py:309
  176.1 4.6 %shard_map.113 = bf16[1,512,1024]{2,1,0:T(8,128)(2,1)S(1)} custom-call(s32[1]{0:T(128)} %bitcast.10.pick, bf16[4,1024,512]{2,1,0:T(8,128)(2,1)} %bitcast.44, bf16[4,1024,512]{2,1,0:T(8,128)(2,1)} %bitcast.60, bf16[1024,1024]{1,0:T(8,128)(2,1)S(1)} %copy-done.1, bf16[1024,1024]{1,0:T(8,128)(2,1)} %collective-permute-done.13.refs_3_), custom_call_target="tpu_custom_call" | custom-call | flops 33554432 | bytes 98304 | tf_op jit(solution)/shard_map/pallas_call | solution.py:285
  180.7 1.5 collective-permute-start.22
  182.2 1.7 collective-permute-start.14
  183.8 10.9 %shard_map.106 = bf16[3,512,1024]{2,1,0:T(8,128)(2,1)} custom-call(s32[3]{0:T(128)S(1)} %pad_add_fusion.pick, bf16[4,1024,512]{2,1,0:T(8,128)(2,1)} %bitcast.45, bf16[4,1024,512]{2,1,0:T(8,128)(2,1)} %bitcast.61, bf16[1024,1024]{1,0:T(8,128)(2,1)S(1)} %copy-done.1, bf16[1024,1024]{1,0:T(8,128)(2,1)} %collective-permute-done.13.refs_3_), custom_call_target="tpu_custom_call" | custom-call | flops 33554432 | bytes 98304 | tf_op jit(solution)/shard_map/pallas_call | solution.py:285
  194.8 9.2 %shard_map.111 = bf16[1024,1024]{1,0:T(8,128)(2,1)} custom-call(s32[6]{0:T(128)S(1)} %stack.37.pick, bf16[4,1024,512]{2,1,0:T(8,128)(2,1)} %bitcast.62, bf16[4,1024,512]{2,1,0:T(8,128)(2,1)} %bitcast.63, bf16[4,1024,512]{2,1,0:T(8,128)(2,1)} %bitcast.64, bf16[4,1024,512]{2,1,0:T(8,128)(2,1)} %bitcast.65, bf16[512,1024]{1,0:T(8,128)(2,1)S(1)} %get-tuple-element.87.refs_4_, ...), custom_call_target="tpu_custom_call" | custom-call | flops 67108864 | bytes 163840 | tf_op jit(solution)/shard_map/pallas_call | solution.py:249
  203.9 9.7 %collective-permute-done.22 = bf16[512,1024]{1,0:T(8,128)(2,1)S(1)} collective-permute-done((bf16[512,1024]{1,0:T(8,128)(2,1)S(1)}, bf16[512,1024]{1,0:T(8,128)(2,1)S(1)}, u32[]{:S(2)}, u32[]{:S(2)}) %collective-permute-start.22) | collective-permute-done | bytes 1048608 | tf_op jit(solution)/shard_map/ppermute | solution.py:309
  213.6 1.6 fusion.8
  215.3 2.4 collective-permute-start.26
  219.0 1.5 collective-permute-start.23
  220.5 9.2 %shard_map.108.own_ref = bf16[1024,1024]{1,0:T(8,128)(2,1)} custom-call(s32[6]{0:T(128)S(1)} %stack.37.pick, bf16[4,1024,512]{2,1,0:T(8,128)(2,1)} %bitcast.46, bf16[4,1024,512]{2,1,0:T(8,128)(2,1)} %bitcast.47, bf16[4,1024,512]{2,1,0:T(8,128)(2,1)} %bitcast.48, bf16[4,1024,512]{2,1,0:T(8,128)(2,1)} %bitcast.49, ...), custom_call_target="tpu_custom_call" | custom-call | flops 67108864 | bytes 163840 | tf_op jit(solution)/shard_map/pallas_call | solution.py:249
  229.7 9.1 %shard_map.107.own_ref = bf16[1024,1024]{1,0:T(8,128)(2,1)} custom-call(s32[6]{0:T(128)S(1)} %stack.37.pick, bf16[4,1024,512]{2,1,0:T(8,128)(2,1)} %bitcast.50, bf16[4,1024,512]{2,1,0:T(8,128)(2,1)} %bitcast.51, bf16[4,1024,512]{2,1,0:T(8,128)(2,1)} %bitcast.52, bf16[4,1024,512]{2,1,0:T(8,128)(2,1)} %bitcast.53, ...), custom_call_target="tpu_custom_call" | custom-call | flops 67108864 | bytes 163840 | tf_op jit(solution)/shard_map/pallas_call | solution.py:249
  238.8 1.6 copy-done.6
  240.4 12.5 %shard_map.109 = (bf16[1024,2048]{1,0:T(8,128)(2,1)}, bf16[1024,1024]{1,0:T(8,128)(2,1)S(1)}, bf16[128,1024]{1,0:T(8,128)(2,1)S(1)}, f32[64,256]{1,0:T(8,128)S(1)}) custom-call(bf16[1024,1024]{1,0:T(8,128)(2,1)S(1)} %copy-done.6, bf16[1024,1024]{1,0:T(8,128)(2,1)} %collective-permute-done.14.refs_0_, bf16[1024,2048]{1,0:T(8,128)(2,1)} %refs_1_.3, ...), custom_call_target="tpu_custom_call" | custom-call | flops 67108864 | bytes 294912 | tf_op jit(solution)/shard_map/pallas_call | solution.py:170
  252.9 5.5 %collective-permute-start.16 = (bf16[128,1024]{1,0:T(8,128)(2,1)S(1)}, bf16[128,1024]{1,0:T(8,128)(2,1)S(1)}, u32[]{:S(2)}, u32[]{:S(2)}) collective-permute-start(bf16[128,1024]{1,0:T(8,128)(2,1)S(1)} %get-tuple-element.120), channel_id=1, source_target_pairs={{4,0},{8,4},{12,8},{16,12},{20,16},{24,20},{28,24},{5,1},{9,5},{13... | collective-permute-start | bytes 786440 | tf_op jit(solution)/shard_map/ppermute | solution.py:309
  258.4 13.9 %collective-permute-done.16.later = bf16[128,1024]{1,0:T(8,128)(2,1)S(1)} collective-permute-done((bf16[128,1024]{1,0:T(8,128)(2,1)S(1)}, bf16[128,1024]{1,0:T(8,128)(2,1)S(1)}, u32[]{:S(2)}, u32[]{:S(2)}) %collective-permute-start.16) | collective-permute-done | bytes 262176 | tf_op jit(solution)/shard_map/ppermute | solution.py:309
  272.3 4.3 %fusion.7 = (bf16[512,1024]{1,0:T(8,128)(2,1)}, bf16[512,1024]{1,0:T(8,128)(2,1)}) fusion(bf16[512,1024]{1,0:T(8,128)(2,1)} %collective-permute-done.25, bf16[512,1024]{1,0:T(8,128)(2,1)} %collective-permute-done.26, pred[]{:T(512)S(6)} %eq.15, bf16[3,512,1024]{2,1,0:T(8,128)(2,1)} %shard_map.106, bf16[1,512,1024]{2,1,0:T(8,128)(2,1)S(1)} %shard_map.113, ...), kind=kLoop, calls=%fused_computation.15 | loop fusion | flops 6291456 | bytes 6291458 | tf_op jit(solution)/shard_map/convert_element_type | solution.py:373
  276.6 4.3 %collective-permute-start.28 = (bf16[512,1024]{1,0:T(8,128)(2,1)}, bf16[512,1024]{1,0:T(8,128)(2,1)}, u32[]{:S(2)}, u32[]{:S(2)}) collective-permute-start(bf16[512,1024]{1,0:T(8,128)(2,1)} %get-tuple-element.151), channel_id=1, source_target_pairs={{8,0},{12,4},{16,8},{20,12},{24,16},{28,20},{9,1},{13,5},{17,9},{2... | collective-permute-start | bytes 3145736 | tf_op jit(solution)/shard_map/ppermute | solution.py:309
  280.9 2.5 collective-permute-start.27
  283.4 3.2 fusion.12
  286.5 10.6 %shard_map.110 = (bf16[1024,2048]{1,0:T(8,128)(2,1)}, bf16[1024,2048]{1,0:T(8,128)(2,1)}) custom-call(bf16[1024,1024]{1,0:T(8,128)(2,1)S(1)} %get-tuple-element.119.gm, bf16[128,1024]{1,0:T(8,128)(2,1)S(1)} %collective-permute-done.16.later, bf16[1024,2048]{1,0:T(8,128)(2,1)} %k.7, bf16[1024,2048]{1,0:T(8,128)(2,1)} %v.7, ...), custom_call_target="tpu_custom_call" | custom-call | flops 67108864 | bytes 229376 | tf_op jit(solution)/shard_map/pallas_call | solution.py:215
  297.1 12.6 %shard_map.114 = (bf16[1024,2048]{1,0:T(8,128)(2,1)}, bf16[1024,1024]{1,0:T(8,128)(2,1)S(1)}, bf16[128,1024]{1,0:T(8,128)(2,1)S(1)}, f32[64,256]{1,0:T(8,128)S(1)}) custom-call(bf16[1024,1024]{1,0:T(8,128)(2,1)S(1)} %copy-done.5, bf16[1024,1024]{1,0:T(8,128)(2,1)} %collective-permute-done.23.refs_0_, ...), custom_call_target="tpu_custom_call", output_to_operand_aliasing={{0}: (7, {})} | custom-call | flops 67108864 | bytes 294912 | tf_op jit(solution)/shard_map/pallas_call | solution.py:170
  310.7 5.7 %all-to-all-start = ((f32[8,16,128]{2,1,0:T(8,128)}), f32[8,16,128]{2,1,0:T(8,128)S(1)}, u32[]{:S(2)}, u32[]{:S(2)}) async-start(f32[8,16,128]{2,1,0:T(8,128)} %bitcast.18), calls=%async_computation | async-start | bytes 131072 | tf_op jit(solution)/shard_map/all_to_all | solution.py:494
  316.4 3.4 collective-permute-start.24
  319.8 1.8 all-to-all-done
  322.1 2.6 fusion.10
  324.7 1.5 pad_maximum_fusion
  326.2 10.4 %shard_map.115 = (bf16[1024,2048]{1,0:T(8,128)(2,1)}, bf16[1024,2048]{1,0:T(8,128)(2,1)}) custom-call(bf16[1024,1024]{1,0:T(8,128)(2,1)S(1)} %get-tuple-element.134.gm, bf16[128,1024]{1,0:T(8,128)(2,1)S(1)} %collective-permute-done.24.later, bf16[1024,2048]{1,0:T(8,128)(2,1)} %k.7, ...), custom_call_target="tpu_custom_call", output_to_operand_aliasing={{0}: (5, {}), {1}: (6, {})} | custom-call | flops 67108864 | bytes 229376 | tf_op jit(solution)/shard_map/pallas_call | solution.py:215
  (75 shorter events, 11.7 us)
Async XLA Ops:
  7.2 51.5 %all-gather.5.cloned.1.call-start = ((), (), s32[]{:S(2)}) async-start(), calls=%async_computation.1 | async-start | bytes 5242880 | tf_op jit(solution)/shard_map/all_gather | solution.py:403
  12.3 21.4 %copy-start.16 = (bf16[128,128]{1,0:T(8,128)(2,1)S(1)}, bf16[128,128]{1,0:T(8,128)(2,1)}, u32[]{:S(2)}) copy-start(bf16[128,128]{1,0:T(8,128)(2,1)} %param.9) | copy-start | bytes 98308
  12.3 99.5 %all-gather.7.cloned.1.call-start = ((), (), s32[]{:S(2)}) async-start(), calls=%async_computation.2 | async-start | bytes 5242880 | tf_op jit(solution)/shard_map/all_gather | solution.py:421
  12.4 10.8 %collective-permute-start = (bf16[128,1024]{1,0:T(8,128)(2,1)S(1)}, bf16[128,1024]{1,0:T(8,128)(2,1)S(1)}, u32[]{:S(2)}, u32[]{:S(2)}) collective-permute-start(bf16[128,1024]{1,0:T(8,128)(2,1)S(1)} %get-tuple-element.150), channel_id=1, source_target_pairs={{0,4},{4,8},{8,12},{12,16},{16,20},{20,24},{24,28},{1,5},{5,9},{9,... | collective-permute-start | bytes 786440 | tf_op jit(solution)/shard_map/ppermute | solution.py:309
  23.2 0.7 copy-start.11
  23.9 34.6 %collective-permute-start.3 = (bf16[1024,512]{1,0:T(8,128)(2,1)}, bf16[1024,512]{1,0:T(8,128)(2,1)}, u32[]{:S(2)}, u32[]{:S(2)}) collective-permute-start(bf16[1024,512]{1,0:T(8,128)(2,1)} %get-tuple-element.79), channel_id=1, source_target_pairs={{0,4},{4,0},{8,12},{12,8},{16,20},{20,16},{24,28},{28,24},{1,5},{5... | collective-permute-start | bytes 3145736 | tf_op jit(solution)/shard_map/ppermute | solution.py:309
  24.6 34.0 %collective-permute-start.2 = (bf16[512,1024]{1,0:T(8,128)(2,1)S(1)}, bf16[512,1024]{1,0:T(8,128)(2,1)S(1)}, u32[]{:S(2)}, u32[]{:S(2)}) collective-permute-start(bf16[512,1024]{1,0:T(8,128)(2,1)S(1)} %get-tuple-element.78.refs_4_), channel_id=1, source_target_pairs={{8,0},{12,4},{16,8},{20,12},{24,16},{28,20},{9,1},{13,5},{17,9},{2... | collective-permute-start | bytes 3145736 | tf_op jit(solution)/shard_map/ppermute | solution.py:309
  26.9 31.7 %collective-permute-start.1 = (bf16[512,1024]{1,0:T(8,128)(2,1)S(1)}, bf16[512,1024]{1,0:T(8,128)(2,1)}, u32[]{:S(2)}, u32[]{:S(2)}) collective-permute-start(bf16[512,1024]{1,0:T(8,128)(2,1)S(1)} %get-tuple-element.78.refs_4_), channel_id=1, source_target_pairs={{0,8},{4,12},{8,16},{12,20},{16,24},{20,28},{1,9},{5,13},{9,17},{1... | collective-permute-start | bytes 3145736 | tf_op jit(solution)/shard_map/ppermute | solution.py:309
  30.4 28.2 %collective-permute-start.4 = (bf16[128,1024]{1,0:T(8,128)(2,1)}, bf16[128,1024]{1,0:T(8,128)(2,1)S(1)}, u32[]{:S(2)}, u32[]{:S(2)}) collective-permute-start(bf16[128,1024]{1,0:T(8,128)(2,1)} %get-tuple-element.83), channel_id=1, source_target_pairs={{0,4},{4,8},{8,12},{12,16},{16,20},{20,24},{24,28},{1,5},{5,9},{9,... | collective-permute-start | bytes 786440 | tf_op jit(solution)/shard_map/ppermute | solution.py:309
  44.5 0.9 copy-start.12
  55.3 1.3 copy-start.2
  56.6 1.3 copy-start.9
  58.6 23.6 %copy-start.7 = (bf16[512,1024]{1,0:T(8,128)(2,1)}, bf16[512,1024]{1,0:T(8,128)(2,1)S(1)}, u32[]{:S(2)}) copy-start(bf16[512,1024]{1,0:T(8,128)(2,1)S(1)} %collective-permute-done.2.refs_6_) | copy-start | bytes 3145732
  58.6 53.2 %collective-permute-start.7 = (bf16[1024,1024]{1,0:T(8,128)(2,1)}, bf16[1024,1024]{1,0:T(8,128)(2,1)}, u32[]{:S(2)}, u32[]{:S(2)}) collective-permute-start(bf16[1024,1024]{1,0:T(8,128)(2,1)} %copy-done.2), channel_id=1, source_target_pairs={{0,4},{4,0},{8,12},{12,8},{16,20},{20,16},{24,28},{28,24},{1,5},{5... | collective-permute-start | bytes 6291464 | tf_op jit(solution)/shard_map/ppermute | solution.py:309
  59.8 28.1 %collective-permute-start.9 = (bf16[512,1024]{1,0:T(8,128)(2,1)S(1)}, bf16[512,1024]{1,0:T(8,128)(2,1)}, u32[]{:S(2)}, u32[]{:S(2)}) collective-permute-start(bf16[512,1024]{1,0:T(8,128)(2,1)S(1)} %get-tuple-element.87.refs_4_), channel_id=1, source_target_pairs={{8,0},{12,4},{16,8},{20,12},{24,16},{28,20},{9,1},{13,5},{17,9},{2... | collective-permute-start | bytes 3145736 | tf_op jit(solution)/shard_map/ppermute | solution.py:309
  62.1 27.2 %collective-permute-start.8 = (bf16[512,1024]{1,0:T(8,128)(2,1)S(1)}, bf16[512,1024]{1,0:T(8,128)(2,1)}, u32[]{:S(2)}, u32[]{:S(2)}) collective-permute-start(bf16[512,1024]{1,0:T(8,128)(2,1)S(1)} %get-tuple-element.87.refs_4_), channel_id=1, source_target_pairs={{0,8},{4,12},{8,16},{12,20},{16,24},{20,28},{1,9},{5,13},{9,17},{1... | collective-permute-start | bytes 3145736 | tf_op jit(solution)/shard_map/ppermute | solution.py:309
  65.7 46.2 %collective-permute-start.5 = (bf16[512,1024]{1,0:T(8,128)(2,1)}, bf16[512,1024]{1,0:T(8,128)(2,1)}, u32[]{:S(2)}, u32[]{:S(2)}) collective-permute-start(bf16[512,1024]{1,0:T(8,128)(2,1)} %collective-permute-done.1.refs_5_), channel_id=1, source_target_pairs={{8,16},{12,20},{16,24},{20,28},{9,17},{13,21},{17,25},{21,29},{10,... | collective-permute-start | bytes 3145736 | tf_op jit(solution)/shard_map/ppermute | solution.py:309
  70.2 41.6 %collective-permute-start.6 = (bf16[512,1024]{1,0:T(8,128)(2,1)S(1)}, bf16[512,1024]{1,0:T(8,128)(2,1)}, u32[]{:S(2)}, u32[]{:S(2)}) collective-permute-start(bf16[512,1024]{1,0:T(8,128)(2,1)S(1)} %collective-permute-done.2.refs_6_), channel_id=1, source_target_pairs={{16,8},{20,12},{8,0},{12,4},{17,9},{21,13},{9,1},{13,5},{18,10},{2... | collective-permute-start | bytes 3145736 | tf_op jit(solution)/shard_map/ppermute | solution.py:309
  82.2 1.3 copy-start
  83.5 1.4 copy-start.10
  89.3 50.7 %collective-permute-start.11 = (bf16[512,1024]{1,0:T(8,128)(2,1)}, bf16[512,1024]{1,0:T(8,128)(2,1)}, u32[]{:S(2)}, u32[]{:S(2)}) collective-permute-start(bf16[512,1024]{1,0:T(8,128)(2,1)} %collective-permute-done.8.refs_5_), channel_id=1, source_target_pairs={{8,16},{12,20},{16,24},{20,28},{9,17},{13,21},{17,25},{21,29},{10,... | collective-permute-start | bytes 3145736 | tf_op jit(solution)/shard_map/ppermute | solution.py:309
  94.7 45.2 %collective-permute-start.12 = (bf16[512,1024]{1,0:T(8,128)(2,1)}, bf16[512,1024]{1,0:T(8,128)(2,1)}, u32[]{:S(2)}, u32[]{:S(2)}) collective-permute-start(bf16[512,1024]{1,0:T(8,128)(2,1)} %collective-permute-done.9.refs_6_), channel_id=1, source_target_pairs={{16,8},{20,12},{8,0},{12,4},{17,9},{21,13},{9,1},{13,5},{18,10},{2... | collective-permute-start | bytes 3145736 | tf_op jit(solution)/shard_map/ppermute | solution.py:309
  111.8 1.6 copy-start.3
  118.7 21.2 %collective-permute-start.17 = (bf16[512,1024]{1,0:T(8,128)(2,1)}, bf16[512,1024]{1,0:T(8,128)(2,1)}, u32[]{:S(2)}, u32[]{:S(2)}) collective-permute-start(bf16[512,1024]{1,0:T(8,128)(2,1)} %bitcast.11), channel_id=1, source_target_pairs={{0,8},{4,12},{24,16},{28,20},{1,9},{5,13},{25,17},{29,21},{2,10},{... | collective-permute-start | bytes 3145736 | tf_op jit(solution)/shard_map/ppermute | solution.py:309
  120.0 56.0 %collective-permute-start.13 = (bf16[1024,1024]{1,0:T(8,128)(2,1)}, bf16[1024,1024]{1,0:T(8,128)(2,1)}, u32[]{:S(2)}, u32[]{:S(2)}) collective-permute-start(bf16[1024,1024]{1,0:T(8,128)(2,1)} %copy-done), channel_id=1, source_target_pairs={{0,4},{4,0},{8,12},{12,8},{16,20},{20,16},{24,28},{28,24},{1,5},{5... | collective-permute-start | bytes 6291464 | tf_op jit(solution)/shard_map/ppermute | solution.py:309
  121.1 7.9 %copy-start.4 = (bf16[1024,1024]{1,0:T(8,128)(2,1)S(1)}, bf16[1024,1024]{1,0:T(8,128)(2,1)}, u32[]{:S(2)}) copy-start(bf16[1024,1024]{1,0:T(8,128)(2,1)} %copy-done.2) | copy-start | bytes 6291460
  122.6 33.6 %collective-permute-start.10 = (bf16[512,1024]{1,0:T(8,128)(2,1)S(1)}, bf16[512,1024]{1,0:T(8,128)(2,1)}, u32[]{:S(2)}, u32[]{:S(2)}) collective-permute-start(bf16[512,1024]{1,0:T(8,128)(2,1)S(1)} %broadcast_select_fusion.1.refs_7_), channel_id=1, source_target_pairs={{16,24},{20,28},{8,0},{12,4},{17,25},{21,29},{9,1},{13,5},{18,26},... | collective-permute-start | bytes 3145736 | tf_op jit(solution)/shard_map/ppermute | solution.py:309
  142.9 22.5 %collective-permute-start.19 = (bf16[512,1024]{1,0:T(8,128)(2,1)}, bf16[512,1024]{1,0:T(8,128)(2,1)}, u32[]{:S(2)}, u32[]{:S(2)}) collective-permute-start(bf16[512,1024]{1,0:T(8,128)(2,1)} %fusion.13), channel_id=1, source_target_pairs={{8,16},{12,20},{16,8},{20,12},{9,17},{13,21},{17,9},{21,13},{10,18... | collective-permute-start | bytes 3145736 | tf_op jit(solution)/shard_map/ppermute | solution.py:309
  147.5 18.4 %collective-permute-start.18 = (bf16[512,1024]{1,0:T(8,128)(2,1)}, bf16[512,1024]{1,0:T(8,128)(2,1)}, u32[]{:S(2)}, u32[]{:S(2)}) collective-permute-start(bf16[512,1024]{1,0:T(8,128)(2,1)} %fusion.13), channel_id=1, source_target_pairs={{0,8},{4,12},{24,16},{28,20},{1,9},{5,13},{25,17},{29,21},{2,10},{... | collective-permute-start | bytes 3145736 | tf_op jit(solution)/shard_map/ppermute | solution.py:309
  148.9 7.3 %copy-start.8 = (bf16[512,1024]{1,0:T(8,128)(2,1)S(1)}, bf16[512,1024]{1,0:T(8,128)(2,1)}, u32[]{:S(2)}) copy-start(bf16[512,1024]{1,0:T(8,128)(2,1)} %copy-done.7) | copy-start | bytes 3145732
  150.4 15.5 %copy-start.14 = (bf16[3,512,1024]{2,1,0:T(8,128)(2,1)S(1)}, bf16[3,512,1024]{2,1,0:T(8,128)(2,1)}, u32[]{:S(2)}) copy-start(bf16[3,512,1024]{2,1,0:T(8,128)(2,1)} %shard_map.104) | copy-start | bytes 9437188
  150.4 44.4 %collective-permute-start.15 = (bf16[512,1024]{1,0:T(8,128)(2,1)S(1)}, bf16[512,1024]{1,0:T(8,128)(2,1)S(1)}, u32[]{:S(2)}, u32[]{:S(2)}) collective-permute-start(bf16[512,1024]{1,0:T(8,128)(2,1)S(1)} %broadcast_select_fusion.refs_7_), channel_id=1, source_target_pairs={{16,24},{20,28},{8,0},{12,4},{17,25},{21,29},{9,1},{13,5},{18,26},... | collective-permute-start | bytes 3145736 | tf_op jit(solution)/shard_map/ppermute | solution.py:309
  165.4 10.7 %copy-start.1 = (bf16[1024,1024]{1,0:T(8,128)(2,1)S(1)}, bf16[1024,1024]{1,0:T(8,128)(2,1)}, u32[]{:S(2)}) copy-start(bf16[1024,1024]{1,0:T(8,128)(2,1)} %copy-done) | copy-start | bytes 6291460
  170.2 33.7 %collective-permute-start.21 = (bf16[512,1024]{1,0:T(8,128)(2,1)}, bf16[512,1024]{1,0:T(8,128)(2,1)}, u32[]{:S(2)}, u32[]{:S(2)}) collective-permute-start(bf16[512,1024]{1,0:T(8,128)(2,1)} %get-tuple-element.153), channel_id=1, source_target_pairs={{8,0},{12,4},{16,8},{20,12},{24,16},{28,20},{9,1},{13,5},{17,9},{2... | collective-permute-start | bytes 3145736 | tf_op jit(solution)/shard_map/ppermute | solution.py:309
  172.1 31.8 %collective-permute-start.20 = (bf16[512,1024]{1,0:T(8,128)(2,1)}, bf16[512,1024]{1,0:T(8,128)(2,1)}, u32[]{:S(2)}, u32[]{:S(2)}) collective-permute-start(bf16[512,1024]{1,0:T(8,128)(2,1)} %get-tuple-element.154), channel_id=1, source_target_pairs={{0,8},{4,12},{8,16},{12,20},{16,24},{20,28},{1,9},{5,13},{9,17},{1... | collective-permute-start | bytes 3145736 | tf_op jit(solution)/shard_map/ppermute | solution.py:309
  180.7 33.0 %collective-permute-start.22 = (bf16[512,1024]{1,0:T(8,128)(2,1)S(1)}, bf16[512,1024]{1,0:T(8,128)(2,1)S(1)}, u32[]{:S(2)}, u32[]{:S(2)}) collective-permute-start(bf16[512,1024]{1,0:T(8,128)(2,1)S(1)} %bitcast.41), channel_id=1, source_target_pairs={{0,8},{4,12},{24,16},{28,20},{1,9},{5,13},{25,17},{29,21},{2,10},{... | collective-permute-start | bytes 3145736 | tf_op jit(solution)/shard_map/ppermute | solution.py:309
  182.2 56.6 %collective-permute-start.14 = (bf16[1024,1024]{1,0:T(8,128)(2,1)}, bf16[1024,1024]{1,0:T(8,128)(2,1)}, u32[]{:S(2)}, u32[]{:S(2)}) collective-permute-start(bf16[1024,1024]{1,0:T(8,128)(2,1)} %shard_map.105), channel_id=1, source_target_pairs={{0,4},{4,0},{8,12},{12,8},{16,20},{20,16},{24,28},{28,24},{1,5},{5... | collective-permute-start | bytes 6291464 | tf_op jit(solution)/shard_map/ppermute | solution.py:309
  215.3 43.1 %collective-permute-start.26 = (bf16[512,1024]{1,0:T(8,128)(2,1)S(1)}, bf16[512,1024]{1,0:T(8,128)(2,1)}, u32[]{:S(2)}, u32[]{:S(2)}) collective-permute-start(bf16[512,1024]{1,0:T(8,128)(2,1)S(1)} %fusion.8), channel_id=1, source_target_pairs={{8,16},{12,20},{16,8},{20,12},{9,17},{13,21},{17,9},{21,13},{10,18... | collective-permute-start | bytes 3145736 | tf_op jit(solution)/shard_map/ppermute | solution.py:309
  217.7 40.7 %collective-permute-start.25 = (bf16[512,1024]{1,0:T(8,128)(2,1)S(1)}, bf16[512,1024]{1,0:T(8,128)(2,1)}, u32[]{:S(2)}, u32[]{:S(2)}) collective-permute-start(bf16[512,1024]{1,0:T(8,128)(2,1)S(1)} %fusion.8), channel_id=1, source_target_pairs={{0,8},{4,12},{24,16},{28,20},{1,9},{5,13},{25,17},{29,21},{2,10},{... | collective-permute-start | bytes 3145736 | tf_op jit(solution)/shard_map/ppermute | solution.py:309
  219.0 78.1 %collective-permute-start.23 = (bf16[1024,1024]{1,0:T(8,128)(2,1)}, bf16[1024,1024]{1,0:T(8,128)(2,1)}, u32[]{:S(2)}, u32[]{:S(2)}) collective-permute-start(bf16[1024,1024]{1,0:T(8,128)(2,1)} %shard_map.111), channel_id=1, source_target_pairs={{0,4},{4,0},{8,12},{12,8},{16,20},{20,16},{24,28},{28,24},{1,5},{5... | collective-permute-start | bytes 6291464 | tf_op jit(solution)/shard_map/ppermute | solution.py:309
  229.7 9.1 %copy-start.13 = (bf16[128,1024]{1,0:T(8,128)(2,1)S(1)}, bf16[128,1024]{1,0:T(8,128)(2,1)}, u32[]{:S(2)}) copy-start(bf16[128,1024]{1,0:T(8,128)(2,1)} %copy-done.11) | copy-start | bytes 786436
  238.8 1.6 copy-start.6
  252.9 19.4 %collective-permute-start.16 = (bf16[128,1024]{1,0:T(8,128)(2,1)S(1)}, bf16[128,1024]{1,0:T(8,128)(2,1)S(1)}, u32[]{:S(2)}, u32[]{:S(2)}) collective-permute-start(bf16[128,1024]{1,0:T(8,128)(2,1)S(1)} %get-tuple-element.120), channel_id=1, source_target_pairs={{4,0},{8,4},{12,8},{16,12},{20,16},{24,20},{28,24},{5,1},{9,5},{13... | collective-permute-start | bytes 786440 | tf_op jit(solution)/shard_map/ppermute | solution.py:309
  276.6 45.5 %collective-permute-start.28 = (bf16[512,1024]{1,0:T(8,128)(2,1)}, bf16[512,1024]{1,0:T(8,128)(2,1)}, u32[]{:S(2)}, u32[]{:S(2)}) collective-permute-start(bf16[512,1024]{1,0:T(8,128)(2,1)} %get-tuple-element.151), channel_id=1, source_target_pairs={{8,0},{12,4},{16,8},{20,12},{24,16},{28,20},{9,1},{13,5},{17,9},{2... | collective-permute-start | bytes 3145736 | tf_op jit(solution)/shard_map/ppermute | solution.py:309
  280.9 41.2 %collective-permute-start.27 = (bf16[512,1024]{1,0:T(8,128)(2,1)}, bf16[512,1024]{1,0:T(8,128)(2,1)}, u32[]{:S(2)}, u32[]{:S(2)}) collective-permute-start(bf16[512,1024]{1,0:T(8,128)(2,1)} %get-tuple-element.152), channel_id=1, source_target_pairs={{0,8},{4,12},{8,16},{12,20},{16,24},{20,28},{1,9},{5,13},{9,17},{1... | collective-permute-start | bytes 3145736 | tf_op jit(solution)/shard_map/ppermute | solution.py:309
  286.5 10.6 %copy-start.5 = (bf16[1024,1024]{1,0:T(8,128)(2,1)S(1)}, bf16[1024,1024]{1,0:T(8,128)(2,1)}, u32[]{:S(2)}) copy-start(bf16[1024,1024]{1,0:T(8,128)(2,1)} %shard_map.108.own_ref) | copy-start | bytes 6291460
  310.7 10.8 %all-to-all-start = ((f32[8,16,128]{2,1,0:T(8,128)}), f32[8,16,128]{2,1,0:T(8,128)S(1)}, u32[]{:S(2)}, u32[]{:S(2)}) async-start(f32[8,16,128]{2,1,0:T(8,128)} %bitcast.18), calls=%async_computation | async-start | bytes 131072 | tf_op jit(solution)/shard_map/all_to_all | solution.py:494
  316.4 9.8 %collective-permute-start.24 = (bf16[128,1024]{1,0:T(8,128)(2,1)S(1)}, bf16[128,1024]{1,0:T(8,128)(2,1)S(1)}, u32[]{:S(2)}, u32[]{:S(2)}) collective-permute-start(bf16[128,1024]{1,0:T(8,128)(2,1)S(1)} %get-tuple-element.135), channel_id=1, source_target_pairs={{4,0},{8,4},{12,8},{16,12},{20,16},{24,20},{28,24},{5,1},{9,5},{13... | collective-permute-start | bytes 786440 | tf_op jit(solution)/shard_map/ppermute | solution.py:309
  322.1 2.6 copy-start.15
Sparse Core Ops, SparseCore 0:
  12.5 34.6 all-gather.4
  58.8 33.9 all-gather.6

commit v6 on v5

--- a/solution.py
+++ b/solution.py
@@ -232,9 +232,8 @@
         second[...],
         jnp.where(pick[LINE + 1] == 1, third[...], down[...]),
     )
-    total = jnp.dot(refs[0][0], slots[0], preferred_element_type=F32)
-    for j in range(1, LINE):
-        total = total + jnp.dot(refs[j][0], slots[j], preferred_element_type=F32)
+    cot = jnp.concatenate([ref[0] for ref in refs[:LINE]], axis=1)
+    total = jnp.dot(cot, jnp.concatenate(slots, axis=0), preferred_element_type=F32)
     out[...] = total.astype(out.dtype)
 
 
@@ -265,35 +264,40 @@
 
 def rows_kernel(n, pick, *refs):
     out = refs[-1]
-    total = None
-    for cot, gated in zip(refs[:n], refs[n : 2 * n]):
-        term = lax.dot_general(
-            cot[0], gated[...], (((0,), (0,)), ((), ())), preferred_element_type=F32
-        )
-        total = term if total is None else total + term
+    cot, gated = refs[0][0], refs[n][...]
+    if n > 1:
+        cot = jnp.concatenate([ref[0] for ref in refs[:n]], axis=0)
+        gated = jnp.concatenate([ref[...] for ref in refs[n : 2 * n]], axis=0)
+    total = lax.dot_general(cot, gated, (((0,), (0,)), ((), ())), preferred_element_type=F32)
+    if len(refs) > 2 * n + 1:
+        total = total + refs[2 * n][0]
     out[0] = total.astype(out.dtype)
 
 
-def weight_rows(pick, cots, gateds):
+def weight_rows(pick, cots, gateds, dtype, base=None, skip=0):
     _, rows, depth = cots[0].shape
     width = gateds[0].shape[1]
     blocks = pick.shape[0]
     tile = width if blocks > 1 else min(512, width)
     n = len(cots)
-    cot_spec = pl.BlockSpec((1, rows, depth), lambda j, i, pick: (pick[j], 0, 0))
-    gated_spec = pl.BlockSpec((rows, tile), lambda j, i, pick: (0, i))
+    in_specs = [pl.BlockSpec((1, rows, depth), lambda j, i, pick: (pick[j], 0, 0))] * n
+    in_specs += [pl.BlockSpec((rows, tile), lambda j, i, pick: (0, i))] * n
+    args = [*cots, *gateds]
+    if base is not None:
+        in_specs.append(pl.BlockSpec((1, depth, tile), lambda j, i, pick: (j + skip, 0, i)))
+        args.append(base)
     return pl.pallas_call(
         functools.partial(rows_kernel, n),
         grid_spec=pltpu.PrefetchScalarGridSpec(
             num_scalar_prefetch=1,
             grid=(blocks, width // tile),
-            in_specs=[cot_spec] * n + [gated_spec] * n,
+            in_specs=in_specs,
             out_specs=pl.BlockSpec((1, depth, tile), lambda j, i, pick: (j, 0, i)),
         ),
-        out_shape=jax.ShapeDtypeStruct((blocks, depth, width), BF16),
+        out_shape=jax.ShapeDtypeStruct((blocks, depth, width), dtype),
         compiler_params=params(),
         cost_estimate=cost(2 * n * rows * depth * width, 2 * n * rows * (depth + width)),
-    )(pick, *cots, *gateds)
+    )(pick, *args)
 
 
 def shards(seq, ch, queries, keys, values, filters, grad_out, out_weight):
@@ -355,8 +359,14 @@
         ]
     ).astype(jnp.int32)
 
-    def rows_of(order, h):
-        return weight_rows(order, cots, [gateds[h]] + got[h])
+    def rows_own(h):
+        return weight_rows(jnp.concatenate([first_pick, rest_pick]), cots[:1], [gateds[h]], F32)
+
+    def rows_first(h):
+        return weight_rows(first_pick, cots[1:], got[h], BF16, base[h])[0]
+
+    def rows_rest(h):
+        return weight_rows(rest_pick, cots[1:], got[h], BF16, base[h], 1)
 
     def send_first(x):
         return along_line(x, [(0, 1), (3, 2)])
@@ -403,7 +413,7 @@
         cots = [lax.all_gather(kept, "ch", axis=0, tiled=False)]
     back, ahead = tables(filters)
     halves = [out_weight[:, h * cols : (h + 1) * cols] for h in each]
-    priors, other, halves = fence(priors, other, halves)
+    priors, other, halves, back = fence(priors, other, halves, back)
     for h in later_halves:
         priors[h] = send(priors[h], next_pairs)
 
@@ -428,19 +438,20 @@
     got[0] = swap_gated(0)
     for h in later_halves:
         gateds[h], mixeds[h] = forward(queries, keys, values, priors[h], back, h, chunks)
-    up1, down1, gateds = fence(up1, down1, gateds)
+    up1, down1, gateds, cots[0] = fence(up1, down1, gateds, cots[0])
 
     for h in later_halves:
         second[h] = second_step(h)
-    second[0], got[0], gateds, cots = fence(second[0], got[0], gateds, cots)
+    base = [rows_own(h) for h in each]
+    second[0], got[0], gateds, cots, base = fence(second[0], got[0], gateds, cots, base)
 
     second[0] = merge(second[0])
     third[0] = third_step(second[0])
     for h in later_halves:
         got[h] = swap_gated(h)
-    first[0] = rows_of(first_pick, 0)[0]
+    first[0] = rows_first(0)
     sums[0] = send_first(first[0])
-    rest[0] = rows_of(rest_pick, 0)
+    rest[0] = rows_rest(0)
     second, rest[0] = fence(second, rest[0])
 
     for h in later_halves:
@@ -454,11 +465,11 @@
     others[0] = send_shares(parts[0])
 
     for h in later_halves:
-        first[h] = rows_of(first_pick, h)[0]
+        first[h] = rows_first(h)
         sums[h] = send_first(first[h])
     sums[0] = send_third(0, *sums[0])
     for h in later_halves:
-        rest[h] = rows_of(rest_pick, h)
+        rest[h] = rows_rest(h)
     third, rest[1:] = fence(third, rest[1:])
 
     for h in later_halves:
@@ -472,22 +483,22 @@
 
     grad_queries = None
     grad_kv = None
-    taps = [None] * chunks
+    taps, gms, laters = ([None] * chunks for _ in range(3))
     for h in each:
-        grad_queries, gm, edge, taps[h] = middle(
+        grad_queries, gms[h], edge, taps[h] = middle(
             owns[h], others[h], queries, keys, values, mixeds[h], priors[h], grad_queries, h, chunks
         )
-        later = send(edge, [(i + 1, i) for i in range(seq - 1)])
+        laters[h] = send(edge, [(i + 1, i) for i in range(seq - 1)])
         if h == 0:
             for g in later_halves:
-                sums[g] = send_third(g, *after(sums[g], later))
-        grad_kv = backward(gm, later, keys, values, ahead, grad_kv, h, chunks)
-        if h == 0:
+                sums[g] = send_third(g, *after(sums[g], edge))
             done = [last_sum(0)]
-            grad_kv, others, owns, done = fence(grad_kv, others, owns, done)
-    for h in later_halves:
-        sums[h], _ = fence(sums[h], edge)
+            others, owns, done = fence(others, owns, done)
+    for h in later_halves:
+        sums[h], gms[0], _ = fence(sums[h], gms[0], edge)
         done.append(last_sum(h))
+    for h in each:
+        grad_kv = backward(gms[h], laters[h], keys, values, ahead, grad_kv, h, chunks)
     grad_weight = jnp.concatenate(done, axis=1)
     taps = jnp.concatenate(taps, axis=0)[:, 1 : FILT + 1][:, ::-1]
     taps = taps.T.reshape(seq, FILT // seq, -1)

time: 348 us -> 339 us (0.974)
  waiting for transfers between devices: 51.9 us -> 29.7 us
  Pallas kernels: 145 us -> 156 us
    ppermute x29, waiting for transfers between devices: 50.1 us -> 29.6 us  [send(): return lax.ppermute(x, 'seq', pairs)]
    pallas_call x4 -> x6, Pallas kernels: 31.7 us -> 41.7 us  [weight_rows(): pl.pallas_call(functools.partial(rows_kernel, n), grid_spec=pltpu.Prefetc...]
    unnamed x34 -> x54, local copies, waits for them, and re-layouts: 10.2 us -> 13.3 us
  transfers between devices with their start and end apart: 32 -> 32, of which waited for: 9 -> 6; matrix products, arithmetic and copies ran while one was open for 8% -> 8% of each run, Pallas kernels for 39% -> 43%
where the time goes in v6:
time: 339 us; the launch traced here: 337 us
  Pallas kernels  156 us (46%)
  starting transfers between devices  90.7 us (27%)
  waiting for transfers between devices  29.7 us (9%)
  other arithmetic  27 us (8%)
  local copies, waits for them, and re-layouts  19.2 us (6%)
  between operations  14.8 us (4%)
    ppermute x29, starting transfers between devices, send(): return lax.ppermute(x, 'seq', pairs)  87.3 us
    pallas_call x6, Pallas kernels, weight_rows(): pl.pallas_call(functools.partial(rows_kernel, n), grid_spec=pltpu.Prefetc...  41.7 us
    pallas_call x4, Pallas kernels, gate_grad(): pl.pallas_call(gate_kernel, grid_spec=pltpu.PrefetchScalarGridSpec(num_sc...  36.6 us
    ppermute x29, waiting for transfers between devices, send(): return lax.ppermute(x, 'seq', pairs)  29.6 us
    pallas_call x2, Pallas kernels, middle(): pl.pallas_call(kernel, grid=(tiles,), in_specs=in_specs, out_specs=[here,...  25.7 us
    pallas_call x2, Pallas kernels, backward(): pl.pallas_call(backward_kernel, grid=(tiles,), in_specs=in_specs, out_spe...  20.9 us
    pallas_call x2, Pallas kernels, forward(): pl.pallas_call(forward_kernel, grid=(tiles,), in_specs=[here, here, here,...  20.3 us
    unnamed x54, local copies, waits for them, and re-layouts  13.3 us
  transfers between devices with their start and end apart: 32, of which 6 were waited for; matrix products, arithmetic and copies ran while one was open for 8% of the time, Pallas kernels for 43%

profile of v6, /device:TPU:10, one launch (start us, length us, event | category | flops | bytes accessed | tf_op | source)
XLA Modules:
  0.0 337.0 jit_solution(6182551054175094430)
XLA Ops:
  7.2 2.1 multiply_convert_fusion
  9.3 3.0 constant_dynamic-slice_fusion
  12.4 3.4 %collective-permute-start = (bf16[128,1024]{1,0:T(8,128)(2,1)S(1)}, bf16[128,1024]{1,0:T(8,128)(2,1)S(1)}, u32[]{:S(2)}, u32[]{:S(2)}) collective-permute-start(bf16[128,1024]{1,0:T(8,128)(2,1)S(1)} %get-tuple-element.154), channel_id=1, source_target_pairs={{0,4},{4,8},{8,12},{12,16},{16,20},{20,24},{24,28},{1,5},{5,9},{9,... | collective-permute-start | bytes 786440 | tf_op jit(solution)/shard_map/ppermute | solution.py:313
  16.1 10.4 %shard_map.101 = (bf16[16384,256]{1,0:T(8,128)(2,1)}, bf16[16384,256]{1,0:T(8,128)(2,1)}) custom-call(f32[128,256]{1,0:T(8,128)S(1)} %maximum_maximum_fusion.back_ref, f32[128,256]{1,0:T(8,128)S(1)} %concatenate.19.ahead_ref), custom_call_target="tpu_custom_call" | custom-call | flops 524288 | bytes 262144 | tf_op jit(solution)/shard_map/pallas_call | solution.py:54
  26.6 1.8 fusion.14
  29.1 1.5 collective-permute-start.3
  30.7 2.4 collective-permute-start.2
  33.0 3.5 %collective-permute-start.1 = (bf16[512,1024]{1,0:T(8,128)(2,1)S(1)}, bf16[512,1024]{1,0:T(8,128)(2,1)}, u32[]{:S(2)}, u32[]{:S(2)}) collective-permute-start(bf16[512,1024]{1,0:T(8,128)(2,1)S(1)} %get-tuple-element.81.refs_4_), channel_id=1, source_target_pairs={{0,8},{4,12},{8,16},{12,20},{16,24},{20,28},{1,9},{5,13},{9,17},{1... | collective-permute-start | bytes 3145736 | tf_op jit(solution)/shard_map/ppermute | solution.py:313
  36.5 2.4 collective-permute-start.4
  39.9 9.9 %shard_map.102 = (bf16[1024,1024]{1,0:T(8,128)(2,1)S(1)}, bf16[1024,1024]{1,0:T(8,128)(2,1)S(1)}) custom-call(bf16[1024,2048]{1,0:T(8,128)(2,1)} %refs_1_.3, bf16[1024,2048]{1,0:T(8,128)(2,1)} %k.7, bf16[1024,2048]{1,0:T(8,128)(2,1)} %v.7, bf16[128,1024]{1,0:T(8,128)(2,1)S(1)} %copy-done.20, bf16[16384,256]{1,0:T(8,128)(2,1)} %get-tuple-element.84.table), custom_call_target="tpu_custom_call" | custom-call | flops 67108864 | bytes 229376 | tf_op jit(solution)/shard_map/pallas_call | solution.py:104
  49.8 1.3 copy-done.11
  52.5 12.1 %collective-permute-done.4.prior.refs_5_ = bf16[128,1024]{1,0:T(8,128)(2,1)S(1)} collective-permute-done((bf16[128,1024]{1,0:T(8,128)(2,1)S(1)}, bf16[128,1024]{1,0:T(8,128)(2,1)S(1)}, u32[]{:S(2)}, u32[]{:S(2)}) %collective-permute-start.4) | collective-permute-done | bytes 262176 | tf_op jit(solution)/shard_map/ppermute | solution.py:313
  64.7 2.0 collective-permute-start.9
  66.7 3.9 %collective-permute-start.8 = (bf16[512,1024]{1,0:T(8,128)(2,1)S(1)}, bf16[512,1024]{1,0:T(8,128)(2,1)}, u32[]{:S(2)}, u32[]{:S(2)}) collective-permute-start(bf16[512,1024]{1,0:T(8,128)(2,1)S(1)} %get-tuple-element.90.refs_4_), channel_id=1, source_target_pairs={{0,8},{4,12},{8,16},{12,20},{16,24},{20,28},{1,9},{5,13},{9,17},{1... | collective-permute-start | bytes 3145736 | tf_op jit(solution)/shard_map/ppermute | solution.py:313
  70.6 5.4 %collective-permute-start.5 = (bf16[512,1024]{1,0:T(8,128)(2,1)}, bf16[512,1024]{1,0:T(8,128)(2,1)}, u32[]{:S(2)}, u32[]{:S(2)}) collective-permute-start(bf16[512,1024]{1,0:T(8,128)(2,1)} %collective-permute-done.1.refs_5_), channel_id=1, source_target_pairs={{8,16},{12,20},{16,24},{20,28},{9,17},{13,21},{17,25},{21,29},{10,... | collective-permute-start | bytes 3145736 | tf_op jit(solution)/shard_map/ppermute | solution.py:313
  76.0 1.9 collective-permute-start.6
  78.1 10.5 %shard_map.103 = (bf16[1024,1024]{1,0:T(8,128)(2,1)}, bf16[1024,1024]{1,0:T(8,128)(2,1)S(1)}) custom-call(bf16[1024,2048]{1,0:T(8,128)(2,1)} %refs_1_.3, bf16[1024,2048]{1,0:T(8,128)(2,1)} %k.7, bf16[1024,2048]{1,0:T(8,128)(2,1)} %v.7, bf16[128,1024]{1,0:T(8,128)(2,1)S(1)} %collective-permute-done.4.prior.refs_5_, bf16[16384,256]{1,0:T(8,128)(2,1)} %get-tuple-element.84.table), custom_call_target="tpu_custom_call" | custom-call | flops 67108864 | bytes 229376 | tf_op jit(solution)/shard_map/pallas_call | solution.py:104
  88.5 4.3 %collective-permute-done.9.refs_6_ = bf16[512,1024]{1,0:T(8,128)(2,1)} collective-permute-done((bf16[512,1024]{1,0:T(8,128)(2,1)S(1)}, bf16[512,1024]{1,0:T(8,128)(2,1)}, u32[]{:S(2)}, u32[]{:S(2)}) %collective-permute-start.9) | collective-permute-done | bytes 1048608 | tf_op jit(solution)/shard_map/ppermute | solution.py:313
  92.8 1.4 collective-permute-done.8.refs_5_
  94.2 5.5 %collective-permute-start.11 = (bf16[512,1024]{1,0:T(8,128)(2,1)}, bf16[512,1024]{1,0:T(8,128)(2,1)}, u32[]{:S(2)}, u32[]{:S(2)}) collective-permute-start(bf16[512,1024]{1,0:T(8,128)(2,1)} %collective-permute-done.8.refs_5_), channel_id=1, source_target_pairs={{8,16},{12,20},{16,24},{20,28},{9,17},{13,21},{17,25},{21,29},{10,... | collective-permute-start | bytes 3145736 | tf_op jit(solution)/shard_map/ppermute | solution.py:313
  99.6 1.9 collective-permute-start.12
  101.6 9.1 %shard_map.104.refs_2_ = f32[4,512,1024]{2,1,0:T(8,128)} custom-call(s32[4]{0:T(128)S(1)} %pad_add_fusion.pick, bf16[4,1024,512]{2,1,0:T(8,128)(2,1)} %bitcast.54, bf16[1024,1024]{1,0:T(8,128)(2,1)S(1)} %copy-done.16), custom_call_target="tpu_custom_call" | custom-call | flops 16777216 | bytes 49152 | tf_op jit(solution)/shard_map/pallas_call | solution.py:289
  110.7 9.7 %shard_map.105.refs_2_ = f32[4,512,1024]{2,1,0:T(8,128)} custom-call(s32[4]{0:T(128)S(1)} %pad_add_fusion.pick, bf16[4,1024,512]{2,1,0:T(8,128)(2,1)} %bitcast.55, bf16[1024,1024]{1,0:T(8,128)(2,1)} %get-tuple-element.112.refs_1_), custom_call_target="tpu_custom_call" | custom-call | flops 16777216 | bytes 49152 | tf_op jit(solution)/shard_map/pallas_call | solution.py:289
  120.4 4.2 %shard_map.112 = bf16[1,512,1024]{2,1,0:T(8,128)(2,1)} custom-call(s32[1]{0:T(128)} %bitcast.8.pick, bf16[4,1024,512]{2,1,0:T(8,128)(2,1)} %bitcast.42, bf16[1024,1024]{1,0:T(8,128)(2,1)} %collective-permute-done.7.refs_1_, f32[4,512,1024]{2,1,0:T(8,128)} %shard_map.104.refs_2_), custom_call_target="tpu_custom_call" | custom-call | flops 16777216 | bytes 49152 | tf_op jit(solution)/shard_map/pallas_call | solution.py:289
  125.9 2.1 collective-permute-start.13
  128.0 2.3 broadcast_select_fusion.1.refs_7_
  130.4 6.5 %collective-permute-start.10 = (bf16[512,1024]{1,0:T(8,128)(2,1)}, bf16[512,1024]{1,0:T(8,128)(2,1)}, u32[]{:S(2)}, u32[]{:S(2)}) collective-permute-start(bf16[512,1024]{1,0:T(8,128)(2,1)} %broadcast_select_fusion.1.refs_7_), channel_id=1, source_target_pairs={{16,24},{20,28},{8,0},{12,4},{17,25},{21,29},{9,1},{13,5},{18,26},... | collective-permute-start | bytes 3145736 | tf_op jit(solution)/shard_map/ppermute | solution.py:313
  136.8 7.6 %shard_map.106 = bf16[3,512,1024]{2,1,0:T(8,128)(2,1)S(1)} custom-call(s32[3]{0:T(128)S(1)} %pad_add_fusion.1.pick, bf16[4,1024,512]{2,1,0:T(8,128)(2,1)} %bitcast.43, bf16[1024,1024]{1,0:T(8,128)(2,1)} %collective-permute-done.7.refs_1_, f32[4,512,1024]{2,1,0:T(8,128)} %shard_map.104.refs_2_), custom_call_target="tpu_custom_call" | custom-call | flops 16777216 | bytes 49152 | tf_op jit(solution)/shard_map/pallas_call | solution.py:289
  145.3 2.6 fusion.13
  147.9 4.6 %collective-permute-start.18 = (bf16[512,1024]{1,0:T(8,128)(2,1)}, bf16[512,1024]{1,0:T(8,128)(2,1)}, u32[]{:S(2)}, u32[]{:S(2)}) collective-permute-start(bf16[512,1024]{1,0:T(8,128)(2,1)} %fusion.13), channel_id=1, source_target_pairs={{8,16},{12,20},{16,8},{20,12},{9,17},{13,21},{17,9},{21,13},{10,18... | collective-permute-start | bytes 3145736 | tf_op jit(solution)/shard_map/ppermute | solution.py:313
  154.0 1.5 broadcast_select_fusion.refs_7_
  155.4 5.6 %collective-permute-start.15 = (bf16[512,1024]{1,0:T(8,128)(2,1)S(1)}, bf16[512,1024]{1,0:T(8,128)(2,1)S(1)}, u32[]{:S(2)}, u32[]{:S(2)}) collective-permute-start(bf16[512,1024]{1,0:T(8,128)(2,1)S(1)} %broadcast_select_fusion.refs_7_), channel_id=1, source_target_pairs={{16,24},{20,28},{8,0},{12,4},{17,25},{21,29},{9,1},{13,5},{18,26},... | collective-permute-start | bytes 3145736 | tf_op jit(solution)/shard_map/ppermute | solution.py:313
  161.1 9.2 %shard_map.107 = bf16[1024,1024]{1,0:T(8,128)(2,1)} custom-call(s32[6]{0:T(128)S(1)} %stack.37.pick, bf16[4,1024,512]{2,1,0:T(8,128)(2,1)} %bitcast.44, bf16[4,1024,512]{2,1,0:T(8,128)(2,1)} %bitcast.45, bf16[4,1024,512]{2,1,0:T(8,128)(2,1)} %bitcast.46, bf16[4,1024,512]{2,1,0:T(8,128)(2,1)} %bitcast.47, bf16[512,1024]{1,0:T(8,128)(2,1)S(1)} %copy-done.2, ...), custom_call_target="tpu_custom_call" | custom-call | flops 67108864 | bytes 163840 | tf_op jit(solution)/shard_map/pallas_call | solution.py:248
  170.3 1.5 collective-permute-done.17
  171.8 4.3 %fusion.3 = (bf16[512,1024]{1,0:T(8,128)(2,1)}, bf16[512,1024]{1,0:T(8,128)(2,1)}) fusion(bf16[512,1024]{1,0:T(8,128)(2,1)} %collective-permute-done.17, bf16[512,1024]{1,0:T(8,128)(2,1)} %collective-permute-done.18, pred[]{:T(512)S(6)} %eq.15, bf16[3,512,1024]{2,1,0:T(8,128)(2,1)S(1)} %shard_map.106, bf16[1,512,1024]{2,1,0:T(8,128)(2,1)} %shard_map.112, ...), kind=kLoop, calls=%fused_computation.11 | loop fusion | flops 6291456 | bytes 6291458 | tf_op jit(solution)/shard_map/convert_element_type | solution.py:383
  176.0 1.9 collective-permute-start.20
  177.9 3.9 %collective-permute-start.19 = (bf16[512,1024]{1,0:T(8,128)(2,1)}, bf16[512,1024]{1,0:T(8,128)(2,1)}, u32[]{:S(2)}, u32[]{:S(2)}) collective-permute-start(bf16[512,1024]{1,0:T(8,128)(2,1)} %get-tuple-element.158), channel_id=1, source_target_pairs={{0,8},{4,12},{8,16},{12,20},{16,24},{20,28},{1,9},{5,13},{9,17},{1... | collective-permute-start | bytes 3145736 | tf_op jit(solution)/shard_map/ppermute | solution.py:313
  181.9 3.5 %shard_map.113 = bf16[1,512,1024]{2,1,0:T(8,128)(2,1)S(1)} custom-call(s32[1]{0:T(128)} %bitcast.8.pick, bf16[4,1024,512]{2,1,0:T(8,128)(2,1)} %bitcast.48, bf16[1024,1024]{1,0:T(8,128)(2,1)} %collective-permute-done.13.refs_1_, f32[4,512,1024]{2,1,0:T(8,128)} %shard_map.105.refs_2_), custom_call_target="tpu_custom_call" | custom-call | flops 16777216 | bytes 49152 | tf_op jit(solution)/shard_map/pallas_call | solution.py:289
  185.4 1.6 collective-permute-start.21
  187.0 1.7 collective-permute-start.14
  188.7 7.6 %shard_map.108 = bf16[3,512,1024]{2,1,0:T(8,128)(2,1)S(1)} custom-call(s32[3]{0:T(128)S(1)} %pad_add_fusion.1.pick, bf16[4,1024,512]{2,1,0:T(8,128)(2,1)} %bitcast.49, bf16[1024,1024]{1,0:T(8,128)(2,1)} %collective-permute-done.13.refs_1_, f32[4,512,1024]{2,1,0:T(8,128)} %shard_map.105.refs_2_), custom_call_target="tpu_custom_call" | custom-call | flops 16777216 | bytes 49152 | tf_op jit(solution)/shard_map/pallas_call | solution.py:289
  197.4 1.6 copy-done.10
  199.0 9.1 %shard_map.111 = bf16[1024,1024]{1,0:T(8,128)(2,1)} custom-call(s32[6]{0:T(128)S(1)} %stack.37.pick, bf16[4,1024,512]{2,1,0:T(8,128)(2,1)} %bitcast.50, bf16[4,1024,512]{2,1,0:T(8,128)(2,1)} %bitcast.51, bf16[4,1024,512]{2,1,0:T(8,128)(2,1)} %bitcast.52, bf16[4,1024,512]{2,1,0:T(8,128)(2,1)} %bitcast.53, bf16[512,1024]{1,0:T(8,128)(2,1)S(1)} %copy-done.4, ...), custom_call_target="tpu_custom_call" | custom-call | flops 67108864 | bytes 163840 | tf_op jit(solution)/shard_map/pallas_call | solution.py:248
  209.2 9.6 %collective-permute-done.21 = bf16[512,1024]{1,0:T(8,128)(2,1)} collective-permute-done((bf16[512,1024]{1,0:T(8,128)(2,1)S(1)}, bf16[512,1024]{1,0:T(8,128)(2,1)}, u32[]{:S(2)}, u32[]{:S(2)}) %collective-permute-start.21) | collective-permute-done | bytes 1048608 | tf_op jit(solution)/shard_map/ppermute | solution.py:313
  218.7 1.6 fusion.10
  220.4 4.4 %collective-permute-start.25 = (bf16[512,1024]{1,0:T(8,128)(2,1)S(1)}, bf16[512,1024]{1,0:T(8,128)(2,1)}, u32[]{:S(2)}, u32[]{:S(2)}) collective-permute-start(bf16[512,1024]{1,0:T(8,128)(2,1)S(1)} %fusion.10), channel_id=1, source_target_pairs={{8,16},{12,20},{16,8},{20,12},{9,17},{13,21},{17,9},{21,13},{10,18... | collective-permute-start | bytes 3145736 | tf_op jit(solution)/shard_map/ppermute | solution.py:313
  226.1 1.5 collective-permute-start.22
  227.6 9.1 %shard_map.110.own_ref = bf16[1024,1024]{1,0:T(8,128)(2,1)} custom-call(s32[6]{0:T(128)S(1)} %stack.37.pick, bf16[4,1024,512]{2,1,0:T(8,128)(2,1)} %bitcast.56, bf16[4,1024,512]{2,1,0:T(8,128)(2,1)} %bitcast.57, bf16[4,1024,512]{2,1,0:T(8,128)(2,1)} %bitcast.58, bf16[4,1024,512]{2,1,0:T(8,128)(2,1)} %bitcast.59, bf16[512,1024]{1,0:T(8,128)(2,1)S(1)} %copy-done.4, ...), custom_call_target="tpu_custom_call" | custom-call | flops 67108864 | bytes 163840 | tf_op jit(solution)/shard_map/pallas_call | solution.py:248
  236.7 9.1 %shard_map.109.own_ref = bf16[1024,1024]{1,0:T(8,128)(2,1)} custom-call(s32[6]{0:T(128)S(1)} %stack.37.pick, bf16[4,1024,512]{2,1,0:T(8,128)(2,1)} %bitcast.60, bf16[4,1024,512]{2,1,0:T(8,128)(2,1)} %bitcast.61, bf16[4,1024,512]{2,1,0:T(8,128)(2,1)} %bitcast.62, bf16[4,1024,512]{2,1,0:T(8,128)(2,1)} %bitcast.63, bf16[512,1024]{1,0:T(8,128)(2,1)S(1)} %copy-done.2, ...), custom_call_target="tpu_custom_call" | custom-call | flops 67108864 | bytes 163840 | tf_op jit(solution)/shard_map/pallas_call | solution.py:248
  245.9 1.6 copy-done.6
  247.4 13.1 %shard_map.114 = (bf16[1024,2048]{1,0:T(8,128)(2,1)}, bf16[1024,1024]{1,0:T(8,128)(2,1)S(1)}, bf16[128,1024]{1,0:T(8,128)(2,1)}, f32[64,256]{1,0:T(8,128)S(1)}) custom-call(bf16[1024,1024]{1,0:T(8,128)(2,1)S(1)} %copy-done.6, bf16[1024,1024]{1,0:T(8,128)(2,1)} %collective-permute-done.14.refs_0_, bf16[1024,2048]{1,0:T(8,128)(2,1)} %refs_1_.3, ...), custom_call_target="tpu_custom_call" | custom-call | flops 67108864 | bytes 294912 | tf_op jit(solution)/shard_map/pallas_call | solution.py:170
  260.5 4.7 %fusion.7 = (bf16[512,1024]{1,0:T(8,128)(2,1)}, bf16[512,1024]{1,0:T(8,128)(2,1)}) fusion(bf16[512,1024]{1,0:T(8,128)(2,1)} %collective-permute-done.24, bf16[512,1024]{1,0:T(8,128)(2,1)} %collective-permute-done.25, pred[]{:T(512)S(6)} %eq.15, bf16[3,512,1024]{2,1,0:T(8,128)(2,1)S(1)} %shard_map.108, bf16[1,512,1024]{2,1,0:T(8,128)(2,1)S(1)} %shard_map.113, ...), kind=kLoop, calls=%fused_computation.15 | loop fusion | flops 6291456 | bytes 6291458 | tf_op jit(solution)/shard_map/convert_element_type | solution.py:383
  265.3 5.5 %collective-permute-start.27 = (bf16[512,1024]{1,0:T(8,128)(2,1)}, bf16[512,1024]{1,0:T(8,128)(2,1)}, u32[]{:S(2)}, u32[]{:S(2)}) collective-permute-start(bf16[512,1024]{1,0:T(8,128)(2,1)} %get-tuple-element.155), channel_id=1, source_target_pairs={{8,0},{12,4},{16,8},{20,12},{24,16},{28,20},{9,1},{13,5},{17,9},{2... | collective-permute-start | bytes 3145736 | tf_op jit(solution)/shard_map/ppermute | solution.py:313
  270.7 2.1 collective-permute-start.26
  272.8 2.8 fusion.12
  275.6 4.9 %collective-permute-start.28 = (bf16[128,1024]{1,0:T(8,128)(2,1)}, bf16[128,1024]{1,0:T(8,128)(2,1)S(1)}, u32[]{:S(2)}, u32[]{:S(2)}) collective-permute-start(bf16[128,1024]{1,0:T(8,128)(2,1)} %get-tuple-element.139), channel_id=1, source_target_pairs={{4,0},{8,4},{12,8},{16,12},{20,16},{24,20},{28,24},{5,1},{9,5},{13... | collective-permute-start | bytes 786440 | tf_op jit(solution)/shard_map/ppermute | solution.py:313
  280.6 12.7 %shard_map.115 = (bf16[1024,2048]{1,0:T(8,128)(2,1)}, bf16[1024,1024]{1,0:T(8,128)(2,1)S(1)}, bf16[128,1024]{1,0:T(8,128)(2,1)S(1)}, f32[64,256]{1,0:T(8,128)S(1)}) custom-call(bf16[1024,1024]{1,0:T(8,128)(2,1)S(1)} %copy-done.5, bf16[1024,1024]{1,0:T(8,128)(2,1)} %collective-permute-done.22.refs_0_, ...), custom_call_target="tpu_custom_call", output_to_operand_aliasing={{0}: (7, {})} | custom-call | flops 67108864 | bytes 294912 | tf_op jit(solution)/shard_map/pallas_call | solution.py:170
  295.5 3.3 all-to-all-start
  298.8 3.4 collective-permute-start.23
  302.2 2.6 fusion.9
  304.8 1.5 pad_maximum_fusion
  307.1 10.4 %shard_map.116 = (bf16[1024,2048]{1,0:T(8,128)(2,1)}, bf16[1024,2048]{1,0:T(8,128)(2,1)}) custom-call(bf16[1024,1024]{1,0:T(8,128)(2,1)S(1)} %copy-done.14, bf16[128,1024]{1,0:T(8,128)(2,1)S(1)} %collective-permute-done.28.later, bf16[1024,2048]{1,0:T(8,128)(2,1)} %k.7, bf16[1024,2048]{1,0:T(8,128)(2,1)} %v.7, bf16[16384,256]{1,0:T(8,128)(2,1)} %get-tuple-element.136.table), custom_call_target="tpu_custom_call" | custom-call | flops 67108864 | bytes 229376 | tf_op jit(solution)/shard_map/pallas_call | solution.py:215
  318.2 1.6 copy-done.18
  319.8 10.4 %shard_map.117 = (bf16[1024,2048]{1,0:T(8,128)(2,1)}, bf16[1024,2048]{1,0:T(8,128)(2,1)}) custom-call(bf16[1024,1024]{1,0:T(8,128)(2,1)S(1)} %copy-done.18, bf16[128,1024]{1,0:T(8,128)(2,1)S(1)} %collective-permute-done.23.later, bf16[1024,2048]{1,0:T(8,128)(2,1)} %k.7, bf16[1024,2048]{1,0:T(8,128)(2,1)} %v.7, ...), custom_call_target="tpu_custom_call", output_to_operand_aliasing={{0}: (5, {}), {1}: (6, {})} | custom-call | flops 67108864 | bytes 229376 | tf_op jit(solution)/shard_map/pallas_call | solution.py:215
  (98 shorter events, 14.1 us)
Async XLA Ops:
  7.2 57.4 %all-gather.5.cloned.1.call-start = ((), (), s32[]{:S(2)}) async-start(), calls=%async_computation.1 | async-start | bytes 5242880 | tf_op jit(solution)/shard_map/all_gather | solution.py:413
  9.3 6.5 %copy-start.26 = (bf16[128,128]{1,0:T(8,128)(2,1)S(1)}, bf16[128,128]{1,0:T(8,128)(2,1)}, u32[]{:S(2)}) copy-start(bf16[128,128]{1,0:T(8,128)(2,1)} %param.9) | copy-start | bytes 98308
  12.3 108.1 %all-gather.7.cloned.1.call-start = ((), (), s32[]{:S(2)}) async-start(), calls=%async_computation.2 | async-start | bytes 5242880 | tf_op jit(solution)/shard_map/all_gather | solution.py:431
  12.4 16.0 %collective-permute-start = (bf16[128,1024]{1,0:T(8,128)(2,1)S(1)}, bf16[128,1024]{1,0:T(8,128)(2,1)S(1)}, u32[]{:S(2)}, u32[]{:S(2)}) collective-permute-start(bf16[128,1024]{1,0:T(8,128)(2,1)S(1)} %get-tuple-element.154), channel_id=1, source_target_pairs={{0,4},{4,8},{8,12},{12,16},{16,20},{20,24},{24,28},{1,5},{5,9},{9,... | collective-permute-start | bytes 786440 | tf_op jit(solution)/shard_map/ppermute | solution.py:313
  26.6 9.9 %copy-start.25 = (bf16[128,1024]{1,0:T(8,128)(2,1)S(1)}, bf16[128,1024]{1,0:T(8,128)(2,1)}, u32[]{:S(2)}) copy-start(bf16[128,1024]{1,0:T(8,128)(2,1)} %get-tuple-element.86) | copy-start | bytes 786436
  28.4 21.4 %copy-start.1 = (bf16[512,1024]{1,0:T(8,128)(2,1)}, bf16[512,1024]{1,0:T(8,128)(2,1)S(1)}, u32[]{:S(2)}) copy-start(bf16[512,1024]{1,0:T(8,128)(2,1)S(1)} %get-tuple-element.81.refs_4_) | copy-start | bytes 3145732
  28.4 38.3 %copy-start.3 = (bf16[512,1024]{1,0:T(8,128)(2,1)}, bf16[512,1024]{1,0:T(8,128)(2,1)S(1)}, u32[]{:S(2)}) copy-start(bf16[512,1024]{1,0:T(8,128)(2,1)S(1)} %get-tuple-element.90.refs_4_) | copy-start | bytes 3145732
  28.4 0.7 copy-start.19
  29.1 35.4 %collective-permute-start.3 = (bf16[1024,512]{1,0:T(8,128)(2,1)}, bf16[1024,512]{1,0:T(8,128)(2,1)}, u32[]{:S(2)}, u32[]{:S(2)}) collective-permute-start(bf16[1024,512]{1,0:T(8,128)(2,1)} %get-tuple-element.82), channel_id=1, source_target_pairs={{0,4},{4,0},{8,12},{12,8},{16,20},{20,16},{24,28},{28,24},{1,5},{5... | collective-permute-start | bytes 3145736 | tf_op jit(solution)/shard_map/ppermute | solution.py:313
  30.7 33.9 %collective-permute-start.2 = (bf16[512,1024]{1,0:T(8,128)(2,1)S(1)}, bf16[512,1024]{1,0:T(8,128)(2,1)S(1)}, u32[]{:S(2)}, u32[]{:S(2)}) collective-permute-start(bf16[512,1024]{1,0:T(8,128)(2,1)S(1)} %get-tuple-element.81.refs_4_), channel_id=1, source_target_pairs={{8,0},{12,4},{16,8},{20,12},{24,16},{28,20},{9,1},{13,5},{17,9},{2... | collective-permute-start | bytes 3145736 | tf_op jit(solution)/shard_map/ppermute | solution.py:313
  33.0 31.5 %collective-permute-start.1 = (bf16[512,1024]{1,0:T(8,128)(2,1)S(1)}, bf16[512,1024]{1,0:T(8,128)(2,1)}, u32[]{:S(2)}, u32[]{:S(2)}) collective-permute-start(bf16[512,1024]{1,0:T(8,128)(2,1)S(1)} %get-tuple-element.81.refs_4_), channel_id=1, source_target_pairs={{0,8},{4,12},{8,16},{12,20},{16,24},{20,28},{1,9},{5,13},{9,17},{1... | collective-permute-start | bytes 3145736 | tf_op jit(solution)/shard_map/ppermute | solution.py:313
  36.5 28.0 %collective-permute-start.4 = (bf16[128,1024]{1,0:T(8,128)(2,1)S(1)}, bf16[128,1024]{1,0:T(8,128)(2,1)S(1)}, u32[]{:S(2)}, u32[]{:S(2)}) collective-permute-start(bf16[128,1024]{1,0:T(8,128)(2,1)S(1)} %copy-done.25), channel_id=1, source_target_pairs={{0,4},{4,8},{8,12},{12,16},{16,20},{20,24},{24,28},{1,5},{5,9},{9,... | collective-permute-start | bytes 786440 | tf_op jit(solution)/shard_map/ppermute | solution.py:313
  38.9 1.0 copy-start.20
  49.8 1.4 copy-start.11
  51.1 1.3 copy-start.15
  64.6 24.0 %copy-start.7 = (bf16[512,1024]{1,0:T(8,128)(2,1)}, bf16[512,1024]{1,0:T(8,128)(2,1)S(1)}, u32[]{:S(2)}) copy-start(bf16[512,1024]{1,0:T(8,128)(2,1)S(1)} %collective-permute-done.2.refs_6_) | copy-start | bytes 3145732
  64.6 55.8 %collective-permute-start.7 = (bf16[1024,1024]{1,0:T(8,128)(2,1)}, bf16[1024,1024]{1,0:T(8,128)(2,1)}, u32[]{:S(2)}, u32[]{:S(2)}) collective-permute-start(bf16[1024,1024]{1,0:T(8,128)(2,1)} %copy-done.15), channel_id=1, source_target_pairs={{0,4},{4,0},{8,12},{12,8},{16,20},{20,16},{24,28},{28,24},{1,5},{5... | collective-permute-start | bytes 6291464 | tf_op jit(solution)/shard_map/ppermute | solution.py:313
  64.7 28.1 %collective-permute-start.9 = (bf16[512,1024]{1,0:T(8,128)(2,1)S(1)}, bf16[512,1024]{1,0:T(8,128)(2,1)}, u32[]{:S(2)}, u32[]{:S(2)}) collective-permute-start(bf16[512,1024]{1,0:T(8,128)(2,1)S(1)} %get-tuple-element.90.refs_4_), channel_id=1, source_target_pairs={{8,0},{12,4},{16,8},{20,12},{24,16},{28,20},{9,1},{13,5},{17,9},{2... | collective-permute-start | bytes 3145736 | tf_op jit(solution)/shard_map/ppermute | solution.py:313
  66.7 27.5 %collective-permute-start.8 = (bf16[512,1024]{1,0:T(8,128)(2,1)S(1)}, bf16[512,1024]{1,0:T(8,128)(2,1)}, u32[]{:S(2)}, u32[]{:S(2)}) collective-permute-start(bf16[512,1024]{1,0:T(8,128)(2,1)S(1)} %get-tuple-element.90.refs_4_), channel_id=1, source_target_pairs={{0,8},{4,12},{8,16},{12,20},{16,24},{20,28},{1,9},{5,13},{9,17},{1... | collective-permute-start | bytes 3145736 | tf_op jit(solution)/shard_map/ppermute | solution.py:313
  70.6 49.8 %collective-permute-start.5 = (bf16[512,1024]{1,0:T(8,128)(2,1)}, bf16[512,1024]{1,0:T(8,128)(2,1)}, u32[]{:S(2)}, u32[]{:S(2)}) collective-permute-start(bf16[512,1024]{1,0:T(8,128)(2,1)} %collective-permute-done.1.refs_5_), channel_id=1, source_target_pairs={{8,16},{12,20},{16,24},{20,28},{9,17},{13,21},{17,25},{21,29},{10,... | collective-permute-start | bytes 3145736 | tf_op jit(solution)/shard_map/ppermute | solution.py:313
  76.0 44.4 %collective-permute-start.6 = (bf16[512,1024]{1,0:T(8,128)(2,1)S(1)}, bf16[512,1024]{1,0:T(8,128)(2,1)}, u32[]{:S(2)}, u32[]{:S(2)}) collective-permute-start(bf16[512,1024]{1,0:T(8,128)(2,1)S(1)} %collective-permute-done.2.refs_6_), channel_id=1, source_target_pairs={{16,8},{20,12},{8,0},{12,4},{17,9},{21,13},{9,1},{13,5},{18,10},{2... | collective-permute-start | bytes 3145736 | tf_op jit(solution)/shard_map/ppermute | solution.py:313
  78.1 23.5 %copy-start.16 = (bf16[1024,1024]{1,0:T(8,128)(2,1)S(1)}, bf16[1024,1024]{1,0:T(8,128)(2,1)}, u32[]{:S(2)}) copy-start(bf16[1024,1024]{1,0:T(8,128)(2,1)} %copy-done.15) | copy-start | bytes 6291460
  88.5 22.2 %copy-start.12 = (bf16[1024,1024]{1,0:T(8,128)(2,1)}, bf16[1024,1024]{1,0:T(8,128)(2,1)S(1)}, u32[]{:S(2)}) copy-start(bf16[1024,1024]{1,0:T(8,128)(2,1)S(1)} %get-tuple-element.129.refs_4_) | copy-start | bytes 6291460
  94.2 50.3 %collective-permute-start.11 = (bf16[512,1024]{1,0:T(8,128)(2,1)}, bf16[512,1024]{1,0:T(8,128)(2,1)}, u32[]{:S(2)}, u32[]{:S(2)}) collective-permute-start(bf16[512,1024]{1,0:T(8,128)(2,1)} %collective-permute-done.8.refs_5_), channel_id=1, source_target_pairs={{8,16},{12,20},{16,24},{20,28},{9,17},{13,21},{17,25},{21,29},{10,... | collective-permute-start | bytes 3145736 | tf_op jit(solution)/shard_map/ppermute | solution.py:313
  99.6 44.9 %collective-permute-start.12 = (bf16[512,1024]{1,0:T(8,128)(2,1)}, bf16[512,1024]{1,0:T(8,128)(2,1)}, u32[]{:S(2)}, u32[]{:S(2)}) collective-permute-start(bf16[512,1024]{1,0:T(8,128)(2,1)} %collective-permute-done.9.refs_6_), channel_id=1, source_target_pairs={{16,8},{20,12},{8,0},{12,4},{17,9},{21,13},{9,1},{13,5},{18,10},{2... | collective-permute-start | bytes 3145736 | tf_op jit(solution)/shard_map/ppermute | solution.py:313
  124.6 20.7 %collective-permute-start.16 = (bf16[512,1024]{1,0:T(8,128)(2,1)}, bf16[512,1024]{1,0:T(8,128)(2,1)}, u32[]{:S(2)}, u32[]{:S(2)}) collective-permute-start(bf16[512,1024]{1,0:T(8,128)(2,1)} %bitcast.11), channel_id=1, source_target_pairs={{0,8},{4,12},{24,16},{28,20},{1,9},{5,13},{25,17},{29,21},{2,10},{... | collective-permute-start | bytes 3145736 | tf_op jit(solution)/shard_map/ppermute | solution.py:313
  125.9 56.0 %collective-permute-start.13 = (bf16[1024,1024]{1,0:T(8,128)(2,1)}, bf16[1024,1024]{1,0:T(8,128)(2,1)}, u32[]{:S(2)}, u32[]{:S(2)}) collective-permute-start(bf16[1024,1024]{1,0:T(8,128)(2,1)} %get-tuple-element.112.refs_1_), channel_id=1, source_target_pairs={{0,4},{4,0},{8,12},{12,8},{16,20},{20,16},{24,28},{28,24},{1,5},{5... | collective-permute-start | bytes 6291464 | tf_op jit(solution)/shard_map/ppermute | solution.py:313
  130.4 30.7 %collective-permute-start.10 = (bf16[512,1024]{1,0:T(8,128)(2,1)}, bf16[512,1024]{1,0:T(8,128)(2,1)}, u32[]{:S(2)}, u32[]{:S(2)}) collective-permute-start(bf16[512,1024]{1,0:T(8,128)(2,1)} %broadcast_select_fusion.1.refs_7_), channel_id=1, source_target_pairs={{16,24},{20,28},{8,0},{12,4},{17,25},{21,29},{9,1},{13,5},{18,26},... | collective-permute-start | bytes 3145736 | tf_op jit(solution)/shard_map/ppermute | solution.py:313
  147.9 22.4 %collective-permute-start.18 = (bf16[512,1024]{1,0:T(8,128)(2,1)}, bf16[512,1024]{1,0:T(8,128)(2,1)}, u32[]{:S(2)}, u32[]{:S(2)}) collective-permute-start(bf16[512,1024]{1,0:T(8,128)(2,1)} %fusion.13), channel_id=1, source_target_pairs={{8,16},{12,20},{16,8},{20,12},{9,17},{13,21},{17,9},{21,13},{10,18... | collective-permute-start | bytes 3145736 | tf_op jit(solution)/shard_map/ppermute | solution.py:313
  152.5 19.2 %collective-permute-start.17 = (bf16[512,1024]{1,0:T(8,128)(2,1)}, bf16[512,1024]{1,0:T(8,128)(2,1)}, u32[]{:S(2)}, u32[]{:S(2)}) collective-permute-start(bf16[512,1024]{1,0:T(8,128)(2,1)} %fusion.13), channel_id=1, source_target_pairs={{0,8},{4,12},{24,16},{28,20},{1,9},{5,13},{25,17},{29,21},{2,10},{... | collective-permute-start | bytes 3145736 | tf_op jit(solution)/shard_map/ppermute | solution.py:313
  153.9 7.1 %copy-start.2 = (bf16[512,1024]{1,0:T(8,128)(2,1)S(1)}, bf16[512,1024]{1,0:T(8,128)(2,1)}, u32[]{:S(2)}) copy-start(bf16[512,1024]{1,0:T(8,128)(2,1)} %copy-done.1) | copy-start | bytes 3145732
  154.0 7.1 %copy-start.8 = (bf16[512,1024]{1,0:T(8,128)(2,1)S(1)}, bf16[512,1024]{1,0:T(8,128)(2,1)}, u32[]{:S(2)}) copy-start(bf16[512,1024]{1,0:T(8,128)(2,1)} %copy-done.7) | copy-start | bytes 3145732
  155.4 40.9 %collective-permute-start.15 = (bf16[512,1024]{1,0:T(8,128)(2,1)S(1)}, bf16[512,1024]{1,0:T(8,128)(2,1)S(1)}, u32[]{:S(2)}, u32[]{:S(2)}) collective-permute-start(bf16[512,1024]{1,0:T(8,128)(2,1)S(1)} %broadcast_select_fusion.refs_7_), channel_id=1, source_target_pairs={{16,24},{20,28},{8,0},{12,4},{17,25},{21,29},{9,1},{13,5},{18,26},... | collective-permute-start | bytes 3145736 | tf_op jit(solution)/shard_map/ppermute | solution.py:313
  176.0 32.1 %collective-permute-start.20 = (bf16[512,1024]{1,0:T(8,128)(2,1)}, bf16[512,1024]{1,0:T(8,128)(2,1)S(1)}, u32[]{:S(2)}, u32[]{:S(2)}) collective-permute-start(bf16[512,1024]{1,0:T(8,128)(2,1)} %get-tuple-element.157), channel_id=1, source_target_pairs={{8,0},{12,4},{16,8},{20,12},{24,16},{28,20},{9,1},{13,5},{17,9},{2... | collective-permute-start | bytes 3145736 | tf_op jit(solution)/shard_map/ppermute | solution.py:313
  177.9 30.2 %collective-permute-start.19 = (bf16[512,1024]{1,0:T(8,128)(2,1)}, bf16[512,1024]{1,0:T(8,128)(2,1)}, u32[]{:S(2)}, u32[]{:S(2)}) collective-permute-start(bf16[512,1024]{1,0:T(8,128)(2,1)} %get-tuple-element.158), channel_id=1, source_target_pairs={{0,8},{4,12},{8,16},{12,20},{16,24},{20,28},{1,9},{5,13},{9,17},{1... | collective-permute-start | bytes 3145736 | tf_op jit(solution)/shard_map/ppermute | solution.py:313
  185.4 12.0 %copy-start.4 = (bf16[512,1024]{1,0:T(8,128)(2,1)S(1)}, bf16[512,1024]{1,0:T(8,128)(2,1)}, u32[]{:S(2)}) copy-start(bf16[512,1024]{1,0:T(8,128)(2,1)} %copy-done.3) | copy-start | bytes 3145732
  185.4 33.4 %collective-permute-start.21 = (bf16[512,1024]{1,0:T(8,128)(2,1)S(1)}, bf16[512,1024]{1,0:T(8,128)(2,1)}, u32[]{:S(2)}, u32[]{:S(2)}) collective-permute-start(bf16[512,1024]{1,0:T(8,128)(2,1)S(1)} %bitcast.41), channel_id=1, source_target_pairs={{0,8},{4,12},{24,16},{28,20},{1,9},{5,13},{25,17},{29,21},{2,10},{... | collective-permute-start | bytes 3145736 | tf_op jit(solution)/shard_map/ppermute | solution.py:313
  187.0 58.9 %collective-permute-start.14 = (bf16[1024,1024]{1,0:T(8,128)(2,1)}, bf16[1024,1024]{1,0:T(8,128)(2,1)}, u32[]{:S(2)}, u32[]{:S(2)}) collective-permute-start(bf16[1024,1024]{1,0:T(8,128)(2,1)} %shard_map.107), channel_id=1, source_target_pairs={{0,4},{4,0},{8,12},{12,8},{16,20},{20,16},{24,28},{28,24},{1,5},{5... | collective-permute-start | bytes 6291464 | tf_op jit(solution)/shard_map/ppermute | solution.py:313
  196.4 64.1 %copy-start = (bf16[3,512,1024]{2,1,0:T(8,128)(2,1)}, bf16[3,512,1024]{2,1,0:T(8,128)(2,1)S(1)}, u32[]{:S(2)}) copy-start(bf16[3,512,1024]{2,1,0:T(8,128)(2,1)S(1)} %shard_map.108) | copy-start | bytes 9437188
  196.4 1.0 copy-start.9
  197.4 1.6 copy-start.10
  208.2 1.0 copy-start.23
  220.4 40.1 %collective-permute-start.25 = (bf16[512,1024]{1,0:T(8,128)(2,1)S(1)}, bf16[512,1024]{1,0:T(8,128)(2,1)}, u32[]{:S(2)}, u32[]{:S(2)}) collective-permute-start(bf16[512,1024]{1,0:T(8,128)(2,1)S(1)} %fusion.10), channel_id=1, source_target_pairs={{8,16},{12,20},{16,8},{20,12},{9,17},{13,21},{17,9},{21,13},{10,18... | collective-permute-start | bytes 3145736 | tf_op jit(solution)/shard_map/ppermute | solution.py:313
  224.8 35.7 %collective-permute-start.24 = (bf16[512,1024]{1,0:T(8,128)(2,1)S(1)}, bf16[512,1024]{1,0:T(8,128)(2,1)}, u32[]{:S(2)}, u32[]{:S(2)}) collective-permute-start(bf16[512,1024]{1,0:T(8,128)(2,1)S(1)} %fusion.10), channel_id=1, source_target_pairs={{0,8},{4,12},{24,16},{28,20},{1,9},{5,13},{25,17},{29,21},{2,10},{... | collective-permute-start | bytes 3145736 | tf_op jit(solution)/shard_map/ppermute | solution.py:313
  226.1 54.5 %collective-permute-start.22 = (bf16[1024,1024]{1,0:T(8,128)(2,1)}, bf16[1024,1024]{1,0:T(8,128)(2,1)}, u32[]{:S(2)}, u32[]{:S(2)}) collective-permute-start(bf16[1024,1024]{1,0:T(8,128)(2,1)} %shard_map.111), channel_id=1, source_target_pairs={{0,4},{4,0},{8,12},{12,8},{16,20},{20,16},{24,28},{28,24},{1,5},{5... | collective-permute-start | bytes 6291464 | tf_op jit(solution)/shard_map/ppermute | solution.py:313
  236.7 9.1 %copy-start.21 = (bf16[128,1024]{1,0:T(8,128)(2,1)S(1)}, bf16[128,1024]{1,0:T(8,128)(2,1)}, u32[]{:S(2)}) copy-start(bf16[128,1024]{1,0:T(8,128)(2,1)} %copy-done.19) | copy-start | bytes 786436
  245.8 1.6 copy-start.6
  260.5 4.8 %copy-start.13 = (bf16[1024,1024]{1,0:T(8,128)(2,1)}, bf16[1024,1024]{1,0:T(8,128)(2,1)S(1)}, u32[]{:S(2)}) copy-start(bf16[1024,1024]{1,0:T(8,128)(2,1)S(1)} %get-tuple-element.143.gm) | copy-start | bytes 6291460
  260.5 12.3 %copy-start.24 = (bf16[512,1024]{1,0:T(8,128)(2,1)S(1)}, bf16[512,1024]{1,0:T(8,128)(2,1)}, u32[]{:S(2)}) copy-start(bf16[512,1024]{1,0:T(8,128)(2,1)} %copy-done.23) | copy-start | bytes 3145732
  265.3 36.9 %collective-permute-start.27 = (bf16[512,1024]{1,0:T(8,128)(2,1)}, bf16[512,1024]{1,0:T(8,128)(2,1)}, u32[]{:S(2)}, u32[]{:S(2)}) collective-permute-start(bf16[512,1024]{1,0:T(8,128)(2,1)} %get-tuple-element.155), channel_id=1, source_target_pairs={{8,0},{12,4},{16,8},{20,12},{24,16},{28,20},{9,1},{13,5},{17,9},{2... | collective-permute-start | bytes 3145736 | tf_op jit(solution)/shard_map/ppermute | solution.py:313
  270.7 9.9 %copy-start.5 = (bf16[1024,1024]{1,0:T(8,128)(2,1)S(1)}, bf16[1024,1024]{1,0:T(8,128)(2,1)}, u32[]{:S(2)}) copy-start(bf16[1024,1024]{1,0:T(8,128)(2,1)} %shard_map.110.own_ref) | copy-start | bytes 6291460
  270.7 31.4 %collective-permute-start.26 = (bf16[512,1024]{1,0:T(8,128)(2,1)}, bf16[512,1024]{1,0:T(8,128)(2,1)}, u32[]{:S(2)}, u32[]{:S(2)}) collective-permute-start(bf16[512,1024]{1,0:T(8,128)(2,1)} %get-tuple-element.156), channel_id=1, source_target_pairs={{0,8},{4,12},{8,16},{12,20},{16,24},{20,28},{1,9},{5,13},{9,17},{1... | collective-permute-start | bytes 3145736 | tf_op jit(solution)/shard_map/ppermute | solution.py:313
  275.6 30.6 %collective-permute-start.28 = (bf16[128,1024]{1,0:T(8,128)(2,1)}, bf16[128,1024]{1,0:T(8,128)(2,1)S(1)}, u32[]{:S(2)}, u32[]{:S(2)}) collective-permute-start(bf16[128,1024]{1,0:T(8,128)(2,1)} %get-tuple-element.139), channel_id=1, source_target_pairs={{4,0},{8,4},{12,8},{16,12},{20,16},{24,20},{28,24},{5,1},{9,5},{13... | collective-permute-start | bytes 786440 | tf_op jit(solution)/shard_map/ppermute | solution.py:313
  293.3 1.3 copy-start.17
  295.5 22.1 %all-to-all-start = ((f32[8,16,128]{2,1,0:T(8,128)}), f32[8,16,128]{2,1,0:T(8,128)S(1)}, u32[]{:S(2)}, u32[]{:S(2)}) async-start(f32[8,16,128]{2,1,0:T(8,128)} %bitcast.21), calls=%async_computation | async-start | bytes 131072 | tf_op jit(solution)/shard_map/all_to_all | solution.py:505
  298.8 19.4 %collective-permute-start.23 = (bf16[128,1024]{1,0:T(8,128)(2,1)S(1)}, bf16[128,1024]{1,0:T(8,128)(2,1)S(1)}, u32[]{:S(2)}, u32[]{:S(2)}) collective-permute-start(bf16[128,1024]{1,0:T(8,128)(2,1)S(1)} %get-tuple-element.135), channel_id=1, source_target_pairs={{4,0},{8,4},{12,8},{16,12},{20,16},{24,20},{28,24},{5,1},{9,5},{13... | collective-permute-start | bytes 786440 | tf_op jit(solution)/shard_map/ppermute | solution.py:313
  302.2 2.6 copy-start.22
  304.8 2.3 copy-start.14
  318.2 1.6 copy-start.18
Sparse Core Ops, SparseCore 0:
  12.5 34.6 all-gather.4
  64.8 33.7 all-gather.6

commit v7 on v6

--- a/solution.py
+++ b/solution.py
@@ -108,7 +108,7 @@
             here,
             here,
             here,
-            pl.BlockSpec((FILT, LANES), lambda i: (0, i)),
+            pl.BlockSpec((FILT, LANES), lambda i: (0, chunk * tiles + i)),
             pl.BlockSpec((GPT * FILT, 2 * FILT), lambda i: (chunk * tiles + i, 0)),
         ],
         out_specs=[out, out],
@@ -161,7 +161,8 @@
         middle_kernel(own_ref, refs[:n_other], *refs[n_other:])
 
     args = [own, *others, q, k, v, mixed, prior]
-    in_specs = [part] * (1 + n_other) + [here] * 3 + [part, edge]
+    in_specs = [part] * (1 + n_other) + [here] * 3 + [part]
+    in_specs.append(pl.BlockSpec((FILT, LANES), lambda i: (0, chunk * tiles + i)))
     aliases = {}
     if filled is not None:
         aliases = {len(args): 0}
@@ -225,12 +226,12 @@
 
 
 def gate_kernel(pick, *refs):
-    own, up, down, second, third, out = refs[LINE:]
+    own, up, down, up2, down2, third, out = refs[LINE:]
     slots = (
         own[...],
         jnp.where(pick[LINE] == 1, down[...], up[...]),
-        second[...],
-        jnp.where(pick[LINE + 1] == 1, third[...], down[...]),
+        jnp.where(pick[LINE + 1] == 1, up2[...], down2[...]),
+        jnp.where(pick[LINE + 2] == 1, third[...], down[...]),
     )
     cot = jnp.concatenate([ref[0] for ref in refs[:LINE]], axis=1)
     total = jnp.dot(cot, jnp.concatenate(slots, axis=0), preferred_element_type=F32)
@@ -300,6 +301,42 @@
     )(pick, *args)
 
 
+def packet_kernel(n, pick, *refs):
+    base, up, down, first_out, packet_out = refs[2 * n :]
+    cot, gated = refs[0][0], refs[n][...]
+    if n > 1:
+        cot = jnp.concatenate([ref[0] for ref in refs[:n]], axis=0)
+        gated = jnp.concatenate([ref[...] for ref in refs[n : 2 * n]], axis=0)
+    total = lax.dot_general(cot, gated, (((0,), (0,)), ((), ())), preferred_element_type=F32)
+    rows = (total + base[0]).astype(BF16)
+    first_out[...] = rows
+    passed = jnp.where(pick[2] == 1, up[...], down[...])
+    packet_out[...] = jnp.where(pick[1] == 1, rows, passed)
+
+
+def packet_rows(pick, cots, gateds, base, up, down):
+    _, rows, depth = cots[0].shape
+    width = gateds[0].shape[1]
+    tile = min(512, width)
+    n = len(cots)
+    part = pl.BlockSpec((depth, tile), lambda i, pick: (0, i))
+    shape = jax.ShapeDtypeStruct((depth, width), BF16)
+    return pl.pallas_call(
+        functools.partial(packet_kernel, n),
+        grid_spec=pltpu.PrefetchScalarGridSpec(
+            num_scalar_prefetch=1,
+            grid=(width // tile,),
+            in_specs=[pl.BlockSpec((1, rows, depth), lambda i, pick: (pick[0], 0, 0))] * n
+            + [pl.BlockSpec((rows, tile), lambda i, pick: (0, i))] * n
+            + [pl.BlockSpec((1, depth, tile), lambda i, pick: (0, 0, i)), part, part],
+            out_specs=[part, part],
+        ),
+        out_shape=[shape, shape],
+        compiler_params=params(),
+        cost_estimate=cost(2 * n * rows * depth * width, 2 * n * rows * (depth + width)),
+    )(pick, *cots, *gateds, base, up, down)
+
+
 def shards(seq, ch, queries, keys, values, filters, grad_out, out_weight):
     inner = seq // LINE
     rows, width = queries.shape
@@ -326,25 +363,21 @@
     def second_step(h):
         return along_line(up1[h], [(1, 2), (2, 3)]), along_line(down1[h], [(2, 1), (1, 0)])
 
-    def third_step(x):
-        return along_line(x, [(2, 3), (1, 0)])
-
-    def merge(pair):
-        return jnp.where(z >= 2, *pair)
-
+    at_end = (z == 0) | (z == 3)
     pick = jnp.stack(
         [
             z,
             jnp.where(z == 0, 1, z - 1),
             jnp.where(z >= 2, z - 2, z + 2),
             jnp.where(z == 3, 0, jnp.where(z == 1, 2, 3)),
-            jnp.where(z == 0, 1, 0),
-            jnp.where((z == 0) | (z == 3), 1, 0),
+            z == 0,
+            z >= 2,
+            at_end,
         ]
     ).astype(jnp.int32)
 
     def weights(h):
-        return [halves[h], up1[h], down1[h], second[h], third[h]]
+        return [halves[h], up1[h], down1[h], *second[h], third[h]]
 
     def swap_gated(h):
         return [around_inner(gateds[h], r) for r in range(1, inner)]
@@ -362,17 +395,20 @@
     def rows_own(h):
         return weight_rows(jnp.concatenate([first_pick, rest_pick]), cots[:1], [gateds[h]], F32)
 
-    def rows_first(h):
-        return weight_rows(first_pick, cots[1:], got[h], BF16, base[h])[0]
+    packet_pick = jnp.concatenate([first_pick, jnp.stack([at_end, z >= 2]).astype(jnp.int32)])
+
+    def packet(h):
+        return packet_rows(packet_pick, cots[1:], got[h], base[h], *second[h])
 
     def rows_rest(h):
         return weight_rows(rest_pick, cots[1:], got[h], BF16, base[h], 1)
 
-    def send_first(x):
-        return along_line(x, [(0, 1), (3, 2)])
+    def send_packet(x):
+        return along_line(x, [(0, 1), (3, 2), (2, 3), (1, 0)])
 
     def send_second(h, came):
-        x = (rest[h][0].astype(F32) + came.astype(F32)).astype(BF16)
+        came = jnp.where(at_end, 0.0, came.astype(F32))
+        x = (rest[h][0].astype(F32) + came).astype(BF16)
         return along_line(x, [(0, 1), (3, 2)]), along_line(x, [(1, 2), (2, 1)])
 
     def send_third(h, outer_in, inner_in):
@@ -397,13 +433,9 @@
     first, rest = ([None] * chunks for _ in range(2))
     later_halves = list(each[1:])
 
-    priors = []
-    for h in each:
-        tail = (slice(rows - FILT, rows), slice(h * cols, (h + 1) * cols))
-        priors.append(product_of(keys[tail], values[tail]))
-    cot_here = after(grad_out, *priors)
-    next_pairs = [(i, i + 1) for i in range(seq - 1)]
-    priors[0] = send(priors[0], next_pairs)
+    prior = product_of(keys[rows - FILT :], values[rows - FILT :])
+    cot_here = after(grad_out, prior)
+    prior = send(prior, [(i, i + 1) for i in range(seq - 1)])
     paired = inner == 2 and ch == LINE
     other = cot_here
     cots = []
@@ -413,16 +445,12 @@
         cots = [lax.all_gather(kept, "ch", axis=0, tiled=False)]
     back, ahead = tables(filters)
     halves = [out_weight[:, h * cols : (h + 1) * cols] for h in each]
-    priors, other, halves, back = fence(priors, other, halves, back)
-    for h in later_halves:
-        priors[h] = send(priors[h], next_pairs)
+    prior, other, halves, back = fence(prior, other, halves, back)
 
     up1[0], down1[0] = along_line(halves[0], up_pairs), along_line(halves[0], down_pairs)
     swapped = around_inner(other, 1) if paired else other
-    gateds[0], mixeds[0] = forward(queries, keys, values, priors[0], back, 0, chunks)
-    up1[0], down1[0], swapped, gateds, cots, priors = fence(
-        up1[0], down1[0], swapped, gateds, cots, priors
-    )
+    gateds[0], mixeds[0] = forward(queries, keys, values, prior, back, 0, chunks)
+    up1[0], down1[0], swapped, gateds, cots = fence(up1[0], down1[0], swapped, gateds, cots)
 
     for h in later_halves:
         up1[h], down1[h] = along_line(halves[h], up_pairs), along_line(halves[h], down_pairs)
@@ -437,36 +465,34 @@
             cots.append(part if shift == 0 else around_inner(part, shift))
     got[0] = swap_gated(0)
     for h in later_halves:
-        gateds[h], mixeds[h] = forward(queries, keys, values, priors[h], back, h, chunks)
+        gateds[h], mixeds[h] = forward(queries, keys, values, prior, back, h, chunks)
     up1, down1, gateds, cots[0] = fence(up1, down1, gateds, cots[0])
 
     for h in later_halves:
         second[h] = second_step(h)
-    base = [rows_own(h) for h in each]
+    base = [None] * chunks
+    base[0] = rows_own(0)
     second[0], got[0], gateds, cots, base = fence(second[0], got[0], gateds, cots, base)
 
-    second[0] = merge(second[0])
-    third[0] = third_step(second[0])
+    first[0], parcel = packet(0)
+    third[0] = send_packet(parcel)
     for h in later_halves:
         got[h] = swap_gated(h)
-    first[0] = rows_first(0)
-    sums[0] = send_first(first[0])
     rest[0] = rows_rest(0)
-    second, rest[0] = fence(second, rest[0])
-
-    for h in later_halves:
-        second[h] = merge(second[h])
-        third[h] = third_step(second[h])
-    sums[0] = send_second(0, sums[0])
-    third[0], second = fence(third[0], second)
+    second, rest[0], gateds = fence(second, rest[0], gateds)
+    for h in later_halves:
+        base[h] = rows_own(h)
+    third[0], second, base = fence(third[0], second, base)
+
+    sums[0] = send_second(0, third[0])
 
     parts[0] = shares(0)
     parts[0], got[1:] = fence(parts[0], got[1:])
     others[0] = send_shares(parts[0])
 
     for h in later_halves:
-        first[h] = rows_first(h)
-        sums[h] = send_first(first[h])
+        first[h], parcel = packet(h)
+        third[h] = send_packet(parcel)
     sums[0] = send_third(0, *sums[0])
     for h in later_halves:
         rest[h] = rows_rest(h)
@@ -477,7 +503,7 @@
     parts[1:], sums = fence(parts[1:], sums)
     for h in later_halves:
         others[h] = send_shares(parts[h])
-        sums[h] = send_second(h, sums[h])
+        sums[h] = send_second(h, third[h])
     owns = [gate_grad(pick, cots[0], weights(h)) for h in each]
     others[0], owns = fence(others[0], owns)
 
@@ -486,7 +512,7 @@
     taps, gms, laters = ([None] * chunks for _ in range(3))
     for h in each:
         grad_queries, gms[h], edge, taps[h] = middle(
-            owns[h], others[h], queries, keys, values, mixeds[h], priors[h], grad_queries, h, chunks
+            owns[h], others[h], queries, keys, values, mixeds[h], prior, grad_queries, h, chunks
         )
         laters[h] = send(edge, [(i + 1, i) for i in range(seq - 1)])
         if h == 0:

time: 339 us -> 338 us (level)
  waiting for transfers between devices: 29.7 us -> 54.3 us
  starting transfers between devices: 90.7 us -> 68.4 us
  other arithmetic: 27 us -> 19.8 us
    ppermute x29 -> x26, starting transfers between devices: 87.3 us -> 61.8 us  [send(): return lax.ppermute(x, 'seq', pairs)]
    ppermute x29 -> x26, waiting for transfers between devices: 29.6 us -> 54.2 us  [send(): return lax.ppermute(x, 'seq', pairs)]
    pallas_call x0 -> x2, Pallas kernels: none -> 8.94 us  [packet_rows(): pl.pallas_call(functools.partial(packet_kernel, n), grid_spec=pltpu.Prefe...]
    pallas_call x6 -> x4, Pallas kernels: 41.7 us -> 34 us  [weight_rows(): pl.pallas_call(functools.partial(rows_kernel, n), grid_spec=pltpu.Prefetc...]
    select_n x2 -> x0, other arithmetic: 3.83 us -> none  [merge(): return jnp.where(z >= 2, *pair)]
    unnamed x54 -> x68, local copies, waits for them, and re-layouts: 13.3 us -> 15.5 us
  transfers between devices with their start and end apart: 32 -> 29, of which waited for: 6 -> 12; matrix products, arithmetic and copies ran while one was open for 8% -> 6% of each run, Pallas kernels for 43% -> 44%
where the time goes in v7:
time: 338 us; the launch traced here: 335 us
  Pallas kernels  157 us (46%)
  starting transfers between devices  68.4 us (20%)
  waiting for transfers between devices  54.3 us (16%)
  local copies, waits for them, and re-layouts  20.9 us (6%)
  other arithmetic  19.8 us (6%)
  between operations  14.8 us (4%)
    ppermute x26, starting transfers between devices, send(): return lax.ppermute(x, 'seq', pairs)  61.8 us
    ppermute x26, waiting for transfers between devices, send(): return lax.ppermute(x, 'seq', pairs)  54.2 us
    pallas_call x4, Pallas kernels, gate_grad(): pl.pallas_call(gate_kernel, grid_spec=pltpu.PrefetchScalarGridSpec(num_sc...  37.3 us
    pallas_call x4, Pallas kernels, weight_rows(): pl.pallas_call(functools.partial(rows_kernel, n), grid_spec=pltpu.Prefetc...  34 us
    pallas_call x2, Pallas kernels, middle(): pl.pallas_call(kernel, grid=(tiles,), in_specs=in_specs, out_specs=[here,...  25.2 us
    pallas_call x2, Pallas kernels, backward(): pl.pallas_call(backward_kernel, grid=(tiles,), in_specs=in_specs, out_spe...  20.9 us
    pallas_call x2, Pallas kernels, forward(): pl.pallas_call(forward_kernel, grid=(tiles,), in_specs=[here, here, here,...  20.3 us
    unnamed x68, local copies, waits for them, and re-layouts  15.5 us
  transfers between devices with their start and end apart: 29, of which 12 were waited for; matrix products, arithmetic and copies ran while one was open for 6% of the time, Pallas kernels for 44%

profile of v7, /device:TPU:10, one launch (start us, length us, event | category | flops | bytes accessed | tf_op | source)
XLA Modules:
  0.0 335.3 jit_solution(10206200160066038842)
XLA Ops:
  7.2 1.3 multiply_convert_fusion
  8.6 2.7 constant_dynamic-slice_fusion
  11.3 3.4 %collective-permute-start = (bf16[128,2048]{1,0:T(8,128)(2,1)S(1)}, bf16[128,2048]{1,0:T(8,128)(2,1)S(1)}, u32[]{:S(2)}, u32[]{:S(2)}) collective-permute-start(bf16[128,2048]{1,0:T(8,128)(2,1)S(1)} %multiply_convert_fusion), channel_id=1, source_target_pairs={{0,4},{4,8},{8,12},{12,16},{16,20},{20,24},{24,28},{1,5},{5,9},{9,... | collective-permute-start | bytes 1572872 | tf_op jit(solution)/shard_map/ppermute | solution.py:350
  15.1 10.4 %shard_map.101 = (bf16[16384,256]{1,0:T(8,128)(2,1)}, bf16[16384,256]{1,0:T(8,128)(2,1)}) custom-call(f32[128,256]{1,0:T(8,128)S(1)} %maximum_maximum_fusion.back_ref, f32[128,256]{1,0:T(8,128)S(1)} %concatenate.22.ahead_ref), custom_call_target="tpu_custom_call" | custom-call | flops 524288 | bytes 262144 | tf_op jit(solution)/shard_map/pallas_call | solution.py:54
  25.5 1.7 fusion.14
  27.8 3.5 %collective-permute-start.1 = (bf16[512,1024]{1,0:T(8,128)(2,1)S(1)}, bf16[512,1024]{1,0:T(8,128)(2,1)}, u32[]{:S(2)}, u32[]{:S(2)}) collective-permute-start(bf16[512,1024]{1,0:T(8,128)(2,1)S(1)} %get-tuple-element.85.refs_4_), channel_id=1, source_target_pairs={{0,8},{4,12},{8,16},{12,20},{16,24},{20,28},{1,9},{5,13},{9,17},{1... | collective-permute-start | bytes 3145736 | tf_op jit(solution)/shard_map/ppermute | solution.py:350
  31.3 3.4 %collective-permute-start.2 = (bf16[512,1024]{1,0:T(8,128)(2,1)S(1)}, bf16[512,1024]{1,0:T(8,128)(2,1)S(1)}, u32[]{:S(2)}, u32[]{:S(2)}) collective-permute-start(bf16[512,1024]{1,0:T(8,128)(2,1)S(1)} %get-tuple-element.85.refs_4_), channel_id=1, source_target_pairs={{8,0},{12,4},{16,8},{20,12},{24,16},{28,20},{9,1},{13,5},{17,9},{2... | collective-permute-start | bytes 3145736 | tf_op jit(solution)/shard_map/ppermute | solution.py:350
  35.7 9.9 %shard_map.102 = (bf16[1024,1024]{1,0:T(8,128)(2,1)S(1)}, bf16[1024,1024]{1,0:T(8,128)(2,1)S(1)}) custom-call(bf16[1024,2048]{1,0:T(8,128)(2,1)} %refs_1_.3, bf16[1024,2048]{1,0:T(8,128)(2,1)} %k.7, bf16[1024,2048]{1,0:T(8,128)(2,1)} %v.7, bf16[128,2048]{1,0:T(8,128)(2,1)S(1)} %collective-permute-done.prior.refs_5_, bf16[16384,256]{1,0:T(8,128)(2,1)} %get-tuple-element.88.table), custom_call_target="tpu_custom_call" | custom-call | flops 67108864 | bytes 229376 | tf_op jit(solution)/shard_map/pallas_call | solution.py:104
  45.7 1.4 copy-done.20
  47.1 1.3 copy-done.24
  48.4 5.5 %collective-permute-done.1.refs_5_ = bf16[512,1024]{1,0:T(8,128)(2,1)} collective-permute-done((bf16[512,1024]{1,0:T(8,128)(2,1)S(1)}, bf16[512,1024]{1,0:T(8,128)(2,1)}, u32[]{:S(2)}, u32[]{:S(2)}) %collective-permute-start.1) | collective-permute-done | bytes 1048608 | tf_op jit(solution)/shard_map/ppermute | solution.py:350
  53.9 3.1 collective-permute-done.2.refs_6_
  58.4 1.6 collective-permute-start.6
  60.0 2.4 collective-permute-start.7
  62.5 4.4 %collective-permute-start.8 = (bf16[512,1024]{1,0:T(8,128)(2,1)S(1)}, bf16[512,1024]{1,0:T(8,128)(2,1)}, u32[]{:S(2)}, u32[]{:S(2)}) collective-permute-start(bf16[512,1024]{1,0:T(8,128)(2,1)S(1)} %get-tuple-element.93.refs_4_), channel_id=1, source_target_pairs={{8,0},{12,4},{16,8},{20,12},{24,16},{28,20},{9,1},{13,5},{17,9},{2... | collective-permute-start | bytes 3145736 | tf_op jit(solution)/shard_map/ppermute | solution.py:350
  66.8 1.5 collective-permute-start.4
  68.4 1.9 collective-permute-start.5
  71.7 10.5 %shard_map.103 = (bf16[1024,1024]{1,0:T(8,128)(2,1)}, bf16[1024,1024]{1,0:T(8,128)(2,1)S(1)}) custom-call(bf16[1024,2048]{1,0:T(8,128)(2,1)} %refs_1_.3, bf16[1024,2048]{1,0:T(8,128)(2,1)} %k.7, bf16[1024,2048]{1,0:T(8,128)(2,1)} %v.7, bf16[128,2048]{1,0:T(8,128)(2,1)S(1)} %copy-done.15, bf16[16384,256]{1,0:T(8,128)(2,1)} %get-tuple-element.88.table), custom_call_target="tpu_custom_call" | custom-call | flops 67108864 | bytes 229376 | tf_op jit(solution)/shard_map/pallas_call | solution.py:104
  82.1 1.3 copy-done.21
  83.4 2.6 collective-permute-done.7.refs_5_
  86.0 4.5 %collective-permute-done.8.refs_6_ = bf16[512,1024]{1,0:T(8,128)(2,1)} collective-permute-done((bf16[512,1024]{1,0:T(8,128)(2,1)S(1)}, bf16[512,1024]{1,0:T(8,128)(2,1)}, u32[]{:S(2)}, u32[]{:S(2)}) %collective-permute-start.8) | collective-permute-done | bytes 1048608 | tf_op jit(solution)/shard_map/ppermute | solution.py:350
  90.6 2.3 collective-permute-start.10
  92.9 3.7 %collective-permute-start.11 = (bf16[512,1024]{1,0:T(8,128)(2,1)}, bf16[512,1024]{1,0:T(8,128)(2,1)}, u32[]{:S(2)}, u32[]{:S(2)}) collective-permute-start(bf16[512,1024]{1,0:T(8,128)(2,1)} %collective-permute-done.8.refs_6_), channel_id=1, source_target_pairs={{16,8},{20,12},{8,0},{12,4},{17,9},{21,13},{9,1},{13,5},{18,10},{2... | collective-permute-start | bytes 3145736 | tf_op jit(solution)/shard_map/ppermute | solution.py:350
  96.6 9.0 %shard_map.104.refs_2_ = f32[4,512,1024]{2,1,0:T(8,128)} custom-call(s32[4]{0:T(128)S(1)} %pad_add_fusion.pick, bf16[4,1024,512]{2,1,0:T(8,128)(2,1)} %bitcast.48, bf16[1024,1024]{1,0:T(8,128)(2,1)S(1)} %copy-done.25), custom_call_target="tpu_custom_call" | custom-call | flops 16777216 | bytes 49152 | tf_op jit(solution)/shard_map/pallas_call | solution.py:290
  105.6 3.0 collective-permute-done.4.refs_3_.refs_7_
  108.6 4.4 %collective-permute-done.5.refs_4_.refs_8_ = bf16[512,1024]{1,0:T(8,128)(2,1)S(1)} collective-permute-done((bf16[512,1024]{1,0:T(8,128)(2,1)}, bf16[512,1024]{1,0:T(8,128)(2,1)S(1)}, u32[]{:S(2)}, u32[]{:S(2)}) %collective-permute-start.5) | collective-permute-done | bytes 1048608 | tf_op jit(solution)/shard_map/ppermute | solution.py:350
  113.0 4.2 %shard_map.105 = (bf16[512,1024]{1,0:T(8,128)(2,1)S(1)}, bf16[512,1024]{1,0:T(8,128)(2,1)S(1)}) custom-call(s32[3]{0:T(128)S(1)} %pad_add_fusion.1.pick, bf16[4,1024,512]{2,1,0:T(8,128)(2,1)} %bitcast.36, bf16[1024,1024]{1,0:T(8,128)(2,1)} %collective-permute-done.6.refs_1_, f32[4,512,1024]{2,1,0:T(8,128)} %shard_map.104.refs_2_, ...), custom_call_target="tpu_custom_call" | custom-call | flops 16777216 | bytes 49152 | tf_op jit(solution)/shard_map/pallas_call | solution.py:324
  118.2 2.4 collective-permute-start.9
  121.1 7.6 %shard_map.106 = bf16[3,512,1024]{2,1,0:T(8,128)(2,1)S(1)} custom-call(s32[3]{0:T(128)S(1)} %pad_add_fusion.2.pick, bf16[4,1024,512]{2,1,0:T(8,128)(2,1)} %bitcast.37, bf16[1024,1024]{1,0:T(8,128)(2,1)} %collective-permute-done.6.refs_1_, f32[4,512,1024]{2,1,0:T(8,128)} %shard_map.104.refs_2_), custom_call_target="tpu_custom_call" | custom-call | flops 16777216 | bytes 49152 | tf_op jit(solution)/shard_map/pallas_call | solution.py:290
  128.8 6.7 %collective-permute-done.11.refs_4_.refs_8_ = bf16[512,1024]{1,0:T(8,128)(2,1)} collective-permute-done((bf16[512,1024]{1,0:T(8,128)(2,1)}, bf16[512,1024]{1,0:T(8,128)(2,1)}, u32[]{:S(2)}, u32[]{:S(2)}) %collective-permute-start.11) | collective-permute-done | bytes 1048608 | tf_op jit(solution)/shard_map/ppermute | solution.py:350
  135.5 9.7 %shard_map.107.refs_2_ = f32[4,512,1024]{2,1,0:T(8,128)} custom-call(s32[4]{0:T(128)S(1)} %pad_add_fusion.pick, bf16[4,1024,512]{2,1,0:T(8,128)(2,1)} %bitcast.49, bf16[1024,1024]{1,0:T(8,128)(2,1)} %get-tuple-element.116.refs_1_), custom_call_target="tpu_custom_call" | custom-call | flops 16777216 | bytes 49152 | tf_op jit(solution)/shard_map/pallas_call | solution.py:290
  145.2 9.1 %collective-permute-done.9.refs_9_ = bf16[512,1024]{1,0:T(8,128)(2,1)S(1)} collective-permute-done((bf16[512,1024]{1,0:T(8,128)(2,1)S(1)}, bf16[512,1024]{1,0:T(8,128)(2,1)S(1)}, u32[]{:S(2)}, u32[]{:S(2)}) %collective-permute-start.9) | collective-permute-done | bytes 1048608 | tf_op jit(solution)/shard_map/ppermute | solution.py:350
  155.3 1.4 fusion.13
  156.7 1.3 collective-permute-start.15
  158.0 1.9 collective-permute-start.16
  165.0 9.3 %shard_map.108 = bf16[1024,1024]{1,0:T(8,128)(2,1)} custom-call(s32[7]{0:T(128)S(1)} %stack.58.pick, bf16[4,1024,512]{2,1,0:T(8,128)(2,1)} %bitcast.38, bf16[4,1024,512]{2,1,0:T(8,128)(2,1)} %bitcast.39, bf16[4,1024,512]{2,1,0:T(8,128)(2,1)} %bitcast.40, bf16[4,1024,512]{2,1,0:T(8,128)(2,1)} %bitcast.41, bf16[512,1024]{1,0:T(8,128)(2,1)S(1)} %copy-done.8, ...), custom_call_target="tpu_custom_call" | custom-call | flops 67108864 | bytes 163840 | tf_op jit(solution)/shard_map/pallas_call | solution.py:249
  174.2 4.8 %shard_map.109 = (bf16[512,1024]{1,0:T(8,128)(2,1)S(1)}, bf16[512,1024]{1,0:T(8,128)(2,1)S(1)}) custom-call(s32[3]{0:T(128)S(1)} %pad_add_fusion.1.pick, bf16[4,1024,512]{2,1,0:T(8,128)(2,1)} %bitcast.42, bf16[1024,1024]{1,0:T(8,128)(2,1)} %collective-permute-done.12.refs_1_, f32[4,512,1024]{2,1,0:T(8,128)} %shard_map.107.refs_2_, ...), custom_call_target="tpu_custom_call" | custom-call | flops 16777216 | bytes 49152 | tf_op jit(solution)/shard_map/pallas_call | solution.py:324
  179.0 3.4 %collective-permute-start.14 = (bf16[512,1024]{1,0:T(8,128)(2,1)S(1)}, bf16[512,1024]{1,0:T(8,128)(2,1)S(1)}, u32[]{:S(2)}, u32[]{:S(2)}) collective-permute-start(bf16[512,1024]{1,0:T(8,128)(2,1)S(1)} %get-tuple-element.125), channel_id=1, source_target_pairs={{0,8},{4,12},{24,16},{28,20},{16,24},{20,28},{8,0},{12,4},{1,9},{5... | collective-permute-start | bytes 3145736 | tf_op jit(solution)/shard_map/ppermute | solution.py:350
  182.8 2.6 fusion.3
  185.4 1.9 collective-permute-start.17
  187.3 5.1 %collective-permute-start.18 = (bf16[512,1024]{1,0:T(8,128)(2,1)S(1)}, bf16[512,1024]{1,0:T(8,128)(2,1)}, u32[]{:S(2)}, u32[]{:S(2)}) collective-permute-start(bf16[512,1024]{1,0:T(8,128)(2,1)S(1)} %get-tuple-element.163), channel_id=1, source_target_pairs={{8,0},{12,4},{16,8},{20,12},{24,16},{28,20},{9,1},{13,5},{17,9},{2... | collective-permute-start | bytes 3145736 | tf_op jit(solution)/shard_map/ppermute | solution.py:350
  192.4 7.6 %shard_map.110 = bf16[3,512,1024]{2,1,0:T(8,128)(2,1)S(1)} custom-call(s32[3]{0:T(128)S(1)} %pad_add_fusion.2.pick, bf16[4,1024,512]{2,1,0:T(8,128)(2,1)} %bitcast.43, bf16[1024,1024]{1,0:T(8,128)(2,1)} %collective-permute-done.12.refs_1_, f32[4,512,1024]{2,1,0:T(8,128)} %shard_map.107.refs_2_), custom_call_target="tpu_custom_call" | custom-call | flops 16777216 | bytes 49152 | tf_op jit(solution)/shard_map/pallas_call | solution.py:290
  200.0 6.5 %collective-permute-done.14.refs_9_ = bf16[512,1024]{1,0:T(8,128)(2,1)S(1)} collective-permute-done((bf16[512,1024]{1,0:T(8,128)(2,1)S(1)}, bf16[512,1024]{1,0:T(8,128)(2,1)S(1)}, u32[]{:S(2)}, u32[]{:S(2)}) %collective-permute-start.14) | collective-permute-done | bytes 1048608 | tf_op jit(solution)/shard_map/ppermute | solution.py:350
  206.5 1.4 fusion.10
  207.9 1.3 collective-permute-start.21
  209.2 2.6 collective-permute-start.22
  211.8 9.4 %shard_map.113 = bf16[1024,1024]{1,0:T(8,128)(2,1)} custom-call(s32[7]{0:T(128)S(1)} %stack.58.pick, bf16[4,1024,512]{2,1,0:T(8,128)(2,1)} %bitcast.44, bf16[4,1024,512]{2,1,0:T(8,128)(2,1)} %bitcast.45, bf16[4,1024,512]{2,1,0:T(8,128)(2,1)} %bitcast.46, bf16[4,1024,512]{2,1,0:T(8,128)(2,1)} %bitcast.47, bf16[512,1024]{1,0:T(8,128)(2,1)S(1)} %copy-done.11, ...), custom_call_target="tpu_custom_call" | custom-call | flops 67108864 | bytes 163840 | tf_op jit(solution)/shard_map/pallas_call | solution.py:249
  221.2 7.9 %collective-permute-done.17 = bf16[512,1024]{1,0:T(8,128)(2,1)} collective-permute-done((bf16[512,1024]{1,0:T(8,128)(2,1)S(1)}, bf16[512,1024]{1,0:T(8,128)(2,1)}, u32[]{:S(2)}, u32[]{:S(2)}) %collective-permute-start.17) | collective-permute-done | bytes 1048608 | tf_op jit(solution)/shard_map/ppermute | solution.py:350
  229.4 9.4 %shard_map.112.own_ref = bf16[1024,1024]{1,0:T(8,128)(2,1)} custom-call(s32[7]{0:T(128)S(1)} %stack.58.pick, bf16[4,1024,512]{2,1,0:T(8,128)(2,1)} %bitcast.50, bf16[4,1024,512]{2,1,0:T(8,128)(2,1)} %bitcast.51, bf16[4,1024,512]{2,1,0:T(8,128)(2,1)} %bitcast.52, bf16[4,1024,512]{2,1,0:T(8,128)(2,1)} %bitcast.53, bf16[512,1024]{1,0:T(8,128)(2,1)S(1)} %copy-done.11, ...), custom_call_target="tpu_custom_call" | custom-call | flops 67108864 | bytes 163840 | tf_op jit(solution)/shard_map/pallas_call | solution.py:249
  238.8 9.2 %shard_map.111.own_ref = bf16[1024,1024]{1,0:T(8,128)(2,1)} custom-call(s32[7]{0:T(128)S(1)} %stack.58.pick, bf16[4,1024,512]{2,1,0:T(8,128)(2,1)} %bitcast.54, bf16[4,1024,512]{2,1,0:T(8,128)(2,1)} %bitcast.55, bf16[4,1024,512]{2,1,0:T(8,128)(2,1)} %bitcast.56, bf16[4,1024,512]{2,1,0:T(8,128)(2,1)} %bitcast.57, bf16[512,1024]{1,0:T(8,128)(2,1)S(1)} %copy-done.9, ...), custom_call_target="tpu_custom_call" | custom-call | flops 67108864 | bytes 163840 | tf_op jit(solution)/shard_map/pallas_call | solution.py:249
  248.1 1.6 copy-done.13
  249.7 12.6 %shard_map.114 = (bf16[1024,2048]{1,0:T(8,128)(2,1)}, bf16[1024,1024]{1,0:T(8,128)(2,1)S(1)}, bf16[128,1024]{1,0:T(8,128)(2,1)S(1)}, f32[64,256]{1,0:T(8,128)S(1)}) custom-call(bf16[1024,1024]{1,0:T(8,128)(2,1)S(1)} %copy-done.13, bf16[1024,1024]{1,0:T(8,128)(2,1)} %collective-permute-done.13.refs_0_, bf16[1024,2048]{1,0:T(8,128)(2,1)} %refs_1_.3, ...), custom_call_target="tpu_custom_call" | custom-call | flops 67108864 | bytes 294912 | tf_op jit(solution)/shard_map/pallas_call | solution.py:171
  262.3 4.8 %fusion.7 = (bf16[512,1024]{1,0:T(8,128)(2,1)}, bf16[512,1024]{1,0:T(8,128)(2,1)}) fusion(bf16[512,1024]{1,0:T(8,128)(2,1)} %collective-permute-done.21, bf16[512,1024]{1,0:T(8,128)(2,1)} %collective-permute-done.22, bf16[512,1024]{1,0:T(8,128)(2,1)S(1)} %copy-done.27, pred[]{:T(512)S(6)} %eq.15, bf16[3,512,1024]{2,1,0:T(8,128)(2,1)S(1)} %shard_map.110, ...), kind=kLoop, calls=%fused_computation.15 | loop fusion | flops 6291456 | bytes 6291458 | tf_op jit(solution)/shard_map/convert_element_type | solution.py:419
  267.1 2.6 collective-permute-start.23
  269.7 4.4 %collective-permute-start.24 = (bf16[512,1024]{1,0:T(8,128)(2,1)}, bf16[512,1024]{1,0:T(8,128)(2,1)}, u32[]{:S(2)}, u32[]{:S(2)}) collective-permute-start(bf16[512,1024]{1,0:T(8,128)(2,1)} %get-tuple-element.161), channel_id=1, source_target_pairs={{8,0},{12,4},{16,8},{20,12},{24,16},{28,20},{9,1},{13,5},{17,9},{2... | collective-permute-start | bytes 3145736 | tf_op jit(solution)/shard_map/ppermute | solution.py:350
  274.1 3.2 fusion.12
  277.2 2.4 collective-permute-start.25
  279.7 12.6 %shard_map.115 = (bf16[1024,2048]{1,0:T(8,128)(2,1)}, bf16[1024,1024]{1,0:T(8,128)(2,1)S(1)}, bf16[128,1024]{1,0:T(8,128)(2,1)S(1)}, f32[64,256]{1,0:T(8,128)S(1)}) custom-call(bf16[1024,1024]{1,0:T(8,128)(2,1)S(1)} %copy-done.12, bf16[1024,1024]{1,0:T(8,128)(2,1)} %collective-permute-done.19.refs_0_, ...), custom_call_target="tpu_custom_call", output_to_operand_aliasing={{0}: (7, {})} | custom-call | flops 67108864 | bytes 294912 | tf_op jit(solution)/shard_map/pallas_call | solution.py:171
  292.3 2.2 collective-permute-start.20
  295.5 6.5 %all-to-all-start = ((f32[8,16,128]{2,1,0:T(8,128)}), f32[8,16,128]{2,1,0:T(8,128)S(1)}, u32[]{:S(2)}, u32[]{:S(2)}) async-start(f32[8,16,128]{2,1,0:T(8,128)} %bitcast.20), calls=%async_computation | async-start | bytes 131072 | tf_op jit(solution)/shard_map/all_to_all | solution.py:531
  302.0 2.6 fusion.9
  304.6 1.5 pad_maximum_fusion
  307.0 10.4 %shard_map.116 = (bf16[1024,2048]{1,0:T(8,128)(2,1)}, bf16[1024,2048]{1,0:T(8,128)(2,1)}) custom-call(bf16[1024,1024]{1,0:T(8,128)(2,1)S(1)} %copy-done.23, bf16[128,1024]{1,0:T(8,128)(2,1)S(1)} %collective-permute-done.25.later, bf16[1024,2048]{1,0:T(8,128)(2,1)} %k.7, bf16[1024,2048]{1,0:T(8,128)(2,1)} %v.7, bf16[16384,256]{1,0:T(8,128)(2,1)} %get-tuple-element.144.table), custom_call_target="tpu_custom_call" | custom-call | flops 67108864 | bytes 229376 | tf_op jit(solution)/shard_map/pallas_call | solution.py:216
  318.0 10.4 %shard_map.117 = (bf16[1024,2048]{1,0:T(8,128)(2,1)}, bf16[1024,2048]{1,0:T(8,128)(2,1)}) custom-call(bf16[1024,1024]{1,0:T(8,128)(2,1)S(1)} %get-tuple-element.142.gm, bf16[128,1024]{1,0:T(8,128)(2,1)S(1)} %collective-permute-done.20.later, bf16[1024,2048]{1,0:T(8,128)(2,1)} %k.7, ...), custom_call_target="tpu_custom_call", output_to_operand_aliasing={{0}: (5, {}), {1}: (6, {})} | custom-call | flops 67108864 | bytes 229376 | tf_op jit(solution)/shard_map/pallas_call | solution.py:216
  (106 shorter events, 15.3 us)
Async XLA Ops:
  7.2 51.2 %all-gather.5.cloned.1.call-start = ((), (), s32[]{:S(2)}) async-start(), calls=%async_computation.1 | async-start | bytes 5242880 | tf_op jit(solution)/shard_map/all_gather | solution.py:445
  8.6 6.2 %copy-start.33 = (bf16[128,128]{1,0:T(8,128)(2,1)S(1)}, bf16[128,128]{1,0:T(8,128)(2,1)}, u32[]{:S(2)}) copy-start(bf16[128,128]{1,0:T(8,128)(2,1)} %param.9) | copy-start | bytes 98308
  11.3 101.7 %all-gather.7.cloned.1.call-start = ((), (), s32[]{:S(2)}) async-start(), calls=%async_computation.2 | async-start | bytes 5242880 | tf_op jit(solution)/shard_map/all_gather | solution.py:459
  11.3 16.5 %collective-permute-start = (bf16[128,2048]{1,0:T(8,128)(2,1)S(1)}, bf16[128,2048]{1,0:T(8,128)(2,1)S(1)}, u32[]{:S(2)}, u32[]{:S(2)}) collective-permute-start(bf16[128,2048]{1,0:T(8,128)(2,1)S(1)} %multiply_convert_fusion), channel_id=1, source_target_pairs={{0,4},{4,8},{8,12},{12,16},{16,20},{20,24},{24,28},{1,5},{5,9},{9,... | collective-permute-start | bytes 1572872 | tf_op jit(solution)/shard_map/ppermute | solution.py:350
  27.2 18.4 %copy-start.7 = (bf16[512,1024]{1,0:T(8,128)(2,1)}, bf16[512,1024]{1,0:T(8,128)(2,1)S(1)}, u32[]{:S(2)}) copy-start(bf16[512,1024]{1,0:T(8,128)(2,1)S(1)} %get-tuple-element.85.refs_4_) | copy-start | bytes 3145732
  27.3 35.2 %copy-start.10 = (bf16[512,1024]{1,0:T(8,128)(2,1)}, bf16[512,1024]{1,0:T(8,128)(2,1)S(1)}, u32[]{:S(2)}) copy-start(bf16[512,1024]{1,0:T(8,128)(2,1)S(1)} %get-tuple-element.93.refs_4_) | copy-start | bytes 3145732
  27.8 17.9 %copy-start.14 = (bf16[128,2048]{1,0:T(8,128)(2,1)}, bf16[128,2048]{1,0:T(8,128)(2,1)S(1)}, u32[]{:S(2)}) copy-start(bf16[128,2048]{1,0:T(8,128)(2,1)S(1)} %collective-permute-done.prior.refs_5_) | copy-start | bytes 1572868
  27.8 26.1 %collective-permute-start.1 = (bf16[512,1024]{1,0:T(8,128)(2,1)S(1)}, bf16[512,1024]{1,0:T(8,128)(2,1)}, u32[]{:S(2)}, u32[]{:S(2)}) collective-permute-start(bf16[512,1024]{1,0:T(8,128)(2,1)S(1)} %get-tuple-element.85.refs_4_), channel_id=1, source_target_pairs={{0,8},{4,12},{8,16},{12,20},{16,24},{20,28},{1,9},{5,13},{9,17},{1... | collective-permute-start | bytes 3145736 | tf_op jit(solution)/shard_map/ppermute | solution.py:350
  31.3 25.7 %collective-permute-start.2 = (bf16[512,1024]{1,0:T(8,128)(2,1)S(1)}, bf16[512,1024]{1,0:T(8,128)(2,1)S(1)}, u32[]{:S(2)}, u32[]{:S(2)}) collective-permute-start(bf16[512,1024]{1,0:T(8,128)(2,1)S(1)} %get-tuple-element.85.refs_4_), channel_id=1, source_target_pairs={{8,0},{12,4},{16,8},{20,12},{24,16},{28,20},{9,1},{13,5},{17,9},{2... | collective-permute-start | bytes 3145736 | tf_op jit(solution)/shard_map/ppermute | solution.py:350
  34.6 23.8 %collective-permute-start.3 = (bf16[1024,512]{1,0:T(8,128)(2,1)S(1)}, bf16[1024,512]{1,0:T(8,128)(2,1)}, u32[]{:S(2)}, u32[]{:S(2)}) collective-permute-start(bf16[1024,512]{1,0:T(8,128)(2,1)S(1)} %get-tuple-element.86), channel_id=1, source_target_pairs={{0,4},{4,0},{8,12},{12,8},{16,20},{20,16},{24,28},{28,24},{1,5},{5... | collective-permute-start | bytes 3145736 | tf_op jit(solution)/shard_map/ppermute | solution.py:350
  45.7 1.5 copy-start.20
  47.1 1.3 copy-start.24
  57.0 1.0 copy-start.17
  58.4 54.6 %collective-permute-start.6 = (bf16[1024,1024]{1,0:T(8,128)(2,1)}, bf16[1024,1024]{1,0:T(8,128)(2,1)}, u32[]{:S(2)}, u32[]{:S(2)}) collective-permute-start(bf16[1024,1024]{1,0:T(8,128)(2,1)} %copy-done.24), channel_id=1, source_target_pairs={{0,4},{4,0},{8,12},{12,8},{16,20},{20,16},{24,28},{28,24},{1,5},{5... | collective-permute-start | bytes 6291464 | tf_op jit(solution)/shard_map/ppermute | solution.py:350
  60.0 26.0 %collective-permute-start.7 = (bf16[512,1024]{1,0:T(8,128)(2,1)S(1)}, bf16[512,1024]{1,0:T(8,128)(2,1)}, u32[]{:S(2)}, u32[]{:S(2)}) collective-permute-start(bf16[512,1024]{1,0:T(8,128)(2,1)S(1)} %get-tuple-element.93.refs_4_), channel_id=1, source_target_pairs={{0,8},{4,12},{8,16},{12,20},{16,24},{20,28},{1,9},{5,13},{9,17},{1... | collective-permute-start | bytes 3145736 | tf_op jit(solution)/shard_map/ppermute | solution.py:350
  62.5 28.1 %collective-permute-start.8 = (bf16[512,1024]{1,0:T(8,128)(2,1)S(1)}, bf16[512,1024]{1,0:T(8,128)(2,1)}, u32[]{:S(2)}, u32[]{:S(2)}) collective-permute-start(bf16[512,1024]{1,0:T(8,128)(2,1)S(1)} %get-tuple-element.93.refs_4_), channel_id=1, source_target_pairs={{8,0},{12,4},{16,8},{20,12},{24,16},{28,20},{9,1},{13,5},{17,9},{2... | collective-permute-start | bytes 3145736 | tf_op jit(solution)/shard_map/ppermute | solution.py:350
  66.8 41.8 %collective-permute-start.4 = (bf16[512,1024]{1,0:T(8,128)(2,1)}, bf16[512,1024]{1,0:T(8,128)(2,1)S(1)}, u32[]{:S(2)}, u32[]{:S(2)}) collective-permute-start(bf16[512,1024]{1,0:T(8,128)(2,1)} %collective-permute-done.1.refs_5_), channel_id=1, source_target_pairs={{8,16},{12,20},{16,24},{20,28},{9,17},{13,21},{17,25},{21,29},{10,... | collective-permute-start | bytes 3145736 | tf_op jit(solution)/shard_map/ppermute | solution.py:350
  68.4 44.6 %collective-permute-start.5 = (bf16[512,1024]{1,0:T(8,128)(2,1)}, bf16[512,1024]{1,0:T(8,128)(2,1)S(1)}, u32[]{:S(2)}, u32[]{:S(2)}) collective-permute-start(bf16[512,1024]{1,0:T(8,128)(2,1)} %copy-done.17), channel_id=1, source_target_pairs={{16,8},{20,12},{8,0},{12,4},{17,9},{21,13},{9,1},{13,5},{18,10},{2... | collective-permute-start | bytes 3145736 | tf_op jit(solution)/shard_map/ppermute | solution.py:350
  70.6 1.1 copy-start.15
  71.7 24.9 %copy-start.25 = (bf16[1024,1024]{1,0:T(8,128)(2,1)S(1)}, bf16[1024,1024]{1,0:T(8,128)(2,1)}, u32[]{:S(2)}) copy-start(bf16[1024,1024]{1,0:T(8,128)(2,1)} %copy-done.24) | copy-start | bytes 6291460
  82.1 1.3 copy-start.21
  90.6 38.2 %collective-permute-start.10 = (bf16[512,1024]{1,0:T(8,128)(2,1)}, bf16[512,1024]{1,0:T(8,128)(2,1)}, u32[]{:S(2)}, u32[]{:S(2)}) collective-permute-start(bf16[512,1024]{1,0:T(8,128)(2,1)} %collective-permute-done.7.refs_5_), channel_id=1, source_target_pairs={{8,16},{12,20},{16,24},{20,28},{9,17},{13,21},{17,25},{21,29},{10,... | collective-permute-start | bytes 3145736 | tf_op jit(solution)/shard_map/ppermute | solution.py:350
  92.9 42.6 %collective-permute-start.11 = (bf16[512,1024]{1,0:T(8,128)(2,1)}, bf16[512,1024]{1,0:T(8,128)(2,1)}, u32[]{:S(2)}, u32[]{:S(2)}) collective-permute-start(bf16[512,1024]{1,0:T(8,128)(2,1)} %collective-permute-done.8.refs_6_), channel_id=1, source_target_pairs={{16,8},{20,12},{8,0},{12,4},{17,9},{21,13},{9,1},{13,5},{18,10},{2... | collective-permute-start | bytes 3145736 | tf_op jit(solution)/shard_map/ppermute | solution.py:350
  108.6 8.6 %copy-start.1 = (bf16[512,1024]{1,0:T(8,128)(2,1)}, bf16[512,1024]{1,0:T(8,128)(2,1)S(1)}, u32[]{:S(2)}) copy-start(bf16[512,1024]{1,0:T(8,128)(2,1)S(1)} %collective-permute-done.4.refs_3_.refs_7_) | copy-start | bytes 3145732
  113.0 4.2 %copy-start.4 = (bf16[512,1024]{1,0:T(8,128)(2,1)}, bf16[512,1024]{1,0:T(8,128)(2,1)S(1)}, u32[]{:S(2)}) copy-start(bf16[512,1024]{1,0:T(8,128)(2,1)S(1)} %collective-permute-done.5.refs_4_.refs_8_) | copy-start | bytes 3145732
  117.2 1.0 copy-start.28
  118.2 36.2 %collective-permute-start.9 = (bf16[512,1024]{1,0:T(8,128)(2,1)S(1)}, bf16[512,1024]{1,0:T(8,128)(2,1)S(1)}, u32[]{:S(2)}, u32[]{:S(2)}) collective-permute-start(bf16[512,1024]{1,0:T(8,128)(2,1)S(1)} %get-tuple-element.107), channel_id=1, source_target_pairs={{0,8},{4,12},{24,16},{28,20},{16,24},{20,28},{8,0},{12,4},{1,9},{5... | collective-permute-start | bytes 3145736 | tf_op jit(solution)/shard_map/ppermute | solution.py:350
  120.5 53.7 %collective-permute-start.12 = (bf16[1024,1024]{1,0:T(8,128)(2,1)}, bf16[1024,1024]{1,0:T(8,128)(2,1)}, u32[]{:S(2)}, u32[]{:S(2)}) collective-permute-start(bf16[1024,1024]{1,0:T(8,128)(2,1)} %get-tuple-element.116.refs_1_), channel_id=1, source_target_pairs={{0,4},{4,0},{8,12},{12,8},{16,20},{20,16},{24,28},{28,24},{1,5},{5... | collective-permute-start | bytes 6291464 | tf_op jit(solution)/shard_map/ppermute | solution.py:350
  154.3 1.0 copy-start.30
  156.7 26.0 %collective-permute-start.15 = (bf16[512,1024]{1,0:T(8,128)(2,1)}, bf16[512,1024]{1,0:T(8,128)(2,1)}, u32[]{:S(2)}, u32[]{:S(2)}) collective-permute-start(bf16[512,1024]{1,0:T(8,128)(2,1)} %fusion.13), channel_id=1, source_target_pairs={{0,8},{4,12},{24,16},{28,20},{1,9},{5,13},{25,17},{29,21},{2,10},{... | collective-permute-start | bytes 3145736 | tf_op jit(solution)/shard_map/ppermute | solution.py:350
  158.0 24.7 %collective-permute-start.16 = (bf16[512,1024]{1,0:T(8,128)(2,1)}, bf16[512,1024]{1,0:T(8,128)(2,1)}, u32[]{:S(2)}, u32[]{:S(2)}) collective-permute-start(bf16[512,1024]{1,0:T(8,128)(2,1)} %fusion.13), channel_id=1, source_target_pairs={{8,16},{12,20},{16,8},{20,12},{9,17},{13,21},{17,9},{21,13},{10,18... | collective-permute-start | bytes 3145736 | tf_op jit(solution)/shard_map/ppermute | solution.py:350
  160.1 1.2 copy-start.2
  161.3 1.2 copy-start.5
  162.5 1.2 copy-start.8
  163.7 1.2 copy-start.18
  174.2 8.5 %copy-start.29 = (bf16[512,1024]{1,0:T(8,128)(2,1)S(1)}, bf16[512,1024]{1,0:T(8,128)(2,1)}, u32[]{:S(2)}) copy-start(bf16[512,1024]{1,0:T(8,128)(2,1)} %copy-done.28) | copy-start | bytes 3145732
  179.0 6.3 %copy-start.26 = (bf16[512,1024]{1,0:T(8,128)(2,1)}, bf16[512,1024]{1,0:T(8,128)(2,1)S(1)}, u32[]{:S(2)}) copy-start(bf16[512,1024]{1,0:T(8,128)(2,1)S(1)} %get-tuple-element.145) | copy-start | bytes 3145732
  179.0 27.5 %collective-permute-start.14 = (bf16[512,1024]{1,0:T(8,128)(2,1)S(1)}, bf16[512,1024]{1,0:T(8,128)(2,1)S(1)}, u32[]{:S(2)}, u32[]{:S(2)}) collective-permute-start(bf16[512,1024]{1,0:T(8,128)(2,1)S(1)} %get-tuple-element.125), channel_id=1, source_target_pairs={{0,8},{4,12},{24,16},{28,20},{16,24},{20,28},{8,0},{12,4},{1,9},{5... | collective-permute-start | bytes 3145736 | tf_op jit(solution)/shard_map/ppermute | solution.py:350
  182.4 65.6 %collective-permute-start.13 = (bf16[1024,1024]{1,0:T(8,128)(2,1)}, bf16[1024,1024]{1,0:T(8,128)(2,1)}, u32[]{:S(2)}, u32[]{:S(2)}) collective-permute-start(bf16[1024,1024]{1,0:T(8,128)(2,1)} %shard_map.108), channel_id=1, source_target_pairs={{0,4},{4,0},{8,12},{12,8},{16,20},{20,16},{24,28},{28,24},{1,5},{5... | collective-permute-start | bytes 6291464 | tf_op jit(solution)/shard_map/ppermute | solution.py:350
  185.4 43.7 %collective-permute-start.17 = (bf16[512,1024]{1,0:T(8,128)(2,1)S(1)}, bf16[512,1024]{1,0:T(8,128)(2,1)}, u32[]{:S(2)}, u32[]{:S(2)}) collective-permute-start(bf16[512,1024]{1,0:T(8,128)(2,1)S(1)} %get-tuple-element.164), channel_id=1, source_target_pairs={{0,8},{4,12},{8,16},{12,20},{16,24},{20,28},{1,9},{5,13},{9,17},{1... | collective-permute-start | bytes 3145736 | tf_op jit(solution)/shard_map/ppermute | solution.py:350
  187.3 41.8 %collective-permute-start.18 = (bf16[512,1024]{1,0:T(8,128)(2,1)S(1)}, bf16[512,1024]{1,0:T(8,128)(2,1)}, u32[]{:S(2)}, u32[]{:S(2)}) collective-permute-start(bf16[512,1024]{1,0:T(8,128)(2,1)S(1)} %get-tuple-element.163), channel_id=1, source_target_pairs={{8,0},{12,4},{16,8},{20,12},{24,16},{28,20},{9,1},{13,5},{17,9},{2... | collective-permute-start | bytes 3145736 | tf_op jit(solution)/shard_map/ppermute | solution.py:350
  200.0 62.3 %copy-start = (bf16[3,512,1024]{2,1,0:T(8,128)(2,1)}, bf16[3,512,1024]{2,1,0:T(8,128)(2,1)S(1)}, u32[]{:S(2)}) copy-start(bf16[3,512,1024]{2,1,0:T(8,128)(2,1)S(1)} %shard_map.110) | copy-start | bytes 9437188
  200.0 11.8 %copy-start.11 = (bf16[512,1024]{1,0:T(8,128)(2,1)S(1)}, bf16[512,1024]{1,0:T(8,128)(2,1)}, u32[]{:S(2)}) copy-start(bf16[512,1024]{1,0:T(8,128)(2,1)} %copy-done.10) | copy-start | bytes 3145732
  206.5 5.3 %copy-start.31 = (bf16[512,1024]{1,0:T(8,128)(2,1)}, bf16[512,1024]{1,0:T(8,128)(2,1)S(1)}, u32[]{:S(2)}) copy-start(bf16[512,1024]{1,0:T(8,128)(2,1)S(1)} %collective-permute-done.14.refs_9_) | copy-start | bytes 3145732
  207.9 54.4 %collective-permute-start.21 = (bf16[512,1024]{1,0:T(8,128)(2,1)}, bf16[512,1024]{1,0:T(8,128)(2,1)}, u32[]{:S(2)}, u32[]{:S(2)}) collective-permute-start(bf16[512,1024]{1,0:T(8,128)(2,1)} %fusion.10), channel_id=1, source_target_pairs={{0,8},{4,12},{24,16},{28,20},{1,9},{5,13},{25,17},{29,21},{2,10},{... | collective-permute-start | bytes 3145736 | tf_op jit(solution)/shard_map/ppermute | solution.py:350
  209.2 53.1 %collective-permute-start.22 = (bf16[512,1024]{1,0:T(8,128)(2,1)}, bf16[512,1024]{1,0:T(8,128)(2,1)}, u32[]{:S(2)}, u32[]{:S(2)}) collective-permute-start(bf16[512,1024]{1,0:T(8,128)(2,1)} %fusion.10), channel_id=1, source_target_pairs={{8,16},{12,20},{16,8},{20,12},{9,17},{13,21},{17,9},{21,13},{10,18... | collective-permute-start | bytes 3145736 | tf_op jit(solution)/shard_map/ppermute | solution.py:350
  221.2 17.6 %copy-start.3 = (bf16[512,1024]{1,0:T(8,128)(2,1)S(1)}, bf16[512,1024]{1,0:T(8,128)(2,1)}, u32[]{:S(2)}) copy-start(bf16[512,1024]{1,0:T(8,128)(2,1)} %copy-done.1) | copy-start | bytes 3145732
  221.2 17.6 %copy-start.6 = (bf16[512,1024]{1,0:T(8,128)(2,1)S(1)}, bf16[512,1024]{1,0:T(8,128)(2,1)}, u32[]{:S(2)}) copy-start(bf16[512,1024]{1,0:T(8,128)(2,1)} %copy-done.4) | copy-start | bytes 3145732
  221.2 17.6 %copy-start.9 = (bf16[512,1024]{1,0:T(8,128)(2,1)S(1)}, bf16[512,1024]{1,0:T(8,128)(2,1)}, u32[]{:S(2)}) copy-start(bf16[512,1024]{1,0:T(8,128)(2,1)} %copy-done.7) | copy-start | bytes 3145732
  221.2 17.6 %copy-start.19 = (bf16[512,1024]{1,0:T(8,128)(2,1)S(1)}, bf16[512,1024]{1,0:T(8,128)(2,1)}, u32[]{:S(2)}) copy-start(bf16[512,1024]{1,0:T(8,128)(2,1)} %copy-done.17) | copy-start | bytes 3145732
  229.1 50.6 %collective-permute-start.19 = (bf16[1024,1024]{1,0:T(8,128)(2,1)}, bf16[1024,1024]{1,0:T(8,128)(2,1)}, u32[]{:S(2)}, u32[]{:S(2)}) collective-permute-start(bf16[1024,1024]{1,0:T(8,128)(2,1)} %shard_map.113), channel_id=1, source_target_pairs={{0,4},{4,0},{8,12},{12,8},{16,20},{20,16},{24,28},{28,24},{1,5},{5... | collective-permute-start | bytes 6291464 | tf_op jit(solution)/shard_map/ppermute | solution.py:350
  238.8 9.3 %copy-start.16 = (bf16[128,2048]{1,0:T(8,128)(2,1)S(1)}, bf16[128,2048]{1,0:T(8,128)(2,1)}, u32[]{:S(2)}) copy-start(bf16[128,2048]{1,0:T(8,128)(2,1)} %copy-done.14) | copy-start | bytes 1572868
  248.1 1.6 copy-start.13
  249.7 12.7 %copy-start.27 = (bf16[512,1024]{1,0:T(8,128)(2,1)S(1)}, bf16[512,1024]{1,0:T(8,128)(2,1)}, u32[]{:S(2)}) copy-start(bf16[512,1024]{1,0:T(8,128)(2,1)} %copy-done.26) | copy-start | bytes 3145732
  262.3 4.8 %copy-start.22 = (bf16[1024,1024]{1,0:T(8,128)(2,1)}, bf16[1024,1024]{1,0:T(8,128)(2,1)S(1)}, u32[]{:S(2)}) copy-start(bf16[1024,1024]{1,0:T(8,128)(2,1)S(1)} %get-tuple-element.151.gm) | copy-start | bytes 6291460
  267.1 34.9 %collective-permute-start.23 = (bf16[512,1024]{1,0:T(8,128)(2,1)}, bf16[512,1024]{1,0:T(8,128)(2,1)}, u32[]{:S(2)}, u32[]{:S(2)}) collective-permute-start(bf16[512,1024]{1,0:T(8,128)(2,1)} %get-tuple-element.162), channel_id=1, source_target_pairs={{0,8},{4,12},{8,16},{12,20},{16,24},{20,28},{1,9},{5,13},{9,17},{1... | collective-permute-start | bytes 3145736 | tf_op jit(solution)/shard_map/ppermute | solution.py:350
  269.7 10.0 %copy-start.12 = (bf16[1024,1024]{1,0:T(8,128)(2,1)S(1)}, bf16[1024,1024]{1,0:T(8,128)(2,1)}, u32[]{:S(2)}) copy-start(bf16[1024,1024]{1,0:T(8,128)(2,1)} %shard_map.112.own_ref) | copy-start | bytes 6291460
  269.7 32.3 %collective-permute-start.24 = (bf16[512,1024]{1,0:T(8,128)(2,1)}, bf16[512,1024]{1,0:T(8,128)(2,1)}, u32[]{:S(2)}, u32[]{:S(2)}) collective-permute-start(bf16[512,1024]{1,0:T(8,128)(2,1)} %get-tuple-element.161), channel_id=1, source_target_pairs={{8,0},{12,4},{16,8},{20,12},{24,16},{28,20},{9,1},{13,5},{17,9},{2... | collective-permute-start | bytes 3145736 | tf_op jit(solution)/shard_map/ppermute | solution.py:350
  277.2 28.9 %collective-permute-start.25 = (bf16[128,1024]{1,0:T(8,128)(2,1)S(1)}, bf16[128,1024]{1,0:T(8,128)(2,1)S(1)}, u32[]{:S(2)}, u32[]{:S(2)}) collective-permute-start(bf16[128,1024]{1,0:T(8,128)(2,1)S(1)} %get-tuple-element.147), channel_id=1, source_target_pairs={{4,0},{8,4},{12,8},{16,12},{20,16},{24,20},{28,24},{5,1},{9,5},{13... | collective-permute-start | bytes 786440 | tf_op jit(solution)/shard_map/ppermute | solution.py:350
  292.3 25.7 %collective-permute-start.20 = (bf16[128,1024]{1,0:T(8,128)(2,1)S(1)}, bf16[128,1024]{1,0:T(8,128)(2,1)S(1)}, u32[]{:S(2)}, u32[]{:S(2)}) collective-permute-start(bf16[128,1024]{1,0:T(8,128)(2,1)S(1)} %get-tuple-element.143), channel_id=1, source_target_pairs={{4,0},{8,4},{12,8},{16,12},{20,16},{24,20},{28,24},{5,1},{9,5},{13... | collective-permute-start | bytes 786440 | tf_op jit(solution)/shard_map/ppermute | solution.py:350
  295.5 21.9 %all-to-all-start = ((f32[8,16,128]{2,1,0:T(8,128)}), f32[8,16,128]{2,1,0:T(8,128)S(1)}, u32[]{:S(2)}, u32[]{:S(2)}) async-start(f32[8,16,128]{2,1,0:T(8,128)} %bitcast.20), calls=%async_computation | async-start | bytes 131072 | tf_op jit(solution)/shard_map/all_to_all | solution.py:531
  302.0 2.6 copy-start.32
  304.6 2.3 copy-start.23
Sparse Core Ops, SparseCore 0:
  11.4 34.6 all-gather.4
  58.5 32.8 all-gather.6

commit v8 on v7

--- a/solution.py
+++ b/solution.py
@@ -225,42 +225,55 @@
     )(*args)
 
 
-def gate_kernel(pick, *refs):
-    own, up, down, up2, down2, third, out = refs[LINE:]
-    slots = (
-        own[...],
-        jnp.where(pick[LINE] == 1, down[...], up[...]),
-        jnp.where(pick[LINE + 1] == 1, up2[...], down2[...]),
-        jnp.where(pick[LINE + 2] == 1, third[...], down[...]),
-    )
-    cot = jnp.concatenate([ref[0] for ref in refs[:LINE]], axis=1)
-    total = jnp.dot(cot, jnp.concatenate(slots, axis=0), preferred_element_type=F32)
+def gate_kernel(slots, pick, *refs):
+    out = refs[-1]
+    cots, refs = refs[: len(slots)], list(refs[len(slots) : -1])
+    blocks = []
+    for slot in slots:
+        block = refs.pop(0)[...]
+        if slot:
+            block = jnp.where(pick[LINE + slot - 1] == 1, block, refs.pop(0)[...])
+        blocks.append(block)
+    cot, block = cots[0][0], blocks[0]
+    if len(slots) > 1:
+        cot = jnp.concatenate([ref[0] for ref in cots], axis=1)
+        block = jnp.concatenate(blocks, axis=0)
+    total = jnp.dot(cot, block, preferred_element_type=F32)
+    if refs:
+        total = total + refs[0][...].astype(F32)
     out[...] = total.astype(out.dtype)
 
 
-def gate_grad(pick, cot, weights):
+def gate_grad(pick, cot, weights, slots=(0, 1, 2, 3), base=None):
     _, rows, depth = cot.shape
-    width = weights[0].shape[1]
+    width = weights[0][0].shape[1]
     tile = min(256, width)
 
     def cot_spec(j):
         return pl.BlockSpec((1, rows, depth), lambda i, pick: (pick[j], 0, 0))
 
-    return pl.pallas_call(
-        gate_kernel,
+    blocks = [x for slot in slots for x in weights[slot]]
+    part = pl.BlockSpec((rows, tile), lambda i, pick: (0, i))
+    in_specs = [cot_spec(j) for j in slots]
+    in_specs += [pl.BlockSpec((depth, tile), lambda i, pick: (0, i))] * len(blocks)
+    args = [cot] * len(slots) + blocks
+    if base is not None:
+        in_specs.append(part)
+        args.append(base)
+    return pl.pallas_call(
+        functools.partial(gate_kernel, slots),
         grid_spec=pltpu.PrefetchScalarGridSpec(
             num_scalar_prefetch=1,
             grid=(width // tile,),
-            in_specs=[cot_spec(j) for j in range(LINE)]
-            + [pl.BlockSpec((depth, tile), lambda i, pick: (0, i))] * len(weights),
-            out_specs=pl.BlockSpec((rows, tile), lambda i, pick: (0, i)),
+            in_specs=in_specs,
+            out_specs=part,
         ),
         out_shape=jax.ShapeDtypeStruct((rows, width), BF16),
         compiler_params=params(),
         cost_estimate=cost(
-            2 * rows * LINE * depth * width, 2 * LINE * depth * (rows + width) + 2 * rows * width
+            2 * rows * len(slots) * depth * width, 2 * len(slots) * depth * (rows + width)
         ),
-    )(pick, *([cot] * LINE), *weights)
+    )(pick, *args)
 
 
 def rows_kernel(n, pick, *refs):
@@ -377,7 +390,7 @@
     ).astype(jnp.int32)
 
     def weights(h):
-        return [halves[h], up1[h], down1[h], *second[h], third[h]]
+        return [[halves[h]], [down1[h], up1[h]], second[h], [third[h], down1[h]]]
 
     def swap_gated(h):
         return [around_inner(gateds[h], r) for r in range(1, inner)]
@@ -479,15 +492,19 @@
     for h in later_halves:
         got[h] = swap_gated(h)
     rest[0] = rows_rest(0)
-    second, rest[0], gateds = fence(second, rest[0], gateds)
+    begun = [gate_grad(pick, cot, weights(0), (0, 1, 2)) for cot in cots[1:]]
+    second, rest[0], gateds, begun = fence(second, rest[0], gateds, begun)
     for h in later_halves:
         base[h] = rows_own(h)
-    third[0], second, base = fence(third[0], second, base)
+    own_begun = gate_grad(pick, cots[0], weights(0), (0, 1, 2))
+    third[0], second, base, own_begun = fence(third[0], second, base, own_begun)
 
     sums[0] = send_second(0, third[0])
 
-    parts[0] = shares(0)
-    parts[0], got[1:] = fence(parts[0], got[1:])
+    parts[0] = [
+        gate_grad(pick, cot, weights(0), (3,), x) for cot, x in zip(cots[1:], begun)
+    ]
+    parts[0], got[1:], own_begun = fence(parts[0], got[1:], own_begun)
     others[0] = send_shares(parts[0])
 
     for h in later_halves:
@@ -496,15 +513,17 @@
     sums[0] = send_third(0, *sums[0])
     for h in later_halves:
         rest[h] = rows_rest(h)
-    third, rest[1:] = fence(third, rest[1:])
+    owns[0] = gate_grad(pick, cots[0], weights(0), (3,), own_begun)
+    third, rest[1:], owns[0] = fence(third, rest[1:], owns[0])
 
     for h in later_halves:
         parts[h] = shares(h)
-    parts[1:], sums = fence(parts[1:], sums)
+    parts[1:], third = fence(parts[1:], third)
     for h in later_halves:
         others[h] = send_shares(parts[h])
         sums[h] = send_second(h, third[h])
-    owns = [gate_grad(pick, cots[0], weights(h)) for h in each]
+    for h in later_halves:
+        owns[h] = gate_grad(pick, cots[0], weights(h))
     others[0], owns = fence(others[0], owns)
 
     grad_queries = None

time: 338 us -> 327 us (0.967)
  waiting for transfers between devices: 54.3 us -> 40.4 us
  Pallas kernels: 157 us -> 164 us
  local copies, waits for them, and re-layouts: 20.9 us -> 16.8 us
    ppermute x26, waiting for transfers between devices: 54.2 us -> 40.3 us  [send(): return lax.ppermute(x, 'seq', pairs)]
    pallas_call x4 -> x6, Pallas kernels: 37.3 us -> 44.4 us  [gate_grad(): pl.pallas_call(functools.partial(gate_kernel, slots), grid_spec=pltpu.Pre...]
    unnamed x68 -> x46, local copies, waits for them, and re-layouts: 15.5 us -> 10.4 us
    convert_element_type x0 -> x1, other arithmetic: none -> 3.91 us  [send_third(): up.astype(BF16)]
    convert_element_type x2 -> x1, other arithmetic: 7.36 us -> 4.02 us  [send_third(): down.astype(BF16)]
  transfers between devices with their start and end apart: 29 -> 29, of which waited for: 12 -> 11; matrix products, arithmetic and copies ran while one was open for 6% -> 8% of each run, Pallas kernels for 44% -> 46%
where the time goes in v8:
time: 327 us; the launch traced here: 325 us
  Pallas kernels  164 us (50%)
  starting transfers between devices  66.2 us (20%)
  waiting for transfers between devices  40.4 us (12%)
  other arithmetic  22.9 us (7%)
  local copies, waits for them, and re-layouts  16.8 us (5%)
  between operations  14.6 us (4%)
    ppermute x26, starting transfers between devices, send(): return lax.ppermute(x, 'seq', pairs)  61.1 us
    pallas_call x6, Pallas kernels, gate_grad(): pl.pallas_call(functools.partial(gate_kernel, slots), grid_spec=pltpu.Pre...  44.4 us
    ppermute x26, waiting for transfers between devices, send(): return lax.ppermute(x, 'seq', pairs)  40.3 us
    pallas_call x4, Pallas kernels, weight_rows(): pl.pallas_call(functools.partial(rows_kernel, n), grid_spec=pltpu.Prefetc...  33.3 us
    pallas_call x2, Pallas kernels, middle(): pl.pallas_call(kernel, grid=(tiles,), in_specs=in_specs, out_specs=[here,...  25.2 us
    pallas_call x2, Pallas kernels, backward(): pl.pallas_call(backward_kernel, grid=(tiles,), in_specs=in_specs, out_spe...  20.9 us
    pallas_call x2, Pallas kernels, forward(): pl.pallas_call(forward_kernel, grid=(tiles,), in_specs=[here, here, here,...  19.9 us
    pallas_call x1, Pallas kernels, tables(): pl.pallas_call(table_kernel, grid=(groups // GPT,), in_specs=[seed, seed]...  10.4 us
  transfers between devices with their start and end apart: 29, of which 11 were waited for; matrix products, arithmetic and copies ran while one was open for 8% of the time, Pallas kernels for 46%

profile of v8, /device:TPU:10, one launch (start us, length us, event | category | flops | bytes accessed | tf_op | source)
XLA Modules:
  0.0 324.9 jit_solution(5032187098596010782)
XLA Ops:
  7.2 1.3 multiply_convert_fusion
  8.6 2.7 constant_dynamic-slice_fusion
  11.3 3.4 %collective-permute-start = (bf16[128,2048]{1,0:T(8,128)(2,1)S(1)}, bf16[128,2048]{1,0:T(8,128)(2,1)S(1)}, u32[]{:S(2)}, u32[]{:S(2)}) collective-permute-start(bf16[128,2048]{1,0:T(8,128)(2,1)S(1)} %multiply_convert_fusion), channel_id=1, source_target_pairs={{0,4},{4,8},{8,12},{12,16},{16,20},{20,24},{24,28},{1,5},{5,9},{9,... | collective-permute-start | bytes 1572872 | tf_op jit(solution)/shard_map/ppermute | solution.py:363
  15.1 10.4 %shard_map.101 = (bf16[16384,256]{1,0:T(8,128)(2,1)}, bf16[16384,256]{1,0:T(8,128)(2,1)}) custom-call(f32[128,256]{1,0:T(8,128)S(1)} %maximum_maximum_fusion.back_ref, f32[128,256]{1,0:T(8,128)S(1)} %concatenate.22.ahead_ref), custom_call_target="tpu_custom_call" | custom-call | flops 524288 | bytes 262144 | tf_op jit(solution)/shard_map/pallas_call | solution.py:54
  25.5 2.8 fusion.14
  28.2 3.5 %collective-permute-start.1 = (bf16[512,1024]{1,0:T(8,128)(2,1)S(1)}, bf16[512,1024]{1,0:T(8,128)(2,1)S(1)}, u32[]{:S(2)}, u32[]{:S(2)}) collective-permute-start(bf16[512,1024]{1,0:T(8,128)(2,1)S(1)} %get-tuple-element.85.refs_3_), channel_id=1, source_target_pairs={{0,8},{4,12},{8,16},{12,20},{16,24},{20,28},{1,9},{5,13},{9,17},{1... | collective-permute-start | bytes 3145736 | tf_op jit(solution)/shard_map/ppermute | solution.py:363
  31.7 2.4 collective-permute-start.2
  34.2 1.6 collective-permute-start.3
  35.7 9.9 %shard_map.102 = (bf16[1024,1024]{1,0:T(8,128)(2,1)S(1)}, bf16[1024,1024]{1,0:T(8,128)(2,1)S(1)}) custom-call(bf16[1024,2048]{1,0:T(8,128)(2,1)} %refs_1_.3, bf16[1024,2048]{1,0:T(8,128)(2,1)} %k.7, bf16[1024,2048]{1,0:T(8,128)(2,1)} %v.7, bf16[128,2048]{1,0:T(8,128)(2,1)S(1)} %collective-permute-done.prior.refs_5_, bf16[16384,256]{1,0:T(8,128)(2,1)} %get-tuple-element.88.table), custom_call_target="tpu_custom_call" | custom-call | flops 67108864 | bytes 229376 | tf_op jit(solution)/shard_map/pallas_call | solution.py:104
  45.7 1.4 copy-done.11
  47.1 1.3 copy-done.13
  48.4 6.4 %collective-permute-done.1.refs_5_ = bf16[512,1024]{1,0:T(8,128)(2,1)S(1)} collective-permute-done((bf16[512,1024]{1,0:T(8,128)(2,1)S(1)}, bf16[512,1024]{1,0:T(8,128)(2,1)S(1)}, u32[]{:S(2)}, u32[]{:S(2)}) %collective-permute-start.1) | collective-permute-done | bytes 1048608 | tf_op jit(solution)/shard_map/ppermute | solution.py:363
  54.8 3.2 collective-permute-done.2.refs_4_.refs_2_
  58.4 1.6 collective-permute-start.6
  60.0 3.4 %collective-permute-start.7 = (bf16[512,1024]{1,0:T(8,128)(2,1)}, bf16[512,1024]{1,0:T(8,128)(2,1)}, u32[]{:S(2)}, u32[]{:S(2)}) collective-permute-start(bf16[512,1024]{1,0:T(8,128)(2,1)} %get-tuple-element.93.refs_4_), channel_id=1, source_target_pairs={{0,8},{4,12},{8,16},{12,20},{16,24},{20,28},{1,9},{5,13},{9,17},{1... | collective-permute-start | bytes 3145736 | tf_op jit(solution)/shard_map/ppermute | solution.py:363
  63.4 3.4 %collective-permute-start.8 = (bf16[512,1024]{1,0:T(8,128)(2,1)}, bf16[512,1024]{1,0:T(8,128)(2,1)S(1)}, u32[]{:S(2)}, u32[]{:S(2)}) collective-permute-start(bf16[512,1024]{1,0:T(8,128)(2,1)} %get-tuple-element.93.refs_4_), channel_id=1, source_target_pairs={{8,0},{12,4},{16,8},{20,12},{24,16},{28,20},{9,1},{13,5},{17,9},{2... | collective-permute-start | bytes 3145736 | tf_op jit(solution)/shard_map/ppermute | solution.py:363
  66.8 2.5 collective-permute-start.4
  69.3 1.9 collective-permute-start.5
  72.4 10.0 %shard_map.103 = (bf16[1024,1024]{1,0:T(8,128)(2,1)S(1)}, bf16[1024,1024]{1,0:T(8,128)(2,1)S(1)}) custom-call(bf16[1024,2048]{1,0:T(8,128)(2,1)} %refs_1_.3, bf16[1024,2048]{1,0:T(8,128)(2,1)} %k.7, bf16[1024,2048]{1,0:T(8,128)(2,1)} %v.7, bf16[128,2048]{1,0:T(8,128)(2,1)S(1)} %copy-done.7, bf16[16384,256]{1,0:T(8,128)(2,1)} %get-tuple-element.88.table), custom_call_target="tpu_custom_call" | custom-call | flops 67108864 | bytes 229376 | tf_op jit(solution)/shard_map/pallas_call | solution.py:104
  83.8 3.5 %collective-permute-done.7.refs_6_ = bf16[512,1024]{1,0:T(8,128)(2,1)} collective-permute-done((bf16[512,1024]{1,0:T(8,128)(2,1)}, bf16[512,1024]{1,0:T(8,128)(2,1)}, u32[]{:S(2)}, u32[]{:S(2)}) %collective-permute-start.7) | collective-permute-done | bytes 1048608 | tf_op jit(solution)/shard_map/ppermute | solution.py:363
  87.3 4.3 %collective-permute-done.8.refs_5_.refs_10_ = bf16[512,1024]{1,0:T(8,128)(2,1)S(1)} collective-permute-done((bf16[512,1024]{1,0:T(8,128)(2,1)}, bf16[512,1024]{1,0:T(8,128)(2,1)S(1)}, u32[]{:S(2)}, u32[]{:S(2)}) %collective-permute-start.8) | collective-permute-done | bytes 1048608 | tf_op jit(solution)/shard_map/ppermute | solution.py:363
  91.6 9.0 %shard_map.104.refs_2_ = f32[4,512,1024]{2,1,0:T(8,128)} custom-call(s32[4]{0:T(128)S(1)} %pad_add_fusion.pick, bf16[4,1024,512]{2,1,0:T(8,128)(2,1)} %bitcast.48, bf16[1024,1024]{1,0:T(8,128)(2,1)S(1)} %copy-done.14), custom_call_target="tpu_custom_call" | custom-call | flops 16777216 | bytes 49152 | tf_op jit(solution)/shard_map/pallas_call | solution.py:303
  100.6 5.9 %collective-permute-done.4.refs_3_.refs_6_ = bf16[512,1024]{1,0:T(8,128)(2,1)S(1)} collective-permute-done((bf16[512,1024]{1,0:T(8,128)(2,1)}, bf16[512,1024]{1,0:T(8,128)(2,1)S(1)}, u32[]{:S(2)}, u32[]{:S(2)}) %collective-permute-start.4) | collective-permute-done | bytes 1048608 | tf_op jit(solution)/shard_map/ppermute | solution.py:363
  106.5 4.1 %collective-permute-done.5.refs_4_.refs_7_ = bf16[512,1024]{1,0:T(8,128)(2,1)} collective-permute-done((bf16[512,1024]{1,0:T(8,128)(2,1)S(1)}, bf16[512,1024]{1,0:T(8,128)(2,1)}, u32[]{:S(2)}, u32[]{:S(2)}) %collective-permute-start.5) | collective-permute-done | bytes 1048608 | tf_op jit(solution)/shard_map/ppermute | solution.py:363
  111.3 2.4 collective-permute-start.10
  113.6 2.7 collective-permute-start.11
  116.4 5.0 %shard_map.105 = (bf16[512,1024]{1,0:T(8,128)(2,1)S(1)}, bf16[512,1024]{1,0:T(8,128)(2,1)}) custom-call(s32[3]{0:T(128)S(1)} %pad_add_fusion.1.pick, bf16[4,1024,512]{2,1,0:T(8,128)(2,1)} %bitcast.36, bf16[1024,1024]{1,0:T(8,128)(2,1)} %collective-permute-done.6.refs_1_, f32[4,512,1024]{2,1,0:T(8,128)} %shard_map.104.refs_2_, ...), custom_call_target="tpu_custom_call" | custom-call | flops 16777216 | bytes 49152 | tf_op jit(solution)/shard_map/pallas_call | solution.py:337
  122.6 7.7 %shard_map.106 = bf16[3,512,1024]{2,1,0:T(8,128)(2,1)S(1)} custom-call(s32[3]{0:T(128)S(1)} %pad_add_fusion.2.pick, bf16[4,1024,512]{2,1,0:T(8,128)(2,1)} %bitcast.37, bf16[1024,1024]{1,0:T(8,128)(2,1)} %collective-permute-done.6.refs_1_, f32[4,512,1024]{2,1,0:T(8,128)} %shard_map.104.refs_2_), custom_call_target="tpu_custom_call" | custom-call | flops 16777216 | bytes 49152 | tf_op jit(solution)/shard_map/pallas_call | solution.py:303
  130.3 7.8 %shard_map.107.refs_3_ = bf16[1024,1024]{1,0:T(8,128)(2,1)} custom-call(s32[7]{0:T(128)S(1)} %stack.58.pick, bf16[4,1024,512]{2,1,0:T(8,128)(2,1)} %bitcast.38, bf16[4,1024,512]{2,1,0:T(8,128)(2,1)} %bitcast.39, bf16[4,1024,512]{2,1,0:T(8,128)(2,1)} %bitcast.40, bf16[512,1024]{1,0:T(8,128)(2,1)S(1)} %copy-done.2, ...), custom_call_target="tpu_custom_call" | custom-call | flops 50331648 | bytes 98304 | tf_op jit(solution)/shard_map/pallas_call | solution.py:263
  138.1 1.8 collective-permute-done.11.refs_4_.refs_8_
  139.9 9.0 %shard_map.108.refs_2_ = f32[4,512,1024]{2,1,0:T(8,128)} custom-call(s32[4]{0:T(128)S(1)} %pad_add_fusion.pick, bf16[4,1024,512]{2,1,0:T(8,128)(2,1)} %bitcast.49, bf16[1024,1024]{1,0:T(8,128)(2,1)S(1)} %copy-done.16), custom_call_target="tpu_custom_call" | custom-call | flops 16777216 | bytes 49152 | tf_op jit(solution)/shard_map/pallas_call | solution.py:303
  148.9 7.8 %shard_map.109.refs_3_ = bf16[1024,1024]{1,0:T(8,128)(2,1)} custom-call(s32[7]{0:T(128)S(1)} %stack.58.pick, bf16[4,1024,512]{2,1,0:T(8,128)(2,1)} %bitcast.50, bf16[4,1024,512]{2,1,0:T(8,128)(2,1)} %bitcast.51, bf16[4,1024,512]{2,1,0:T(8,128)(2,1)} %bitcast.52, bf16[512,1024]{1,0:T(8,128)(2,1)S(1)} %copy-done.2, ...), custom_call_target="tpu_custom_call" | custom-call | flops 50331648 | bytes 98304 | tf_op jit(solution)/shard_map/pallas_call | solution.py:263
  157.8 4.8 %shard_map.110 = bf16[1024,1024]{1,0:T(8,128)(2,1)S(1)} custom-call(s32[7]{0:T(128)S(1)} %stack.58.pick, bf16[4,1024,512]{2,1,0:T(8,128)(2,1)} %bitcast.41, bf16[512,1024]{1,0:T(8,128)(2,1)} %collective-permute-done.9.refs_1_, bf16[512,1024]{1,0:T(8,128)(2,1)S(1)} %collective-permute-done.2.refs_4_.refs_2_, bf16[1024,1024]{1,0:T(8,128)(2,1)} %shard_map.107.refs_3_), custom_call_target="tpu_custom_call" | custom-call | flops 16777216 | bytes 32768 | tf_op jit(solution)/shard_map/pallas_call | solution.py:263
  162.6 4.8 %shard_map.111 = (bf16[512,1024]{1,0:T(8,128)(2,1)S(1)}, bf16[512,1024]{1,0:T(8,128)(2,1)S(1)}) custom-call(s32[3]{0:T(128)S(1)} %pad_add_fusion.1.pick, bf16[4,1024,512]{2,1,0:T(8,128)(2,1)} %bitcast.42, bf16[1024,1024]{1,0:T(8,128)(2,1)} %collective-permute-done.12.refs_1_, f32[4,512,1024]{2,1,0:T(8,128)} %shard_map.108.refs_2_, ...), custom_call_target="tpu_custom_call" | custom-call | flops 16777216 | bytes 49152 | tf_op jit(solution)/shard_map/pallas_call | solution.py:337
  167.4 2.6 collective-permute-start.14
  170.0 1.5 collective-permute-start.13
  171.5 2.6 fusion.11
  175.4 2.1 collective-permute-start.17
  177.6 7.6 %shard_map.112 = bf16[3,512,1024]{2,1,0:T(8,128)(2,1)S(1)} custom-call(s32[3]{0:T(128)S(1)} %pad_add_fusion.2.pick, bf16[4,1024,512]{2,1,0:T(8,128)(2,1)} %bitcast.43, bf16[1024,1024]{1,0:T(8,128)(2,1)} %collective-permute-done.12.refs_1_, f32[4,512,1024]{2,1,0:T(8,128)} %shard_map.108.refs_2_), custom_call_target="tpu_custom_call" | custom-call | flops 16777216 | bytes 49152 | tf_op jit(solution)/shard_map/pallas_call | solution.py:303
  185.2 5.3 %shard_map.113.own_ref = bf16[1024,1024]{1,0:T(8,128)(2,1)S(1)} custom-call(s32[7]{0:T(128)S(1)} %stack.58.pick, bf16[4,1024,512]{2,1,0:T(8,128)(2,1)} %bitcast.53, bf16[512,1024]{1,0:T(8,128)(2,1)} %collective-permute-done.9.refs_1_, bf16[512,1024]{1,0:T(8,128)(2,1)S(1)} %collective-permute-done.2.refs_4_.refs_2_, bf16[1024,1024]{1,0:T(8,128)(2,1)} %shard_map.109.refs_3_), custom_call_target="tpu_custom_call" | custom-call | flops 16777216 | bytes 32768 | tf_op jit(solution)/shard_map/pallas_call | solution.py:263
  191.8 2.3 collective-permute-done.14.refs_9_
  194.2 9.4 %shard_map.114 = bf16[1024,1024]{1,0:T(8,128)(2,1)} custom-call(s32[7]{0:T(128)S(1)} %stack.58.pick, bf16[4,1024,512]{2,1,0:T(8,128)(2,1)} %bitcast.44, bf16[4,1024,512]{2,1,0:T(8,128)(2,1)} %bitcast.45, bf16[4,1024,512]{2,1,0:T(8,128)(2,1)} %bitcast.46, bf16[4,1024,512]{2,1,0:T(8,128)(2,1)} %bitcast.47, bf16[512,1024]{1,0:T(8,128)(2,1)} %get-tuple-element.93.refs_4_, ...), custom_call_target="tpu_custom_call" | custom-call | flops 67108864 | bytes 131072 | tf_op jit(solution)/shard_map/pallas_call | solution.py:263
  203.6 2.7 fusion.10
  207.5 1.9 collective-permute-start.22
  209.5 7.2 %collective-permute-done.16 = bf16[512,1024]{1,0:T(8,128)(2,1)} collective-permute-done((bf16[512,1024]{1,0:T(8,128)(2,1)}, bf16[512,1024]{1,0:T(8,128)(2,1)}, u32[]{:S(2)}, u32[]{:S(2)}) %collective-permute-start.16) | collective-permute-done | bytes 1048608 | tf_op jit(solution)/shard_map/ppermute | solution.py:363
  216.7 1.5 collective-permute-start.15
  218.2 3.9 %fusion.1 = (bf16[512,1024]{1,0:T(8,128)(2,1)}, bf16[512,1024]{1,0:T(8,128)(2,1)}) fusion(bf16[512,1024]{1,0:T(8,128)(2,1)} %collective-permute-done.17, bf16[512,1024]{1,0:T(8,128)(2,1)} %collective-permute-done.16, bf16[512,1024]{1,0:T(8,128)(2,1)S(1)} %copy-done.20, pred[]{:T(512)S(6)} %eq.15, pred[]{:T(512)S(6)} %eq.17, ...), kind=kLoop, calls=%fused_computation.9 | loop fusion | flops 6291456 | bytes 6291458 | tf_op jit(solution)/shard_map/convert_element_type | solution.py:432
  222.1 1.9 collective-permute-start.18
  224.1 5.1 %collective-permute-start.19 = (bf16[512,1024]{1,0:T(8,128)(2,1)}, bf16[512,1024]{1,0:T(8,128)(2,1)}, u32[]{:S(2)}, u32[]{:S(2)}) collective-permute-start(bf16[512,1024]{1,0:T(8,128)(2,1)} %get-tuple-element.164), channel_id=1, source_target_pairs={{8,0},{12,4},{16,8},{20,12},{24,16},{28,20},{9,1},{13,5},{17,9},{2... | collective-permute-start | bytes 3145736 | tf_op jit(solution)/shard_map/ppermute | solution.py:363
  229.2 9.4 %shard_map.115.own_ref = bf16[1024,1024]{1,0:T(8,128)(2,1)} custom-call(s32[7]{0:T(128)S(1)} %stack.58.pick, bf16[4,1024,512]{2,1,0:T(8,128)(2,1)} %bitcast.54, bf16[4,1024,512]{2,1,0:T(8,128)(2,1)} %bitcast.55, bf16[4,1024,512]{2,1,0:T(8,128)(2,1)} %bitcast.56, bf16[4,1024,512]{2,1,0:T(8,128)(2,1)} %bitcast.57, ...), custom_call_target="tpu_custom_call" | custom-call | flops 67108864 | bytes 131072 | tf_op jit(solution)/shard_map/pallas_call | solution.py:263
  238.6 12.5 %shard_map.116 = (bf16[1024,2048]{1,0:T(8,128)(2,1)}, bf16[1024,1024]{1,0:T(8,128)(2,1)S(1)}, bf16[128,1024]{1,0:T(8,128)(2,1)S(1)}, f32[64,256]{1,0:T(8,128)S(1)}) custom-call(bf16[1024,1024]{1,0:T(8,128)(2,1)S(1)} %copy-done.5, bf16[1024,1024]{1,0:T(8,128)(2,1)} %collective-permute-done.13.refs_0_, bf16[1024,2048]{1,0:T(8,128)(2,1)} %refs_1_.3, ...), custom_call_target="tpu_custom_call" | custom-call | flops 67108864 | bytes 294912 | tf_op jit(solution)/shard_map/pallas_call | solution.py:171
  251.2 4.0 %fusion.7 = (bf16[512,1024]{1,0:T(8,128)(2,1)}, bf16[512,1024]{1,0:T(8,128)(2,1)}) fusion(bf16[512,1024]{1,0:T(8,128)(2,1)} %collective-permute-done.21, bf16[512,1024]{1,0:T(8,128)(2,1)} %collective-permute-done.22, bf16[512,1024]{1,0:T(8,128)(2,1)S(1)} %get-tuple-element.145, pred[]{:T(512)S(6)} %eq.15, bf16[3,512,1024]{2,1,0:T(8,128)(2,1)S(1)} %shard_map.112, ...), kind=kLoop, calls=%fused_computation.15 | loop fusion | flops 6291456 | bytes 6291458 | tf_op jit(solution)/shard_map/convert_element_type | solution.py:432
  255.2 1.9 collective-permute-start.23
  257.1 5.1 %collective-permute-start.24 = (bf16[512,1024]{1,0:T(8,128)(2,1)}, bf16[512,1024]{1,0:T(8,128)(2,1)}, u32[]{:S(2)}, u32[]{:S(2)}) collective-permute-start(bf16[512,1024]{1,0:T(8,128)(2,1)} %get-tuple-element.161), channel_id=1, source_target_pairs={{8,0},{12,4},{16,8},{20,12},{24,16},{28,20},{9,1},{13,5},{17,9},{2... | collective-permute-start | bytes 3145736 | tf_op jit(solution)/shard_map/ppermute | solution.py:363
  262.2 3.2 fusion.13
  265.5 1.9 collective-permute-start.25
  267.4 12.6 %shard_map.117 = (bf16[1024,2048]{1,0:T(8,128)(2,1)}, bf16[1024,1024]{1,0:T(8,128)(2,1)S(1)}, bf16[128,1024]{1,0:T(8,128)(2,1)S(1)}, f32[64,256]{1,0:T(8,128)S(1)}) custom-call(bf16[1024,1024]{1,0:T(8,128)(2,1)S(1)} %copy-done.3, bf16[1024,1024]{1,0:T(8,128)(2,1)} %collective-permute-done.15.refs_0_, ...), custom_call_target="tpu_custom_call", output_to_operand_aliasing={{0}: (7, {})} | custom-call | flops 67108864 | bytes 294912 | tf_op jit(solution)/shard_map/pallas_call | solution.py:171
  282.2 5.1 %all-to-all-start = ((f32[8,16,128]{2,1,0:T(8,128)}), f32[8,16,128]{2,1,0:T(8,128)S(1)}, u32[]{:S(2)}, u32[]{:S(2)}) async-start(f32[8,16,128]{2,1,0:T(8,128)} %bitcast.20), calls=%async_computation | async-start | bytes 131072 | tf_op jit(solution)/shard_map/all_to_all | solution.py:550
  287.3 3.6 %collective-permute-start.20 = (bf16[128,1024]{1,0:T(8,128)(2,1)S(1)}, bf16[128,1024]{1,0:T(8,128)(2,1)S(1)}, u32[]{:S(2)}, u32[]{:S(2)}) collective-permute-start(bf16[128,1024]{1,0:T(8,128)(2,1)S(1)} %get-tuple-element.143), channel_id=1, source_target_pairs={{4,0},{8,4},{12,8},{16,12},{20,16},{24,20},{28,24},{5,1},{9,5},{13... | collective-permute-start | bytes 786440 | tf_op jit(solution)/shard_map/ppermute | solution.py:363
  290.9 2.6 fusion.9
  293.5 1.5 pad_maximum_fusion
  295.0 10.4 %shard_map.118 = (bf16[1024,2048]{1,0:T(8,128)(2,1)}, bf16[1024,2048]{1,0:T(8,128)(2,1)}) custom-call(bf16[1024,1024]{1,0:T(8,128)(2,1)S(1)} %get-tuple-element.151.gm, bf16[128,1024]{1,0:T(8,128)(2,1)S(1)} %collective-permute-done.25.later, bf16[1024,2048]{1,0:T(8,128)(2,1)} %k.7, bf16[1024,2048]{1,0:T(8,128)(2,1)} %v.7, ...), custom_call_target="tpu_custom_call" | custom-call | flops 67108864 | bytes 229376 | tf_op jit(solution)/shard_map/pallas_call | solution.py:216
  306.1 1.6 copy-done.18
  307.7 10.4 %shard_map.119 = (bf16[1024,2048]{1,0:T(8,128)(2,1)}, bf16[1024,2048]{1,0:T(8,128)(2,1)}) custom-call(bf16[1024,1024]{1,0:T(8,128)(2,1)S(1)} %copy-done.18, bf16[128,1024]{1,0:T(8,128)(2,1)S(1)} %collective-permute-done.20.later, bf16[1024,2048]{1,0:T(8,128)(2,1)} %k.7, bf16[1024,2048]{1,0:T(8,128)(2,1)} %v.7, ...), custom_call_target="tpu_custom_call", output_to_operand_aliasing={{0}: (5, {}), {1}: (6, {})} | custom-call | flops 67108864 | bytes 229376 | tf_op jit(solution)/shard_map/pallas_call | solution.py:216
  (86 shorter events, 13.0 us)
Async XLA Ops:
  7.2 51.2 %all-gather.5.cloned.1.call-start = ((), (), s32[]{:S(2)}) async-start(), calls=%async_computation.1 | async-start | bytes 5242880 | tf_op jit(solution)/shard_map/all_gather | solution.py:458
  8.6 6.2 %copy-start.22 = (bf16[128,128]{1,0:T(8,128)(2,1)S(1)}, bf16[128,128]{1,0:T(8,128)(2,1)}, u32[]{:S(2)}) copy-start(bf16[128,128]{1,0:T(8,128)(2,1)} %param.9) | copy-start | bytes 98308
  11.3 99.4 %all-gather.7.cloned.1.call-start = ((), (), s32[]{:S(2)}) async-start(), calls=%async_computation.2 | async-start | bytes 5242880 | tf_op jit(solution)/shard_map/all_gather | solution.py:472
  11.3 16.9 %collective-permute-start = (bf16[128,2048]{1,0:T(8,128)(2,1)S(1)}, bf16[128,2048]{1,0:T(8,128)(2,1)S(1)}, u32[]{:S(2)}, u32[]{:S(2)}) collective-permute-start(bf16[128,2048]{1,0:T(8,128)(2,1)S(1)} %multiply_convert_fusion), channel_id=1, source_target_pairs={{0,4},{4,8},{8,12},{12,16},{16,20},{20,24},{24,28},{1,5},{5,9},{9,... | collective-permute-start | bytes 1572872 | tf_op jit(solution)/shard_map/ppermute | solution.py:363
  28.2 17.4 %copy-start.1 = (bf16[512,1024]{1,0:T(8,128)(2,1)}, bf16[512,1024]{1,0:T(8,128)(2,1)S(1)}, u32[]{:S(2)}) copy-start(bf16[512,1024]{1,0:T(8,128)(2,1)S(1)} %get-tuple-element.85.refs_3_) | copy-start | bytes 3145732
  28.2 17.4 %copy-start.6 = (bf16[128,2048]{1,0:T(8,128)(2,1)}, bf16[128,2048]{1,0:T(8,128)(2,1)S(1)}, u32[]{:S(2)}) copy-start(bf16[128,2048]{1,0:T(8,128)(2,1)S(1)} %collective-permute-done.prior.refs_5_) | copy-start | bytes 1572868
  28.2 26.5 %collective-permute-start.1 = (bf16[512,1024]{1,0:T(8,128)(2,1)S(1)}, bf16[512,1024]{1,0:T(8,128)(2,1)S(1)}, u32[]{:S(2)}, u32[]{:S(2)}) collective-permute-start(bf16[512,1024]{1,0:T(8,128)(2,1)S(1)} %get-tuple-element.85.refs_3_), channel_id=1, source_target_pairs={{0,8},{4,12},{8,16},{12,20},{16,24},{20,28},{1,9},{5,13},{9,17},{1... | collective-permute-start | bytes 3145736 | tf_op jit(solution)/shard_map/ppermute | solution.py:363
  31.7 26.2 %collective-permute-start.2 = (bf16[512,1024]{1,0:T(8,128)(2,1)S(1)}, bf16[512,1024]{1,0:T(8,128)(2,1)S(1)}, u32[]{:S(2)}, u32[]{:S(2)}) collective-permute-start(bf16[512,1024]{1,0:T(8,128)(2,1)S(1)} %get-tuple-element.85.refs_3_), channel_id=1, source_target_pairs={{8,0},{12,4},{16,8},{20,12},{24,16},{28,20},{9,1},{13,5},{17,9},{2... | collective-permute-start | bytes 3145736 | tf_op jit(solution)/shard_map/ppermute | solution.py:363
  34.2 24.2 %collective-permute-start.3 = (bf16[1024,512]{1,0:T(8,128)(2,1)S(1)}, bf16[1024,512]{1,0:T(8,128)(2,1)}, u32[]{:S(2)}, u32[]{:S(2)}) collective-permute-start(bf16[1024,512]{1,0:T(8,128)(2,1)S(1)} %get-tuple-element.86), channel_id=1, source_target_pairs={{0,4},{4,0},{8,12},{12,8},{16,20},{20,16},{24,28},{28,24},{1,5},{5... | collective-permute-start | bytes 3145736 | tf_op jit(solution)/shard_map/ppermute | solution.py:363
  45.6 1.4 copy-start.11
  47.1 1.3 copy-start.13
  54.8 3.2 copy-start.9
  58.4 52.2 %collective-permute-start.6 = (bf16[1024,1024]{1,0:T(8,128)(2,1)}, bf16[1024,1024]{1,0:T(8,128)(2,1)}, u32[]{:S(2)}, u32[]{:S(2)}) collective-permute-start(bf16[1024,1024]{1,0:T(8,128)(2,1)} %copy-done.13), channel_id=1, source_target_pairs={{0,4},{4,0},{8,12},{12,8},{16,20},{20,16},{24,28},{28,24},{1,5},{5... | collective-permute-start | bytes 6291464 | tf_op jit(solution)/shard_map/ppermute | solution.py:363
  60.0 27.3 %collective-permute-start.7 = (bf16[512,1024]{1,0:T(8,128)(2,1)}, bf16[512,1024]{1,0:T(8,128)(2,1)}, u32[]{:S(2)}, u32[]{:S(2)}) collective-permute-start(bf16[512,1024]{1,0:T(8,128)(2,1)} %get-tuple-element.93.refs_4_), channel_id=1, source_target_pairs={{0,8},{4,12},{8,16},{12,20},{16,24},{20,28},{1,9},{5,13},{9,17},{1... | collective-permute-start | bytes 3145736 | tf_op jit(solution)/shard_map/ppermute | solution.py:363
  63.4 28.2 %collective-permute-start.8 = (bf16[512,1024]{1,0:T(8,128)(2,1)}, bf16[512,1024]{1,0:T(8,128)(2,1)S(1)}, u32[]{:S(2)}, u32[]{:S(2)}) collective-permute-start(bf16[512,1024]{1,0:T(8,128)(2,1)} %get-tuple-element.93.refs_4_), channel_id=1, source_target_pairs={{8,0},{12,4},{16,8},{20,12},{24,16},{28,20},{9,1},{13,5},{17,9},{2... | collective-permute-start | bytes 3145736 | tf_op jit(solution)/shard_map/ppermute | solution.py:363
  66.8 39.7 %collective-permute-start.4 = (bf16[512,1024]{1,0:T(8,128)(2,1)}, bf16[512,1024]{1,0:T(8,128)(2,1)S(1)}, u32[]{:S(2)}, u32[]{:S(2)}) collective-permute-start(bf16[512,1024]{1,0:T(8,128)(2,1)} %copy-done.9), channel_id=1, source_target_pairs={{8,16},{12,20},{16,24},{20,28},{9,17},{13,21},{17,25},{21,29},{10,... | collective-permute-start | bytes 3145736 | tf_op jit(solution)/shard_map/ppermute | solution.py:363
  69.3 41.3 %collective-permute-start.5 = (bf16[512,1024]{1,0:T(8,128)(2,1)S(1)}, bf16[512,1024]{1,0:T(8,128)(2,1)}, u32[]{:S(2)}, u32[]{:S(2)}) collective-permute-start(bf16[512,1024]{1,0:T(8,128)(2,1)S(1)} %collective-permute-done.2.refs_4_.refs_2_), channel_id=1, source_target_pairs={{16,8},{20,12},{8,0},{12,4},{17,9},{21,13},{9,1},{13,5},{18,10},{2... | collective-permute-start | bytes 3145736 | tf_op jit(solution)/shard_map/ppermute | solution.py:363
  71.4 1.0 copy-start.7
  72.4 19.2 %copy-start.14 = (bf16[1024,1024]{1,0:T(8,128)(2,1)S(1)}, bf16[1024,1024]{1,0:T(8,128)(2,1)}, u32[]{:S(2)}) copy-start(bf16[1024,1024]{1,0:T(8,128)(2,1)} %copy-done.13) | copy-start | bytes 6291460
  82.5 1.3 copy-start.12
  83.8 16.8 %copy-start.15 = (bf16[1024,1024]{1,0:T(8,128)(2,1)}, bf16[1024,1024]{1,0:T(8,128)(2,1)S(1)}, u32[]{:S(2)}) copy-start(bf16[1024,1024]{1,0:T(8,128)(2,1)S(1)} %get-tuple-element.116.refs_1_) | copy-start | bytes 6291460
  110.7 51.9 %collective-permute-start.12 = (bf16[1024,1024]{1,0:T(8,128)(2,1)}, bf16[1024,1024]{1,0:T(8,128)(2,1)}, u32[]{:S(2)}, u32[]{:S(2)}) collective-permute-start(bf16[1024,1024]{1,0:T(8,128)(2,1)} %copy-done.15), channel_id=1, source_target_pairs={{0,4},{4,0},{8,12},{12,8},{16,20},{20,16},{24,28},{28,24},{1,5},{5... | collective-permute-start | bytes 6291464 | tf_op jit(solution)/shard_map/ppermute | solution.py:363
  111.3 26.8 %collective-permute-start.10 = (bf16[512,1024]{1,0:T(8,128)(2,1)}, bf16[512,1024]{1,0:T(8,128)(2,1)}, u32[]{:S(2)}, u32[]{:S(2)}) collective-permute-start(bf16[512,1024]{1,0:T(8,128)(2,1)} %collective-permute-done.7.refs_6_), channel_id=1, source_target_pairs={{8,16},{12,20},{16,24},{20,28},{9,17},{13,21},{17,25},{21,29},{10,... | collective-permute-start | bytes 3145736 | tf_op jit(solution)/shard_map/ppermute | solution.py:363
  113.6 26.3 %collective-permute-start.11 = (bf16[512,1024]{1,0:T(8,128)(2,1)S(1)}, bf16[512,1024]{1,0:T(8,128)(2,1)}, u32[]{:S(2)}, u32[]{:S(2)}) collective-permute-start(bf16[512,1024]{1,0:T(8,128)(2,1)S(1)} %collective-permute-done.8.refs_5_.refs_10_), channel_id=1, source_target_pairs={{16,8},{20,12},{8,0},{12,4},{17,9},{21,13},{9,1},{13,5},{18,10},{2... | collective-permute-start | bytes 3145736 | tf_op jit(solution)/shard_map/ppermute | solution.py:363
  121.4 1.0 copy-start.19
  122.4 35.4 %collective-permute-start.9 = (bf16[512,1024]{1,0:T(8,128)(2,1)}, bf16[512,1024]{1,0:T(8,128)(2,1)}, u32[]{:S(2)}, u32[]{:S(2)}) collective-permute-start(bf16[512,1024]{1,0:T(8,128)(2,1)} %get-tuple-element.105), channel_id=1, source_target_pairs={{0,8},{4,12},{24,16},{28,20},{16,24},{20,28},{8,0},{12,4},{1,9},{5... | collective-permute-start | bytes 3145736 | tf_op jit(solution)/shard_map/ppermute | solution.py:363
  122.6 7.7 %copy-start.2 = (bf16[512,1024]{1,0:T(8,128)(2,1)S(1)}, bf16[512,1024]{1,0:T(8,128)(2,1)}, u32[]{:S(2)}) copy-start(bf16[512,1024]{1,0:T(8,128)(2,1)} %copy-done.1) | copy-start | bytes 3145732
  122.6 7.7 %copy-start.10 = (bf16[512,1024]{1,0:T(8,128)(2,1)S(1)}, bf16[512,1024]{1,0:T(8,128)(2,1)}, u32[]{:S(2)}) copy-start(bf16[512,1024]{1,0:T(8,128)(2,1)} %copy-done.9) | copy-start | bytes 3145732
  130.3 9.6 %copy-start.16 = (bf16[1024,1024]{1,0:T(8,128)(2,1)S(1)}, bf16[1024,1024]{1,0:T(8,128)(2,1)}, u32[]{:S(2)}) copy-start(bf16[1024,1024]{1,0:T(8,128)(2,1)} %copy-done.15) | copy-start | bytes 6291460
  167.4 26.8 %collective-permute-start.14 = (bf16[512,1024]{1,0:T(8,128)(2,1)S(1)}, bf16[512,1024]{1,0:T(8,128)(2,1)}, u32[]{:S(2)}, u32[]{:S(2)}) collective-permute-start(bf16[512,1024]{1,0:T(8,128)(2,1)S(1)} %get-tuple-element.125), channel_id=1, source_target_pairs={{0,8},{4,12},{24,16},{28,20},{16,24},{20,28},{8,0},{12,4},{1,9},{5... | collective-permute-start | bytes 3145736 | tf_op jit(solution)/shard_map/ppermute | solution.py:363
  170.0 54.0 %collective-permute-start.13 = (bf16[1024,1024]{1,0:T(8,128)(2,1)S(1)}, bf16[1024,1024]{1,0:T(8,128)(2,1)}, u32[]{:S(2)}, u32[]{:S(2)}) collective-permute-start(bf16[1024,1024]{1,0:T(8,128)(2,1)S(1)} %shard_map.110), channel_id=1, source_target_pairs={{0,4},{4,0},{8,12},{12,8},{16,20},{20,16},{24,28},{28,24},{1,5},{5... | collective-permute-start | bytes 6291464 | tf_op jit(solution)/shard_map/ppermute | solution.py:363
  174.2 42.5 %collective-permute-start.16 = (bf16[512,1024]{1,0:T(8,128)(2,1)}, bf16[512,1024]{1,0:T(8,128)(2,1)}, u32[]{:S(2)}, u32[]{:S(2)}) collective-permute-start(bf16[512,1024]{1,0:T(8,128)(2,1)} %fusion.11), channel_id=1, source_target_pairs={{0,8},{4,12},{24,16},{28,20},{1,9},{5,13},{25,17},{29,21},{2,10},{... | collective-permute-start | bytes 3145736 | tf_op jit(solution)/shard_map/ppermute | solution.py:363
  175.4 42.8 %collective-permute-start.17 = (bf16[512,1024]{1,0:T(8,128)(2,1)}, bf16[512,1024]{1,0:T(8,128)(2,1)}, u32[]{:S(2)}, u32[]{:S(2)}) collective-permute-start(bf16[512,1024]{1,0:T(8,128)(2,1)} %fusion.11), channel_id=1, source_target_pairs={{8,16},{12,20},{16,8},{20,12},{9,17},{13,21},{17,9},{21,13},{10,18... | collective-permute-start | bytes 3145736 | tf_op jit(solution)/shard_map/ppermute | solution.py:363
  185.2 66.0 %copy-start = (bf16[3,512,1024]{2,1,0:T(8,128)(2,1)}, bf16[3,512,1024]{2,1,0:T(8,128)(2,1)S(1)}, u32[]{:S(2)}) copy-start(bf16[3,512,1024]{2,1,0:T(8,128)(2,1)S(1)} %shard_map.112) | copy-start | bytes 9437188
  190.5 1.3 copy-start.4
  203.6 14.6 %copy-start.20 = (bf16[512,1024]{1,0:T(8,128)(2,1)S(1)}, bf16[512,1024]{1,0:T(8,128)(2,1)}, u32[]{:S(2)}) copy-start(bf16[512,1024]{1,0:T(8,128)(2,1)} %copy-done.19) | copy-start | bytes 3145732
  206.3 44.9 %collective-permute-start.21 = (bf16[512,1024]{1,0:T(8,128)(2,1)}, bf16[512,1024]{1,0:T(8,128)(2,1)}, u32[]{:S(2)}, u32[]{:S(2)}) collective-permute-start(bf16[512,1024]{1,0:T(8,128)(2,1)} %fusion.10), channel_id=1, source_target_pairs={{0,8},{4,12},{24,16},{28,20},{1,9},{5,13},{25,17},{29,21},{2,10},{... | collective-permute-start | bytes 3145736 | tf_op jit(solution)/shard_map/ppermute | solution.py:363
  207.5 43.6 %collective-permute-start.22 = (bf16[512,1024]{1,0:T(8,128)(2,1)}, bf16[512,1024]{1,0:T(8,128)(2,1)}, u32[]{:S(2)}, u32[]{:S(2)}) collective-permute-start(bf16[512,1024]{1,0:T(8,128)(2,1)} %fusion.10), channel_id=1, source_target_pairs={{8,16},{12,20},{16,8},{20,12},{9,17},{13,21},{17,9},{21,13},{10,18... | collective-permute-start | bytes 3145736 | tf_op jit(solution)/shard_map/ppermute | solution.py:363
  216.7 50.7 %collective-permute-start.15 = (bf16[1024,1024]{1,0:T(8,128)(2,1)}, bf16[1024,1024]{1,0:T(8,128)(2,1)}, u32[]{:S(2)}, u32[]{:S(2)}) collective-permute-start(bf16[1024,1024]{1,0:T(8,128)(2,1)} %shard_map.114), channel_id=1, source_target_pairs={{0,4},{4,0},{8,12},{12,8},{16,20},{20,16},{24,28},{28,24},{1,5},{5... | collective-permute-start | bytes 6291464 | tf_op jit(solution)/shard_map/ppermute | solution.py:363
  222.1 40.1 %collective-permute-start.18 = (bf16[512,1024]{1,0:T(8,128)(2,1)}, bf16[512,1024]{1,0:T(8,128)(2,1)}, u32[]{:S(2)}, u32[]{:S(2)}) collective-permute-start(bf16[512,1024]{1,0:T(8,128)(2,1)} %get-tuple-element.163), channel_id=1, source_target_pairs={{0,8},{4,12},{8,16},{12,20},{16,24},{20,28},{1,9},{5,13},{9,17},{1... | collective-permute-start | bytes 3145736 | tf_op jit(solution)/shard_map/ppermute | solution.py:363
  224.0 14.6 %copy-start.5 = (bf16[1024,1024]{1,0:T(8,128)(2,1)S(1)}, bf16[1024,1024]{1,0:T(8,128)(2,1)}, u32[]{:S(2)}) copy-start(bf16[1024,1024]{1,0:T(8,128)(2,1)} %copy-done.4) | copy-start | bytes 6291460
  224.1 14.5 %copy-start.8 = (bf16[128,2048]{1,0:T(8,128)(2,1)S(1)}, bf16[128,2048]{1,0:T(8,128)(2,1)}, u32[]{:S(2)}) copy-start(bf16[128,2048]{1,0:T(8,128)(2,1)} %copy-done.6) | copy-start | bytes 1572868
  224.1 38.2 %collective-permute-start.19 = (bf16[512,1024]{1,0:T(8,128)(2,1)}, bf16[512,1024]{1,0:T(8,128)(2,1)}, u32[]{:S(2)}, u32[]{:S(2)}) collective-permute-start(bf16[512,1024]{1,0:T(8,128)(2,1)} %get-tuple-element.164), channel_id=1, source_target_pairs={{8,0},{12,4},{16,8},{20,12},{24,16},{28,20},{9,1},{13,5},{17,9},{2... | collective-permute-start | bytes 3145736 | tf_op jit(solution)/shard_map/ppermute | solution.py:363
  255.2 35.7 %collective-permute-start.23 = (bf16[512,1024]{1,0:T(8,128)(2,1)}, bf16[512,1024]{1,0:T(8,128)(2,1)}, u32[]{:S(2)}, u32[]{:S(2)}) collective-permute-start(bf16[512,1024]{1,0:T(8,128)(2,1)} %get-tuple-element.162), channel_id=1, source_target_pairs={{0,8},{4,12},{8,16},{12,20},{16,24},{20,28},{1,9},{5,13},{9,17},{1... | collective-permute-start | bytes 3145736 | tf_op jit(solution)/shard_map/ppermute | solution.py:363
  257.1 10.3 %copy-start.3 = (bf16[1024,1024]{1,0:T(8,128)(2,1)S(1)}, bf16[1024,1024]{1,0:T(8,128)(2,1)}, u32[]{:S(2)}) copy-start(bf16[1024,1024]{1,0:T(8,128)(2,1)} %shard_map.115.own_ref) | copy-start | bytes 6291460
  257.1 33.8 %collective-permute-start.24 = (bf16[512,1024]{1,0:T(8,128)(2,1)}, bf16[512,1024]{1,0:T(8,128)(2,1)}, u32[]{:S(2)}, u32[]{:S(2)}) collective-permute-start(bf16[512,1024]{1,0:T(8,128)(2,1)} %get-tuple-element.161), channel_id=1, source_target_pairs={{8,0},{12,4},{16,8},{20,12},{24,16},{28,20},{9,1},{13,5},{17,9},{2... | collective-permute-start | bytes 3145736 | tf_op jit(solution)/shard_map/ppermute | solution.py:363
  265.5 29.6 %collective-permute-start.25 = (bf16[128,1024]{1,0:T(8,128)(2,1)S(1)}, bf16[128,1024]{1,0:T(8,128)(2,1)S(1)}, u32[]{:S(2)}, u32[]{:S(2)}) collective-permute-start(bf16[128,1024]{1,0:T(8,128)(2,1)S(1)} %get-tuple-element.147), channel_id=1, source_target_pairs={{4,0},{8,4},{12,8},{16,12},{20,16},{24,20},{28,24},{5,1},{9,5},{13... | collective-permute-start | bytes 786440 | tf_op jit(solution)/shard_map/ppermute | solution.py:363
  280.0 1.3 copy-start.17
  282.2 23.2 %all-to-all-start = ((f32[8,16,128]{2,1,0:T(8,128)}), f32[8,16,128]{2,1,0:T(8,128)S(1)}, u32[]{:S(2)}, u32[]{:S(2)}) async-start(f32[8,16,128]{2,1,0:T(8,128)} %bitcast.20), calls=%async_computation | async-start | bytes 131072 | tf_op jit(solution)/shard_map/all_to_all | solution.py:550
  287.3 18.8 %collective-permute-start.20 = (bf16[128,1024]{1,0:T(8,128)(2,1)S(1)}, bf16[128,1024]{1,0:T(8,128)(2,1)S(1)}, u32[]{:S(2)}, u32[]{:S(2)}) collective-permute-start(bf16[128,1024]{1,0:T(8,128)(2,1)S(1)} %get-tuple-element.143), channel_id=1, source_target_pairs={{4,0},{8,4},{12,8},{16,12},{20,16},{24,20},{28,24},{5,1},{9,5},{13... | collective-permute-start | bytes 786440 | tf_op jit(solution)/shard_map/ppermute | solution.py:363
  290.9 2.6 copy-start.21
  306.1 1.6 copy-start.18
Sparse Core Ops, SparseCore 0:
  11.4 34.6 all-gather.4
  58.5 33.7 all-gather.6

commit v9 on v8

--- a/solution.py
+++ b/solution.py
@@ -465,8 +465,6 @@
     gateds[0], mixeds[0] = forward(queries, keys, values, prior, back, 0, chunks)
     up1[0], down1[0], swapped, gateds, cots = fence(up1[0], down1[0], swapped, gateds, cots)
 
-    for h in later_halves:
-        up1[h], down1[h] = along_line(halves[h], up_pairs), along_line(halves[h], down_pairs)
     second[0] = second_step(0)
     if paired:
         cots.append(lax.all_gather(swapped, "ch", axis=0, tiled=False))
@@ -477,20 +475,21 @@
             part = lax.dynamic_index_in_dim(full, (y + shift) % inner, 0, keepdims=False)
             cots.append(part if shift == 0 else around_inner(part, shift))
     got[0] = swap_gated(0)
-    for h in later_halves:
-        gateds[h], mixeds[h] = forward(queries, keys, values, prior, back, h, chunks)
-    up1, down1, gateds, cots[0] = fence(up1, down1, gateds, cots[0])
-
-    for h in later_halves:
-        second[h] = second_step(h)
     base = [None] * chunks
     base[0] = rows_own(0)
+    for h in later_halves:
+        gateds[h], mixeds[h] = forward(queries, keys, values, prior, back, h, chunks)
+        held = after(halves[h], gateds[h])
+        up1[h], down1[h] = along_line(held, up_pairs), along_line(held, down_pairs)
     second[0], got[0], gateds, cots, base = fence(second[0], got[0], gateds, cots, base)
 
     first[0], parcel = packet(0)
     third[0] = send_packet(parcel)
     for h in later_halves:
         got[h] = swap_gated(h)
+    up1, down1, parcel = fence(up1, down1, parcel)
+    for h in later_halves:
+        second[h] = second_step(h)
     rest[0] = rows_rest(0)
     begun = [gate_grad(pick, cot, weights(0), (0, 1, 2)) for cot in cots[1:]]
     second, rest[0], gateds, begun = fence(second, rest[0], gateds, begun)

time: 327 us -> 330 us (level)
    unnamed x46 -> x50, local copies, waits for them, and re-layouts: 10.4 us -> 10.6 us
  transfers between devices with their start and end apart: 29 -> 29, of which waited for: 11 -> 10; matrix products, arithmetic and copies ran while one was open for 8% -> 8% of each run, Pallas kernels for 46% -> 46%
where the time goes in v9:
time: 330 us; the launch traced here: 328 us
  Pallas kernels  164 us (50%)
  starting transfers between devices  67.7 us (21%)
  waiting for transfers between devices  40.4 us (12%)
  other arithmetic  22.9 us (7%)
  local copies, waits for them, and re-layouts  17.5 us (5%)
  between operations  14.7 us (4%)
    ppermute x26, starting transfers between devices, send(): return lax.ppermute(x, 'seq', pairs)  62.3 us
    pallas_call x6, Pallas kernels, gate_grad(): pl.pallas_call(functools.partial(gate_kernel, slots), grid_spec=pltpu.Pre...  44.4 us
    ppermute x26, waiting for transfers between devices, send(): return lax.ppermute(x, 'seq', pairs)  40.4 us
    pallas_call x4, Pallas kernels, weight_rows(): pl.pallas_call(functools.partial(rows_kernel, n), grid_spec=pltpu.Prefetc...  33.4 us
    pallas_call x2, Pallas kernels, middle(): pl.pallas_call(kernel, grid=(tiles,), in_specs=in_specs, out_specs=[here,...  25.3 us
    pallas_call x2, Pallas kernels, backward(): pl.pallas_call(backward_kernel, grid=(tiles,), in_specs=in_specs, out_spe...  20.9 us
    pallas_call x2, Pallas kernels, forward(): pl.pallas_call(forward_kernel, grid=(tiles,), in_specs=[here, here, here,...  20.2 us
    unnamed x50, local copies, waits for them, and re-layouts  10.6 us
  transfers between devices with their start and end apart: 29, of which 10 were waited for; matrix products, arithmetic and copies ran while one was open for 8% of the time, Pallas kernels for 46%

profile of v9, /device:TPU:10, one launch (start us, length us, event | category | flops | bytes accessed | tf_op | source)
XLA Modules:
  0.0 327.6 jit_solution(2959973850174580739)
XLA Ops:
  7.2 1.3 multiply_convert_fusion
  8.6 3.0 constant_dynamic-slice_fusion
  11.7 3.4 %collective-permute-start = (bf16[128,2048]{1,0:T(8,128)(2,1)S(1)}, bf16[128,2048]{1,0:T(8,128)(2,1)S(1)}, u32[]{:S(2)}, u32[]{:S(2)}) collective-permute-start(bf16[128,2048]{1,0:T(8,128)(2,1)S(1)} %multiply_convert_fusion), channel_id=1, source_target_pairs={{0,4},{4,8},{8,12},{12,16},{16,20},{20,24},{24,28},{1,5},{5,9},{9,... | collective-permute-start | bytes 1572872 | tf_op jit(solution)/shard_map/ppermute | solution.py:363
  15.4 10.4 %shard_map.101 = (bf16[16384,256]{1,0:T(8,128)(2,1)}, bf16[16384,256]{1,0:T(8,128)(2,1)}) custom-call(f32[128,256]{1,0:T(8,128)S(1)} %maximum_maximum_fusion.back_ref, f32[128,256]{1,0:T(8,128)S(1)} %concatenate.22.ahead_ref), custom_call_target="tpu_custom_call" | custom-call | flops 524288 | bytes 262144 | tf_op jit(solution)/shard_map/pallas_call | solution.py:54
  25.8 2.8 fusion.14
  28.7 3.5 %collective-permute-start.1 = (bf16[512,1024]{1,0:T(8,128)(2,1)S(1)}, bf16[512,1024]{1,0:T(8,128)(2,1)S(1)}, u32[]{:S(2)}, u32[]{:S(2)}) collective-permute-start(bf16[512,1024]{1,0:T(8,128)(2,1)S(1)} %get-tuple-element.83.refs_3_), channel_id=1, source_target_pairs={{0,8},{4,12},{8,16},{12,20},{16,24},{20,28},{1,9},{5,13},{9,17},{1... | collective-permute-start | bytes 3145736 | tf_op jit(solution)/shard_map/ppermute | solution.py:363
  32.2 2.4 collective-permute-start.2
  34.6 1.6 collective-permute-start.3
  36.2 9.9 %shard_map.102 = (bf16[1024,1024]{1,0:T(8,128)(2,1)S(1)}, bf16[1024,1024]{1,0:T(8,128)(2,1)S(1)}) custom-call(bf16[1024,2048]{1,0:T(8,128)(2,1)} %refs_1_.3, bf16[1024,2048]{1,0:T(8,128)(2,1)} %k.7, bf16[1024,2048]{1,0:T(8,128)(2,1)} %v.7, bf16[128,2048]{1,0:T(8,128)(2,1)S(1)} %collective-permute-done.prior.refs_5_, bf16[16384,256]{1,0:T(8,128)(2,1)} %get-tuple-element.86.table), custom_call_target="tpu_custom_call" | custom-call | flops 67108864 | bytes 229376 | tf_op jit(solution)/shard_map/pallas_call | solution.py:104
  46.1 1.4 copy-done.10
  47.5 1.3 copy-done.14
  48.8 6.4 %collective-permute-done.1.refs_5_ = bf16[512,1024]{1,0:T(8,128)(2,1)S(1)} collective-permute-done((bf16[512,1024]{1,0:T(8,128)(2,1)S(1)}, bf16[512,1024]{1,0:T(8,128)(2,1)S(1)}, u32[]{:S(2)}, u32[]{:S(2)}) %collective-permute-start.1) | collective-permute-done | bytes 1048608 | tf_op jit(solution)/shard_map/ppermute | solution.py:363
  55.2 3.2 collective-permute-done.2.refs_4_.refs_2_
  58.9 1.6 collective-permute-start.6
  60.5 3.5 %collective-permute-start.4 = (bf16[512,1024]{1,0:T(8,128)(2,1)}, bf16[512,1024]{1,0:T(8,128)(2,1)S(1)}, u32[]{:S(2)}, u32[]{:S(2)}) collective-permute-start(bf16[512,1024]{1,0:T(8,128)(2,1)} %copy-done.8), channel_id=1, source_target_pairs={{8,16},{12,20},{16,24},{20,28},{9,17},{13,21},{17,25},{21,29},{10,... | collective-permute-start | bytes 3145736 | tf_op jit(solution)/shard_map/ppermute | solution.py:363
  63.9 1.9 collective-permute-start.5
  65.9 10.3 %shard_map.103 = (bf16[1024,1024]{1,0:T(8,128)(2,1)S(1)}, bf16[1024,1024]{1,0:T(8,128)(2,1)S(1)}) custom-call(bf16[1024,2048]{1,0:T(8,128)(2,1)} %refs_1_.3, bf16[1024,2048]{1,0:T(8,128)(2,1)} %k.7, bf16[1024,2048]{1,0:T(8,128)(2,1)} %v.7, bf16[128,2048]{1,0:T(8,128)(2,1)S(1)} %collective-permute-done.prior.refs_5_, bf16[16384,256]{1,0:T(8,128)(2,1)} %get-tuple-element.86.table), custom_call_target="tpu_custom_call" | custom-call | flops 67108864 | bytes 229376 | tf_op jit(solution)/shard_map/pallas_call | solution.py:104
  76.2 1.3 copy-done.11
  77.5 1.3 copy-done.12
  78.8 4.8 %collective-permute-start.8 = (bf16[512,1024]{1,0:T(8,128)(2,1)}, bf16[512,1024]{1,0:T(8,128)(2,1)}, u32[]{:S(2)}, u32[]{:S(2)}) collective-permute-start(bf16[512,1024]{1,0:T(8,128)(2,1)} %get-tuple-element.101.refs_4_), channel_id=1, source_target_pairs={{0,8},{4,12},{8,16},{12,20},{16,24},{20,28},{1,9},{5,13},{9,17},{1... | collective-permute-start | bytes 3145736 | tf_op jit(solution)/shard_map/ppermute | solution.py:363
  83.7 2.0 collective-permute-start.9
  85.7 9.0 %shard_map.104.refs_2_ = f32[4,512,1024]{2,1,0:T(8,128)} custom-call(s32[4]{0:T(128)S(1)} %pad_add_fusion.pick, bf16[4,1024,512]{2,1,0:T(8,128)(2,1)} %bitcast.48, bf16[1024,1024]{1,0:T(8,128)(2,1)S(1)} %copy-done.15), custom_call_target="tpu_custom_call" | custom-call | flops 16777216 | bytes 49152 | tf_op jit(solution)/shard_map/pallas_call | solution.py:303
  94.7 10.1 %collective-permute-done.6.refs_1_ = bf16[1024,1024]{1,0:T(8,128)(2,1)} collective-permute-done((bf16[1024,1024]{1,0:T(8,128)(2,1)}, bf16[1024,1024]{1,0:T(8,128)(2,1)}, u32[]{:S(2)}, u32[]{:S(2)}) %collective-permute-start.6) | collective-permute-done | bytes 2097184 | tf_op jit(solution)/shard_map/ppermute | solution.py:363
  104.9 1.5 collective-permute-start.12
  106.5 5.0 %shard_map.105 = (bf16[512,1024]{1,0:T(8,128)(2,1)S(1)}, bf16[512,1024]{1,0:T(8,128)(2,1)}) custom-call(s32[3]{0:T(128)S(1)} %pad_add_fusion.1.pick, bf16[4,1024,512]{2,1,0:T(8,128)(2,1)} %bitcast.36, bf16[1024,1024]{1,0:T(8,128)(2,1)} %collective-permute-done.6.refs_1_, f32[4,512,1024]{2,1,0:T(8,128)} %shard_map.104.refs_2_, ...), custom_call_target="tpu_custom_call" | custom-call | flops 16777216 | bytes 49152 | tf_op jit(solution)/shard_map/pallas_call | solution.py:337
  112.5 4.4 %collective-permute-start.10 = (bf16[512,1024]{1,0:T(8,128)(2,1)}, bf16[512,1024]{1,0:T(8,128)(2,1)}, u32[]{:S(2)}, u32[]{:S(2)}) collective-permute-start(bf16[512,1024]{1,0:T(8,128)(2,1)} %collective-permute-done.8.refs_6_), channel_id=1, source_target_pairs={{8,16},{12,20},{16,24},{20,28},{9,17},{13,21},{17,25},{21,29},{10,... | collective-permute-start | bytes 3145736 | tf_op jit(solution)/shard_map/ppermute | solution.py:363
  116.9 1.9 collective-permute-start.11
  119.1 7.7 %shard_map.106 = bf16[3,512,1024]{2,1,0:T(8,128)(2,1)S(1)} custom-call(s32[3]{0:T(128)S(1)} %pad_add_fusion.2.pick, bf16[4,1024,512]{2,1,0:T(8,128)(2,1)} %bitcast.37, bf16[1024,1024]{1,0:T(8,128)(2,1)} %collective-permute-done.6.refs_1_, f32[4,512,1024]{2,1,0:T(8,128)} %shard_map.104.refs_2_), custom_call_target="tpu_custom_call" | custom-call | flops 16777216 | bytes 49152 | tf_op jit(solution)/shard_map/pallas_call | solution.py:303
  126.9 7.8 %shard_map.107.refs_3_ = bf16[1024,1024]{1,0:T(8,128)(2,1)} custom-call(s32[7]{0:T(128)S(1)} %stack.58.pick, bf16[4,1024,512]{2,1,0:T(8,128)(2,1)} %bitcast.38, bf16[4,1024,512]{2,1,0:T(8,128)(2,1)} %bitcast.39, bf16[4,1024,512]{2,1,0:T(8,128)(2,1)} %bitcast.40, bf16[512,1024]{1,0:T(8,128)(2,1)S(1)} %copy-done.2, ...), custom_call_target="tpu_custom_call" | custom-call | flops 50331648 | bytes 98304 | tf_op jit(solution)/shard_map/pallas_call | solution.py:263
  135.7 6.8 %collective-permute-done.11.refs_4_.refs_8_ = bf16[512,1024]{1,0:T(8,128)(2,1)} collective-permute-done((bf16[512,1024]{1,0:T(8,128)(2,1)S(1)}, bf16[512,1024]{1,0:T(8,128)(2,1)}, u32[]{:S(2)}, u32[]{:S(2)}) %collective-permute-start.11) | collective-permute-done | bytes 1048608 | tf_op jit(solution)/shard_map/ppermute | solution.py:363
  142.5 9.1 %shard_map.108.refs_2_ = f32[4,512,1024]{2,1,0:T(8,128)} custom-call(s32[4]{0:T(128)S(1)} %pad_add_fusion.pick, bf16[4,1024,512]{2,1,0:T(8,128)(2,1)} %bitcast.49, bf16[1024,1024]{1,0:T(8,128)(2,1)S(1)} %copy-done.13), custom_call_target="tpu_custom_call" | custom-call | flops 16777216 | bytes 49152 | tf_op jit(solution)/shard_map/pallas_call | solution.py:303
  151.5 7.8 %shard_map.109.refs_3_ = bf16[1024,1024]{1,0:T(8,128)(2,1)} custom-call(s32[7]{0:T(128)S(1)} %stack.58.pick, bf16[4,1024,512]{2,1,0:T(8,128)(2,1)} %bitcast.50, bf16[4,1024,512]{2,1,0:T(8,128)(2,1)} %bitcast.51, bf16[4,1024,512]{2,1,0:T(8,128)(2,1)} %bitcast.52, bf16[512,1024]{1,0:T(8,128)(2,1)S(1)} %copy-done.2, ...), custom_call_target="tpu_custom_call" | custom-call | flops 50331648 | bytes 98304 | tf_op jit(solution)/shard_map/pallas_call | solution.py:263
  159.3 1.5 collective-permute-done.7.refs_1_
  160.9 4.8 %shard_map.110 = bf16[1024,1024]{1,0:T(8,128)(2,1)S(1)} custom-call(s32[7]{0:T(128)S(1)} %stack.58.pick, bf16[4,1024,512]{2,1,0:T(8,128)(2,1)} %bitcast.41, bf16[512,1024]{1,0:T(8,128)(2,1)} %collective-permute-done.7.refs_1_, bf16[512,1024]{1,0:T(8,128)(2,1)S(1)} %collective-permute-done.2.refs_4_.refs_2_, bf16[1024,1024]{1,0:T(8,128)(2,1)} %shard_map.107.refs_3_), custom_call_target="tpu_custom_call" | custom-call | flops 16777216 | bytes 32768 | tf_op jit(solution)/shard_map/pallas_call | solution.py:263
  165.7 4.8 %shard_map.111 = (bf16[512,1024]{1,0:T(8,128)(2,1)S(1)}, bf16[512,1024]{1,0:T(8,128)(2,1)S(1)}) custom-call(s32[3]{0:T(128)S(1)} %pad_add_fusion.1.pick, bf16[4,1024,512]{2,1,0:T(8,128)(2,1)} %bitcast.42, bf16[1024,1024]{1,0:T(8,128)(2,1)} %collective-permute-done.12.refs_1_, f32[4,512,1024]{2,1,0:T(8,128)} %shard_map.108.refs_2_, ...), custom_call_target="tpu_custom_call" | custom-call | flops 16777216 | bytes 49152 | tf_op jit(solution)/shard_map/pallas_call | solution.py:337
  170.5 2.6 collective-permute-start.14
  173.6 2.6 fusion.11
  177.6 2.1 collective-permute-start.17
  179.7 7.6 %shard_map.112 = bf16[3,512,1024]{2,1,0:T(8,128)(2,1)S(1)} custom-call(s32[3]{0:T(128)S(1)} %pad_add_fusion.2.pick, bf16[4,1024,512]{2,1,0:T(8,128)(2,1)} %bitcast.43, bf16[1024,1024]{1,0:T(8,128)(2,1)} %collective-permute-done.12.refs_1_, f32[4,512,1024]{2,1,0:T(8,128)} %shard_map.108.refs_2_), custom_call_target="tpu_custom_call" | custom-call | flops 16777216 | bytes 49152 | tf_op jit(solution)/shard_map/pallas_call | solution.py:303
  187.3 5.3 %shard_map.113.own_ref = bf16[1024,1024]{1,0:T(8,128)(2,1)S(1)} custom-call(s32[7]{0:T(128)S(1)} %stack.58.pick, bf16[4,1024,512]{2,1,0:T(8,128)(2,1)} %bitcast.53, bf16[512,1024]{1,0:T(8,128)(2,1)} %collective-permute-done.7.refs_1_, bf16[512,1024]{1,0:T(8,128)(2,1)S(1)} %collective-permute-done.2.refs_4_.refs_2_, bf16[1024,1024]{1,0:T(8,128)(2,1)} %shard_map.109.refs_3_), custom_call_target="tpu_custom_call" | custom-call | flops 16777216 | bytes 32768 | tf_op jit(solution)/shard_map/pallas_call | solution.py:263
  192.6 1.3 copy-done.4
  194.0 3.3 %collective-permute-done.14.refs_9_ = bf16[512,1024]{1,0:T(8,128)(2,1)} collective-permute-done((bf16[512,1024]{1,0:T(8,128)(2,1)S(1)}, bf16[512,1024]{1,0:T(8,128)(2,1)}, u32[]{:S(2)}, u32[]{:S(2)}) %collective-permute-start.14) | collective-permute-done | bytes 1048608 | tf_op jit(solution)/shard_map/ppermute | solution.py:363
  197.3 9.4 %shard_map.114 = bf16[1024,1024]{1,0:T(8,128)(2,1)} custom-call(s32[7]{0:T(128)S(1)} %stack.58.pick, bf16[4,1024,512]{2,1,0:T(8,128)(2,1)} %bitcast.44, bf16[4,1024,512]{2,1,0:T(8,128)(2,1)} %bitcast.45, bf16[4,1024,512]{2,1,0:T(8,128)(2,1)} %bitcast.46, bf16[4,1024,512]{2,1,0:T(8,128)(2,1)} %bitcast.47, bf16[512,1024]{1,0:T(8,128)(2,1)} %get-tuple-element.101.refs_4_, ...), custom_call_target="tpu_custom_call" | custom-call | flops 67108864 | bytes 131072 | tf_op jit(solution)/shard_map/pallas_call | solution.py:263
  206.7 2.7 fusion.10
  210.7 1.9 collective-permute-start.22
  212.6 7.2 %collective-permute-done.16 = bf16[512,1024]{1,0:T(8,128)(2,1)} collective-permute-done((bf16[512,1024]{1,0:T(8,128)(2,1)}, bf16[512,1024]{1,0:T(8,128)(2,1)}, u32[]{:S(2)}, u32[]{:S(2)}) %collective-permute-start.16) | collective-permute-done | bytes 1048608 | tf_op jit(solution)/shard_map/ppermute | solution.py:363
  220.3 3.9 %fusion.1 = (bf16[512,1024]{1,0:T(8,128)(2,1)}, bf16[512,1024]{1,0:T(8,128)(2,1)}) fusion(bf16[512,1024]{1,0:T(8,128)(2,1)} %collective-permute-done.17, bf16[512,1024]{1,0:T(8,128)(2,1)} %collective-permute-done.16, bf16[512,1024]{1,0:T(8,128)(2,1)S(1)} %copy-done.19, pred[]{:T(512)S(6)} %eq.15, pred[]{:T(512)S(6)} %eq.17, ...), kind=kLoop, calls=%fused_computation.9 | loop fusion | flops 6291456 | bytes 6291458 | tf_op jit(solution)/shard_map/convert_element_type | solution.py:432
  224.2 1.9 collective-permute-start.18
  226.2 5.1 %collective-permute-start.19 = (bf16[512,1024]{1,0:T(8,128)(2,1)}, bf16[512,1024]{1,0:T(8,128)(2,1)}, u32[]{:S(2)}, u32[]{:S(2)}) collective-permute-start(bf16[512,1024]{1,0:T(8,128)(2,1)} %get-tuple-element.160), channel_id=1, source_target_pairs={{8,0},{12,4},{16,8},{20,12},{24,16},{28,20},{9,1},{13,5},{17,9},{2... | collective-permute-start | bytes 3145736 | tf_op jit(solution)/shard_map/ppermute | solution.py:363
  231.3 9.4 %shard_map.115.own_ref = bf16[1024,1024]{1,0:T(8,128)(2,1)} custom-call(s32[7]{0:T(128)S(1)} %stack.58.pick, bf16[4,1024,512]{2,1,0:T(8,128)(2,1)} %bitcast.54, bf16[4,1024,512]{2,1,0:T(8,128)(2,1)} %bitcast.55, bf16[4,1024,512]{2,1,0:T(8,128)(2,1)} %bitcast.56, bf16[4,1024,512]{2,1,0:T(8,128)(2,1)} %bitcast.57, ...), custom_call_target="tpu_custom_call" | custom-call | flops 67108864 | bytes 131072 | tf_op jit(solution)/shard_map/pallas_call | solution.py:263
  240.7 12.6 %shard_map.116 = (bf16[1024,2048]{1,0:T(8,128)(2,1)}, bf16[1024,1024]{1,0:T(8,128)(2,1)S(1)}, bf16[128,1024]{1,0:T(8,128)(2,1)S(1)}, f32[64,256]{1,0:T(8,128)S(1)}) custom-call(bf16[1024,1024]{1,0:T(8,128)(2,1)S(1)} %copy-done.5, bf16[1024,1024]{1,0:T(8,128)(2,1)} %collective-permute-done.13.refs_0_, bf16[1024,2048]{1,0:T(8,128)(2,1)} %refs_1_.3, ...), custom_call_target="tpu_custom_call" | custom-call | flops 67108864 | bytes 294912 | tf_op jit(solution)/shard_map/pallas_call | solution.py:171
  253.4 4.0 %fusion.7 = (bf16[512,1024]{1,0:T(8,128)(2,1)}, bf16[512,1024]{1,0:T(8,128)(2,1)}) fusion(bf16[512,1024]{1,0:T(8,128)(2,1)} %collective-permute-done.21, bf16[512,1024]{1,0:T(8,128)(2,1)} %collective-permute-done.22, bf16[512,1024]{1,0:T(8,128)(2,1)S(1)} %copy-done.21, pred[]{:T(512)S(6)} %eq.15, bf16[3,512,1024]{2,1,0:T(8,128)(2,1)S(1)} %shard_map.112, ...), kind=kLoop, calls=%fused_computation.15 | loop fusion | flops 6291456 | bytes 6291458 | tf_op jit(solution)/shard_map/convert_element_type | solution.py:432
  257.4 1.9 collective-permute-start.23
  259.3 5.1 %collective-permute-start.24 = (bf16[512,1024]{1,0:T(8,128)(2,1)}, bf16[512,1024]{1,0:T(8,128)(2,1)}, u32[]{:S(2)}, u32[]{:S(2)}) collective-permute-start(bf16[512,1024]{1,0:T(8,128)(2,1)} %get-tuple-element.157), channel_id=1, source_target_pairs={{8,0},{12,4},{16,8},{20,12},{24,16},{28,20},{9,1},{13,5},{17,9},{2... | collective-permute-start | bytes 3145736 | tf_op jit(solution)/shard_map/ppermute | solution.py:363
  264.7 3.2 fusion.13
  267.8 1.9 collective-permute-start.25
  269.8 12.6 %shard_map.117 = (bf16[1024,2048]{1,0:T(8,128)(2,1)}, bf16[1024,1024]{1,0:T(8,128)(2,1)S(1)}, bf16[128,1024]{1,0:T(8,128)(2,1)S(1)}, f32[64,256]{1,0:T(8,128)S(1)}) custom-call(bf16[1024,1024]{1,0:T(8,128)(2,1)S(1)} %copy-done.3, bf16[1024,1024]{1,0:T(8,128)(2,1)} %collective-permute-done.15.refs_0_, ...), custom_call_target="tpu_custom_call", output_to_operand_aliasing={{0}: (7, {})} | custom-call | flops 67108864 | bytes 294912 | tf_op jit(solution)/shard_map/pallas_call | solution.py:171
  284.6 5.4 %all-to-all-start = ((f32[8,16,128]{2,1,0:T(8,128)}), f32[8,16,128]{2,1,0:T(8,128)S(1)}, u32[]{:S(2)}, u32[]{:S(2)}) async-start(f32[8,16,128]{2,1,0:T(8,128)} %bitcast.20), calls=%async_computation | async-start | bytes 131072 | tf_op jit(solution)/shard_map/all_to_all | solution.py:549
  290.0 3.6 %collective-permute-start.20 = (bf16[128,1024]{1,0:T(8,128)(2,1)S(1)}, bf16[128,1024]{1,0:T(8,128)(2,1)S(1)}, u32[]{:S(2)}, u32[]{:S(2)}) collective-permute-start(bf16[128,1024]{1,0:T(8,128)(2,1)S(1)} %get-tuple-element.139), channel_id=1, source_target_pairs={{4,0},{8,4},{12,8},{16,12},{20,16},{24,20},{28,24},{5,1},{9,5},{13... | collective-permute-start | bytes 786440 | tf_op jit(solution)/shard_map/ppermute | solution.py:363
  293.6 2.6 fusion.9
  296.2 1.5 pad_maximum_fusion
  297.7 10.4 %shard_map.118 = (bf16[1024,2048]{1,0:T(8,128)(2,1)}, bf16[1024,2048]{1,0:T(8,128)(2,1)}) custom-call(bf16[1024,1024]{1,0:T(8,128)(2,1)S(1)} %get-tuple-element.147.gm, bf16[128,1024]{1,0:T(8,128)(2,1)S(1)} %collective-permute-done.25.later, bf16[1024,2048]{1,0:T(8,128)(2,1)} %k.7, bf16[1024,2048]{1,0:T(8,128)(2,1)} %v.7, ...), custom_call_target="tpu_custom_call" | custom-call | flops 67108864 | bytes 229376 | tf_op jit(solution)/shard_map/pallas_call | solution.py:216
  308.8 1.6 copy-done.17
  310.4 10.4 %shard_map.119 = (bf16[1024,2048]{1,0:T(8,128)(2,1)}, bf16[1024,2048]{1,0:T(8,128)(2,1)}) custom-call(bf16[1024,1024]{1,0:T(8,128)(2,1)S(1)} %copy-done.17, bf16[128,1024]{1,0:T(8,128)(2,1)S(1)} %collective-permute-done.20.later, bf16[1024,2048]{1,0:T(8,128)(2,1)} %k.7, bf16[1024,2048]{1,0:T(8,128)(2,1)} %v.7, ...), custom_call_target="tpu_custom_call", output_to_operand_aliasing={{0}: (5, {}), {1}: (6, {})} | custom-call | flops 67108864 | bytes 229376 | tf_op jit(solution)/shard_map/pallas_call | solution.py:216
  (90 shorter events, 10.2 us)
Async XLA Ops:
  7.2 51.7 %all-gather.5.cloned.1.call-start = ((), (), s32[]{:S(2)}) async-start(), calls=%async_computation.1 | async-start | bytes 5242880 | tf_op jit(solution)/shard_map/all_gather | solution.py:458
  8.6 6.5 %copy-start.24 = (bf16[128,128]{1,0:T(8,128)(2,1)S(1)}, bf16[128,128]{1,0:T(8,128)(2,1)}, u32[]{:S(2)}) copy-start(bf16[128,128]{1,0:T(8,128)(2,1)} %param.9) | copy-start | bytes 98308
  11.6 93.3 %all-gather.7.cloned.1.call-start = ((), (), s32[]{:S(2)}) async-start(), calls=%async_computation.2 | async-start | bytes 5242880 | tf_op jit(solution)/shard_map/all_gather | solution.py:470
  11.7 17.0 %collective-permute-start = (bf16[128,2048]{1,0:T(8,128)(2,1)S(1)}, bf16[128,2048]{1,0:T(8,128)(2,1)S(1)}, u32[]{:S(2)}, u32[]{:S(2)}) collective-permute-start(bf16[128,2048]{1,0:T(8,128)(2,1)S(1)} %multiply_convert_fusion), channel_id=1, source_target_pairs={{0,4},{4,8},{8,12},{12,16},{16,20},{20,24},{24,28},{1,5},{5,9},{9,... | collective-permute-start | bytes 1572872 | tf_op jit(solution)/shard_map/ppermute | solution.py:363
  25.8 8.8 %copy-start.23 = (bf16[1024,512]{1,0:T(8,128)(2,1)S(1)}, bf16[1024,512]{1,0:T(8,128)(2,1)}, u32[]{:S(2)}) copy-start(bf16[1024,512]{1,0:T(8,128)(2,1)} %get-tuple-element.84) | copy-start | bytes 3145732
  28.7 17.4 %copy-start.1 = (bf16[512,1024]{1,0:T(8,128)(2,1)}, bf16[512,1024]{1,0:T(8,128)(2,1)S(1)}, u32[]{:S(2)}) copy-start(bf16[512,1024]{1,0:T(8,128)(2,1)S(1)} %get-tuple-element.83.refs_3_) | copy-start | bytes 3145732
  28.7 37.2 %copy-start.6 = (bf16[128,2048]{1,0:T(8,128)(2,1)}, bf16[128,2048]{1,0:T(8,128)(2,1)S(1)}, u32[]{:S(2)}) copy-start(bf16[128,2048]{1,0:T(8,128)(2,1)S(1)} %collective-permute-done.prior.refs_5_) | copy-start | bytes 1572868
  28.7 26.5 %collective-permute-start.1 = (bf16[512,1024]{1,0:T(8,128)(2,1)S(1)}, bf16[512,1024]{1,0:T(8,128)(2,1)S(1)}, u32[]{:S(2)}, u32[]{:S(2)}) collective-permute-start(bf16[512,1024]{1,0:T(8,128)(2,1)S(1)} %get-tuple-element.83.refs_3_), channel_id=1, source_target_pairs={{0,8},{4,12},{8,16},{12,20},{16,24},{20,28},{1,9},{5,13},{9,17},{1... | collective-permute-start | bytes 3145736 | tf_op jit(solution)/shard_map/ppermute | solution.py:363
  32.2 26.2 %collective-permute-start.2 = (bf16[512,1024]{1,0:T(8,128)(2,1)S(1)}, bf16[512,1024]{1,0:T(8,128)(2,1)S(1)}, u32[]{:S(2)}, u32[]{:S(2)}) collective-permute-start(bf16[512,1024]{1,0:T(8,128)(2,1)S(1)} %get-tuple-element.83.refs_3_), channel_id=1, source_target_pairs={{8,0},{12,4},{16,8},{20,12},{24,16},{28,20},{9,1},{13,5},{17,9},{2... | collective-permute-start | bytes 3145736 | tf_op jit(solution)/shard_map/ppermute | solution.py:363
  34.6 24.2 %collective-permute-start.3 = (bf16[1024,512]{1,0:T(8,128)(2,1)S(1)}, bf16[1024,512]{1,0:T(8,128)(2,1)}, u32[]{:S(2)}, u32[]{:S(2)}) collective-permute-start(bf16[1024,512]{1,0:T(8,128)(2,1)S(1)} %copy-done.23), channel_id=1, source_target_pairs={{0,4},{4,0},{8,12},{12,8},{16,20},{20,16},{24,28},{28,24},{1,5},{5... | collective-permute-start | bytes 3145736 | tf_op jit(solution)/shard_map/ppermute | solution.py:363
  46.1 1.4 copy-start.10
  47.5 1.3 copy-start.14
  55.2 3.2 copy-start.8
  58.9 46.0 %collective-permute-start.6 = (bf16[1024,1024]{1,0:T(8,128)(2,1)}, bf16[1024,1024]{1,0:T(8,128)(2,1)}, u32[]{:S(2)}, u32[]{:S(2)}) collective-permute-start(bf16[1024,1024]{1,0:T(8,128)(2,1)} %copy-done.14), channel_id=1, source_target_pairs={{0,4},{4,0},{8,12},{12,8},{16,20},{20,16},{24,28},{28,24},{1,5},{5... | collective-permute-start | bytes 6291464 | tf_op jit(solution)/shard_map/ppermute | solution.py:363
  60.5 34.3 %collective-permute-start.4 = (bf16[512,1024]{1,0:T(8,128)(2,1)}, bf16[512,1024]{1,0:T(8,128)(2,1)S(1)}, u32[]{:S(2)}, u32[]{:S(2)}) collective-permute-start(bf16[512,1024]{1,0:T(8,128)(2,1)} %copy-done.8), channel_id=1, source_target_pairs={{8,16},{12,20},{16,24},{20,28},{9,17},{13,21},{17,25},{21,29},{10,... | collective-permute-start | bytes 3145736 | tf_op jit(solution)/shard_map/ppermute | solution.py:363
  63.9 30.8 %collective-permute-start.5 = (bf16[512,1024]{1,0:T(8,128)(2,1)S(1)}, bf16[512,1024]{1,0:T(8,128)(2,1)}, u32[]{:S(2)}, u32[]{:S(2)}) collective-permute-start(bf16[512,1024]{1,0:T(8,128)(2,1)S(1)} %collective-permute-done.2.refs_4_.refs_2_), channel_id=1, source_target_pairs={{16,8},{20,12},{8,0},{12,4},{17,9},{21,13},{9,1},{13,5},{18,10},{2... | collective-permute-start | bytes 3145736 | tf_op jit(solution)/shard_map/ppermute | solution.py:363
  65.9 19.8 %copy-start.15 = (bf16[1024,1024]{1,0:T(8,128)(2,1)S(1)}, bf16[1024,1024]{1,0:T(8,128)(2,1)}, u32[]{:S(2)}) copy-start(bf16[1024,1024]{1,0:T(8,128)(2,1)} %copy-done.14) | copy-start | bytes 6291460
  76.2 1.3 copy-start.11
  77.5 1.3 copy-start.12
  78.8 33.7 %collective-permute-start.8 = (bf16[512,1024]{1,0:T(8,128)(2,1)}, bf16[512,1024]{1,0:T(8,128)(2,1)}, u32[]{:S(2)}, u32[]{:S(2)}) collective-permute-start(bf16[512,1024]{1,0:T(8,128)(2,1)} %get-tuple-element.101.refs_4_), channel_id=1, source_target_pairs={{0,8},{4,12},{8,16},{12,20},{16,24},{20,28},{1,9},{5,13},{9,17},{1... | collective-permute-start | bytes 3145736 | tf_op jit(solution)/shard_map/ppermute | solution.py:363
  83.7 28.9 %collective-permute-start.9 = (bf16[512,1024]{1,0:T(8,128)(2,1)}, bf16[512,1024]{1,0:T(8,128)(2,1)S(1)}, u32[]{:S(2)}, u32[]{:S(2)}) collective-permute-start(bf16[512,1024]{1,0:T(8,128)(2,1)} %get-tuple-element.101.refs_4_), channel_id=1, source_target_pairs={{8,0},{12,4},{16,8},{20,12},{24,16},{28,20},{9,1},{13,5},{17,9},{2... | collective-permute-start | bytes 3145736 | tf_op jit(solution)/shard_map/ppermute | solution.py:363
  104.9 60.8 %collective-permute-start.12 = (bf16[1024,1024]{1,0:T(8,128)(2,1)}, bf16[1024,1024]{1,0:T(8,128)(2,1)}, u32[]{:S(2)}, u32[]{:S(2)}) collective-permute-start(bf16[1024,1024]{1,0:T(8,128)(2,1)} %copy-done.12), channel_id=1, source_target_pairs={{0,4},{4,0},{8,12},{12,8},{16,20},{20,16},{24,28},{28,24},{1,5},{5... | collective-permute-start | bytes 6291464 | tf_op jit(solution)/shard_map/ppermute | solution.py:363
  111.5 1.0 copy-start.18
  112.5 23.1 %collective-permute-start.10 = (bf16[512,1024]{1,0:T(8,128)(2,1)}, bf16[512,1024]{1,0:T(8,128)(2,1)}, u32[]{:S(2)}, u32[]{:S(2)}) collective-permute-start(bf16[512,1024]{1,0:T(8,128)(2,1)} %collective-permute-done.8.refs_6_), channel_id=1, source_target_pairs={{8,16},{12,20},{16,24},{20,28},{9,17},{13,21},{17,25},{21,29},{10,... | collective-permute-start | bytes 3145736 | tf_op jit(solution)/shard_map/ppermute | solution.py:363
  116.9 25.5 %collective-permute-start.11 = (bf16[512,1024]{1,0:T(8,128)(2,1)S(1)}, bf16[512,1024]{1,0:T(8,128)(2,1)}, u32[]{:S(2)}, u32[]{:S(2)}) collective-permute-start(bf16[512,1024]{1,0:T(8,128)(2,1)S(1)} %collective-permute-done.9.refs_5_.refs_10_), channel_id=1, source_target_pairs={{16,8},{20,12},{8,0},{12,4},{17,9},{21,13},{9,1},{13,5},{18,10},{2... | collective-permute-start | bytes 3145736 | tf_op jit(solution)/shard_map/ppermute | solution.py:363
  118.9 42.0 %collective-permute-start.7 = (bf16[512,1024]{1,0:T(8,128)(2,1)}, bf16[512,1024]{1,0:T(8,128)(2,1)}, u32[]{:S(2)}, u32[]{:S(2)}) collective-permute-start(bf16[512,1024]{1,0:T(8,128)(2,1)} %get-tuple-element.99), channel_id=1, source_target_pairs={{0,8},{4,12},{24,16},{28,20},{16,24},{20,28},{8,0},{12,4},{1,9},{5... | collective-permute-start | bytes 3145736 | tf_op jit(solution)/shard_map/ppermute | solution.py:363
  119.1 7.7 %copy-start.2 = (bf16[512,1024]{1,0:T(8,128)(2,1)S(1)}, bf16[512,1024]{1,0:T(8,128)(2,1)}, u32[]{:S(2)}) copy-start(bf16[512,1024]{1,0:T(8,128)(2,1)} %copy-done.1) | copy-start | bytes 3145732
  119.1 7.7 %copy-start.9 = (bf16[512,1024]{1,0:T(8,128)(2,1)S(1)}, bf16[512,1024]{1,0:T(8,128)(2,1)}, u32[]{:S(2)}) copy-start(bf16[512,1024]{1,0:T(8,128)(2,1)} %copy-done.8) | copy-start | bytes 3145732
  126.9 15.6 %copy-start.13 = (bf16[1024,1024]{1,0:T(8,128)(2,1)S(1)}, bf16[1024,1024]{1,0:T(8,128)(2,1)}, u32[]{:S(2)}) copy-start(bf16[1024,1024]{1,0:T(8,128)(2,1)} %copy-done.12) | copy-start | bytes 6291460
  170.5 7.0 %copy-start.20 = (bf16[512,1024]{1,0:T(8,128)(2,1)}, bf16[512,1024]{1,0:T(8,128)(2,1)S(1)}, u32[]{:S(2)}) copy-start(bf16[512,1024]{1,0:T(8,128)(2,1)S(1)} %get-tuple-element.141) | copy-start | bytes 3145732
  170.5 26.8 %collective-permute-start.14 = (bf16[512,1024]{1,0:T(8,128)(2,1)S(1)}, bf16[512,1024]{1,0:T(8,128)(2,1)}, u32[]{:S(2)}, u32[]{:S(2)}) collective-permute-start(bf16[512,1024]{1,0:T(8,128)(2,1)S(1)} %get-tuple-element.121), channel_id=1, source_target_pairs={{0,8},{4,12},{24,16},{28,20},{16,24},{20,28},{8,0},{12,4},{1,9},{5... | collective-permute-start | bytes 3145736 | tf_op jit(solution)/shard_map/ppermute | solution.py:363
  173.1 53.0 %collective-permute-start.13 = (bf16[1024,1024]{1,0:T(8,128)(2,1)S(1)}, bf16[1024,1024]{1,0:T(8,128)(2,1)}, u32[]{:S(2)}, u32[]{:S(2)}) collective-permute-start(bf16[1024,1024]{1,0:T(8,128)(2,1)S(1)} %shard_map.110), channel_id=1, source_target_pairs={{0,4},{4,0},{8,12},{12,8},{16,20},{20,16},{24,28},{28,24},{1,5},{5... | collective-permute-start | bytes 6291464 | tf_op jit(solution)/shard_map/ppermute | solution.py:363
  176.3 43.5 %collective-permute-start.16 = (bf16[512,1024]{1,0:T(8,128)(2,1)}, bf16[512,1024]{1,0:T(8,128)(2,1)}, u32[]{:S(2)}, u32[]{:S(2)}) collective-permute-start(bf16[512,1024]{1,0:T(8,128)(2,1)} %fusion.11), channel_id=1, source_target_pairs={{0,8},{4,12},{24,16},{28,20},{1,9},{5,13},{25,17},{29,21},{2,10},{... | collective-permute-start | bytes 3145736 | tf_op jit(solution)/shard_map/ppermute | solution.py:363
  177.6 42.7 %collective-permute-start.17 = (bf16[512,1024]{1,0:T(8,128)(2,1)}, bf16[512,1024]{1,0:T(8,128)(2,1)}, u32[]{:S(2)}, u32[]{:S(2)}) collective-permute-start(bf16[512,1024]{1,0:T(8,128)(2,1)} %fusion.11), channel_id=1, source_target_pairs={{8,16},{12,20},{16,8},{20,12},{9,17},{13,21},{17,9},{21,13},{10,18... | collective-permute-start | bytes 3145736 | tf_op jit(solution)/shard_map/ppermute | solution.py:363
  187.3 66.0 %copy-start = (bf16[3,512,1024]{2,1,0:T(8,128)(2,1)}, bf16[3,512,1024]{2,1,0:T(8,128)(2,1)S(1)}, u32[]{:S(2)}) copy-start(bf16[3,512,1024]{2,1,0:T(8,128)(2,1)S(1)} %shard_map.112) | copy-start | bytes 9437188
  192.6 1.3 copy-start.4
  206.7 13.6 %copy-start.19 = (bf16[512,1024]{1,0:T(8,128)(2,1)S(1)}, bf16[512,1024]{1,0:T(8,128)(2,1)}, u32[]{:S(2)}) copy-start(bf16[512,1024]{1,0:T(8,128)(2,1)} %copy-done.18) | copy-start | bytes 3145732
  209.4 44.0 %collective-permute-start.21 = (bf16[512,1024]{1,0:T(8,128)(2,1)}, bf16[512,1024]{1,0:T(8,128)(2,1)}, u32[]{:S(2)}, u32[]{:S(2)}) collective-permute-start(bf16[512,1024]{1,0:T(8,128)(2,1)} %fusion.10), channel_id=1, source_target_pairs={{0,8},{4,12},{24,16},{28,20},{1,9},{5,13},{25,17},{29,21},{2,10},{... | collective-permute-start | bytes 3145736 | tf_op jit(solution)/shard_map/ppermute | solution.py:363
  210.7 42.7 %collective-permute-start.22 = (bf16[512,1024]{1,0:T(8,128)(2,1)}, bf16[512,1024]{1,0:T(8,128)(2,1)}, u32[]{:S(2)}, u32[]{:S(2)}) collective-permute-start(bf16[512,1024]{1,0:T(8,128)(2,1)} %fusion.10), channel_id=1, source_target_pairs={{8,16},{12,20},{16,8},{20,12},{9,17},{13,21},{17,9},{21,13},{10,18... | collective-permute-start | bytes 3145736 | tf_op jit(solution)/shard_map/ppermute | solution.py:363
  219.8 50.0 %collective-permute-start.15 = (bf16[1024,1024]{1,0:T(8,128)(2,1)}, bf16[1024,1024]{1,0:T(8,128)(2,1)}, u32[]{:S(2)}, u32[]{:S(2)}) collective-permute-start(bf16[1024,1024]{1,0:T(8,128)(2,1)} %shard_map.114), channel_id=1, source_target_pairs={{0,4},{4,0},{8,12},{12,8},{16,20},{20,16},{24,28},{28,24},{1,5},{5... | collective-permute-start | bytes 6291464 | tf_op jit(solution)/shard_map/ppermute | solution.py:363
  224.2 40.5 %collective-permute-start.18 = (bf16[512,1024]{1,0:T(8,128)(2,1)}, bf16[512,1024]{1,0:T(8,128)(2,1)}, u32[]{:S(2)}, u32[]{:S(2)}) collective-permute-start(bf16[512,1024]{1,0:T(8,128)(2,1)} %get-tuple-element.159), channel_id=1, source_target_pairs={{0,8},{4,12},{8,16},{12,20},{16,24},{20,28},{1,9},{5,13},{9,17},{1... | collective-permute-start | bytes 3145736 | tf_op jit(solution)/shard_map/ppermute | solution.py:363
  226.1 14.5 %copy-start.5 = (bf16[1024,1024]{1,0:T(8,128)(2,1)S(1)}, bf16[1024,1024]{1,0:T(8,128)(2,1)}, u32[]{:S(2)}) copy-start(bf16[1024,1024]{1,0:T(8,128)(2,1)} %copy-done.4) | copy-start | bytes 6291460
  226.2 14.5 %copy-start.7 = (bf16[128,2048]{1,0:T(8,128)(2,1)S(1)}, bf16[128,2048]{1,0:T(8,128)(2,1)}, u32[]{:S(2)}) copy-start(bf16[128,2048]{1,0:T(8,128)(2,1)} %copy-done.6) | copy-start | bytes 1572868
  226.2 38.5 %collective-permute-start.19 = (bf16[512,1024]{1,0:T(8,128)(2,1)}, bf16[512,1024]{1,0:T(8,128)(2,1)}, u32[]{:S(2)}, u32[]{:S(2)}) collective-permute-start(bf16[512,1024]{1,0:T(8,128)(2,1)} %get-tuple-element.160), channel_id=1, source_target_pairs={{8,0},{12,4},{16,8},{20,12},{24,16},{28,20},{9,1},{13,5},{17,9},{2... | collective-permute-start | bytes 3145736 | tf_op jit(solution)/shard_map/ppermute | solution.py:363
  240.7 12.7 %copy-start.21 = (bf16[512,1024]{1,0:T(8,128)(2,1)S(1)}, bf16[512,1024]{1,0:T(8,128)(2,1)}, u32[]{:S(2)}) copy-start(bf16[512,1024]{1,0:T(8,128)(2,1)} %copy-done.20) | copy-start | bytes 3145732
  257.4 36.2 %collective-permute-start.23 = (bf16[512,1024]{1,0:T(8,128)(2,1)}, bf16[512,1024]{1,0:T(8,128)(2,1)}, u32[]{:S(2)}, u32[]{:S(2)}) collective-permute-start(bf16[512,1024]{1,0:T(8,128)(2,1)} %get-tuple-element.158), channel_id=1, source_target_pairs={{0,8},{4,12},{8,16},{12,20},{16,24},{20,28},{1,9},{5,13},{9,17},{1... | collective-permute-start | bytes 3145736 | tf_op jit(solution)/shard_map/ppermute | solution.py:363
  259.3 10.5 %copy-start.3 = (bf16[1024,1024]{1,0:T(8,128)(2,1)S(1)}, bf16[1024,1024]{1,0:T(8,128)(2,1)}, u32[]{:S(2)}) copy-start(bf16[1024,1024]{1,0:T(8,128)(2,1)} %shard_map.115.own_ref) | copy-start | bytes 6291460
  259.3 34.3 %collective-permute-start.24 = (bf16[512,1024]{1,0:T(8,128)(2,1)}, bf16[512,1024]{1,0:T(8,128)(2,1)}, u32[]{:S(2)}, u32[]{:S(2)}) collective-permute-start(bf16[512,1024]{1,0:T(8,128)(2,1)} %get-tuple-element.157), channel_id=1, source_target_pairs={{8,0},{12,4},{16,8},{20,12},{24,16},{28,20},{9,1},{13,5},{17,9},{2... | collective-permute-start | bytes 3145736 | tf_op jit(solution)/shard_map/ppermute | solution.py:363
  267.8 29.9 %collective-permute-start.25 = (bf16[128,1024]{1,0:T(8,128)(2,1)S(1)}, bf16[128,1024]{1,0:T(8,128)(2,1)S(1)}, u32[]{:S(2)}, u32[]{:S(2)}) collective-permute-start(bf16[128,1024]{1,0:T(8,128)(2,1)S(1)} %get-tuple-element.143), channel_id=1, source_target_pairs={{4,0},{8,4},{12,8},{16,12},{20,16},{24,20},{28,24},{5,1},{9,5},{13... | collective-permute-start | bytes 786440 | tf_op jit(solution)/shard_map/ppermute | solution.py:363
  282.4 1.3 copy-start.16
  284.6 23.5 %all-to-all-start = ((f32[8,16,128]{2,1,0:T(8,128)}), f32[8,16,128]{2,1,0:T(8,128)S(1)}, u32[]{:S(2)}, u32[]{:S(2)}) async-start(f32[8,16,128]{2,1,0:T(8,128)} %bitcast.20), calls=%async_computation | async-start | bytes 131072 | tf_op jit(solution)/shard_map/all_to_all | solution.py:549
  290.0 18.8 %collective-permute-start.20 = (bf16[128,1024]{1,0:T(8,128)(2,1)S(1)}, bf16[128,1024]{1,0:T(8,128)(2,1)S(1)}, u32[]{:S(2)}, u32[]{:S(2)}) collective-permute-start(bf16[128,1024]{1,0:T(8,128)(2,1)S(1)} %get-tuple-element.139), channel_id=1, source_target_pairs={{4,0},{8,4},{12,8},{16,12},{20,16},{24,20},{28,24},{5,1},{9,5},{13... | collective-permute-start | bytes 786440 | tf_op jit(solution)/shard_map/ppermute | solution.py:363
  293.6 2.6 copy-start.22
  308.8 1.6 copy-start.17
Sparse Core Ops, SparseCore 0:
  11.7 34.6 all-gather.4
  59.0 33.7 all-gather.6

commit v10 on v8

--- a/solution.py
+++ b/solution.py
@@ -226,19 +226,25 @@
 
 
 def gate_kernel(slots, pick, *refs):
-    out = refs[-1]
-    cots, refs = refs[: len(slots)], list(refs[len(slots) : -1])
-    blocks = []
+    out, held = refs[-2:]
+    cots, refs = refs[: len(slots)], list(refs[len(slots) : -2])
+    choices = []
     for slot in slots:
-        block = refs.pop(0)[...]
-        if slot:
-            block = jnp.where(pick[LINE + slot - 1] == 1, block, refs.pop(0)[...])
-        blocks.append(block)
-    cot, block = cots[0][0], blocks[0]
+        choices.append([refs.pop(0)] + ([refs.pop(0)] if slot else []))
+    depth = choices[0][0].shape[0]
+
+    @pl.when(pl.program_id(0) == 0)
+    def _():
+        for n, (slot, choice) in enumerate(zip(slots, choices)):
+            block = choice[0][...]
+            if slot:
+                block = jnp.where(pick[LINE + slot - 1] == 1, block, choice[1][...])
+            held[n * depth : (n + 1) * depth] = block
+
+    cot = cots[0][0]
     if len(slots) > 1:
         cot = jnp.concatenate([ref[0] for ref in cots], axis=1)
-        block = jnp.concatenate(blocks, axis=0)
-    total = jnp.dot(cot, block, preferred_element_type=F32)
+    total = jnp.dot(cot, held[...], preferred_element_type=F32)
     if refs:
         total = total + refs[0][...].astype(F32)
     out[...] = total.astype(out.dtype)
@@ -247,15 +253,15 @@
 def gate_grad(pick, cot, weights, slots=(0, 1, 2, 3), base=None):
     _, rows, depth = cot.shape
     width = weights[0][0].shape[1]
-    tile = min(256, width)
+    tile = min(256, rows)
 
     def cot_spec(j):
-        return pl.BlockSpec((1, rows, depth), lambda i, pick: (pick[j], 0, 0))
+        return pl.BlockSpec((1, tile, depth), lambda i, pick: (pick[j], i, 0))
 
     blocks = [x for slot in slots for x in weights[slot]]
-    part = pl.BlockSpec((rows, tile), lambda i, pick: (0, i))
+    part = pl.BlockSpec((tile, width), lambda i, pick: (i, 0))
     in_specs = [cot_spec(j) for j in slots]
-    in_specs += [pl.BlockSpec((depth, tile), lambda i, pick: (0, i))] * len(blocks)
+    in_specs += [pl.BlockSpec((depth, width), lambda i, pick: (0, 0))] * len(blocks)
     args = [cot] * len(slots) + blocks
     if base is not None:
         in_specs.append(part)
@@ -264,9 +270,10 @@
         functools.partial(gate_kernel, slots),
         grid_spec=pltpu.PrefetchScalarGridSpec(
             num_scalar_prefetch=1,
-            grid=(width // tile,),
+            grid=(rows // tile,),
             in_specs=in_specs,
             out_specs=part,
+            scratch_shapes=[pltpu.VMEM((len(slots) * depth, width), BF16)],
         ),
         out_shape=jax.ShapeDtypeStruct((rows, width), BF16),
         compiler_params=params(),

time: 327 us -> 327 us (level)
  no operation moved by 1% of the time
where the time goes in v10:
time: 327 us; the launch traced here: 325 us
  Pallas kernels  164 us (50%)
  starting transfers between devices  65.9 us (20%)
  waiting for transfers between devices  40.3 us (12%)
  other arithmetic  22.9 us (7%)
  local copies, waits for them, and re-layouts  16.8 us (5%)
  between operations  14.6 us (4%)
    ppermute x26, starting transfers between devices, send(): return lax.ppermute(x, 'seq', pairs)  61.1 us
    pallas_call x6, Pallas kernels, gate_grad(): pl.pallas_call(functools.partial(gate_kernel, slots), grid_spec=pltpu.Pre...  45 us
    ppermute x26, waiting for transfers between devices, send(): return lax.ppermute(x, 'seq', pairs)  40.2 us
    pallas_call x4, Pallas kernels, weight_rows(): pl.pallas_call(functools.partial(rows_kernel, n), grid_spec=pltpu.Prefetc...  33.3 us
    pallas_call x2, Pallas kernels, middle(): pl.pallas_call(kernel, grid=(tiles,), in_specs=in_specs, out_specs=[here,...  25.2 us
    pallas_call x2, Pallas kernels, backward(): pl.pallas_call(backward_kernel, grid=(tiles,), in_specs=in_specs, out_spe...  20.9 us
    pallas_call x2, Pallas kernels, forward(): pl.pallas_call(forward_kernel, grid=(tiles,), in_specs=[here, here, here,...  19.9 us
    pallas_call x1, Pallas kernels, tables(): pl.pallas_call(table_kernel, grid=(groups // GPT,), in_specs=[seed, seed]...  10.4 us
  transfers between devices with their start and end apart: 29, of which 11 were waited for; matrix products, arithmetic and copies ran while one was open for 8% of the time, Pallas kernels for 46%

profile of v10, /device:TPU:10, one launch (start us, length us, event | category | flops | bytes accessed | tf_op | source)
XLA Modules:
  0.0 325.1 jit_solution(7546273818098612298)
XLA Ops:
  7.2 1.3 multiply_convert_fusion
  8.6 2.7 constant_dynamic-slice_fusion
  11.3 3.4 %collective-permute-start = (bf16[128,2048]{1,0:T(8,128)(2,1)S(1)}, bf16[128,2048]{1,0:T(8,128)(2,1)S(1)}, u32[]{:S(2)}, u32[]{:S(2)}) collective-permute-start(bf16[128,2048]{1,0:T(8,128)(2,1)S(1)} %multiply_convert_fusion), channel_id=1, source_target_pairs={{0,4},{4,8},{8,12},{12,16},{16,20},{20,24},{24,28},{1,5},{5,9},{9,... | collective-permute-start | bytes 1572872 | tf_op jit(solution)/shard_map/ppermute | solution.py:370
  15.1 10.4 %shard_map.101 = (bf16[16384,256]{1,0:T(8,128)(2,1)}, bf16[16384,256]{1,0:T(8,128)(2,1)}) custom-call(f32[128,256]{1,0:T(8,128)S(1)} %maximum_maximum_fusion.back_ref, f32[128,256]{1,0:T(8,128)S(1)} %concatenate.22.ahead_ref), custom_call_target="tpu_custom_call" | custom-call | flops 524288 | bytes 262144 | tf_op jit(solution)/shard_map/pallas_call | solution.py:54
  25.5 2.8 fusion.14
  28.2 3.5 %collective-permute-start.1 = (bf16[512,1024]{1,0:T(8,128)(2,1)S(1)}, bf16[512,1024]{1,0:T(8,128)(2,1)S(1)}, u32[]{:S(2)}, u32[]{:S(2)}) collective-permute-start(bf16[512,1024]{1,0:T(8,128)(2,1)S(1)} %get-tuple-element.85.refs_3_), channel_id=1, source_target_pairs={{0,8},{4,12},{8,16},{12,20},{16,24},{20,28},{1,9},{5,13},{9,17},{1... | collective-permute-start | bytes 3145736 | tf_op jit(solution)/shard_map/ppermute | solution.py:370
  31.7 2.4 collective-permute-start.2
  34.2 1.6 collective-permute-start.3
  35.7 9.9 %shard_map.102 = (bf16[1024,1024]{1,0:T(8,128)(2,1)S(1)}, bf16[1024,1024]{1,0:T(8,128)(2,1)S(1)}) custom-call(bf16[1024,2048]{1,0:T(8,128)(2,1)} %refs_1_.3, bf16[1024,2048]{1,0:T(8,128)(2,1)} %k.7, bf16[1024,2048]{1,0:T(8,128)(2,1)} %v.7, bf16[128,2048]{1,0:T(8,128)(2,1)S(1)} %collective-permute-done.prior.refs_5_, bf16[16384,256]{1,0:T(8,128)(2,1)} %get-tuple-element.88.table), custom_call_target="tpu_custom_call" | custom-call | flops 67108864 | bytes 229376 | tf_op jit(solution)/shard_map/pallas_call | solution.py:104
  45.7 1.4 copy-done.11
  47.1 1.3 copy-done.13
  48.4 6.4 %collective-permute-done.1.refs_5_ = bf16[512,1024]{1,0:T(8,128)(2,1)S(1)} collective-permute-done((bf16[512,1024]{1,0:T(8,128)(2,1)S(1)}, bf16[512,1024]{1,0:T(8,128)(2,1)S(1)}, u32[]{:S(2)}, u32[]{:S(2)}) %collective-permute-start.1) | collective-permute-done | bytes 1048608 | tf_op jit(solution)/shard_map/ppermute | solution.py:370
  54.8 3.2 collective-permute-done.2.refs_4_.refs_2_
  58.4 1.6 collective-permute-start.6
  60.0 3.4 %collective-permute-start.7 = (bf16[512,1024]{1,0:T(8,128)(2,1)}, bf16[512,1024]{1,0:T(8,128)(2,1)}, u32[]{:S(2)}, u32[]{:S(2)}) collective-permute-start(bf16[512,1024]{1,0:T(8,128)(2,1)} %get-tuple-element.93.refs_4_), channel_id=1, source_target_pairs={{0,8},{4,12},{8,16},{12,20},{16,24},{20,28},{1,9},{5,13},{9,17},{1... | collective-permute-start | bytes 3145736 | tf_op jit(solution)/shard_map/ppermute | solution.py:370
  63.4 3.4 %collective-permute-start.8 = (bf16[512,1024]{1,0:T(8,128)(2,1)}, bf16[512,1024]{1,0:T(8,128)(2,1)S(1)}, u32[]{:S(2)}, u32[]{:S(2)}) collective-permute-start(bf16[512,1024]{1,0:T(8,128)(2,1)} %get-tuple-element.93.refs_4_), channel_id=1, source_target_pairs={{8,0},{12,4},{16,8},{20,12},{24,16},{28,20},{9,1},{13,5},{17,9},{2... | collective-permute-start | bytes 3145736 | tf_op jit(solution)/shard_map/ppermute | solution.py:370
  66.8 2.5 collective-permute-start.4
  69.3 1.9 collective-permute-start.5
  72.4 10.0 %shard_map.103 = (bf16[1024,1024]{1,0:T(8,128)(2,1)S(1)}, bf16[1024,1024]{1,0:T(8,128)(2,1)S(1)}) custom-call(bf16[1024,2048]{1,0:T(8,128)(2,1)} %refs_1_.3, bf16[1024,2048]{1,0:T(8,128)(2,1)} %k.7, bf16[1024,2048]{1,0:T(8,128)(2,1)} %v.7, bf16[128,2048]{1,0:T(8,128)(2,1)S(1)} %copy-done.7, bf16[16384,256]{1,0:T(8,128)(2,1)} %get-tuple-element.88.table), custom_call_target="tpu_custom_call" | custom-call | flops 67108864 | bytes 229376 | tf_op jit(solution)/shard_map/pallas_call | solution.py:104
  83.8 3.5 %collective-permute-done.7.refs_6_ = bf16[512,1024]{1,0:T(8,128)(2,1)} collective-permute-done((bf16[512,1024]{1,0:T(8,128)(2,1)}, bf16[512,1024]{1,0:T(8,128)(2,1)}, u32[]{:S(2)}, u32[]{:S(2)}) %collective-permute-start.7) | collective-permute-done | bytes 1048608 | tf_op jit(solution)/shard_map/ppermute | solution.py:370
  87.3 4.3 %collective-permute-done.8.refs_5_.refs_10_ = bf16[512,1024]{1,0:T(8,128)(2,1)S(1)} collective-permute-done((bf16[512,1024]{1,0:T(8,128)(2,1)}, bf16[512,1024]{1,0:T(8,128)(2,1)S(1)}, u32[]{:S(2)}, u32[]{:S(2)}) %collective-permute-start.8) | collective-permute-done | bytes 1048608 | tf_op jit(solution)/shard_map/ppermute | solution.py:370
  91.6 9.0 %shard_map.104.refs_2_ = f32[4,512,1024]{2,1,0:T(8,128)} custom-call(s32[4]{0:T(128)S(1)} %pad_add_fusion.pick, bf16[4,1024,512]{2,1,0:T(8,128)(2,1)} %bitcast.48, bf16[1024,1024]{1,0:T(8,128)(2,1)S(1)} %copy-done.14), custom_call_target="tpu_custom_call" | custom-call | flops 16777216 | bytes 49152 | tf_op jit(solution)/shard_map/pallas_call | solution.py:310
  100.6 5.9 %collective-permute-done.4.refs_3_.refs_6_ = bf16[512,1024]{1,0:T(8,128)(2,1)S(1)} collective-permute-done((bf16[512,1024]{1,0:T(8,128)(2,1)}, bf16[512,1024]{1,0:T(8,128)(2,1)S(1)}, u32[]{:S(2)}, u32[]{:S(2)}) %collective-permute-start.4) | collective-permute-done | bytes 1048608 | tf_op jit(solution)/shard_map/ppermute | solution.py:370
  106.5 4.1 %collective-permute-done.5.refs_4_.refs_7_ = bf16[512,1024]{1,0:T(8,128)(2,1)} collective-permute-done((bf16[512,1024]{1,0:T(8,128)(2,1)S(1)}, bf16[512,1024]{1,0:T(8,128)(2,1)}, u32[]{:S(2)}, u32[]{:S(2)}) %collective-permute-start.5) | collective-permute-done | bytes 1048608 | tf_op jit(solution)/shard_map/ppermute | solution.py:370
  111.3 2.4 collective-permute-start.10
  113.6 2.7 collective-permute-start.11
  116.4 5.0 %shard_map.105 = (bf16[512,1024]{1,0:T(8,128)(2,1)S(1)}, bf16[512,1024]{1,0:T(8,128)(2,1)}) custom-call(s32[3]{0:T(128)S(1)} %pad_add_fusion.1.pick, bf16[4,1024,512]{2,1,0:T(8,128)(2,1)} %bitcast.36, bf16[1024,1024]{1,0:T(8,128)(2,1)} %collective-permute-done.6.refs_1_, f32[4,512,1024]{2,1,0:T(8,128)} %shard_map.104.refs_2_, ...), custom_call_target="tpu_custom_call" | custom-call | flops 16777216 | bytes 49152 | tf_op jit(solution)/shard_map/pallas_call | solution.py:344
  122.6 7.7 %shard_map.106 = bf16[3,512,1024]{2,1,0:T(8,128)(2,1)S(1)} custom-call(s32[3]{0:T(128)S(1)} %pad_add_fusion.2.pick, bf16[4,1024,512]{2,1,0:T(8,128)(2,1)} %bitcast.37, bf16[1024,1024]{1,0:T(8,128)(2,1)} %collective-permute-done.6.refs_1_, f32[4,512,1024]{2,1,0:T(8,128)} %shard_map.104.refs_2_), custom_call_target="tpu_custom_call" | custom-call | flops 16777216 | bytes 49152 | tf_op jit(solution)/shard_map/pallas_call | solution.py:310
  130.3 7.6 %shard_map.107.refs_3_ = bf16[1024,1024]{1,0:T(8,128)(2,1)} custom-call(s32[7]{0:T(128)S(1)} %stack.58.pick, bf16[4,1024,512]{2,1,0:T(8,128)(2,1)} %bitcast.38, bf16[4,1024,512]{2,1,0:T(8,128)(2,1)} %bitcast.39, bf16[4,1024,512]{2,1,0:T(8,128)(2,1)} %bitcast.40, bf16[512,1024]{1,0:T(8,128)(2,1)S(1)} %copy-done.2, ...), custom_call_target="tpu_custom_call" | custom-call | flops 50331648 | bytes 98304 | tf_op jit(solution)/shard_map/pallas_call | solution.py:269
  137.9 2.0 collective-permute-done.11.refs_4_.refs_8_
  139.9 9.0 %shard_map.108.refs_2_ = f32[4,512,1024]{2,1,0:T(8,128)} custom-call(s32[4]{0:T(128)S(1)} %pad_add_fusion.pick, bf16[4,1024,512]{2,1,0:T(8,128)(2,1)} %bitcast.49, bf16[1024,1024]{1,0:T(8,128)(2,1)S(1)} %copy-done.16), custom_call_target="tpu_custom_call" | custom-call | flops 16777216 | bytes 49152 | tf_op jit(solution)/shard_map/pallas_call | solution.py:310
  148.9 7.6 %shard_map.109.refs_3_ = bf16[1024,1024]{1,0:T(8,128)(2,1)} custom-call(s32[7]{0:T(128)S(1)} %stack.58.pick, bf16[4,1024,512]{2,1,0:T(8,128)(2,1)} %bitcast.50, bf16[4,1024,512]{2,1,0:T(8,128)(2,1)} %bitcast.51, bf16[4,1024,512]{2,1,0:T(8,128)(2,1)} %bitcast.52, bf16[512,1024]{1,0:T(8,128)(2,1)S(1)} %copy-done.2, ...), custom_call_target="tpu_custom_call" | custom-call | flops 50331648 | bytes 98304 | tf_op jit(solution)/shard_map/pallas_call | solution.py:269
  157.8 4.7 %shard_map.110 = bf16[1024,1024]{1,0:T(8,128)(2,1)S(1)} custom-call(s32[7]{0:T(128)S(1)} %stack.58.pick, bf16[4,1024,512]{2,1,0:T(8,128)(2,1)} %bitcast.41, bf16[512,1024]{1,0:T(8,128)(2,1)} %collective-permute-done.9.refs_1_, bf16[512,1024]{1,0:T(8,128)(2,1)S(1)} %collective-permute-done.2.refs_4_.refs_2_, bf16[1024,1024]{1,0:T(8,128)(2,1)} %shard_map.107.refs_3_), custom_call_target="tpu_custom_call" | custom-call | flops 16777216 | bytes 32768 | tf_op jit(solution)/shard_map/pallas_call | solution.py:269
  162.5 4.8 %shard_map.111 = (bf16[512,1024]{1,0:T(8,128)(2,1)S(1)}, bf16[512,1024]{1,0:T(8,128)(2,1)S(1)}) custom-call(s32[3]{0:T(128)S(1)} %pad_add_fusion.1.pick, bf16[4,1024,512]{2,1,0:T(8,128)(2,1)} %bitcast.42, bf16[1024,1024]{1,0:T(8,128)(2,1)} %collective-permute-done.12.refs_1_, f32[4,512,1024]{2,1,0:T(8,128)} %shard_map.108.refs_2_, ...), custom_call_target="tpu_custom_call" | custom-call | flops 16777216 | bytes 49152 | tf_op jit(solution)/shard_map/pallas_call | solution.py:344
  167.3 2.6 collective-permute-start.14
  169.9 1.5 collective-permute-start.13
  171.5 2.6 fusion.11
  175.4 2.1 collective-permute-start.17
  177.5 7.6 %shard_map.112 = bf16[3,512,1024]{2,1,0:T(8,128)(2,1)S(1)} custom-call(s32[3]{0:T(128)S(1)} %pad_add_fusion.2.pick, bf16[4,1024,512]{2,1,0:T(8,128)(2,1)} %bitcast.43, bf16[1024,1024]{1,0:T(8,128)(2,1)} %collective-permute-done.12.refs_1_, f32[4,512,1024]{2,1,0:T(8,128)} %shard_map.108.refs_2_), custom_call_target="tpu_custom_call" | custom-call | flops 16777216 | bytes 49152 | tf_op jit(solution)/shard_map/pallas_call | solution.py:310
  185.1 5.2 %shard_map.113.own_ref = bf16[1024,1024]{1,0:T(8,128)(2,1)S(1)} custom-call(s32[7]{0:T(128)S(1)} %stack.58.pick, bf16[4,1024,512]{2,1,0:T(8,128)(2,1)} %bitcast.53, bf16[512,1024]{1,0:T(8,128)(2,1)} %collective-permute-done.9.refs_1_, bf16[512,1024]{1,0:T(8,128)(2,1)S(1)} %collective-permute-done.2.refs_4_.refs_2_, bf16[1024,1024]{1,0:T(8,128)(2,1)} %shard_map.109.refs_3_), custom_call_target="tpu_custom_call" | custom-call | flops 16777216 | bytes 32768 | tf_op jit(solution)/shard_map/pallas_call | solution.py:269
  191.7 2.4 collective-permute-done.14.refs_9_
  194.1 9.9 %shard_map.114 = bf16[1024,1024]{1,0:T(8,128)(2,1)} custom-call(s32[7]{0:T(128)S(1)} %stack.58.pick, bf16[4,1024,512]{2,1,0:T(8,128)(2,1)} %bitcast.44, bf16[4,1024,512]{2,1,0:T(8,128)(2,1)} %bitcast.45, bf16[4,1024,512]{2,1,0:T(8,128)(2,1)} %bitcast.46, bf16[4,1024,512]{2,1,0:T(8,128)(2,1)} %bitcast.47, bf16[512,1024]{1,0:T(8,128)(2,1)} %get-tuple-element.93.refs_4_, ...), custom_call_target="tpu_custom_call" | custom-call | flops 67108864 | bytes 131072 | tf_op jit(solution)/shard_map/pallas_call | solution.py:269
  204.0 2.7 fusion.10
  208.0 1.9 collective-permute-start.22
  209.9 6.7 %collective-permute-done.16 = bf16[512,1024]{1,0:T(8,128)(2,1)} collective-permute-done((bf16[512,1024]{1,0:T(8,128)(2,1)}, bf16[512,1024]{1,0:T(8,128)(2,1)}, u32[]{:S(2)}, u32[]{:S(2)}) %collective-permute-start.16) | collective-permute-done | bytes 1048608 | tf_op jit(solution)/shard_map/ppermute | solution.py:370
  216.6 1.5 collective-permute-start.15
  218.1 3.9 %fusion.1 = (bf16[512,1024]{1,0:T(8,128)(2,1)}, bf16[512,1024]{1,0:T(8,128)(2,1)}) fusion(bf16[512,1024]{1,0:T(8,128)(2,1)} %collective-permute-done.17, bf16[512,1024]{1,0:T(8,128)(2,1)} %collective-permute-done.16, bf16[512,1024]{1,0:T(8,128)(2,1)S(1)} %copy-done.20, pred[]{:T(512)S(6)} %eq.15, pred[]{:T(512)S(6)} %eq.17, ...), kind=kLoop, calls=%fused_computation.9 | loop fusion | flops 6291456 | bytes 6291458 | tf_op jit(solution)/shard_map/convert_element_type | solution.py:439
  222.0 1.9 collective-permute-start.18
  224.0 5.1 %collective-permute-start.19 = (bf16[512,1024]{1,0:T(8,128)(2,1)}, bf16[512,1024]{1,0:T(8,128)(2,1)}, u32[]{:S(2)}, u32[]{:S(2)}) collective-permute-start(bf16[512,1024]{1,0:T(8,128)(2,1)} %get-tuple-element.164), channel_id=1, source_target_pairs={{8,0},{12,4},{16,8},{20,12},{24,16},{28,20},{9,1},{13,5},{17,9},{2... | collective-permute-start | bytes 3145736 | tf_op jit(solution)/shard_map/ppermute | solution.py:370
  229.1 9.9 %shard_map.115.own_ref = bf16[1024,1024]{1,0:T(8,128)(2,1)} custom-call(s32[7]{0:T(128)S(1)} %stack.58.pick, bf16[4,1024,512]{2,1,0:T(8,128)(2,1)} %bitcast.54, bf16[4,1024,512]{2,1,0:T(8,128)(2,1)} %bitcast.55, bf16[4,1024,512]{2,1,0:T(8,128)(2,1)} %bitcast.56, bf16[4,1024,512]{2,1,0:T(8,128)(2,1)} %bitcast.57, ...), custom_call_target="tpu_custom_call" | custom-call | flops 67108864 | bytes 131072 | tf_op jit(solution)/shard_map/pallas_call | solution.py:269
  239.0 12.5 %shard_map.116 = (bf16[1024,2048]{1,0:T(8,128)(2,1)}, bf16[1024,1024]{1,0:T(8,128)(2,1)S(1)}, bf16[128,1024]{1,0:T(8,128)(2,1)S(1)}, f32[64,256]{1,0:T(8,128)S(1)}) custom-call(bf16[1024,1024]{1,0:T(8,128)(2,1)S(1)} %copy-done.5, bf16[1024,1024]{1,0:T(8,128)(2,1)} %collective-permute-done.13.refs_0_, bf16[1024,2048]{1,0:T(8,128)(2,1)} %refs_1_.3, ...), custom_call_target="tpu_custom_call" | custom-call | flops 67108864 | bytes 294912 | tf_op jit(solution)/shard_map/pallas_call | solution.py:171
  251.6 4.0 %fusion.7 = (bf16[512,1024]{1,0:T(8,128)(2,1)}, bf16[512,1024]{1,0:T(8,128)(2,1)}) fusion(bf16[512,1024]{1,0:T(8,128)(2,1)} %collective-permute-done.21, bf16[512,1024]{1,0:T(8,128)(2,1)} %collective-permute-done.22, bf16[512,1024]{1,0:T(8,128)(2,1)S(1)} %get-tuple-element.145, pred[]{:T(512)S(6)} %eq.15, bf16[3,512,1024]{2,1,0:T(8,128)(2,1)S(1)} %shard_map.112, ...), kind=kLoop, calls=%fused_computation.15 | loop fusion | flops 6291456 | bytes 6291458 | tf_op jit(solution)/shard_map/convert_element_type | solution.py:439
  255.7 1.9 collective-permute-start.23
  257.6 5.1 %collective-permute-start.24 = (bf16[512,1024]{1,0:T(8,128)(2,1)}, bf16[512,1024]{1,0:T(8,128)(2,1)}, u32[]{:S(2)}, u32[]{:S(2)}) collective-permute-start(bf16[512,1024]{1,0:T(8,128)(2,1)} %get-tuple-element.161), channel_id=1, source_target_pairs={{8,0},{12,4},{16,8},{20,12},{24,16},{28,20},{9,1},{13,5},{17,9},{2... | collective-permute-start | bytes 3145736 | tf_op jit(solution)/shard_map/ppermute | solution.py:370
  262.7 3.2 fusion.13
  265.9 1.9 collective-permute-start.25
  267.8 12.6 %shard_map.117 = (bf16[1024,2048]{1,0:T(8,128)(2,1)}, bf16[1024,1024]{1,0:T(8,128)(2,1)S(1)}, bf16[128,1024]{1,0:T(8,128)(2,1)S(1)}, f32[64,256]{1,0:T(8,128)S(1)}) custom-call(bf16[1024,1024]{1,0:T(8,128)(2,1)S(1)} %copy-done.3, bf16[1024,1024]{1,0:T(8,128)(2,1)} %collective-permute-done.15.refs_0_, ...), custom_call_target="tpu_custom_call", output_to_operand_aliasing={{0}: (7, {})} | custom-call | flops 67108864 | bytes 294912 | tf_op jit(solution)/shard_map/pallas_call | solution.py:171
  282.7 4.7 %all-to-all-start = ((f32[8,16,128]{2,1,0:T(8,128)}), f32[8,16,128]{2,1,0:T(8,128)S(1)}, u32[]{:S(2)}, u32[]{:S(2)}) async-start(f32[8,16,128]{2,1,0:T(8,128)} %bitcast.20), calls=%async_computation | async-start | bytes 131072 | tf_op jit(solution)/shard_map/all_to_all | solution.py:557
  287.4 3.6 %collective-permute-start.20 = (bf16[128,1024]{1,0:T(8,128)(2,1)S(1)}, bf16[128,1024]{1,0:T(8,128)(2,1)S(1)}, u32[]{:S(2)}, u32[]{:S(2)}) collective-permute-start(bf16[128,1024]{1,0:T(8,128)(2,1)S(1)} %get-tuple-element.143), channel_id=1, source_target_pairs={{4,0},{8,4},{12,8},{16,12},{20,16},{24,20},{28,24},{5,1},{9,5},{13... | collective-permute-start | bytes 786440 | tf_op jit(solution)/shard_map/ppermute | solution.py:370
  291.0 2.6 fusion.9
  293.6 1.5 pad_maximum_fusion
  295.1 10.4 %shard_map.118 = (bf16[1024,2048]{1,0:T(8,128)(2,1)}, bf16[1024,2048]{1,0:T(8,128)(2,1)}) custom-call(bf16[1024,1024]{1,0:T(8,128)(2,1)S(1)} %get-tuple-element.151.gm, bf16[128,1024]{1,0:T(8,128)(2,1)S(1)} %collective-permute-done.25.later, bf16[1024,2048]{1,0:T(8,128)(2,1)} %k.7, bf16[1024,2048]{1,0:T(8,128)(2,1)} %v.7, ...), custom_call_target="tpu_custom_call" | custom-call | flops 67108864 | bytes 229376 | tf_op jit(solution)/shard_map/pallas_call | solution.py:216
  306.2 1.6 copy-done.18
  307.8 10.4 %shard_map.119 = (bf16[1024,2048]{1,0:T(8,128)(2,1)}, bf16[1024,2048]{1,0:T(8,128)(2,1)}) custom-call(bf16[1024,1024]{1,0:T(8,128)(2,1)S(1)} %copy-done.18, bf16[128,1024]{1,0:T(8,128)(2,1)S(1)} %collective-permute-done.20.later, bf16[1024,2048]{1,0:T(8,128)(2,1)} %k.7, bf16[1024,2048]{1,0:T(8,128)(2,1)} %v.7, ...), custom_call_target="tpu_custom_call", output_to_operand_aliasing={{0}: (5, {}), {1}: (6, {})} | custom-call | flops 67108864 | bytes 229376 | tf_op jit(solution)/shard_map/pallas_call | solution.py:216
  (86 shorter events, 13.2 us)
Async XLA Ops:
  7.2 51.2 %all-gather.5.cloned.1.call-start = ((), (), s32[]{:S(2)}) async-start(), calls=%async_computation.1 | async-start | bytes 5242880 | tf_op jit(solution)/shard_map/all_gather | solution.py:465
  8.6 6.2 %copy-start.22 = (bf16[128,128]{1,0:T(8,128)(2,1)S(1)}, bf16[128,128]{1,0:T(8,128)(2,1)}, u32[]{:S(2)}) copy-start(bf16[128,128]{1,0:T(8,128)(2,1)} %param.9) | copy-start | bytes 98308
  11.3 99.4 %all-gather.7.cloned.1.call-start = ((), (), s32[]{:S(2)}) async-start(), calls=%async_computation.2 | async-start | bytes 5242880 | tf_op jit(solution)/shard_map/all_gather | solution.py:479
  11.3 16.9 %collective-permute-start = (bf16[128,2048]{1,0:T(8,128)(2,1)S(1)}, bf16[128,2048]{1,0:T(8,128)(2,1)S(1)}, u32[]{:S(2)}, u32[]{:S(2)}) collective-permute-start(bf16[128,2048]{1,0:T(8,128)(2,1)S(1)} %multiply_convert_fusion), channel_id=1, source_target_pairs={{0,4},{4,8},{8,12},{12,16},{16,20},{20,24},{24,28},{1,5},{5,9},{9,... | collective-permute-start | bytes 1572872 | tf_op jit(solution)/shard_map/ppermute | solution.py:370
  28.2 17.4 %copy-start.1 = (bf16[512,1024]{1,0:T(8,128)(2,1)}, bf16[512,1024]{1,0:T(8,128)(2,1)S(1)}, u32[]{:S(2)}) copy-start(bf16[512,1024]{1,0:T(8,128)(2,1)S(1)} %get-tuple-element.85.refs_3_) | copy-start | bytes 3145732
  28.2 17.4 %copy-start.6 = (bf16[128,2048]{1,0:T(8,128)(2,1)}, bf16[128,2048]{1,0:T(8,128)(2,1)S(1)}, u32[]{:S(2)}) copy-start(bf16[128,2048]{1,0:T(8,128)(2,1)S(1)} %collective-permute-done.prior.refs_5_) | copy-start | bytes 1572868
  28.2 26.5 %collective-permute-start.1 = (bf16[512,1024]{1,0:T(8,128)(2,1)S(1)}, bf16[512,1024]{1,0:T(8,128)(2,1)S(1)}, u32[]{:S(2)}, u32[]{:S(2)}) collective-permute-start(bf16[512,1024]{1,0:T(8,128)(2,1)S(1)} %get-tuple-element.85.refs_3_), channel_id=1, source_target_pairs={{0,8},{4,12},{8,16},{12,20},{16,24},{20,28},{1,9},{5,13},{9,17},{1... | collective-permute-start | bytes 3145736 | tf_op jit(solution)/shard_map/ppermute | solution.py:370
  31.7 26.2 %collective-permute-start.2 = (bf16[512,1024]{1,0:T(8,128)(2,1)S(1)}, bf16[512,1024]{1,0:T(8,128)(2,1)S(1)}, u32[]{:S(2)}, u32[]{:S(2)}) collective-permute-start(bf16[512,1024]{1,0:T(8,128)(2,1)S(1)} %get-tuple-element.85.refs_3_), channel_id=1, source_target_pairs={{8,0},{12,4},{16,8},{20,12},{24,16},{28,20},{9,1},{13,5},{17,9},{2... | collective-permute-start | bytes 3145736 | tf_op jit(solution)/shard_map/ppermute | solution.py:370
  34.2 24.2 %collective-permute-start.3 = (bf16[1024,512]{1,0:T(8,128)(2,1)S(1)}, bf16[1024,512]{1,0:T(8,128)(2,1)}, u32[]{:S(2)}, u32[]{:S(2)}) collective-permute-start(bf16[1024,512]{1,0:T(8,128)(2,1)S(1)} %get-tuple-element.86), channel_id=1, source_target_pairs={{0,4},{4,0},{8,12},{12,8},{16,20},{20,16},{24,28},{28,24},{1,5},{5... | collective-permute-start | bytes 3145736 | tf_op jit(solution)/shard_map/ppermute | solution.py:370
  45.6 1.4 copy-start.11
  47.1 1.3 copy-start.13
  54.8 3.2 copy-start.9
  58.4 52.2 %collective-permute-start.6 = (bf16[1024,1024]{1,0:T(8,128)(2,1)}, bf16[1024,1024]{1,0:T(8,128)(2,1)}, u32[]{:S(2)}, u32[]{:S(2)}) collective-permute-start(bf16[1024,1024]{1,0:T(8,128)(2,1)} %copy-done.13), channel_id=1, source_target_pairs={{0,4},{4,0},{8,12},{12,8},{16,20},{20,16},{24,28},{28,24},{1,5},{5... | collective-permute-start | bytes 6291464 | tf_op jit(solution)/shard_map/ppermute | solution.py:370
  60.0 27.3 %collective-permute-start.7 = (bf16[512,1024]{1,0:T(8,128)(2,1)}, bf16[512,1024]{1,0:T(8,128)(2,1)}, u32[]{:S(2)}, u32[]{:S(2)}) collective-permute-start(bf16[512,1024]{1,0:T(8,128)(2,1)} %get-tuple-element.93.refs_4_), channel_id=1, source_target_pairs={{0,8},{4,12},{8,16},{12,20},{16,24},{20,28},{1,9},{5,13},{9,17},{1... | collective-permute-start | bytes 3145736 | tf_op jit(solution)/shard_map/ppermute | solution.py:370
  63.4 28.2 %collective-permute-start.8 = (bf16[512,1024]{1,0:T(8,128)(2,1)}, bf16[512,1024]{1,0:T(8,128)(2,1)S(1)}, u32[]{:S(2)}, u32[]{:S(2)}) collective-permute-start(bf16[512,1024]{1,0:T(8,128)(2,1)} %get-tuple-element.93.refs_4_), channel_id=1, source_target_pairs={{8,0},{12,4},{16,8},{20,12},{24,16},{28,20},{9,1},{13,5},{17,9},{2... | collective-permute-start | bytes 3145736 | tf_op jit(solution)/shard_map/ppermute | solution.py:370
  66.8 39.7 %collective-permute-start.4 = (bf16[512,1024]{1,0:T(8,128)(2,1)}, bf16[512,1024]{1,0:T(8,128)(2,1)S(1)}, u32[]{:S(2)}, u32[]{:S(2)}) collective-permute-start(bf16[512,1024]{1,0:T(8,128)(2,1)} %copy-done.9), channel_id=1, source_target_pairs={{8,16},{12,20},{16,24},{20,28},{9,17},{13,21},{17,25},{21,29},{10,... | collective-permute-start | bytes 3145736 | tf_op jit(solution)/shard_map/ppermute | solution.py:370
  69.3 41.3 %collective-permute-start.5 = (bf16[512,1024]{1,0:T(8,128)(2,1)S(1)}, bf16[512,1024]{1,0:T(8,128)(2,1)}, u32[]{:S(2)}, u32[]{:S(2)}) collective-permute-start(bf16[512,1024]{1,0:T(8,128)(2,1)S(1)} %collective-permute-done.2.refs_4_.refs_2_), channel_id=1, source_target_pairs={{16,8},{20,12},{8,0},{12,4},{17,9},{21,13},{9,1},{13,5},{18,10},{2... | collective-permute-start | bytes 3145736 | tf_op jit(solution)/shard_map/ppermute | solution.py:370
  71.4 1.0 copy-start.7
  72.4 19.2 %copy-start.14 = (bf16[1024,1024]{1,0:T(8,128)(2,1)S(1)}, bf16[1024,1024]{1,0:T(8,128)(2,1)}, u32[]{:S(2)}) copy-start(bf16[1024,1024]{1,0:T(8,128)(2,1)} %copy-done.13) | copy-start | bytes 6291460
  82.5 1.3 copy-start.12
  83.8 16.8 %copy-start.15 = (bf16[1024,1024]{1,0:T(8,128)(2,1)}, bf16[1024,1024]{1,0:T(8,128)(2,1)S(1)}, u32[]{:S(2)}) copy-start(bf16[1024,1024]{1,0:T(8,128)(2,1)S(1)} %get-tuple-element.116.refs_1_) | copy-start | bytes 6291460
  110.7 51.8 %collective-permute-start.12 = (bf16[1024,1024]{1,0:T(8,128)(2,1)}, bf16[1024,1024]{1,0:T(8,128)(2,1)}, u32[]{:S(2)}, u32[]{:S(2)}) collective-permute-start(bf16[1024,1024]{1,0:T(8,128)(2,1)} %copy-done.15), channel_id=1, source_target_pairs={{0,4},{4,0},{8,12},{12,8},{16,20},{20,16},{24,28},{28,24},{1,5},{5... | collective-permute-start | bytes 6291464 | tf_op jit(solution)/shard_map/ppermute | solution.py:370
  111.3 26.7 %collective-permute-start.10 = (bf16[512,1024]{1,0:T(8,128)(2,1)}, bf16[512,1024]{1,0:T(8,128)(2,1)}, u32[]{:S(2)}, u32[]{:S(2)}) collective-permute-start(bf16[512,1024]{1,0:T(8,128)(2,1)} %collective-permute-done.7.refs_6_), channel_id=1, source_target_pairs={{8,16},{12,20},{16,24},{20,28},{9,17},{13,21},{17,25},{21,29},{10,... | collective-permute-start | bytes 3145736 | tf_op jit(solution)/shard_map/ppermute | solution.py:370
  113.6 26.3 %collective-permute-start.11 = (bf16[512,1024]{1,0:T(8,128)(2,1)S(1)}, bf16[512,1024]{1,0:T(8,128)(2,1)}, u32[]{:S(2)}, u32[]{:S(2)}) collective-permute-start(bf16[512,1024]{1,0:T(8,128)(2,1)S(1)} %collective-permute-done.8.refs_5_.refs_10_), channel_id=1, source_target_pairs={{16,8},{20,12},{8,0},{12,4},{17,9},{21,13},{9,1},{13,5},{18,10},{2... | collective-permute-start | bytes 3145736 | tf_op jit(solution)/shard_map/ppermute | solution.py:370
  121.4 1.0 copy-start.19
  122.4 35.4 %collective-permute-start.9 = (bf16[512,1024]{1,0:T(8,128)(2,1)}, bf16[512,1024]{1,0:T(8,128)(2,1)}, u32[]{:S(2)}, u32[]{:S(2)}) collective-permute-start(bf16[512,1024]{1,0:T(8,128)(2,1)} %get-tuple-element.105), channel_id=1, source_target_pairs={{0,8},{4,12},{24,16},{28,20},{16,24},{20,28},{8,0},{12,4},{1,9},{5... | collective-permute-start | bytes 3145736 | tf_op jit(solution)/shard_map/ppermute | solution.py:370
  122.6 7.7 %copy-start.2 = (bf16[512,1024]{1,0:T(8,128)(2,1)S(1)}, bf16[512,1024]{1,0:T(8,128)(2,1)}, u32[]{:S(2)}) copy-start(bf16[512,1024]{1,0:T(8,128)(2,1)} %copy-done.1) | copy-start | bytes 3145732
  122.6 7.7 %copy-start.10 = (bf16[512,1024]{1,0:T(8,128)(2,1)S(1)}, bf16[512,1024]{1,0:T(8,128)(2,1)}, u32[]{:S(2)}) copy-start(bf16[512,1024]{1,0:T(8,128)(2,1)} %copy-done.9) | copy-start | bytes 3145732
  130.3 9.6 %copy-start.16 = (bf16[1024,1024]{1,0:T(8,128)(2,1)S(1)}, bf16[1024,1024]{1,0:T(8,128)(2,1)}, u32[]{:S(2)}) copy-start(bf16[1024,1024]{1,0:T(8,128)(2,1)} %copy-done.15) | copy-start | bytes 6291460
  167.3 26.8 %collective-permute-start.14 = (bf16[512,1024]{1,0:T(8,128)(2,1)S(1)}, bf16[512,1024]{1,0:T(8,128)(2,1)}, u32[]{:S(2)}, u32[]{:S(2)}) collective-permute-start(bf16[512,1024]{1,0:T(8,128)(2,1)S(1)} %get-tuple-element.125), channel_id=1, source_target_pairs={{0,8},{4,12},{24,16},{28,20},{16,24},{20,28},{8,0},{12,4},{1,9},{5... | collective-permute-start | bytes 3145736 | tf_op jit(solution)/shard_map/ppermute | solution.py:370
  169.9 54.0 %collective-permute-start.13 = (bf16[1024,1024]{1,0:T(8,128)(2,1)S(1)}, bf16[1024,1024]{1,0:T(8,128)(2,1)}, u32[]{:S(2)}, u32[]{:S(2)}) collective-permute-start(bf16[1024,1024]{1,0:T(8,128)(2,1)S(1)} %shard_map.110), channel_id=1, source_target_pairs={{0,4},{4,0},{8,12},{12,8},{16,20},{20,16},{24,28},{28,24},{1,5},{5... | collective-permute-start | bytes 6291464 | tf_op jit(solution)/shard_map/ppermute | solution.py:370
  174.1 42.5 %collective-permute-start.16 = (bf16[512,1024]{1,0:T(8,128)(2,1)}, bf16[512,1024]{1,0:T(8,128)(2,1)}, u32[]{:S(2)}, u32[]{:S(2)}) collective-permute-start(bf16[512,1024]{1,0:T(8,128)(2,1)} %fusion.11), channel_id=1, source_target_pairs={{0,8},{4,12},{24,16},{28,20},{1,9},{5,13},{25,17},{29,21},{2,10},{... | collective-permute-start | bytes 3145736 | tf_op jit(solution)/shard_map/ppermute | solution.py:370
  175.4 42.8 %collective-permute-start.17 = (bf16[512,1024]{1,0:T(8,128)(2,1)}, bf16[512,1024]{1,0:T(8,128)(2,1)}, u32[]{:S(2)}, u32[]{:S(2)}) collective-permute-start(bf16[512,1024]{1,0:T(8,128)(2,1)} %fusion.11), channel_id=1, source_target_pairs={{8,16},{12,20},{16,8},{20,12},{9,17},{13,21},{17,9},{21,13},{10,18... | collective-permute-start | bytes 3145736 | tf_op jit(solution)/shard_map/ppermute | solution.py:370
  185.1 66.5 %copy-start = (bf16[3,512,1024]{2,1,0:T(8,128)(2,1)}, bf16[3,512,1024]{2,1,0:T(8,128)(2,1)S(1)}, u32[]{:S(2)}) copy-start(bf16[3,512,1024]{2,1,0:T(8,128)(2,1)S(1)} %shard_map.112) | copy-start | bytes 9437188
  190.4 1.3 copy-start.4
  204.0 14.1 %copy-start.20 = (bf16[512,1024]{1,0:T(8,128)(2,1)S(1)}, bf16[512,1024]{1,0:T(8,128)(2,1)}, u32[]{:S(2)}) copy-start(bf16[512,1024]{1,0:T(8,128)(2,1)} %copy-done.19) | copy-start | bytes 3145732
  206.7 44.9 %collective-permute-start.21 = (bf16[512,1024]{1,0:T(8,128)(2,1)}, bf16[512,1024]{1,0:T(8,128)(2,1)}, u32[]{:S(2)}, u32[]{:S(2)}) collective-permute-start(bf16[512,1024]{1,0:T(8,128)(2,1)} %fusion.10), channel_id=1, source_target_pairs={{0,8},{4,12},{24,16},{28,20},{1,9},{5,13},{25,17},{29,21},{2,10},{... | collective-permute-start | bytes 3145736 | tf_op jit(solution)/shard_map/ppermute | solution.py:370
  208.0 43.6 %collective-permute-start.22 = (bf16[512,1024]{1,0:T(8,128)(2,1)}, bf16[512,1024]{1,0:T(8,128)(2,1)}, u32[]{:S(2)}, u32[]{:S(2)}) collective-permute-start(bf16[512,1024]{1,0:T(8,128)(2,1)} %fusion.10), channel_id=1, source_target_pairs={{8,16},{12,20},{16,8},{20,12},{9,17},{13,21},{17,9},{21,13},{10,18... | collective-permute-start | bytes 3145736 | tf_op jit(solution)/shard_map/ppermute | solution.py:370
  216.6 51.2 %collective-permute-start.15 = (bf16[1024,1024]{1,0:T(8,128)(2,1)}, bf16[1024,1024]{1,0:T(8,128)(2,1)}, u32[]{:S(2)}, u32[]{:S(2)}) collective-permute-start(bf16[1024,1024]{1,0:T(8,128)(2,1)} %shard_map.114), channel_id=1, source_target_pairs={{0,4},{4,0},{8,12},{12,8},{16,20},{20,16},{24,28},{28,24},{1,5},{5... | collective-permute-start | bytes 6291464 | tf_op jit(solution)/shard_map/ppermute | solution.py:370
  222.0 40.6 %collective-permute-start.18 = (bf16[512,1024]{1,0:T(8,128)(2,1)}, bf16[512,1024]{1,0:T(8,128)(2,1)}, u32[]{:S(2)}, u32[]{:S(2)}) collective-permute-start(bf16[512,1024]{1,0:T(8,128)(2,1)} %get-tuple-element.163), channel_id=1, source_target_pairs={{0,8},{4,12},{8,16},{12,20},{16,24},{20,28},{1,9},{5,13},{9,17},{1... | collective-permute-start | bytes 3145736 | tf_op jit(solution)/shard_map/ppermute | solution.py:370
  224.0 15.1 %copy-start.5 = (bf16[1024,1024]{1,0:T(8,128)(2,1)S(1)}, bf16[1024,1024]{1,0:T(8,128)(2,1)}, u32[]{:S(2)}) copy-start(bf16[1024,1024]{1,0:T(8,128)(2,1)} %copy-done.4) | copy-start | bytes 6291460
  224.0 15.1 %copy-start.8 = (bf16[128,2048]{1,0:T(8,128)(2,1)S(1)}, bf16[128,2048]{1,0:T(8,128)(2,1)}, u32[]{:S(2)}) copy-start(bf16[128,2048]{1,0:T(8,128)(2,1)} %copy-done.6) | copy-start | bytes 1572868
  224.0 38.7 %collective-permute-start.19 = (bf16[512,1024]{1,0:T(8,128)(2,1)}, bf16[512,1024]{1,0:T(8,128)(2,1)}, u32[]{:S(2)}, u32[]{:S(2)}) collective-permute-start(bf16[512,1024]{1,0:T(8,128)(2,1)} %get-tuple-element.164), channel_id=1, source_target_pairs={{8,0},{12,4},{16,8},{20,12},{24,16},{28,20},{9,1},{13,5},{17,9},{2... | collective-permute-start | bytes 3145736 | tf_op jit(solution)/shard_map/ppermute | solution.py:370
  255.7 35.4 %collective-permute-start.23 = (bf16[512,1024]{1,0:T(8,128)(2,1)}, bf16[512,1024]{1,0:T(8,128)(2,1)}, u32[]{:S(2)}, u32[]{:S(2)}) collective-permute-start(bf16[512,1024]{1,0:T(8,128)(2,1)} %get-tuple-element.162), channel_id=1, source_target_pairs={{0,8},{4,12},{8,16},{12,20},{16,24},{20,28},{1,9},{5,13},{9,17},{1... | collective-permute-start | bytes 3145736 | tf_op jit(solution)/shard_map/ppermute | solution.py:370
  257.6 10.3 %copy-start.3 = (bf16[1024,1024]{1,0:T(8,128)(2,1)S(1)}, bf16[1024,1024]{1,0:T(8,128)(2,1)}, u32[]{:S(2)}) copy-start(bf16[1024,1024]{1,0:T(8,128)(2,1)} %shard_map.115.own_ref) | copy-start | bytes 6291460
  257.6 33.4 %collective-permute-start.24 = (bf16[512,1024]{1,0:T(8,128)(2,1)}, bf16[512,1024]{1,0:T(8,128)(2,1)}, u32[]{:S(2)}, u32[]{:S(2)}) collective-permute-start(bf16[512,1024]{1,0:T(8,128)(2,1)} %get-tuple-element.161), channel_id=1, source_target_pairs={{8,0},{12,4},{16,8},{20,12},{24,16},{28,20},{9,1},{13,5},{17,9},{2... | collective-permute-start | bytes 3145736 | tf_op jit(solution)/shard_map/ppermute | solution.py:370
  265.9 29.2 %collective-permute-start.25 = (bf16[128,1024]{1,0:T(8,128)(2,1)S(1)}, bf16[128,1024]{1,0:T(8,128)(2,1)S(1)}, u32[]{:S(2)}, u32[]{:S(2)}) collective-permute-start(bf16[128,1024]{1,0:T(8,128)(2,1)S(1)} %get-tuple-element.147), channel_id=1, source_target_pairs={{4,0},{8,4},{12,8},{16,12},{20,16},{24,20},{28,24},{5,1},{9,5},{13... | collective-permute-start | bytes 786440 | tf_op jit(solution)/shard_map/ppermute | solution.py:370
  280.5 1.3 copy-start.17
  282.7 22.9 %all-to-all-start = ((f32[8,16,128]{2,1,0:T(8,128)}), f32[8,16,128]{2,1,0:T(8,128)S(1)}, u32[]{:S(2)}, u32[]{:S(2)}) async-start(f32[8,16,128]{2,1,0:T(8,128)} %bitcast.20), calls=%async_computation | async-start | bytes 131072 | tf_op jit(solution)/shard_map/all_to_all | solution.py:557
  287.4 18.8 %collective-permute-start.20 = (bf16[128,1024]{1,0:T(8,128)(2,1)S(1)}, bf16[128,1024]{1,0:T(8,128)(2,1)S(1)}, u32[]{:S(2)}, u32[]{:S(2)}) collective-permute-start(bf16[128,1024]{1,0:T(8,128)(2,1)S(1)} %get-tuple-element.143), channel_id=1, source_target_pairs={{4,0},{8,4},{12,8},{16,12},{20,16},{24,20},{28,24},{5,1},{9,5},{13... | collective-permute-start | bytes 786440 | tf_op jit(solution)/shard_map/ppermute | solution.py:370
  291.0 2.6 copy-start.21
  306.2 1.6 copy-start.18
Sparse Core Ops, SparseCore 0:
  11.4 34.6 all-gather.4
  58.5 33.7 all-gather.6

commit v11 on v10

--- a/solution.py
+++ b/solution.py
@@ -75,12 +75,12 @@
     group = group_of_lane(FILT, 2 * LANES)
     rows = []
     for b in range(0, blocks, 2):
-        out = jnp.dot(table, windows(ext, b), preferred_element_type=F32)
+        out = jnp.dot(table, windows(ext, b), preferred_element_type=F32).astype(BF16)
         picked = out[:FILT]
         for g in range(1, GPT):
             picked = jnp.where(group == g, out[g * FILT : (g + 1) * FILT], picked)
         rows += [picked[:, :LANES], picked[:, LANES:]]
-    return jnp.concatenate(rows, axis=0)
+    return jnp.concatenate(rows, axis=0).astype(F32)
 
 
 def product_of(k, v):

time: 327 us -> 328 us (level)
  no operation moved by 1% of the time
where the time goes in v11:
time: 328 us; the launch traced here: 325 us
  Pallas kernels  165 us (50%)
  starting transfers between devices  65.9 us (20%)
  waiting for transfers between devices  40.1 us (12%)
  other arithmetic  22.9 us (7%)
  local copies, waits for them, and re-layouts  16.8 us (5%)
  between operations  14.6 us (4%)
    ppermute x26, starting transfers between devices, send(): return lax.ppermute(x, 'seq', pairs)  61.1 us
    pallas_call x6, Pallas kernels, gate_grad(): pl.pallas_call(functools.partial(gate_kernel, slots), grid_spec=pltpu.Pre...  45 us
    ppermute x26, waiting for transfers between devices, send(): return lax.ppermute(x, 'seq', pairs)  40.1 us
    pallas_call x4, Pallas kernels, weight_rows(): pl.pallas_call(functools.partial(rows_kernel, n), grid_spec=pltpu.Prefetc...  33.3 us
    pallas_call x2, Pallas kernels, middle(): pl.pallas_call(kernel, grid=(tiles,), in_specs=in_specs, out_specs=[here,...  25.2 us
    pallas_call x2, Pallas kernels, backward(): pl.pallas_call(backward_kernel, grid=(tiles,), in_specs=in_specs, out_spe...  21 us
    pallas_call x2, Pallas kernels, forward(): pl.pallas_call(forward_kernel, grid=(tiles,), in_specs=[here, here, here,...  20.1 us
    pallas_call x1, Pallas kernels, tables(): pl.pallas_call(table_kernel, grid=(groups // GPT,), in_specs=[seed, seed]...  10.4 us
  transfers between devices with their start and end apart: 29, of which 11 were waited for; matrix products, arithmetic and copies ran while one was open for 8% of the time, Pallas kernels for 46%

profile of v11, /device:TPU:10, one launch (start us, length us, event | category | flops | bytes accessed | tf_op | source)
XLA Modules:
  0.0 325.2 jit_solution(18011578985310587608)
XLA Ops:
  7.2 1.3 multiply_convert_fusion
  8.6 2.7 constant_dynamic-slice_fusion
  11.3 3.4 %collective-permute-start = (bf16[128,2048]{1,0:T(8,128)(2,1)S(1)}, bf16[128,2048]{1,0:T(8,128)(2,1)S(1)}, u32[]{:S(2)}, u32[]{:S(2)}) collective-permute-start(bf16[128,2048]{1,0:T(8,128)(2,1)S(1)} %multiply_convert_fusion), channel_id=1, source_target_pairs={{0,4},{4,8},{8,12},{12,16},{16,20},{20,24},{24,28},{1,5},{5,9},{9,... | collective-permute-start | bytes 1572872 | tf_op jit(solution)/shard_map/ppermute | solution.py:370
  15.1 10.4 %shard_map.101 = (bf16[16384,256]{1,0:T(8,128)(2,1)}, bf16[16384,256]{1,0:T(8,128)(2,1)}) custom-call(f32[128,256]{1,0:T(8,128)S(1)} %maximum_maximum_fusion.back_ref, f32[128,256]{1,0:T(8,128)S(1)} %concatenate.22.ahead_ref), custom_call_target="tpu_custom_call" | custom-call | flops 524288 | bytes 262144 | tf_op jit(solution)/shard_map/pallas_call | solution.py:54
  25.5 2.8 fusion.14
  28.2 3.5 %collective-permute-start.1 = (bf16[512,1024]{1,0:T(8,128)(2,1)S(1)}, bf16[512,1024]{1,0:T(8,128)(2,1)S(1)}, u32[]{:S(2)}, u32[]{:S(2)}) collective-permute-start(bf16[512,1024]{1,0:T(8,128)(2,1)S(1)} %get-tuple-element.85.refs_3_), channel_id=1, source_target_pairs={{0,8},{4,12},{8,16},{12,20},{16,24},{20,28},{1,9},{5,13},{9,17},{1... | collective-permute-start | bytes 3145736 | tf_op jit(solution)/shard_map/ppermute | solution.py:370
  31.7 2.4 collective-permute-start.2
  34.2 1.6 collective-permute-start.3
  35.7 10.0 %shard_map.102 = (bf16[1024,1024]{1,0:T(8,128)(2,1)S(1)}, bf16[1024,1024]{1,0:T(8,128)(2,1)S(1)}) custom-call(bf16[1024,2048]{1,0:T(8,128)(2,1)} %refs_1_.3, bf16[1024,2048]{1,0:T(8,128)(2,1)} %k.7, bf16[1024,2048]{1,0:T(8,128)(2,1)} %v.7, bf16[128,2048]{1,0:T(8,128)(2,1)S(1)} %collective-permute-done.prior.refs_5_, bf16[16384,256]{1,0:T(8,128)(2,1)} %get-tuple-element.88.table), custom_call_target="tpu_custom_call" | custom-call | flops 67108864 | bytes 229376 | tf_op jit(solution)/shard_map/pallas_call | solution.py:104
  45.7 1.4 copy-done.11
  47.1 1.3 copy-done.13
  48.5 6.3 %collective-permute-done.1.refs_5_ = bf16[512,1024]{1,0:T(8,128)(2,1)S(1)} collective-permute-done((bf16[512,1024]{1,0:T(8,128)(2,1)S(1)}, bf16[512,1024]{1,0:T(8,128)(2,1)S(1)}, u32[]{:S(2)}, u32[]{:S(2)}) %collective-permute-start.1) | collective-permute-done | bytes 1048608 | tf_op jit(solution)/shard_map/ppermute | solution.py:370
  54.8 3.2 collective-permute-done.2.refs_4_.refs_2_
  58.4 1.6 collective-permute-start.6
  60.0 3.4 %collective-permute-start.7 = (bf16[512,1024]{1,0:T(8,128)(2,1)}, bf16[512,1024]{1,0:T(8,128)(2,1)}, u32[]{:S(2)}, u32[]{:S(2)}) collective-permute-start(bf16[512,1024]{1,0:T(8,128)(2,1)} %get-tuple-element.93.refs_4_), channel_id=1, source_target_pairs={{0,8},{4,12},{8,16},{12,20},{16,24},{20,28},{1,9},{5,13},{9,17},{1... | collective-permute-start | bytes 3145736 | tf_op jit(solution)/shard_map/ppermute | solution.py:370
  63.4 3.4 %collective-permute-start.8 = (bf16[512,1024]{1,0:T(8,128)(2,1)}, bf16[512,1024]{1,0:T(8,128)(2,1)S(1)}, u32[]{:S(2)}, u32[]{:S(2)}) collective-permute-start(bf16[512,1024]{1,0:T(8,128)(2,1)} %get-tuple-element.93.refs_4_), channel_id=1, source_target_pairs={{8,0},{12,4},{16,8},{20,12},{24,16},{28,20},{9,1},{13,5},{17,9},{2... | collective-permute-start | bytes 3145736 | tf_op jit(solution)/shard_map/ppermute | solution.py:370
  66.8 2.5 collective-permute-start.4
  69.3 1.9 collective-permute-start.5
  72.4 10.1 %shard_map.103 = (bf16[1024,1024]{1,0:T(8,128)(2,1)S(1)}, bf16[1024,1024]{1,0:T(8,128)(2,1)S(1)}) custom-call(bf16[1024,2048]{1,0:T(8,128)(2,1)} %refs_1_.3, bf16[1024,2048]{1,0:T(8,128)(2,1)} %k.7, bf16[1024,2048]{1,0:T(8,128)(2,1)} %v.7, bf16[128,2048]{1,0:T(8,128)(2,1)S(1)} %copy-done.7, bf16[16384,256]{1,0:T(8,128)(2,1)} %get-tuple-element.88.table), custom_call_target="tpu_custom_call" | custom-call | flops 67108864 | bytes 229376 | tf_op jit(solution)/shard_map/pallas_call | solution.py:104
  83.9 3.4 %collective-permute-done.7.refs_6_ = bf16[512,1024]{1,0:T(8,128)(2,1)} collective-permute-done((bf16[512,1024]{1,0:T(8,128)(2,1)}, bf16[512,1024]{1,0:T(8,128)(2,1)}, u32[]{:S(2)}, u32[]{:S(2)}) %collective-permute-start.7) | collective-permute-done | bytes 1048608 | tf_op jit(solution)/shard_map/ppermute | solution.py:370
  87.3 4.3 %collective-permute-done.8.refs_5_.refs_10_ = bf16[512,1024]{1,0:T(8,128)(2,1)S(1)} collective-permute-done((bf16[512,1024]{1,0:T(8,128)(2,1)}, bf16[512,1024]{1,0:T(8,128)(2,1)S(1)}, u32[]{:S(2)}, u32[]{:S(2)}) %collective-permute-start.8) | collective-permute-done | bytes 1048608 | tf_op jit(solution)/shard_map/ppermute | solution.py:370
  91.6 9.0 %shard_map.104.refs_2_ = f32[4,512,1024]{2,1,0:T(8,128)} custom-call(s32[4]{0:T(128)S(1)} %pad_add_fusion.pick, bf16[4,1024,512]{2,1,0:T(8,128)(2,1)} %bitcast.48, bf16[1024,1024]{1,0:T(8,128)(2,1)S(1)} %copy-done.14), custom_call_target="tpu_custom_call" | custom-call | flops 16777216 | bytes 49152 | tf_op jit(solution)/shard_map/pallas_call | solution.py:310
  100.6 5.9 %collective-permute-done.4.refs_3_.refs_6_ = bf16[512,1024]{1,0:T(8,128)(2,1)S(1)} collective-permute-done((bf16[512,1024]{1,0:T(8,128)(2,1)}, bf16[512,1024]{1,0:T(8,128)(2,1)S(1)}, u32[]{:S(2)}, u32[]{:S(2)}) %collective-permute-start.4) | collective-permute-done | bytes 1048608 | tf_op jit(solution)/shard_map/ppermute | solution.py:370
  106.5 4.1 %collective-permute-done.5.refs_4_.refs_7_ = bf16[512,1024]{1,0:T(8,128)(2,1)} collective-permute-done((bf16[512,1024]{1,0:T(8,128)(2,1)S(1)}, bf16[512,1024]{1,0:T(8,128)(2,1)}, u32[]{:S(2)}, u32[]{:S(2)}) %collective-permute-start.5) | collective-permute-done | bytes 1048608 | tf_op jit(solution)/shard_map/ppermute | solution.py:370
  111.3 2.4 collective-permute-start.10
  113.6 2.7 collective-permute-start.11
  116.4 5.0 %shard_map.105 = (bf16[512,1024]{1,0:T(8,128)(2,1)S(1)}, bf16[512,1024]{1,0:T(8,128)(2,1)}) custom-call(s32[3]{0:T(128)S(1)} %pad_add_fusion.1.pick, bf16[4,1024,512]{2,1,0:T(8,128)(2,1)} %bitcast.36, bf16[1024,1024]{1,0:T(8,128)(2,1)} %collective-permute-done.6.refs_1_, f32[4,512,1024]{2,1,0:T(8,128)} %shard_map.104.refs_2_, ...), custom_call_target="tpu_custom_call" | custom-call | flops 16777216 | bytes 49152 | tf_op jit(solution)/shard_map/pallas_call | solution.py:344
  122.6 7.7 %shard_map.106 = bf16[3,512,1024]{2,1,0:T(8,128)(2,1)S(1)} custom-call(s32[3]{0:T(128)S(1)} %pad_add_fusion.2.pick, bf16[4,1024,512]{2,1,0:T(8,128)(2,1)} %bitcast.37, bf16[1024,1024]{1,0:T(8,128)(2,1)} %collective-permute-done.6.refs_1_, f32[4,512,1024]{2,1,0:T(8,128)} %shard_map.104.refs_2_), custom_call_target="tpu_custom_call" | custom-call | flops 16777216 | bytes 49152 | tf_op jit(solution)/shard_map/pallas_call | solution.py:310
  130.3 7.6 %shard_map.107.refs_3_ = bf16[1024,1024]{1,0:T(8,128)(2,1)} custom-call(s32[7]{0:T(128)S(1)} %stack.58.pick, bf16[4,1024,512]{2,1,0:T(8,128)(2,1)} %bitcast.38, bf16[4,1024,512]{2,1,0:T(8,128)(2,1)} %bitcast.39, bf16[4,1024,512]{2,1,0:T(8,128)(2,1)} %bitcast.40, bf16[512,1024]{1,0:T(8,128)(2,1)S(1)} %copy-done.2, ...), custom_call_target="tpu_custom_call" | custom-call | flops 50331648 | bytes 98304 | tf_op jit(solution)/shard_map/pallas_call | solution.py:269
  137.9 2.0 collective-permute-done.11.refs_4_.refs_8_
  139.9 9.0 %shard_map.108.refs_2_ = f32[4,512,1024]{2,1,0:T(8,128)} custom-call(s32[4]{0:T(128)S(1)} %pad_add_fusion.pick, bf16[4,1024,512]{2,1,0:T(8,128)(2,1)} %bitcast.49, bf16[1024,1024]{1,0:T(8,128)(2,1)S(1)} %copy-done.16), custom_call_target="tpu_custom_call" | custom-call | flops 16777216 | bytes 49152 | tf_op jit(solution)/shard_map/pallas_call | solution.py:310
  148.9 7.6 %shard_map.109.refs_3_ = bf16[1024,1024]{1,0:T(8,128)(2,1)} custom-call(s32[7]{0:T(128)S(1)} %stack.58.pick, bf16[4,1024,512]{2,1,0:T(8,128)(2,1)} %bitcast.50, bf16[4,1024,512]{2,1,0:T(8,128)(2,1)} %bitcast.51, bf16[4,1024,512]{2,1,0:T(8,128)(2,1)} %bitcast.52, bf16[512,1024]{1,0:T(8,128)(2,1)S(1)} %copy-done.2, ...), custom_call_target="tpu_custom_call" | custom-call | flops 50331648 | bytes 98304 | tf_op jit(solution)/shard_map/pallas_call | solution.py:269
  157.8 4.7 %shard_map.110 = bf16[1024,1024]{1,0:T(8,128)(2,1)S(1)} custom-call(s32[7]{0:T(128)S(1)} %stack.58.pick, bf16[4,1024,512]{2,1,0:T(8,128)(2,1)} %bitcast.41, bf16[512,1024]{1,0:T(8,128)(2,1)} %collective-permute-done.9.refs_1_, bf16[512,1024]{1,0:T(8,128)(2,1)S(1)} %collective-permute-done.2.refs_4_.refs_2_, bf16[1024,1024]{1,0:T(8,128)(2,1)} %shard_map.107.refs_3_), custom_call_target="tpu_custom_call" | custom-call | flops 16777216 | bytes 32768 | tf_op jit(solution)/shard_map/pallas_call | solution.py:269
  162.5 4.8 %shard_map.111 = (bf16[512,1024]{1,0:T(8,128)(2,1)S(1)}, bf16[512,1024]{1,0:T(8,128)(2,1)S(1)}) custom-call(s32[3]{0:T(128)S(1)} %pad_add_fusion.1.pick, bf16[4,1024,512]{2,1,0:T(8,128)(2,1)} %bitcast.42, bf16[1024,1024]{1,0:T(8,128)(2,1)} %collective-permute-done.12.refs_1_, f32[4,512,1024]{2,1,0:T(8,128)} %shard_map.108.refs_2_, ...), custom_call_target="tpu_custom_call" | custom-call | flops 16777216 | bytes 49152 | tf_op jit(solution)/shard_map/pallas_call | solution.py:344
  167.3 2.6 collective-permute-start.14
  169.9 1.5 collective-permute-start.13
  171.5 2.6 fusion.11
  175.4 2.1 collective-permute-start.17
  177.5 7.6 %shard_map.112 = bf16[3,512,1024]{2,1,0:T(8,128)(2,1)S(1)} custom-call(s32[3]{0:T(128)S(1)} %pad_add_fusion.2.pick, bf16[4,1024,512]{2,1,0:T(8,128)(2,1)} %bitcast.43, bf16[1024,1024]{1,0:T(8,128)(2,1)} %collective-permute-done.12.refs_1_, f32[4,512,1024]{2,1,0:T(8,128)} %shard_map.108.refs_2_), custom_call_target="tpu_custom_call" | custom-call | flops 16777216 | bytes 49152 | tf_op jit(solution)/shard_map/pallas_call | solution.py:310
  185.1 5.2 %shard_map.113.own_ref = bf16[1024,1024]{1,0:T(8,128)(2,1)S(1)} custom-call(s32[7]{0:T(128)S(1)} %stack.58.pick, bf16[4,1024,512]{2,1,0:T(8,128)(2,1)} %bitcast.53, bf16[512,1024]{1,0:T(8,128)(2,1)} %collective-permute-done.9.refs_1_, bf16[512,1024]{1,0:T(8,128)(2,1)S(1)} %collective-permute-done.2.refs_4_.refs_2_, bf16[1024,1024]{1,0:T(8,128)(2,1)} %shard_map.109.refs_3_), custom_call_target="tpu_custom_call" | custom-call | flops 16777216 | bytes 32768 | tf_op jit(solution)/shard_map/pallas_call | solution.py:269
  191.7 2.4 collective-permute-done.14.refs_9_
  194.1 9.9 %shard_map.114 = bf16[1024,1024]{1,0:T(8,128)(2,1)} custom-call(s32[7]{0:T(128)S(1)} %stack.58.pick, bf16[4,1024,512]{2,1,0:T(8,128)(2,1)} %bitcast.44, bf16[4,1024,512]{2,1,0:T(8,128)(2,1)} %bitcast.45, bf16[4,1024,512]{2,1,0:T(8,128)(2,1)} %bitcast.46, bf16[4,1024,512]{2,1,0:T(8,128)(2,1)} %bitcast.47, bf16[512,1024]{1,0:T(8,128)(2,1)} %get-tuple-element.93.refs_4_, ...), custom_call_target="tpu_custom_call" | custom-call | flops 67108864 | bytes 131072 | tf_op jit(solution)/shard_map/pallas_call | solution.py:269
  204.0 2.7 fusion.10
  208.0 1.9 collective-permute-start.22
  209.9 6.7 %collective-permute-done.16 = bf16[512,1024]{1,0:T(8,128)(2,1)} collective-permute-done((bf16[512,1024]{1,0:T(8,128)(2,1)}, bf16[512,1024]{1,0:T(8,128)(2,1)}, u32[]{:S(2)}, u32[]{:S(2)}) %collective-permute-start.16) | collective-permute-done | bytes 1048608 | tf_op jit(solution)/shard_map/ppermute | solution.py:370
  216.6 1.5 collective-permute-start.15
  218.1 3.9 %fusion.1 = (bf16[512,1024]{1,0:T(8,128)(2,1)}, bf16[512,1024]{1,0:T(8,128)(2,1)}) fusion(bf16[512,1024]{1,0:T(8,128)(2,1)} %collective-permute-done.17, bf16[512,1024]{1,0:T(8,128)(2,1)} %collective-permute-done.16, bf16[512,1024]{1,0:T(8,128)(2,1)S(1)} %copy-done.20, pred[]{:T(512)S(6)} %eq.15, pred[]{:T(512)S(6)} %eq.17, ...), kind=kLoop, calls=%fused_computation.9 | loop fusion | flops 6291456 | bytes 6291458 | tf_op jit(solution)/shard_map/convert_element_type | solution.py:439
  222.0 1.9 collective-permute-start.18
  224.0 5.1 %collective-permute-start.19 = (bf16[512,1024]{1,0:T(8,128)(2,1)}, bf16[512,1024]{1,0:T(8,128)(2,1)}, u32[]{:S(2)}, u32[]{:S(2)}) collective-permute-start(bf16[512,1024]{1,0:T(8,128)(2,1)} %get-tuple-element.164), channel_id=1, source_target_pairs={{8,0},{12,4},{16,8},{20,12},{24,16},{28,20},{9,1},{13,5},{17,9},{2... | collective-permute-start | bytes 3145736 | tf_op jit(solution)/shard_map/ppermute | solution.py:370
  229.1 9.9 %shard_map.115.own_ref = bf16[1024,1024]{1,0:T(8,128)(2,1)} custom-call(s32[7]{0:T(128)S(1)} %stack.58.pick, bf16[4,1024,512]{2,1,0:T(8,128)(2,1)} %bitcast.54, bf16[4,1024,512]{2,1,0:T(8,128)(2,1)} %bitcast.55, bf16[4,1024,512]{2,1,0:T(8,128)(2,1)} %bitcast.56, bf16[4,1024,512]{2,1,0:T(8,128)(2,1)} %bitcast.57, ...), custom_call_target="tpu_custom_call" | custom-call | flops 67108864 | bytes 131072 | tf_op jit(solution)/shard_map/pallas_call | solution.py:269
  239.0 12.5 %shard_map.116 = (bf16[1024,2048]{1,0:T(8,128)(2,1)}, bf16[1024,1024]{1,0:T(8,128)(2,1)S(1)}, bf16[128,1024]{1,0:T(8,128)(2,1)S(1)}, f32[64,256]{1,0:T(8,128)S(1)}) custom-call(bf16[1024,1024]{1,0:T(8,128)(2,1)S(1)} %copy-done.5, bf16[1024,1024]{1,0:T(8,128)(2,1)} %collective-permute-done.13.refs_0_, bf16[1024,2048]{1,0:T(8,128)(2,1)} %refs_1_.3, ...), custom_call_target="tpu_custom_call" | custom-call | flops 67108864 | bytes 294912 | tf_op jit(solution)/shard_map/pallas_call | solution.py:171
  251.6 4.0 %fusion.7 = (bf16[512,1024]{1,0:T(8,128)(2,1)}, bf16[512,1024]{1,0:T(8,128)(2,1)}) fusion(bf16[512,1024]{1,0:T(8,128)(2,1)} %collective-permute-done.21, bf16[512,1024]{1,0:T(8,128)(2,1)} %collective-permute-done.22, bf16[512,1024]{1,0:T(8,128)(2,1)S(1)} %get-tuple-element.145, pred[]{:T(512)S(6)} %eq.15, bf16[3,512,1024]{2,1,0:T(8,128)(2,1)S(1)} %shard_map.112, ...), kind=kLoop, calls=%fused_computation.15 | loop fusion | flops 6291456 | bytes 6291458 | tf_op jit(solution)/shard_map/convert_element_type | solution.py:439
  255.7 1.9 collective-permute-start.23
  257.6 5.1 %collective-permute-start.24 = (bf16[512,1024]{1,0:T(8,128)(2,1)}, bf16[512,1024]{1,0:T(8,128)(2,1)}, u32[]{:S(2)}, u32[]{:S(2)}) collective-permute-start(bf16[512,1024]{1,0:T(8,128)(2,1)} %get-tuple-element.161), channel_id=1, source_target_pairs={{8,0},{12,4},{16,8},{20,12},{24,16},{28,20},{9,1},{13,5},{17,9},{2... | collective-permute-start | bytes 3145736 | tf_op jit(solution)/shard_map/ppermute | solution.py:370
  262.7 3.2 fusion.13
  265.9 1.9 collective-permute-start.25
  267.8 12.6 %shard_map.117 = (bf16[1024,2048]{1,0:T(8,128)(2,1)}, bf16[1024,1024]{1,0:T(8,128)(2,1)S(1)}, bf16[128,1024]{1,0:T(8,128)(2,1)S(1)}, f32[64,256]{1,0:T(8,128)S(1)}) custom-call(bf16[1024,1024]{1,0:T(8,128)(2,1)S(1)} %copy-done.3, bf16[1024,1024]{1,0:T(8,128)(2,1)} %collective-permute-done.15.refs_0_, ...), custom_call_target="tpu_custom_call", output_to_operand_aliasing={{0}: (7, {})} | custom-call | flops 67108864 | bytes 294912 | tf_op jit(solution)/shard_map/pallas_call | solution.py:171
  282.7 4.7 %all-to-all-start = ((f32[8,16,128]{2,1,0:T(8,128)}), f32[8,16,128]{2,1,0:T(8,128)S(1)}, u32[]{:S(2)}, u32[]{:S(2)}) async-start(f32[8,16,128]{2,1,0:T(8,128)} %bitcast.20), calls=%async_computation | async-start | bytes 131072 | tf_op jit(solution)/shard_map/all_to_all | solution.py:557
  287.4 3.6 %collective-permute-start.20 = (bf16[128,1024]{1,0:T(8,128)(2,1)S(1)}, bf16[128,1024]{1,0:T(8,128)(2,1)S(1)}, u32[]{:S(2)}, u32[]{:S(2)}) collective-permute-start(bf16[128,1024]{1,0:T(8,128)(2,1)S(1)} %get-tuple-element.143), channel_id=1, source_target_pairs={{4,0},{8,4},{12,8},{16,12},{20,16},{24,20},{28,24},{5,1},{9,5},{13... | collective-permute-start | bytes 786440 | tf_op jit(solution)/shard_map/ppermute | solution.py:370
  291.0 2.6 fusion.9
  293.6 1.5 pad_maximum_fusion
  295.1 10.5 %shard_map.118 = (bf16[1024,2048]{1,0:T(8,128)(2,1)}, bf16[1024,2048]{1,0:T(8,128)(2,1)}) custom-call(bf16[1024,1024]{1,0:T(8,128)(2,1)S(1)} %get-tuple-element.151.gm, bf16[128,1024]{1,0:T(8,128)(2,1)S(1)} %collective-permute-done.25.later, bf16[1024,2048]{1,0:T(8,128)(2,1)} %k.7, bf16[1024,2048]{1,0:T(8,128)(2,1)} %v.7, ...), custom_call_target="tpu_custom_call" | custom-call | flops 67108864 | bytes 229376 | tf_op jit(solution)/shard_map/pallas_call | solution.py:216
  306.2 1.6 copy-done.18
  307.8 10.5 %shard_map.119 = (bf16[1024,2048]{1,0:T(8,128)(2,1)}, bf16[1024,2048]{1,0:T(8,128)(2,1)}) custom-call(bf16[1024,1024]{1,0:T(8,128)(2,1)S(1)} %copy-done.18, bf16[128,1024]{1,0:T(8,128)(2,1)S(1)} %collective-permute-done.20.later, bf16[1024,2048]{1,0:T(8,128)(2,1)} %k.7, bf16[1024,2048]{1,0:T(8,128)(2,1)} %v.7, ...), custom_call_target="tpu_custom_call", output_to_operand_aliasing={{0}: (5, {}), {1}: (6, {})} | custom-call | flops 67108864 | bytes 229376 | tf_op jit(solution)/shard_map/pallas_call | solution.py:216
  (86 shorter events, 13.2 us)
Async XLA Ops:
  7.2 51.2 %all-gather.5.cloned.1.call-start = ((), (), s32[]{:S(2)}) async-start(), calls=%async_computation.1 | async-start | bytes 5242880 | tf_op jit(solution)/shard_map/all_gather | solution.py:465
  8.6 6.2 %copy-start.22 = (bf16[128,128]{1,0:T(8,128)(2,1)S(1)}, bf16[128,128]{1,0:T(8,128)(2,1)}, u32[]{:S(2)}) copy-start(bf16[128,128]{1,0:T(8,128)(2,1)} %param.9) | copy-start | bytes 98308
  11.3 99.4 %all-gather.7.cloned.1.call-start = ((), (), s32[]{:S(2)}) async-start(), calls=%async_computation.2 | async-start | bytes 5242880 | tf_op jit(solution)/shard_map/all_gather | solution.py:479
  11.3 16.9 %collective-permute-start = (bf16[128,2048]{1,0:T(8,128)(2,1)S(1)}, bf16[128,2048]{1,0:T(8,128)(2,1)S(1)}, u32[]{:S(2)}, u32[]{:S(2)}) collective-permute-start(bf16[128,2048]{1,0:T(8,128)(2,1)S(1)} %multiply_convert_fusion), channel_id=1, source_target_pairs={{0,4},{4,8},{8,12},{12,16},{16,20},{20,24},{24,28},{1,5},{5,9},{9,... | collective-permute-start | bytes 1572872 | tf_op jit(solution)/shard_map/ppermute | solution.py:370
  28.2 17.5 %copy-start.1 = (bf16[512,1024]{1,0:T(8,128)(2,1)}, bf16[512,1024]{1,0:T(8,128)(2,1)S(1)}, u32[]{:S(2)}) copy-start(bf16[512,1024]{1,0:T(8,128)(2,1)S(1)} %get-tuple-element.85.refs_3_) | copy-start | bytes 3145732
  28.2 17.5 %copy-start.6 = (bf16[128,2048]{1,0:T(8,128)(2,1)}, bf16[128,2048]{1,0:T(8,128)(2,1)S(1)}, u32[]{:S(2)}) copy-start(bf16[128,2048]{1,0:T(8,128)(2,1)S(1)} %collective-permute-done.prior.refs_5_) | copy-start | bytes 1572868
  28.2 26.5 %collective-permute-start.1 = (bf16[512,1024]{1,0:T(8,128)(2,1)S(1)}, bf16[512,1024]{1,0:T(8,128)(2,1)S(1)}, u32[]{:S(2)}, u32[]{:S(2)}) collective-permute-start(bf16[512,1024]{1,0:T(8,128)(2,1)S(1)} %get-tuple-element.85.refs_3_), channel_id=1, source_target_pairs={{0,8},{4,12},{8,16},{12,20},{16,24},{20,28},{1,9},{5,13},{9,17},{1... | collective-permute-start | bytes 3145736 | tf_op jit(solution)/shard_map/ppermute | solution.py:370
  31.7 26.2 %collective-permute-start.2 = (bf16[512,1024]{1,0:T(8,128)(2,1)S(1)}, bf16[512,1024]{1,0:T(8,128)(2,1)S(1)}, u32[]{:S(2)}, u32[]{:S(2)}) collective-permute-start(bf16[512,1024]{1,0:T(8,128)(2,1)S(1)} %get-tuple-element.85.refs_3_), channel_id=1, source_target_pairs={{8,0},{12,4},{16,8},{20,12},{24,16},{28,20},{9,1},{13,5},{17,9},{2... | collective-permute-start | bytes 3145736 | tf_op jit(solution)/shard_map/ppermute | solution.py:370
  34.2 24.2 %collective-permute-start.3 = (bf16[1024,512]{1,0:T(8,128)(2,1)S(1)}, bf16[1024,512]{1,0:T(8,128)(2,1)}, u32[]{:S(2)}, u32[]{:S(2)}) collective-permute-start(bf16[1024,512]{1,0:T(8,128)(2,1)S(1)} %get-tuple-element.86), channel_id=1, source_target_pairs={{0,4},{4,0},{8,12},{12,8},{16,20},{20,16},{24,28},{28,24},{1,5},{5... | collective-permute-start | bytes 3145736 | tf_op jit(solution)/shard_map/ppermute | solution.py:370
  45.7 1.4 copy-start.11
  47.1 1.3 copy-start.13
  54.8 3.2 copy-start.9
  58.4 52.2 %collective-permute-start.6 = (bf16[1024,1024]{1,0:T(8,128)(2,1)}, bf16[1024,1024]{1,0:T(8,128)(2,1)}, u32[]{:S(2)}, u32[]{:S(2)}) collective-permute-start(bf16[1024,1024]{1,0:T(8,128)(2,1)} %copy-done.13), channel_id=1, source_target_pairs={{0,4},{4,0},{8,12},{12,8},{16,20},{20,16},{24,28},{28,24},{1,5},{5... | collective-permute-start | bytes 6291464 | tf_op jit(solution)/shard_map/ppermute | solution.py:370
  60.0 27.3 %collective-permute-start.7 = (bf16[512,1024]{1,0:T(8,128)(2,1)}, bf16[512,1024]{1,0:T(8,128)(2,1)}, u32[]{:S(2)}, u32[]{:S(2)}) collective-permute-start(bf16[512,1024]{1,0:T(8,128)(2,1)} %get-tuple-element.93.refs_4_), channel_id=1, source_target_pairs={{0,8},{4,12},{8,16},{12,20},{16,24},{20,28},{1,9},{5,13},{9,17},{1... | collective-permute-start | bytes 3145736 | tf_op jit(solution)/shard_map/ppermute | solution.py:370
  63.4 28.2 %collective-permute-start.8 = (bf16[512,1024]{1,0:T(8,128)(2,1)}, bf16[512,1024]{1,0:T(8,128)(2,1)S(1)}, u32[]{:S(2)}, u32[]{:S(2)}) collective-permute-start(bf16[512,1024]{1,0:T(8,128)(2,1)} %get-tuple-element.93.refs_4_), channel_id=1, source_target_pairs={{8,0},{12,4},{16,8},{20,12},{24,16},{28,20},{9,1},{13,5},{17,9},{2... | collective-permute-start | bytes 3145736 | tf_op jit(solution)/shard_map/ppermute | solution.py:370
  66.8 39.7 %collective-permute-start.4 = (bf16[512,1024]{1,0:T(8,128)(2,1)}, bf16[512,1024]{1,0:T(8,128)(2,1)S(1)}, u32[]{:S(2)}, u32[]{:S(2)}) collective-permute-start(bf16[512,1024]{1,0:T(8,128)(2,1)} %copy-done.9), channel_id=1, source_target_pairs={{8,16},{12,20},{16,24},{20,28},{9,17},{13,21},{17,25},{21,29},{10,... | collective-permute-start | bytes 3145736 | tf_op jit(solution)/shard_map/ppermute | solution.py:370
  69.3 41.3 %collective-permute-start.5 = (bf16[512,1024]{1,0:T(8,128)(2,1)S(1)}, bf16[512,1024]{1,0:T(8,128)(2,1)}, u32[]{:S(2)}, u32[]{:S(2)}) collective-permute-start(bf16[512,1024]{1,0:T(8,128)(2,1)S(1)} %collective-permute-done.2.refs_4_.refs_2_), channel_id=1, source_target_pairs={{16,8},{20,12},{8,0},{12,4},{17,9},{21,13},{9,1},{13,5},{18,10},{2... | collective-permute-start | bytes 3145736 | tf_op jit(solution)/shard_map/ppermute | solution.py:370
  71.4 1.0 copy-start.7
  72.4 19.2 %copy-start.14 = (bf16[1024,1024]{1,0:T(8,128)(2,1)S(1)}, bf16[1024,1024]{1,0:T(8,128)(2,1)}, u32[]{:S(2)}) copy-start(bf16[1024,1024]{1,0:T(8,128)(2,1)} %copy-done.13) | copy-start | bytes 6291460
  82.6 1.3 copy-start.12
  83.9 16.7 %copy-start.15 = (bf16[1024,1024]{1,0:T(8,128)(2,1)}, bf16[1024,1024]{1,0:T(8,128)(2,1)S(1)}, u32[]{:S(2)}) copy-start(bf16[1024,1024]{1,0:T(8,128)(2,1)S(1)} %get-tuple-element.116.refs_1_) | copy-start | bytes 6291460
  110.7 51.8 %collective-permute-start.12 = (bf16[1024,1024]{1,0:T(8,128)(2,1)}, bf16[1024,1024]{1,0:T(8,128)(2,1)}, u32[]{:S(2)}, u32[]{:S(2)}) collective-permute-start(bf16[1024,1024]{1,0:T(8,128)(2,1)} %copy-done.15), channel_id=1, source_target_pairs={{0,4},{4,0},{8,12},{12,8},{16,20},{20,16},{24,28},{28,24},{1,5},{5... | collective-permute-start | bytes 6291464 | tf_op jit(solution)/shard_map/ppermute | solution.py:370
  111.3 26.7 %collective-permute-start.10 = (bf16[512,1024]{1,0:T(8,128)(2,1)}, bf16[512,1024]{1,0:T(8,128)(2,1)}, u32[]{:S(2)}, u32[]{:S(2)}) collective-permute-start(bf16[512,1024]{1,0:T(8,128)(2,1)} %collective-permute-done.7.refs_6_), channel_id=1, source_target_pairs={{8,16},{12,20},{16,24},{20,28},{9,17},{13,21},{17,25},{21,29},{10,... | collective-permute-start | bytes 3145736 | tf_op jit(solution)/shard_map/ppermute | solution.py:370
  113.6 26.3 %collective-permute-start.11 = (bf16[512,1024]{1,0:T(8,128)(2,1)S(1)}, bf16[512,1024]{1,0:T(8,128)(2,1)}, u32[]{:S(2)}, u32[]{:S(2)}) collective-permute-start(bf16[512,1024]{1,0:T(8,128)(2,1)S(1)} %collective-permute-done.8.refs_5_.refs_10_), channel_id=1, source_target_pairs={{16,8},{20,12},{8,0},{12,4},{17,9},{21,13},{9,1},{13,5},{18,10},{2... | collective-permute-start | bytes 3145736 | tf_op jit(solution)/shard_map/ppermute | solution.py:370
  121.4 1.0 copy-start.19
  122.4 35.4 %collective-permute-start.9 = (bf16[512,1024]{1,0:T(8,128)(2,1)}, bf16[512,1024]{1,0:T(8,128)(2,1)}, u32[]{:S(2)}, u32[]{:S(2)}) collective-permute-start(bf16[512,1024]{1,0:T(8,128)(2,1)} %get-tuple-element.105), channel_id=1, source_target_pairs={{0,8},{4,12},{24,16},{28,20},{16,24},{20,28},{8,0},{12,4},{1,9},{5... | collective-permute-start | bytes 3145736 | tf_op jit(solution)/shard_map/ppermute | solution.py:370
  122.6 7.7 %copy-start.2 = (bf16[512,1024]{1,0:T(8,128)(2,1)S(1)}, bf16[512,1024]{1,0:T(8,128)(2,1)}, u32[]{:S(2)}) copy-start(bf16[512,1024]{1,0:T(8,128)(2,1)} %copy-done.1) | copy-start | bytes 3145732
  122.6 7.7 %copy-start.10 = (bf16[512,1024]{1,0:T(8,128)(2,1)S(1)}, bf16[512,1024]{1,0:T(8,128)(2,1)}, u32[]{:S(2)}) copy-start(bf16[512,1024]{1,0:T(8,128)(2,1)} %copy-done.9) | copy-start | bytes 3145732
  130.3 9.6 %copy-start.16 = (bf16[1024,1024]{1,0:T(8,128)(2,1)S(1)}, bf16[1024,1024]{1,0:T(8,128)(2,1)}, u32[]{:S(2)}) copy-start(bf16[1024,1024]{1,0:T(8,128)(2,1)} %copy-done.15) | copy-start | bytes 6291460
  167.3 26.8 %collective-permute-start.14 = (bf16[512,1024]{1,0:T(8,128)(2,1)S(1)}, bf16[512,1024]{1,0:T(8,128)(2,1)}, u32[]{:S(2)}, u32[]{:S(2)}) collective-permute-start(bf16[512,1024]{1,0:T(8,128)(2,1)S(1)} %get-tuple-element.125), channel_id=1, source_target_pairs={{0,8},{4,12},{24,16},{28,20},{16,24},{20,28},{8,0},{12,4},{1,9},{5... | collective-permute-start | bytes 3145736 | tf_op jit(solution)/shard_map/ppermute | solution.py:370
  169.9 54.0 %collective-permute-start.13 = (bf16[1024,1024]{1,0:T(8,128)(2,1)S(1)}, bf16[1024,1024]{1,0:T(8,128)(2,1)}, u32[]{:S(2)}, u32[]{:S(2)}) collective-permute-start(bf16[1024,1024]{1,0:T(8,128)(2,1)S(1)} %shard_map.110), channel_id=1, source_target_pairs={{0,4},{4,0},{8,12},{12,8},{16,20},{20,16},{24,28},{28,24},{1,5},{5... | collective-permute-start | bytes 6291464 | tf_op jit(solution)/shard_map/ppermute | solution.py:370
  174.1 42.5 %collective-permute-start.16 = (bf16[512,1024]{1,0:T(8,128)(2,1)}, bf16[512,1024]{1,0:T(8,128)(2,1)}, u32[]{:S(2)}, u32[]{:S(2)}) collective-permute-start(bf16[512,1024]{1,0:T(8,128)(2,1)} %fusion.11), channel_id=1, source_target_pairs={{0,8},{4,12},{24,16},{28,20},{1,9},{5,13},{25,17},{29,21},{2,10},{... | collective-permute-start | bytes 3145736 | tf_op jit(solution)/shard_map/ppermute | solution.py:370
  175.4 42.8 %collective-permute-start.17 = (bf16[512,1024]{1,0:T(8,128)(2,1)}, bf16[512,1024]{1,0:T(8,128)(2,1)}, u32[]{:S(2)}, u32[]{:S(2)}) collective-permute-start(bf16[512,1024]{1,0:T(8,128)(2,1)} %fusion.11), channel_id=1, source_target_pairs={{8,16},{12,20},{16,8},{20,12},{9,17},{13,21},{17,9},{21,13},{10,18... | collective-permute-start | bytes 3145736 | tf_op jit(solution)/shard_map/ppermute | solution.py:370
  185.1 66.5 %copy-start = (bf16[3,512,1024]{2,1,0:T(8,128)(2,1)}, bf16[3,512,1024]{2,1,0:T(8,128)(2,1)S(1)}, u32[]{:S(2)}) copy-start(bf16[3,512,1024]{2,1,0:T(8,128)(2,1)S(1)} %shard_map.112) | copy-start | bytes 9437188
  190.4 1.3 copy-start.4
  204.0 14.1 %copy-start.20 = (bf16[512,1024]{1,0:T(8,128)(2,1)S(1)}, bf16[512,1024]{1,0:T(8,128)(2,1)}, u32[]{:S(2)}) copy-start(bf16[512,1024]{1,0:T(8,128)(2,1)} %copy-done.19) | copy-start | bytes 3145732
  206.7 44.9 %collective-permute-start.21 = (bf16[512,1024]{1,0:T(8,128)(2,1)}, bf16[512,1024]{1,0:T(8,128)(2,1)}, u32[]{:S(2)}, u32[]{:S(2)}) collective-permute-start(bf16[512,1024]{1,0:T(8,128)(2,1)} %fusion.10), channel_id=1, source_target_pairs={{0,8},{4,12},{24,16},{28,20},{1,9},{5,13},{25,17},{29,21},{2,10},{... | collective-permute-start | bytes 3145736 | tf_op jit(solution)/shard_map/ppermute | solution.py:370
  208.0 43.6 %collective-permute-start.22 = (bf16[512,1024]{1,0:T(8,128)(2,1)}, bf16[512,1024]{1,0:T(8,128)(2,1)}, u32[]{:S(2)}, u32[]{:S(2)}) collective-permute-start(bf16[512,1024]{1,0:T(8,128)(2,1)} %fusion.10), channel_id=1, source_target_pairs={{8,16},{12,20},{16,8},{20,12},{9,17},{13,21},{17,9},{21,13},{10,18... | collective-permute-start | bytes 3145736 | tf_op jit(solution)/shard_map/ppermute | solution.py:370
  216.6 51.2 %collective-permute-start.15 = (bf16[1024,1024]{1,0:T(8,128)(2,1)}, bf16[1024,1024]{1,0:T(8,128)(2,1)}, u32[]{:S(2)}, u32[]{:S(2)}) collective-permute-start(bf16[1024,1024]{1,0:T(8,128)(2,1)} %shard_map.114), channel_id=1, source_target_pairs={{0,4},{4,0},{8,12},{12,8},{16,20},{20,16},{24,28},{28,24},{1,5},{5... | collective-permute-start | bytes 6291464 | tf_op jit(solution)/shard_map/ppermute | solution.py:370
  222.0 40.6 %collective-permute-start.18 = (bf16[512,1024]{1,0:T(8,128)(2,1)}, bf16[512,1024]{1,0:T(8,128)(2,1)}, u32[]{:S(2)}, u32[]{:S(2)}) collective-permute-start(bf16[512,1024]{1,0:T(8,128)(2,1)} %get-tuple-element.163), channel_id=1, source_target_pairs={{0,8},{4,12},{8,16},{12,20},{16,24},{20,28},{1,9},{5,13},{9,17},{1... | collective-permute-start | bytes 3145736 | tf_op jit(solution)/shard_map/ppermute | solution.py:370
  224.0 15.1 %copy-start.5 = (bf16[1024,1024]{1,0:T(8,128)(2,1)S(1)}, bf16[1024,1024]{1,0:T(8,128)(2,1)}, u32[]{:S(2)}) copy-start(bf16[1024,1024]{1,0:T(8,128)(2,1)} %copy-done.4) | copy-start | bytes 6291460
  224.0 15.1 %copy-start.8 = (bf16[128,2048]{1,0:T(8,128)(2,1)S(1)}, bf16[128,2048]{1,0:T(8,128)(2,1)}, u32[]{:S(2)}) copy-start(bf16[128,2048]{1,0:T(8,128)(2,1)} %copy-done.6) | copy-start | bytes 1572868
  224.0 38.7 %collective-permute-start.19 = (bf16[512,1024]{1,0:T(8,128)(2,1)}, bf16[512,1024]{1,0:T(8,128)(2,1)}, u32[]{:S(2)}, u32[]{:S(2)}) collective-permute-start(bf16[512,1024]{1,0:T(8,128)(2,1)} %get-tuple-element.164), channel_id=1, source_target_pairs={{8,0},{12,4},{16,8},{20,12},{24,16},{28,20},{9,1},{13,5},{17,9},{2... | collective-permute-start | bytes 3145736 | tf_op jit(solution)/shard_map/ppermute | solution.py:370
  255.7 35.4 %collective-permute-start.23 = (bf16[512,1024]{1,0:T(8,128)(2,1)}, bf16[512,1024]{1,0:T(8,128)(2,1)}, u32[]{:S(2)}, u32[]{:S(2)}) collective-permute-start(bf16[512,1024]{1,0:T(8,128)(2,1)} %get-tuple-element.162), channel_id=1, source_target_pairs={{0,8},{4,12},{8,16},{12,20},{16,24},{20,28},{1,9},{5,13},{9,17},{1... | collective-permute-start | bytes 3145736 | tf_op jit(solution)/shard_map/ppermute | solution.py:370
  257.6 10.3 %copy-start.3 = (bf16[1024,1024]{1,0:T(8,128)(2,1)S(1)}, bf16[1024,1024]{1,0:T(8,128)(2,1)}, u32[]{:S(2)}) copy-start(bf16[1024,1024]{1,0:T(8,128)(2,1)} %shard_map.115.own_ref) | copy-start | bytes 6291460
  257.6 33.4 %collective-permute-start.24 = (bf16[512,1024]{1,0:T(8,128)(2,1)}, bf16[512,1024]{1,0:T(8,128)(2,1)}, u32[]{:S(2)}, u32[]{:S(2)}) collective-permute-start(bf16[512,1024]{1,0:T(8,128)(2,1)} %get-tuple-element.161), channel_id=1, source_target_pairs={{8,0},{12,4},{16,8},{20,12},{24,16},{28,20},{9,1},{13,5},{17,9},{2... | collective-permute-start | bytes 3145736 | tf_op jit(solution)/shard_map/ppermute | solution.py:370
  265.9 29.2 %collective-permute-start.25 = (bf16[128,1024]{1,0:T(8,128)(2,1)S(1)}, bf16[128,1024]{1,0:T(8,128)(2,1)S(1)}, u32[]{:S(2)}, u32[]{:S(2)}) collective-permute-start(bf16[128,1024]{1,0:T(8,128)(2,1)S(1)} %get-tuple-element.147), channel_id=1, source_target_pairs={{4,0},{8,4},{12,8},{16,12},{20,16},{24,20},{28,24},{5,1},{9,5},{13... | collective-permute-start | bytes 786440 | tf_op jit(solution)/shard_map/ppermute | solution.py:370
  280.5 1.3 copy-start.17
  282.7 22.9 %all-to-all-start = ((f32[8,16,128]{2,1,0:T(8,128)}), f32[8,16,128]{2,1,0:T(8,128)S(1)}, u32[]{:S(2)}, u32[]{:S(2)}) async-start(f32[8,16,128]{2,1,0:T(8,128)} %bitcast.20), calls=%async_computation | async-start | bytes 131072 | tf_op jit(solution)/shard_map/all_to_all | solution.py:557
  287.4 18.8 %collective-permute-start.20 = (bf16[128,1024]{1,0:T(8,128)(2,1)S(1)}, bf16[128,1024]{1,0:T(8,128)(2,1)S(1)}, u32[]{:S(2)}, u32[]{:S(2)}) collective-permute-start(bf16[128,1024]{1,0:T(8,128)(2,1)S(1)} %get-tuple-element.143), channel_id=1, source_target_pairs={{4,0},{8,4},{12,8},{16,12},{20,16},{24,20},{28,24},{5,1},{9,5},{13... | collective-permute-start | bytes 786440 | tf_op jit(solution)/shard_map/ppermute | solution.py:370
  291.0 2.6 copy-start.21
  306.2 1.6 copy-start.18
Sparse Core Ops, SparseCore 0:
  11.4 34.6 all-gather.4
  58.5 33.7 all-gather.6
